TPU v7x, 32 devices: a whole 2x2x4 slice. The times are simulated.
32 devices in a mesh: rep: 16 (over z, y, core), inner: 2 (over x).
Axes of the slice: x: 2, y: 2, z: 4, core: 2. Of those that a mesh axis runs over, the one named last changes fastest.
Arguments:
- hidden: bfloat16 [16, 2048, 768], P('rep', 'inner'), may hold values from -6 to 6
- frames: bfloat16 [16, 1500, 768], P('rep', None, 'inner'), may hold values from -6 to 6
- segment: int32 [16, 2048], P('rep'), may hold values from 0 to 8, as said below
- cotangent: bfloat16 [16, 2048, 768], P('rep', 'inner'), may hold values from -8.4 to 8.4
- norm_gain: float32 [4, 768], P(None, 'inner'), may hold values from 0.5 to 1.5
- norm_bias: float32 [4, 768], P(None, 'inner'), may hold values from -1.2 to 1.2
- self_qkv: float32 [768, 2304], P('inner'), may hold values from -0.21875 to 0.21875
- self_out: float32 [768, 768], P('inner'), may hold values from -1.5 to 1.5
- cross_q: float32 [768, 768], P('inner'), may hold values from -0.21875 to 0.21875
- cross_kv: float32 [768, 1536], P(None, 'inner'), may hold values from -0.21875 to 0.21875
- cross_out: float32 [768, 768], P('inner'), may hold values from -1.5 to 1.5
- fc1: float32 [768, 3072], P('inner'), may hold values from -0.21875 to 0.21875
- fc2: float32 [3072, 768], P('inner'), may hold values from -0.109375 to 0.109375
- proj_bias: float32 [7, 768], P(None, 'inner'), may hold values from -1.2 to 1.2
- fc1_bias: float32 [3072], P('inner'), may hold values from -1.2 to 1.2
Outputs:
- output: bfloat16 [16, 2048, 768], P('rep', 'inner')
- grad_hidden: bfloat16 [16, 2048, 768], P('rep', 'inner')
- grad_frames: bfloat16 [16, 1500, 768], P('rep', None, 'inner')
- grad_norm_gain: float32 [4, 768], P(None, 'inner')
- grad_norm_bias: float32 [4, 768], P(None, 'inner')
- grad_self_qkv: float32 [768, 2304], P('inner')
- grad_self_out: float32 [768, 768], P('inner')
- grad_cross_q: float32 [768, 768], P('inner')
- grad_cross_kv: float32 [768, 1536], P(None, 'inner')
- grad_cross_out: float32 [768, 768], P('inner')
- grad_fc1: float32 [768, 3072], P('inner')
- grad_fc2: float32 [3072, 768], P('inner')
- grad_proj_bias: float32 [7, 768], P(None, 'inner')
- grad_fc1_bias: float32 [3072], P('inner')
Inputs may be any that keep to these rules, and one draw needn't show every extreme that they name: `segment`: in every group the first 1024 tokens have id 0; the other 1024 tokens hold continuations 1 to 8 in order, ids never falling; each continuation has 64 to 192 tokens, and in every group one has exactly 192.
All inputs are finite; a program needn't handle non-finite values.
Results may differ from a plain program's by a relative error of at most 0.017.
The roundings to bfloat16 on the way count: a program that leaves them out, or rounds other values in their place, can miss the bound.
Values may be sent and summed in bfloat16 or wider, within the bound.
No kernel may reach another device: no remote copies, remote signals or barrier semaphores. Data moves between devices by JAX's collectives and lax.ppermute only.
A program may use at most 320 MiB of HBM per device.

v0:
```python
import math

import jax
import jax.numpy as jnp
from jax import lax
from jax.sharding import PartitionSpec as P

HEADS = 12


EPSILON = 1e-05
NEGATIVE = -1e30


def layer_norm(hidden_rows, gain_row, shift_row):
    centered = hidden_rows - jnp.mean(hidden_rows, axis=-1, keepdims=True)
    variance = jnp.mean(centered * centered, axis=-1, keepdims=True)
    return centered * lax.rsqrt(variance + EPSILON) * gain_row + shift_row


def exact_gelu(values):
    return jax.nn.gelu(values, approximate=False)


def product(first_matrix, second_matrix):
    return jnp.dot(first_matrix, second_matrix, preferred_element_type=jnp.float32)


def product_inner(first_matrix, second_matrix):
    return jnp.einsum("tm,tn->mn", first_matrix, second_matrix, preferred_element_type=jnp.float32)


def product_back(first_matrix, second_matrix):
    return jnp.einsum("tm,nm->tn", first_matrix, second_matrix, preferred_element_type=jnp.float32)


def split_heads(rows_value, head_count):
    return rows_value.reshape(rows_value.shape[0], head_count, -1).transpose(1, 0, 2)


def join_heads(stacked):
    return stacked.transpose(1, 0, 2).reshape(stacked.shape[1], -1)


def attend_forward(queries, key_heads, value_heads, allowed):
    score_scale = queries.shape[-1] ** (-0.5)

    def one_head(triple):
        query_head, key_head, value_head = triple
        scores = (
            jnp.einsum("qd,kd->qk", query_head, key_head, preferred_element_type=jnp.float32)
            * score_scale
        )
        if allowed is not None:
            scores = jnp.where(allowed, scores, NEGATIVE)
        row_top = jnp.max(scores, axis=1, keepdims=True)
        raised = jnp.exp(scores - row_top)
        row_total = jnp.sum(raised, axis=1, keepdims=True)
        soft_weights = (raised / row_total).astype(jnp.bfloat16)
        return (product(soft_weights, value_head), (row_top + jnp.log(row_total))[:, 0])

    return lax.map(one_head, (queries, key_heads, value_heads))


def attend_backward(queries, key_heads, value_heads, allowed, log_totals, grad_out):
    score_scale = queries.shape[-1] ** (-0.5)

    def one_head(bundle):
        query_head, key_head, value_head, log_total, grad_head = bundle
        scores = (
            jnp.einsum("qd,kd->qk", query_head, key_head, preferred_element_type=jnp.float32)
            * score_scale
        )
        if allowed is not None:
            scores = jnp.where(allowed, scores, NEGATIVE)
        soft_weights = jnp.exp(scores - log_total[:, None])
        value_grads = jnp.einsum(
            "qk,qd->kd",
            soft_weights.astype(jnp.bfloat16),
            grad_head,
            preferred_element_type=jnp.float32,
        )
        weight_grads = jnp.einsum(
            "qd,kd->qk", grad_head, value_head, preferred_element_type=jnp.float32
        )
        row_dot = jnp.sum(weight_grads * soft_weights, axis=1, keepdims=True)
        score_grads = (soft_weights * (weight_grads - row_dot)).astype(jnp.bfloat16)
        query_grads = product(score_grads, key_head) * score_scale
        key_grads = (
            jnp.einsum("qk,qd->kd", score_grads, query_head, preferred_element_type=jnp.float32)
            * score_scale
        )
        return (query_grads, key_grads, value_grads)

    return lax.map(one_head, (queries, key_heads, value_heads, log_totals, grad_out))


def row_blocks(matrix, shard_count):
    return matrix.reshape(shard_count, -1)


def column_blocks(matrix, shard_count):
    return (
        matrix.reshape(matrix.shape[0], shard_count, -1).transpose(1, 0, 2).reshape(shard_count, -1)
    )


def unpack(flat, targets):
    pieces = []
    offset = 0
    for target in targets:
        count = math.prod(target)
        pieces.append(flat[offset : offset + count].reshape(target))
        offset += count
    return pieces


def body(
    hidden,
    frames,
    segment,
    cotangent,
    norm_gain,
    norm_bias,
    self_qkv,
    self_out,
    cross_q,
    cross_kv,
    cross_out,
    fc1,
    fc2,
    proj_bias,
    fc1_bias,
):
    shard_count = lax.axis_size("inner")
    inner_index = lax.axis_index("inner")
    own_rows = hidden.shape[1]
    all_rows = segment.shape[1]
    model_width = self_out.shape[1]
    kv_width = cross_kv.shape[1]
    head_count = HEADS
    bf16 = jnp.bfloat16
    f32 = jnp.float32
    (
        qkv_full,
        selfout_full,
        crossq_full,
        crossout_full,
        fc1_full,
        fc2_full,
        gain_half,
        shift_half,
        bias_half,
        fc1_half,
    ) = (
        lax.all_gather(self_qkv.astype(bf16), "inner", axis=0, tiled=True),
        lax.all_gather(self_out.astype(bf16), "inner", axis=0, tiled=True),
        lax.all_gather(cross_q.astype(bf16), "inner", axis=0, tiled=True),
        lax.all_gather(cross_out.astype(bf16), "inner", axis=0, tiled=True),
        lax.all_gather(fc1.astype(bf16), "inner", axis=0, tiled=True),
        lax.all_gather(fc2.astype(bf16), "inner", axis=0, tiled=True),
        lax.all_gather(norm_gain.astype(bf16), "inner", axis=1, tiled=True),
        lax.all_gather(norm_bias.astype(bf16), "inner", axis=1, tiled=True),
        lax.all_gather(proj_bias.astype(bf16), "inner", axis=1, tiled=True),
        lax.all_gather(fc1_bias.astype(bf16), "inner", axis=0, tiled=True),
    )
    gain_rows = gain_half.astype(f32)
    shifts = shift_half.astype(f32)
    biases = bias_half.astype(f32)
    fc1_shift = fc1_half.astype(f32)
    inputs = hidden[0].astype(f32)
    seg_all = segment[0]
    own_start = inner_index * own_rows
    seg_own = lax.dynamic_slice_in_dim(seg_all, own_start, own_rows)
    query_pos = own_start + jnp.arange(own_rows, dtype=jnp.int32)
    zeros_row = jnp.zeros((model_width,), f32)
    normed_one = layer_norm(inputs, gain_rows[0], shifts[0]).astype(bf16)
    qkv_bias = jnp.concatenate([biases[0], zeros_row, biases[1]])
    projected = (product(normed_one, qkv_full) + qkv_bias).astype(bf16)
    self_query = projected[:, :model_width]
    own_keys = projected[:, model_width : 2 * model_width]
    own_values = projected[:, 2 * model_width :]
    query_heads = split_heads(self_query, head_count)
    key_pos = jnp.arange(all_rows, dtype=jnp.int32)
    self_allowed = (key_pos[None, :] <= query_pos[:, None]) & (
        (seg_all[None, :] == seg_own[:, None]) | (seg_all[None, :] == 0)
    )
    all_keys, all_values = (
        lax.all_gather(own_keys, "inner", axis=0, tiled=True),
        lax.all_gather(own_values, "inner", axis=0, tiled=True),
    )
    key_heads = split_heads(all_keys, head_count)
    value_heads = split_heads(all_values, head_count)
    self_mixed, self_lse = attend_forward(query_heads, key_heads, value_heads, self_allowed)
    self_context = join_heads(self_mixed).astype(bf16)
    after_self = inputs + product(self_context, selfout_full) + biases[2]
    normed_two = layer_norm(after_self, gain_rows[1], shifts[1]).astype(bf16)
    cross_query = (product(normed_two, crossq_full) + biases[3]).astype(bf16)
    frame_rows = lax.all_gather(frames, "inner", axis=2, tiled=True)[0]
    kv_bias = lax.dynamic_slice_in_dim(
        jnp.concatenate([zeros_row, biases[4]]), inner_index * kv_width, kv_width
    )
    kv_weight = cross_kv.astype(bf16)
    own_frame_kv = (product(frame_rows, kv_weight) + kv_bias).astype(bf16)
    frame_kv = lax.all_gather(own_frame_kv, "inner", axis=1, tiled=True)
    cross_heads = split_heads(cross_query, head_count)
    frame_keys = split_heads(frame_kv[:, :model_width], head_count)
    frame_values = split_heads(frame_kv[:, model_width:], head_count)
    cross_mixed, cross_lse = attend_forward(cross_heads, frame_keys, frame_values, None)
    cross_context = join_heads(cross_mixed).astype(bf16)
    after_cross = after_self + product(cross_context, crossout_full) + biases[5]
    normed_three = layer_norm(after_cross, gain_rows[2], shifts[2]).astype(bf16)
    hidden_units = (product(normed_three, fc1_full) + fc1_shift).astype(bf16)
    activated = exact_gelu(hidden_units.astype(f32)).astype(bf16)
    after_mlp = after_cross + product(activated, fc2_full) + biases[6]
    output_rows = layer_norm(after_mlp, gain_rows[3], shifts[3])
    (
        qkv_use,
        selfout_use,
        crossq_use,
        crossout_use,
        fc1_use,
        fc2_use,
        gain_again,
        shift_again,
        bias_again,
        fc1_again,
    ) = (
        lax.all_gather(self_qkv.astype(bf16), "inner", axis=0, tiled=True),
        lax.all_gather(self_out.astype(bf16), "inner", axis=0, tiled=True),
        lax.all_gather(cross_q.astype(bf16), "inner", axis=0, tiled=True),
        lax.all_gather(cross_out.astype(bf16), "inner", axis=0, tiled=True),
        lax.all_gather(fc1.astype(bf16), "inner", axis=0, tiled=True),
        lax.all_gather(fc2.astype(bf16), "inner", axis=0, tiled=True),
        lax.all_gather(norm_gain.astype(bf16), "inner", axis=1, tiled=True),
        lax.all_gather(norm_bias.astype(bf16), "inner", axis=1, tiled=True),
        lax.all_gather(proj_bias.astype(bf16), "inner", axis=1, tiled=True),
        lax.all_gather(fc1_bias.astype(bf16), "inner", axis=0, tiled=True),
    )
    gain_use = gain_again.astype(f32)
    shift_use = shift_again.astype(f32)
    cot_rows = cotangent[0].astype(f32)
    _, pull_four = jax.vjp(layer_norm, after_mlp, gain_use[3], shift_use[3])
    grad_mlp_res, gain_four, shift_four = pull_four(cot_rows)
    grad_branch = grad_mlp_res.astype(bf16)
    grad_fc2 = product_inner(activated, grad_branch)
    grad_activated = product_back(grad_branch, fc2_use)
    _, pull_gelu = jax.vjp(exact_gelu, hidden_units.astype(f32))
    grad_units = pull_gelu(grad_activated)[0].astype(bf16)
    grad_fc1 = product_inner(normed_three, grad_units)
    grad_normed = product_back(grad_units, fc1_use)
    _, pull_three = jax.vjp(layer_norm, after_cross, gain_use[2], shift_use[2])
    part_rows, gain_three, shift_three = pull_three(grad_normed)
    grad_cross_res = grad_mlp_res + part_rows
    cross_branch = grad_cross_res.astype(bf16)
    grad_crossout = product_inner(cross_context, cross_branch)
    grad_context = product_back(cross_branch, crossout_use).astype(bf16)
    query_grads, key_grads, value_grads = attend_backward(
        cross_heads,
        frame_keys,
        frame_values,
        None,
        cross_lse,
        split_heads(grad_context, head_count),
    )
    grad_cross_query = join_heads(query_grads).astype(bf16)
    kv_partial = jnp.concatenate([join_heads(key_grads), join_heads(value_grads)], axis=1)
    grad_own_kv = (
        lax.psum_scatter(kv_partial.astype(jnp.bfloat16), "inner", scatter_dimension=1, tiled=True)
        .astype(jnp.float32)
        .astype(bf16)
    )
    grad_kv_weight = product_inner(frame_rows, grad_own_kv)
    kv_column_sums = jnp.sum(grad_own_kv.astype(f32), axis=0)
    frame_partial = product_back(grad_own_kv, kv_weight)
    grad_frame_own = (
        lax.psum_scatter(
            frame_partial.astype(jnp.bfloat16), "inner", scatter_dimension=1, tiled=True
        )
        .astype(jnp.float32)
        .astype(bf16)
    )
    grad_crossq = product_inner(normed_two, grad_cross_query)
    grad_normed = product_back(grad_cross_query, crossq_use)
    _, pull_two = jax.vjp(layer_norm, after_self, gain_use[1], shift_use[1])
    part_rows, gain_two, shift_two = pull_two(grad_normed)
    grad_self_res = grad_cross_res + part_rows
    self_branch = grad_self_res.astype(bf16)
    grad_selfout = product_inner(self_context, self_branch)
    grad_context = product_back(self_branch, selfout_use).astype(bf16)
    query_grads, key_grads, value_grads = attend_backward(
        query_heads,
        key_heads,
        value_heads,
        self_allowed,
        self_lse,
        split_heads(grad_context, head_count),
    )
    grad_own_keys, grad_own_values = (
        lax.psum_scatter(
            join_heads(key_grads).astype(jnp.bfloat16), "inner", scatter_dimension=0, tiled=True
        ).astype(jnp.float32),
        lax.psum_scatter(
            join_heads(value_grads).astype(jnp.bfloat16), "inner", scatter_dimension=0, tiled=True
        ).astype(jnp.float32),
    )
    grad_own_pair = jnp.concatenate([grad_own_keys, grad_own_values], axis=1).astype(bf16)
    grad_projected = jnp.concatenate([join_heads(query_grads).astype(bf16), grad_own_pair], axis=1)
    grad_qkv = product_inner(normed_one, grad_projected)
    grad_normed = product_back(grad_projected, qkv_use)
    _, pull_one = jax.vjp(layer_norm, inputs, gain_use[0], shift_use[0])
    part_rows, gain_one, shift_one = pull_one(grad_normed)
    grad_inputs = grad_self_res + part_rows
    projected_sums = jnp.sum(grad_projected.astype(f32), axis=0)
    placed_kv = lax.dynamic_update_slice(
        jnp.zeros((2 * model_width,), f32), kv_column_sums, (inner_index * kv_width,)
    )
    bias_grads = jnp.stack(
        [
            projected_sums[:model_width],
            projected_sums[2 * model_width :],
            jnp.sum(self_branch.astype(f32), axis=0),
            jnp.sum(grad_cross_query.astype(f32), axis=0),
            placed_kv[model_width:],
            jnp.sum(cross_branch.astype(f32), axis=0),
            jnp.sum(grad_branch.astype(f32), axis=0),
        ]
    )
    gain_grads = jnp.stack([gain_one, gain_two, gain_three, gain_four])
    shift_grads = jnp.stack([shift_one, shift_two, shift_three, shift_four])
    fc1_shift_grads = jnp.sum(grad_units.astype(f32), axis=0)
    blocks = jnp.concatenate(
        [
            row_blocks(grad_qkv, shard_count),
            row_blocks(grad_selfout, shard_count),
            row_blocks(grad_crossq, shard_count),
            row_blocks(grad_crossout, shard_count),
            row_blocks(grad_fc1, shard_count),
            row_blocks(grad_fc2, shard_count),
            column_blocks(gain_grads, shard_count),
            column_blocks(shift_grads, shard_count),
            column_blocks(bias_grads, shard_count),
            row_blocks(fc1_shift_grads, shard_count),
        ],
        axis=1,
    )
    flat_length = blocks.shape[1]
    slice_part, kv_part = (
        lax.psum_scatter(
            blocks.astype(jnp.bfloat16), "rep", scatter_dimension=1, tiled=True
        ).astype(jnp.float32),
        lax.psum_scatter(
            grad_kv_weight.astype(jnp.bfloat16), "rep", scatter_dimension=0, tiled=True
        ).astype(jnp.float32),
    )
    slice_part = lax.psum_scatter(
        slice_part.astype(jnp.bfloat16), "inner", scatter_dimension=0, tiled=True
    ).astype(jnp.float32)
    joined, kv_grad_final = (
        lax.all_gather(slice_part.astype(jnp.bfloat16), "rep", axis=1, tiled=True).astype(
            slice_part.dtype
        ),
        lax.all_gather(kv_part.astype(jnp.bfloat16), "rep", axis=0, tiled=True).astype(
            kv_part.dtype
        ),
    )
    flat = joined[0, :flat_length]
    targets = [
        self_qkv.shape,
        self_out.shape,
        cross_q.shape,
        cross_out.shape,
        fc1.shape,
        fc2.shape,
        norm_gain.shape,
        norm_bias.shape,
        proj_bias.shape,
        fc1_bias.shape,
    ]
    (
        qkv_grad,
        selfout_grad,
        crossq_grad,
        crossout_grad,
        fc1_grad,
        fc2_grad,
        gain_grad,
        shift_grad,
        bias_grad,
        fc1b_grad,
    ) = unpack(flat, targets)
    return (
        output_rows.astype(bf16)[None],
        grad_inputs.astype(bf16)[None],
        grad_frame_own[None],
        gain_grad,
        shift_grad,
        qkv_grad,
        selfout_grad,
        crossq_grad,
        kv_grad_final,
        crossout_grad,
        fc1_grad,
        fc2_grad,
        bias_grad,
        fc1b_grad,
    )


def solution(mesh):
    return jax.shard_map(
        body,
        mesh=mesh,
        in_specs=(
            P("rep", "inner", None),
            P("rep", None, "inner"),
            P("rep", None),
            P("rep", "inner", None),
            P(None, "inner"),
            P(None, "inner"),
            P("inner", None),
            P("inner", None),
            P("inner", None),
            P(None, "inner"),
            P("inner", None),
            P("inner", None),
            P("inner", None),
            P(None, "inner"),
            P("inner"),
        ),
        out_specs=(
            P("rep", "inner", None),
            P("rep", "inner", None),
            P("rep", None, "inner"),
            P(None, "inner"),
            P(None, "inner"),
            P("inner", None),
            P("inner", None),
            P("inner", None),
            P(None, "inner"),
            P("inner", None),
            P("inner", None),
            P("inner", None),
            P(None, "inner"),
            P("inner"),
        ),
        check_vma=False,
    )
```

profile of v0, /device:TPU:1, one launch (start us, length us, event | category | flops | bytes accessed | tf_op | source)
XLA Modules:
  0.0 2168.9 jit_solution(7149676556791409679)
XLA Ops:
  25.7 36.6 %all-gather.13.cloned.1.call-done = bf16[768,2304]{1,0:T(8,128)(2,1)} async-done(((bf16[384,2304]{1,0:T(8,128)(2,1)}), bf16[768,2304]{1,0:T(8,128)(2,1)}) %all-gather.13.cloned.1.call-update) | async-done | bytes 3538960 | tf_op jit(solution)/shard_map/all_gather | solution.py:156
  62.4 6.4 add_convert_fusion.1
  75.9 23.6 %all-gather.23.cloned.1.call-done = bf16[1,1500,768]{2,1,0:T(8,128)(2,1)} async-done(((bf16[1,1500,384]{2,1,0:T(8,128)(2,1)}), bf16[1,1500,768]{2,1,0:T(8,128)(2,1)}) %all-gather.23.cloned.1.call-update) | async-done | bytes 2304016 | tf_op jit(solution)/shard_map/all_gather | solution.py:199
  126.0 20.8 all-gather.15.cloned.1.call-done
  151.4 6.7 copy.84
  158.1 35.6 %all-gather.17.cloned.1.call-done = bf16[2048,768]{1,0:T(8,128)(2,1)} async-done(((bf16[1024,768]{1,0:T(8,128)(2,1)}), bf16[2048,768]{1,0:T(8,128)(2,1)}) %all-gather.17.cloned.1.call-update) | async-done | bytes 3145744 | tf_op jit(solution)/shard_map/all_gather | solution.py:190
  198.3 6.7 copy.85
  205.2 158.6 %while.56 = (s32[]{:T(128)}, bf16[12,1024,64]{1,2,0:T(8,128)(2,1)S(1)}, f32[12,1024]{1,0:T(8,128)S(1)}, bf16[12,1024,64]{2,1,0:T(8,128)(2,1)}, bf16[12,2048,64]{...) while((s32[]{:T(128)}, ...), condition=%wide.region_5.6_spmd.clone, body=%wide.region_2.5_spmd.clone.sunk | while | flops 562035712 | bytes 60354708 | solution.py:62
  252.2 6.3 fusion.272
  404.6 127.0 %while.54 = (s32[]{:T(128)}, bf16[12,1024,64]{1,2,0:T(8,128)(2,1)}, f32[12,1024]{1,0:T(8,128)S(1)}, bf16[12,1024,64]{2,1,0:T(8,128)(2,1)S(1)}, bf16[12,1500,64]{...) while((s32[]{:T(128)}, bf16[12,1024,64]{1,2,0:T(8,128)(2,1)}, ...), condition=%wide.region_11.12_spmd, body=%wide.region_8.11_spmd.sunk | while | flops 407038976 | bytes 44361844 | solution.py:62
  538.3 37.1 %fusion.132 = (f32[1024,3072]{1,0:T(8,128)}, bf16[1024,3072]{1,0:T(8,128)(2,1)}) fusion(f32[3072]{0:T(1024)S(1)} %bitcast.376, bf16[768,3072]{1,0:T(8,128)(2,1)} %all-gather.29.cloned.1.call-done, f32[1024,768]{0,1:T(8,128)S(1)} %get-tuple-element.514, f32[768]{0:T(1024)S(1)} %copy-done.93, f32[768]{0:T(1024)S(1)} %copy-done.53, f32[1024]{0:T(1024)S(1)} %fusion.168, ...), kind=kOutput, calls=%fused_computation.147 | convolution fusion | flops 5040242688 | bytes 26765312 | tf_op jit(solution)/shard_map/dot_general | solution.py:26
  575.5 10.6 fusion.191
  592.3 15.4 fusion.195
  607.7 11.9 fusion.192
  638.5 159.0 %while.55 = (s32[]{:T(128)}, bf16[12,1024,64]{1,2,0:T(8,128)(2,1)}, bf16[12,1500,64]{1,2,0:T(8,128)(2,1)}, bf16[12,1500,64]{1,2,0:T(8,128)(2,1)}, bf16[12,1024,6...) while((s32[]{:T(128)}, bf16[12,1024,64]{1,2,0:T(8,128)(2,1)}, ...), condition=%wide.region_22.23_spmd, body=%wide.region_20.22_spmd.sunk | while | flops 995488512 | bytes 49390696 | solution.py:95
  819.4 325.6 %while.57 = (s32[]{:T(128)}, bf16[12,1024,64]{1,2,0:T(8,128)(2,1)}, bf16[12,2048,64]{1,2,0:T(8,128)(2,1)}, bf16[12,2048,64]{1,2,0:T(8,128)(2,1)}, bf16[12,1024,6...) while((s32[]{:T(128)}, bf16[12,1024,64]{1,2,0:T(8,128)(2,1)}, ...), condition=%wide.region_27.28_spmd.clone, body=%wide.region_25.27_spmd.clone.sunk | while | flops 1369635840 | bytes 146582784 | solution.py:95
  831.6 6.6 multiply_convert_fusion.5
  858.7 6.6 multiply_convert_fusion.5
  885.8 6.6 multiply_convert_fusion.5
  912.9 6.6 multiply_convert_fusion.5
  940.0 6.6 multiply_convert_fusion.5
  967.2 6.6 multiply_convert_fusion.5
  994.3 6.6 multiply_convert_fusion.5
  1021.4 6.6 multiply_convert_fusion.5
  1048.5 6.6 multiply_convert_fusion.5
  1075.7 6.6 multiply_convert_fusion.5
  1102.8 6.6 multiply_convert_fusion.5
  1129.9 6.6 multiply_convert_fusion.5
  1147.4 12.6 convolution_convert_fusion
  1165.9 9.9 convolution_convert_fusion.1
  1175.8 8.1 reshape.424
  1208.9 25.5 %reduce-scatter.13.cloned.1.call-done = bf16[1024,768]{0,1:T(8,128)(2,1)} async-done(((bf16[2048,768]{0,1:T(8,128)(2,1)}), bf16[1024,768]{0,1:T(8,128)(2,1)}) %reduce-scatter.13.cloned.1.call-update) | async-done | bytes 1572880 | tf_op jit(solution)/shard_map/reduce_scatter | solution.py:303
  1234.5 7.8 convolution_convert_fusion.2
  1247.5 7.8 constant_dynamic-update-slice_fusion.16
  1272.2 8.5 fusion.194
  1289.8 7.5 reduce-scatter.15.cloned.1.call-done
  1308.7 288.4 %all-reduce.10.cloned.1.call-done = bf16[2,4136064]{1,0:T(2,128)(2,1)} async-done(((bf16[2,4136064]{1,0:T(2,128)(2,1)}), bf16[2,4136064]{1,0:T(2,128)(2,1)}) %all-reduce.10.cloned.1.call-update) | async-done | bytes 16544272
  1600.3 57.0 %reduce-scatter.19.cloned.1.call-done = bf16[48,768]{1,0:T(8,128)(2,1)} async-done(((bf16[768,768]{1,0:T(8,128)(2,1)}), bf16[48,768]{1,0:T(8,128)(2,1)}) %reduce-scatter.19.cloned.1.call-update) | async-done | bytes 73744 | tf_op jit(solution)/shard_map/reduce_scatter | solution.py:352
  1669.0 31.8 %all-reduce.12.cloned.1.call-done = bf16[2,258504]{1,0:T(2,128)(2,1)} async-done(((bf16[2,258504]{1,0:T(2,128)(2,1)}), bf16[2,258504]{1,0:T(2,128)(2,1)}) %all-reduce.12.cloned.1.call-update) | async-done | bytes 1034032
  1700.7 12.4 dynamic-slice_reduce_fusion
  1716.8 8.7 dynamic-update-slice
  1735.4 6.6 all-gather.33.cloned.1.call-done
  1744.8 33.1 %reduce-scatter.17.cloned.1.call-done = bf16[384,1500]{1,0:T(8,128)(2,1)} async-done(((bf16[768,1500]{1,0:T(8,128)(2,1)}), bf16[384,1500]{1,0:T(8,128)(2,1)}) %reduce-scatter.17.cloned.1.call-update) | async-done | bytes 1152016
  1780.3 170.8 %all-reduce.8.cloned.1.call-done = bf16[4136064]{0:T(1024)(128)(2,1)} async-done(((bf16[4136064]{0:T(1024)(128)(2,1)}), bf16[4136064]{0:T(1024)(128)(2,1)}) %all-reduce.8.cloned.1.call-update) | async-done | bytes 8272144
  1951.1 79.8 %reshape.445 = f32[1,4136064]{1,0:T(1,128)} reshape(bf16[4136064]{0:T(1024)(128)(2,1)} %all-reduce.8.cloned.1.call-done) | data formatting | bytes 24816384 | tf_op jit(solution)/shard_map/convert_element_type | solution.py:360
  2030.9 54.4 %slice_reduce_fusion = (f32[1179648]{0:T(1024)}, f32[1179648]{0:T(1024)}) fusion(f32[1,4136064]{1,0:T(1,128)} %reshape.445), kind=kLoop, calls=%fused_computation.157 | loop fusion | bytes 18874368 | tf_op jit(solution)/shard_map/slice | solution.py:113
  2085.3 37.6 %slice_reduce_fusion.2 = f32[884736]{0:T(1024)S(1)} fusion(f32[1,4136064]{1,0:T(1,128)} %reshape.445), kind=kLoop, calls=%fused_computation.177 | loop fusion | bytes 7077888 | tf_op jit(solution)/shard_map/slice | solution.py:113
  2122.9 15.8 slice_reduce_fusion.3
  (843 shorter events, 968.8 us)
Async XLA Ops:
  7.2 55.2 %all-gather.13.cloned.1.call-start = ((), (), s32[]{:S(2)}) async-start(), calls=%async_computation.5 | async-start | bytes 5308416 | tf_op jit(solution)/shard_map/all_gather | solution.py:156
  10.7 9.8 copy-start.87
  10.8 88.8 %all-gather.23.cloned.1.call-start = ((), (), s32[]{:S(2)}) async-start(), calls=%async_computation.10 | async-start | bytes 3465216 | tf_op jit(solution)/shard_map/all_gather | solution.py:199
  11.5 135.2 %all-gather.15.cloned.1.call-start = ((), (), s32[]{:S(2)}) async-start(), calls=%async_computation.6 | async-start | bytes 4718592 | tf_op jit(solution)/shard_map/all_gather | solution.py:189
  12.3 351.5 %copy-start.4 = (bf16[1,1024,768]{1,2,0:T(8,128)(2,1)}, bf16[1,1024,768]{1,2,0:T(8,128)(2,1)S(1)}, u32[]{:S(2)}) copy-start(bf16[1,1024,768]{1,2,0:T(8,128)(2,1)S(1)} %copy.79) | copy-start | bytes 4718596
  20.6 48.2 %copy-start.51 = (f32[768]{0:T(1024)}, f32[768]{0:T(1024)S(1)}, u32[]{:S(2)}) copy-start(f32[768]{0:T(1024)S(1)} %get-tuple-element.402) | copy-start | bytes 9220
  20.6 349.5 %copy-start.68 = (f32[768]{0:T(1024)}, f32[768]{0:T(1024)S(1)}, u32[]{:S(2)}) copy-start(f32[768]{0:T(1024)S(1)} %get-tuple-element.401) | copy-start | bytes 9220
  24.4 44.4 %copy-start.89 = (f32[768]{0:T(1024)}, f32[768]{0:T(1024)S(1)}, u32[]{:S(2)}) copy-start(f32[768]{0:T(1024)S(1)} %get-tuple-element.406) | copy-start | bytes 9220
  24.4 345.7 %copy-start.91 = (f32[768]{0:T(1024)}, f32[768]{0:T(1024)S(1)}, u32[]{:S(2)}) copy-start(f32[768]{0:T(1024)S(1)} %get-tuple-element.405) | copy-start | bytes 9220
  24.7 44.1 %copy-start.46 = (f32[1024]{0:T(1024)}, f32[1024]{0:T(1024)S(1)}, u32[]{:S(2)}) copy-start(f32[1024]{0:T(1024)S(1)} %broadcast_multiply_fusion.3) | copy-start | bytes 12292
  25.7 43.1 %copy-start.58 = (f32[1024]{0:T(1024)}, f32[1024]{0:T(1024)S(1)}, u32[]{:S(2)}) copy-start(f32[1024]{0:T(1024)S(1)} %fusion.166) | copy-start | bytes 12292
  71.1 122.6 %all-gather.17.cloned.1.call-start = ((), (), s32[]{:S(2)}) async-start(), calls=%async_computation.7 | async-start | bytes 4718592 | tf_op jit(solution)/shard_map/all_gather | solution.py:190
  71.7 292.1 %all-gather.19.cloned.1.call-start = ((), (), s32[]{:S(2)}) async-start(), calls=%async_computation.8 | async-start | bytes 1769472 | tf_op jit(solution)/shard_map/all_gather | solution.py:157
  73.4 296.6 %all-gather.21.cloned.1.call-start = ((), (), s32[]{:S(2)}) async-start(), calls=%async_computation.9 | async-start | bytes 1769472 | tf_op jit(solution)/shard_map/all_gather | solution.py:158
  75.8 302.4 %all-gather.25.cloned.1.call-start = ((), (), s32[]{:S(2)}) async-start(), calls=%async_computation.11 | async-start | bytes 6930432 | tf_op jit(solution)/shard_map/all_gather | solution.py:205
  75.9 29.4 %copy-start.43 = (f32[384,768]{1,0:T(8,128)S(1)}, f32[384,768]{1,0:T(8,128)}, u32[]{:S(2)}) copy-start(f32[384,768]{1,0:T(8,128)} %param.33) | copy-start | bytes 3538948
  105.3 426.4 %all-gather.27.cloned.1.call-start = ((), (), s32[]{:S(2)}) async-start(), calls=%async_computation.12 | async-start | bytes 1769472 | tf_op jit(solution)/shard_map/all_gather | solution.py:159
  106.2 431.8 %all-gather.29.cloned.1.call-start = ((), (), s32[]{:S(2)}) async-start(), calls=%async_computation.13 | async-start | bytes 7077888 | tf_op jit(solution)/shard_map/all_gather | solution.py:160
  110.7 9.2 copy-start.25
  110.7 464.8 %all-gather.31.cloned.1.call-start = ((), (), s32[]{:S(2)}) async-start(), calls=%async_computation.14 | async-start | bytes 7077888 | tf_op jit(solution)/shard_map/all_gather | solution.py:161
  115.2 1093.7 %reduce-scatter.11.cloned.1.call-start = ((), (), s32[]{:S(2)}) async-start(), calls=%async_computation.15 | async-start | bytes 4718592 | tf_op jit(solution)/shard_map/reduce_scatter | solution.py:300
  404.6 128.7 %copy-start.96 = (f32[768]{0:T(1024)S(1)}, f32[768]{0:T(1024)}, u32[]{:S(2)}) copy-start(f32[768]{0:T(1024)} %get-tuple-element.393) | copy-start | bytes 9220
  537.6 90.4 %copy-start.6 = (f32[1024,768]{0,1:T(8,128)}, f32[1024,768]{0,1:T(8,128)S(1)}, u32[]{:S(2)}) copy-start(f32[1024,768]{0,1:T(8,128)S(1)} %get-tuple-element.514) | copy-start | bytes 9437188
  537.6 90.4 %copy-start.49 = (f32[1024]{0:T(1024)}, f32[1024]{0:T(1024)S(1)}, u32[]{:S(2)}) copy-start(f32[1024]{0:T(1024)S(1)} %broadcast_multiply_fusion.1) | copy-start | bytes 12292
  538.0 90.0 %copy-start.62 = (f32[1024]{0:T(1024)}, f32[1024]{0:T(1024)S(1)}, u32[]{:S(2)}) copy-start(f32[1024]{0:T(1024)S(1)} %fusion.168) | copy-start | bytes 12292
  538.3 37.2 %copy-start.95 = (f32[768]{0:T(1024)S(1)}, f32[768]{0:T(1024)}, u32[]{:S(2)}) copy-start(f32[768]{0:T(1024)} %get-tuple-element.392) | copy-start | bytes 9220
  575.5 10.6 copy-start.12
  575.5 10.6 copy-start.48
  592.3 15.4 copy-start.40
  607.7 11.9 copy-start.108
  1145.0 89.4 %reduce-scatter.13.cloned.1.call-start = ((), (), s32[]{:S(2)}) async-start(), calls=%async_computation.16 | async-start | bytes 4718592 | tf_op jit(solution)/shard_map/reduce_scatter | solution.py:303
  1145.6 151.8 %reduce-scatter.15.cloned.1.call-start = ((), (), s32[]{:S(2)}) async-start(), calls=%async_computation.17 | async-start | bytes 7077888 | tf_op jit(solution)/shard_map/reduce_scatter | solution.py:269
  1175.8 8.1 copy-start.19
  1175.8 8.1 copy-start.57
  1175.8 8.1 copy-start.70
  1208.8 25.7 %copy-start.5 = (bf16[1,1024,768]{1,2,0:T(8,128)(2,1)S(1)}, bf16[1,1024,768]{1,2,0:T(8,128)(2,1)}, u32[]{:S(2)}) copy-start(bf16[1,1024,768]{1,2,0:T(8,128)(2,1)} %copy-done.4) | copy-start | bytes 4718596
  1208.8 25.7 %copy-start.28 = (bf16[12,1024,64]{1,2,0:T(8,128)(2,1)S(1)}, bf16[12,1024,64]{1,2,0:T(8,128)(2,1)}, u32[]{:S(2)}) copy-start(bf16[12,1024,64]{1,2,0:T(8,128)(2,1)} %get-tuple-element.193) | copy-start | bytes 4718596
  1208.8 25.7 %copy-start.47 = (f32[1024]{0:T(1024)S(1)}, f32[1024]{0:T(1024)}, u32[]{:S(2)}) copy-start(f32[1024]{0:T(1024)} %copy-done.46) | copy-start | bytes 12292
  1208.8 25.7 %copy-start.52 = (f32[768]{0:T(1024)S(1)}, f32[768]{0:T(1024)}, u32[]{:S(2)}) copy-start(f32[768]{0:T(1024)} %copy-done.51) | copy-start | bytes 9220
  1208.8 25.7 %copy-start.59 = (f32[1024]{0:T(1024)S(1)}, f32[1024]{0:T(1024)}, u32[]{:S(2)}) copy-start(f32[1024]{0:T(1024)} %copy-done.58) | copy-start | bytes 12292
  1208.8 25.7 %copy-start.90 = (f32[768]{0:T(1024)S(1)}, f32[768]{0:T(1024)}, u32[]{:S(2)}) copy-start(f32[768]{0:T(1024)} %copy-done.89) | copy-start | bytes 9220
  1208.8 388.3 %all-reduce.10.cloned.1.call-start = ((), (), s32[]{:S(2)}) async-start(), calls=%async_computation.22 | async-start | bytes 33088512
  1247.5 9.9 copy-start.32
  1301.0 356.3 %reduce-scatter.19.cloned.1.call-start = ((), (), s32[]{:S(2)}) async-start(), calls=%async_computation.21 | async-start | bytes 1253376 | tf_op jit(solution)/shard_map/reduce_scatter | solution.py:352
  1308.7 392.1 %all-reduce.12.cloned.1.call-start = ((), (), s32[]{:S(2)}) async-start(), calls=%async_computation.23 | async-start | bytes 2068480
  1600.2 141.8 %all-gather.33.cloned.1.call-start = ((), (), s32[]{:S(2)}) async-start(), calls=%async_computation.18 | async-start | bytes 1253376 | tf_op jit(solution)/shard_map/all_gather | solution.py:363
  1657.3 120.7 %reduce-scatter.17.cloned.1.call-start = ((), (), s32[]{:S(2)}) async-start(), calls=%async_computation.20 | async-start | bytes 3538944
  1667.7 283.4 %all-reduce.8.cloned.1.call-start = ((), (), s32[]{:S(2)}) async-start(), calls=%async_computation.19 | async-start | bytes 16547840
  (148 other events, 591.0 us)
Sparse Core Ops, SparseCore 0:
  10.9 51.4 all-gather.12
  63.9 35.5 all-gather.22
  101.6 45.0 all-gather.14
  148.7 44.9 all-gather.16
  195.7 22.7 all-gather.18
  220.4 22.7 all-gather.20
  245.4 61.5 all-gather.24
  309.1 22.7 all-gather.26
  333.4 62.6 all-gather.28
  397.5 62.6 all-gather.30
  1145.1 43.7 reduce-scatter.10
  1191.1 43.3 reduce-scatter.12
  1237.3 59.9 reduce-scatter.14
  1301.7 295.4 all-reduce.9
  1601.6 55.6 reduce-scatter.18
  1660.1 40.5 all-reduce.11
  1702.9 39.0 all-gather.32
  1744.7 33.2 reduce-scatter.16
  1782.1 168.8 all-reduce.7
where the time goes:
time: 2180 us; the launch traced here: 2170 us
  waiting for transfers between devices  739 us (34%)
  matrix products  736 us (34%)
  local copies, waits for them, and re-layouts  476 us (22%)
  other arithmetic  183 us (8%)
    unnamed x23, waiting for transfers between devices  526 us
    dot_general x55, matrix products, product(): jnp.dot(first_matrix, second_matrix, preferred_element_type=jnp.float32)  261 us
    dot_general x48, matrix products, one_head(): jnp.einsum('qd,kd->qk', query_head, key_head, preferred_element_type=jnp....  162 us
    slice x5, local copies, waits for them, and re-layouts, unpack(): pieces.append(flat[offset:offset + count].reshape(target))  110 us
    convert_element_type x24, other arithmetic, one_head(): score_grads = (soft_weights * (weight_grads - row_dot)).astype(jnp.bfloat16)  99.3 us
    dot_general x24, matrix products, one_head(): jnp.einsum('qd,kd->qk', grad_head, value_head, preferred_element_type=jnp...  96.7 us
    unnamed x242, local copies, waits for them, and re-layouts  96.2 us
    convert_element_type x1, local copies, waits for them, and re-layouts, body(): lax.all_gather(slice_part.astype(jnp.bfloat16), 'rep', axis=1, tiled=True)  79.8 us
  transfers between devices with their start and end apart: 19, of which 12 were waited for; matrix products, arithmetic and copies ran while one was open for 25% of the time, Pallas kernels for 0%

commit v1 on v0

v1 whole, which is shorter than its diff:
```python
import jax
import jax.numpy as jnp
import numpy as np
from jax import lax
from jax.experimental import pallas as pl
from jax.experimental.pallas import tpu as pltpu
from jax.sharding import Mesh
from jax.sharding import PartitionSpec as P

HEADS = 12
HD = 64
EPSILON = 1e-05
NEG = -1e30
PROMPT = 1024
REACH = 256
bf16 = jnp.bfloat16
f32 = jnp.float32

def _nt(a,b): return lax.dot_general(a,b,(((1,),(1,)),((),())),preferred_element_type=f32)
def _nn(a,b): return lax.dot_general(a,b,(((1,),(0,)),((),())),preferred_element_type=f32)

def cross_fwd(q,k,v,valid,qb=1024):
    tq,width=q.shape; tk=k.shape[0]; pairs=width//128
    qb=min(qb,tq)
    def kern(q_ref,k_ref,v_ref,o_ref,l_ref,ks,vts):
        @pl.when(pl.program_id(1)==0)
        def _():
            low=lax.broadcasted_iota(jnp.int32,(tk,128),1)
            row=lax.broadcasted_iota(jnp.int32,(tk,128),0)
            kk=k_ref[...]
            bias=jnp.where(row>=valid,NEG,0.0).astype(bf16)
            ks[0]=jnp.where(low<HD,kk,bias)
            ks[1]=jnp.where(low>=HD,kk,bias)
            vv=v_ref[...]
            one=jnp.ones((tk,128),bf16)
            vts[0]=jnp.where(low<HD,vv,one).T
            vts[1]=jnp.where(low>=HD,vv,one).T
        lane=lax.broadcasted_iota(jnp.int32,(qb,128),1)
        qq=q_ref[...]*bf16(0.125)
        outs=[]
        scores=[]
        for h in range(2):
            mine=(lane<HD) if h==0 else (lane>=HD)
            inj=(lane==HD) if h==0 else (lane==0)
            qh=jnp.where(mine,qq,jnp.where(inj,1.0,0.0).astype(bf16))
            scores.append(_nt(ks[h],qh))
        for h,s in enumerate(scores):
            m=jnp.max(s,axis=0,keepdims=True)
            p=jnp.exp(s-m).astype(bf16)
            o=_nn(vts[h],p)
            tot=o[HD:HD+1] if h==0 else o[0:1]
            outs.append(o*(1.0/tot))
            l_ref[0,h:h+1,:]=m+jnp.log(tot)
        sub=lax.broadcasted_iota(jnp.int32,(128,qb),0)
        o_ref[...]=jnp.where(sub<HD,outs[0],outs[1]).T.astype(bf16)
    return pl.pallas_call(kern,grid=(pairs,tq//qb),
        in_specs=[pl.BlockSpec((qb,128),lambda p,i:(i,p)),pl.BlockSpec((tk,128),lambda p,i:(0,p)),pl.BlockSpec((tk,128),lambda p,i:(0,p))],
        out_specs=[pl.BlockSpec((qb,128),lambda p,i:(i,p)),pl.BlockSpec((1,8,qb),lambda p,i:(p,0,i))],
        out_shape=[jax.ShapeDtypeStruct((tq,width),bf16),jax.ShapeDtypeStruct((pairs,8,tq),f32)],
        scratch_shapes=[pltpu.VMEM((2,tk,128),bf16),pltpu.VMEM((2,128,tk),bf16)],
        compiler_params=pltpu.CompilerParams(vmem_limit_bytes=58*2**20))(q,k,v)

def delta_of(do,o,rows):
    x=do.astype(f32)*o.astype(f32)
    hi=x.astype(bf16); lo=(x-hi.astype(f32)).astype(bf16)
    r=lax.broadcasted_iota(jnp.int32,(8,128),0); c=lax.broadcasted_iota(jnp.int32,(8,128),1)
    pick=jnp.where((c//HD)==r,1.0,0.0).astype(bf16)
    return _nt(pick,hi)+_nt(pick,lo)

def cross_bwd(q,k,v,o,do,lse,valid,qb=1024):
    tq,width=q.shape; tk=k.shape[0]; pairs=width//128
    qb=min(qb,tq); nq=tq//qb
    def kern(q_ref,k_ref,v_ref,o_ref,do_ref,l_ref,dq_ref,dk_ref,dv_ref,ks,kts,dka,dva):
        i=pl.program_id(1)
        @pl.when(i==0)
        def _():
            low=lax.broadcasted_iota(jnp.int32,(tk,128),1)
            row=lax.broadcasted_iota(jnp.int32,(tk,128),0)
            kk=k_ref[...]
            bias=jnp.where(row>=valid,NEG,0.0).astype(bf16)
            ks[0]=jnp.where(low<HD,kk,bias)
            ks[1]=jnp.where(low>=HD,kk,bias)
            zero=jnp.zeros((tk,128),bf16)
            kts[0]=jnp.where(low<HD,kk,zero).T
            kts[1]=jnp.where(low>=HD,kk,zero).T
            dka[...]=jnp.zeros((tk,128),f32)
            dva[...]=jnp.zeros((tk,128),f32)
        lane=lax.broadcasted_iota(jnp.int32,(qb,128),1)
        qq=q_ref[...]*bf16(0.125)
        dd=do_ref[...]
        delta=delta_of(dd,o_ref[...],8)
        dqt=None; dk=dka[...]; dv=dva[...]
        for h in range(2):
            mine=(lane<HD) if h==0 else (lane>=HD)
            inj=(lane==HD) if h==0 else (lane==0)
            zero=jnp.zeros((qb,128),bf16)
            qc=jnp.where(mine,qq,zero)
            qs=jnp.where(inj,jnp.ones((qb,128),bf16),qc)
            dh=jnp.where(mine,dd,zero)
            s=_nt(ks[h],qs)
            p=jnp.exp(s-l_ref[0,h:h+1,:])
            dp=_nt(v_ref[...],dh)
            ds=(p*(dp-delta[h:h+1])).astype(bf16)
            dv=dv+_nn(p.astype(bf16),dh)
            dk=dk+_nn(ds,qc)
            t=_nn(kts[h],ds)
            dqt=t if dqt is None else dqt+t
        dka[...]=dk; dva[...]=dv
        dq_ref[...]=(dqt*0.125).T.astype(bf16)
        @pl.when(i==nq-1)
        def _():
            dk_ref[...]=dka[...].astype(bf16); dv_ref[...]=dva[...].astype(bf16)
    qs=pl.BlockSpec((qb,128),lambda p,i:(i,p)); kspec=pl.BlockSpec((tk,128),lambda p,i:(0,p))
    return pl.pallas_call(kern,grid=(pairs,nq),
        in_specs=[qs,kspec,kspec,qs,qs,pl.BlockSpec((1,8,qb),lambda p,i:(p,0,i))],
        out_specs=[qs,kspec,kspec],
        out_shape=[jax.ShapeDtypeStruct((tq,width),bf16),jax.ShapeDtypeStruct((tk,width),bf16),jax.ShapeDtypeStruct((tk,width),bf16)],
        scratch_shapes=[pltpu.VMEM((2,tk,128),bf16),pltpu.VMEM((2,128,tk),bf16),pltpu.VMEM((tk,128),f32),pltpu.VMEM((tk,128),f32)],
        compiler_params=pltpu.CompilerParams(vmem_limit_bytes=58*2**20))(q,k,v,o,do,lse)

def spans(r0,qb,prompt,reach):
    if r0<prompt: out=[(0,r0)] if r0 else []
    else:
        left=max(prompt,r0-reach)
        out=[(0,r0)] if left==prompt and r0>prompt else [(0,prompt)]
        if left>prompt: out.append((left,r0))
    return out,(r0,r0+qb)

def seg_marks(seg):
    lane=lax.broadcasted_iota(jnp.int32,(seg.shape[0],128),1)%HD
    same=lane==seg[:,None]
    kmark=jnp.where(same,1.0,0.0).astype(bf16)
    qmark=jnp.where(same|(lane==0)|(lane>8),0.0,NEG).astype(bf16)
    return kmark,qmark

def part_specs(t):
    return [pl.BlockSpec((1,t,128),lambda p,j=j:(j,0,p)) for j in range(3)]

def self_fwd(qkv,kmark,qmark,prompt=PROMPT,reach=REACH,qb=512):
    _,t,width=qkv.shape; pairs=width//128
    blocks=[spans(r0,qb,prompt,reach)+(r0,) for r0 in range(0,t,qb)]
    def kern(q_ref,k_ref,v_ref,km_ref,qm_ref,o_ref,l_ref,ks,vts):
        low=lax.broadcasted_iota(jnp.int32,(t,128),1)
        kk=k_ref[0]; vv=v_ref[0]; km=km_ref[...]
        one=jnp.ones((t,128),bf16)
        ks[0]=jnp.where(low<HD,kk,km); ks[1]=jnp.where(low>=HD,kk,km)
        vts[0]=jnp.where(low<HD,vv,one).T; vts[1]=jnp.where(low>=HD,vv,one).T
        lane=lax.broadcasted_iota(jnp.int32,(qb,128),1)
        hide=lax.broadcasted_iota(jnp.int32,(qb,qb),0)>lax.broadcasted_iota(jnp.int32,(qb,qb),1)
        tasks=[(b,h) for b in blocks for h in range(2)]
        def scores(task):
            (before,own,r0),h=task
            mine=(lane<HD) if h==0 else (lane>=HD)
            qs=jnp.where(mine,q_ref[0,pl.ds(r0,qb),:]*bf16(0.125),qm_ref[pl.ds(r0,qb),:])
            out=[_nt(ks[h,pl.ds(a,b-a),:],qs) for a,b in before]
            out.append(jnp.where(hide,NEG,_nt(ks[h,pl.ds(r0,qb),:],qs)))
            return out
        cur=scores(tasks[0]); res=[None,None]
        for i,task in enumerate(tasks):
            nxt=scores(tasks[i+1]) if i+1<len(tasks) else None
            (before,own,r0),h=task
            m=None
            for s in cur:
                x=jnp.max(s,axis=0,keepdims=True); m=x if m is None else jnp.maximum(m,x)
            o=None
            for s,(a,b) in zip(cur,before+[own]):
                y=_nn(vts[h,:,pl.ds(a,b-a)],jnp.exp(s-m).astype(bf16)); o=y if o is None else o+y
            tot=o[HD:HD+1] if h==0 else o[0:1]
            l_ref[0,h:h+1,pl.ds(r0,qb)]=m+jnp.log(tot)
            res[h]=o*(1.0/tot)
            if h==1:
                sub=lax.broadcasted_iota(jnp.int32,(128,qb),0)
                o_ref[pl.ds(r0,qb),:]=jnp.where(sub<HD,res[0],res[1]).T.astype(bf16)
            cur=nxt
    spec=pl.BlockSpec((t,128),lambda p:(0,p)); whole=pl.BlockSpec((t,128),lambda p:(0,0))
    return pl.pallas_call(kern,grid=(pairs,),in_specs=part_specs(t)+[whole,whole],
        out_specs=[spec,pl.BlockSpec((1,8,t),lambda p:(p,0,0))],
        out_shape=[jax.ShapeDtypeStruct((t,width),bf16),jax.ShapeDtypeStruct((pairs,8,t),f32)],
        scratch_shapes=[pltpu.VMEM((2,t,128),bf16),pltpu.VMEM((2,128,t),bf16)],
        compiler_params=pltpu.CompilerParams(vmem_limit_bytes=58*2**20))(qkv,qkv,qkv,kmark,qmark)

def self_bwd(qkv,o,do,lse,kmark,qmark,prompt=PROMPT,reach=REACH,qb=256):
    _,t,width=qkv.shape; pairs=width//128
    blocks=[spans(r0,qb,prompt,reach)+(r0,) for r0 in range(0,t,qb)]
    def kern(q_ref,k_ref,v_ref,o_ref,do_ref,l_ref,km_ref,qm_ref,d_ref,ks,kts,dka,dva):
        low=lax.broadcasted_iota(jnp.int32,(t,128),1)
        kk=k_ref[0]; km=km_ref[...]
        zero=jnp.zeros((t,128),bf16)
        ks[0]=jnp.where(low<HD,kk,km); ks[1]=jnp.where(low>=HD,kk,km)
        kts[0]=jnp.where(low<HD,kk,zero).T; kts[1]=jnp.where(low>=HD,kk,zero).T
        dka[...]=jnp.zeros((t,128),f32); dva[...]=jnp.zeros((t,128),f32)
        lane=lax.broadcasted_iota(jnp.int32,(qb,128),1)
        hide=lax.broadcasted_iota(jnp.int32,(qb,qb),0)>lax.broadcasted_iota(jnp.int32,(qb,qb),1)
        for before,own,r0 in blocks:
            rows=pl.ds(r0,qb)
            qq=q_ref[0,rows,:]*bf16(0.125); dd=do_ref[rows,:]; qm=qm_ref[rows,:]
            delta=delta_of(dd,o_ref[rows,:],8)
            dqt=None
            zq=jnp.zeros((qb,128),bf16)
            for h in range(2):
                mine=(lane<HD) if h==0 else (lane>=HD)
                qc=jnp.where(mine,qq,zq); qs=jnp.where(mine,qq,qm); dh=jnp.where(mine,dd,zq)
                lrow=l_ref[0,h:h+1,pl.ds(r0,qb)]
                for a,b in before+[own]:
                    keys=pl.ds(a,b-a)
                    s=_nt(ks[h,keys,:],qs)
                    if a==r0: s=jnp.where(hide,NEG,s)
                    p=jnp.exp(s-lrow)
                    dp=_nt(v_ref[0,keys,:],dh)
                    ds=(p*(dp-delta[h:h+1])).astype(bf16)
                    dva[keys,:]+=_nn(p.astype(bf16),dh)
                    dka[keys,:]+=_nn(ds,qc)
                    y=_nn(kts[h,:,keys],ds); dqt=y if dqt is None else dqt+y
            d_ref[0,rows,:]=(dqt*0.125).T.astype(bf16)
        d_ref[1]=dka[...].astype(bf16); d_ref[2]=dva[...].astype(bf16)
    spec=pl.BlockSpec((t,128),lambda p:(0,p)); whole=pl.BlockSpec((t,128),lambda p:(0,0))
    return pl.pallas_call(kern,grid=(pairs,),in_specs=part_specs(t)+[spec]*2+[pl.BlockSpec((1,8,t),lambda p:(p,0,0)),whole,whole],
        out_specs=pl.BlockSpec((3,t,128),lambda p:(0,0,p)),out_shape=jax.ShapeDtypeStruct((3,t,width),bf16),
        scratch_shapes=[pltpu.VMEM((2,t,128),bf16),pltpu.VMEM((2,128,t),bf16),pltpu.VMEM((t,128),f32),pltpu.VMEM((t,128),f32)],
        compiler_params=pltpu.CompilerParams(vmem_limit_bytes=58*2**20))(qkv,qkv,qkv,o,do,lse,kmark,qmark)


def norm_stats(rows):
    centered = rows - jnp.mean(rows, axis=-1, keepdims=True)
    inv = lax.rsqrt(jnp.mean(centered * centered, axis=-1, keepdims=True) + EPSILON)
    return centered * inv, inv


def norm(rows, gain, shift):
    return norm_stats(rows)[0] * gain + shift


def norm_back(rows, gain, dy):
    n, inv = norm_stats(rows)
    dn = dy * gain
    dh = inv * (dn - jnp.mean(dn, axis=-1, keepdims=True) - n * jnp.mean(dn * n, axis=-1, keepdims=True))
    return dh, jnp.sum(dy * n, axis=0), jnp.sum(dy, axis=0)


def mm(a, b):
    return jnp.dot(a, b, preferred_element_type=f32)


def mm_t(a, b):
    return lax.dot_general(a, b, (((1,), (1,)), ((), ())), preferred_element_type=f32)


def t_mm(a, b):
    return lax.dot_general(a, b, (((0,), (0,)), ((), ())), preferred_element_type=f32)


def gelu_parts(u):
    phi = jnp.exp(-0.5 * u * u) * 0.3989422804014327
    return 0.5 * lax.erfc(-u * 0.7071067811865476), phi


GROUP = ("core", "ilo")
SHARD = ("ihi", "ilo")
REP = ("rz", "core")
SPREAD = ("ihi", "ilo", "rz", "core")
FLIP = [(0, 1), (1, 0)]


def body(hidden, frames, segment, cotangent, norm_gain, norm_bias, self_qkv, self_out, cross_q, cross_kv, cross_out, fc1, fc2, proj_bias, fc1_bias):
    c = lax.axis_index("core")
    hi = lax.axis_index("ihi")
    n = lax.axis_size("core") * lax.axis_size("ilo")
    reps = lax.axis_size("rz") * lax.axis_size("core")
    rep_at = lax.axis_index(REP)
    width = self_out.shape[1]
    ff = fc1.shape[1]

    def swap(x):
        return lax.ppermute(x, ("core", "ihi"), [(0, 0), (1, 2), (2, 1), (3, 3)])

    def whole(own):
        if n != 2:
            return lax.all_gather(own, SHARD, axis=0, tiled=True)
        half = own.shape[0] // 2
        mine = lax.ppermute(lax.dynamic_slice_in_dim(own, c * half, half), "ihi", FLIP)
        sib = lax.ppermute(mine, "core", FLIP)
        other = jnp.where(c == 0, jnp.concatenate([mine, sib]), jnp.concatenate([sib, mine]))
        return jnp.where(hi == 0, jnp.concatenate([own, other]), jnp.concatenate([other, own]))

    def slices(own):
        rows = own.shape[0] // reps
        return lax.dynamic_slice_in_dim(own, rep_at * rows, rows)

    rows_in = swap(hidden[0])
    qkv_w = whole(self_qkv.astype(bf16))
    small = jnp.concatenate([norm_gain.astype(bf16), norm_bias.astype(bf16), proj_bias.astype(bf16), fc1_bias.astype(bf16).reshape(-1, norm_gain.shape[1]), jnp.zeros((1, norm_gain.shape[1]), bf16)])
    small = lax.all_gather(small, SHARD, axis=1, tiled=False).astype(f32)
    table = small[:15].reshape(15, width)
    gains, shifts, biases = table[:4], table[4:8], table[8:15]
    fc1_shift = small[15:19].transpose(1, 0, 2).reshape(ff)
    seg = swap(segment)[0]
    frames_half = swap(frames[0])
    if n == 2:
        twin = lax.ppermute(frames_half, "core", FLIP)
        frame_rows = jnp.concatenate([jnp.where(c == 0, frames_half, twin), jnp.where(c == 0, twin, frames_half)], axis=1)
    else:
        frame_rows = lax.all_gather(frames_half, GROUP, axis=1, tiled=True)
    selfout_w = whole(self_out.astype(bf16))
    crossq_w = whole(cross_q.astype(bf16))
    kv_w = whole(cross_kv.astype(bf16)) if n == 2 else None
    if n == 2:
        k_w, v_w = kv_w[:width], kv_w[width:]
    else:
        kv_w = lax.all_gather(cross_kv.astype(bf16), SHARD, axis=1, tiled=True)
        k_w, v_w = kv_w[:, :width], kv_w[:, width:]
    crossout_w = whole(cross_out.astype(bf16))
    cot = swap(cotangent[0])
    units = ff // width
    part1 = slices(fc1.astype(bf16))
    part2 = slices(fc2.astype(bf16))
    few = part1.shape[0]
    parts = jnp.concatenate([part1[:, j * width : (j + 1) * width] for j in range(units)] + [part2])
    ffw = lax.all_gather(parts, SPREAD, axis=0, tiled=False)
    fc1_w = jnp.concatenate([ffw[:, j * few : (j + 1) * few].reshape(width, width) for j in range(units)], axis=1)
    fc2_w = ffw[:, units * few :].reshape(ff, width)

    own_rows = rows_in.shape[0]
    hw = -(-HEADS // n)
    padded = hw * n * HD - width

    lanes = hw * HD

    def to_heads(x):
        x = x.reshape(own_rows, -1, width)
        if padded:
            x = jnp.pad(x, ((0, 0), (0, 0), (0, padded)))
        x = x.reshape(own_rows, -1, n, lanes).transpose(1, 2, 0, 3)
        x = lax.all_to_all(x, GROUP, 1, 1, tiled=True)
        return x.reshape(-1, n * own_rows, lanes)

    def to_tokens(x):
        x = lax.all_to_all(x.reshape(-1, n, own_rows, lanes), GROUP, 1, 1, tiled=True)
        return x.transpose(2, 0, 1, 3).reshape(own_rows, -1, n * lanes)[:, :, :width].reshape(own_rows, -1)

    h0 = rows_in.astype(f32)
    a1 = norm(h0, gains[0], shifts[0]).astype(bf16)
    zeros_row = jnp.zeros((width,), f32)
    qkv = (mm(a1, qkv_w) + jnp.concatenate([biases[0], zeros_row, biases[1]])).astype(bf16)
    heads = to_heads(qkv)
    kmark, qmark = seg_marks(seg)
    ctx, self_lse = self_fwd(heads, kmark, qmark)
    c1 = to_tokens(ctx)
    h1 = h0 + mm(c1, selfout_w) + biases[2]
    a2 = norm(h1, gains[1], shifts[1]).astype(bf16)
    qc = (mm(a2, crossq_w) + biases[3]).astype(bf16)
    count = frame_rows.shape[0]
    pad = -count % 256
    frame_pad = jnp.pad(frame_rows, ((0, pad), (0, 0)))
    kc = mm(frame_pad, k_w).astype(bf16)
    live = lax.broadcasted_iota(jnp.int32, (count + pad, 1), 0) < count
    vc = (mm(frame_pad, v_w) + jnp.where(live, biases[4], 0.0)).astype(bf16)
    c2, cross_lse = cross_fwd(qc, kc, vc, count)
    h2 = h1 + mm(c2, crossout_w) + biases[5]
    a3 = norm(h2, gains[2], shifts[2]).astype(bf16)
    u = (mm(a3, fc1_w) + fc1_shift).astype(bf16)
    uf = u.astype(f32)
    cdf, pdf = gelu_parts(uf)
    g = (uf * cdf).astype(bf16)
    slope = (cdf + uf * pdf).astype(f32)
    h3 = h2 + mm(g, fc2_w) + biases[6]
    output = norm(h3, gains[3], shifts[3]).astype(bf16)
    output = swap(output)

    def total(x):
        return jnp.sum(x.astype(f32), axis=0)

    dh3, gain3, shift3 = norm_back(h3, gains[3], cot.astype(f32))
    dm = dh3.astype(bf16)
    g_fc2 = t_mm(g, dm).astype(bf16)
    du = (slope * mm_t(dm, fc2_w)).astype(bf16)
    g_fc1 = t_mm(a3, du).astype(bf16)

    def reduce_rows(parts, extra=None):
        total = n * reps
        cut = [p.reshape(total, -1, width) for p in parts]
        if extra is not None:
            cut.append(extra)
        flat = jnp.concatenate(cut, axis=1)
        mine = lax.psum_scatter(flat, SPREAD, scatter_dimension=0, tiled=False)
        got = lax.all_gather(mine, REP, axis=0, tiled=False)
        out, at = [], 0
        for p in cut:
            out.append(got[:, at : at + p.shape[1]].reshape(-1, width).astype(f32))
            at += p.shape[1]
        return out

    ff_grads = reduce_rows([g_fc1[:, j * width : (j + 1) * width] for j in range(units)] + [g_fc2])
    fc1_grad = jnp.concatenate(ff_grads[:units], axis=1)
    fc2_grad = ff_grads[units]

    da3 = mm_t(du, fc1_w)
    dres, gain2, shift2 = norm_back(h2, gains[2], da3)
    dh2 = dh3 + dres
    d2 = dh2.astype(bf16)
    g_crossout = t_mm(c2, d2).astype(bf16)
    dc2 = mm_t(d2, crossout_w).astype(bf16)
    dqc, dkc, dvc = cross_bwd(qc, kc, vc, c2, dc2, cross_lse, count)
    share = width // n

    def sum_columns(x):
        return lax.psum_scatter(x, GROUP, scatter_dimension=1, tiled=True)

    if n == 2:

        def sum_columns(x):
            give = lax.dynamic_slice_in_dim(x, (1 - c) * share, share, axis=1)
            keep = lax.dynamic_slice_in_dim(x, c * share, share, axis=1)
            return (keep.astype(f32) + lax.ppermute(give, "core", FLIP).astype(f32)).astype(bf16)

    dk_own = sum_columns(dkc)[:count]
    dv_own = sum_columns(dvc)[:count]
    place = lax.axis_index(GROUP) * share
    kw_own = lax.dynamic_slice_in_dim(k_w, place, share, axis=1)
    vw_own = lax.dynamic_slice_in_dim(v_w, place, share, axis=1)
    dframe = (mm_t(dk_own, kw_own) + mm_t(dv_own, vw_own)).astype(bf16)
    grad_frames = swap(sum_columns(dframe))
    g_k = t_mm(frame_rows, dk_own).astype(bf16)
    g_v = t_mm(frame_rows, dv_own).astype(bf16)
    vb_own = jnp.sum(dv_own.astype(f32), axis=0)

    g_crossq = t_mm(a2, dqc).astype(bf16)
    da2 = mm_t(dqc, crossq_w)
    dres, gain1, shift1 = norm_back(h1, gains[1], da2)
    dh1 = dh2 + dres
    d1 = dh1.astype(bf16)
    g_selfout = t_mm(c1, d1).astype(bf16)
    dctx = mm_t(d1, selfout_w).astype(bf16)
    dctx = to_heads(dctx)[0]
    dqkv = to_tokens(self_bwd(heads, ctx, dctx, self_lse, kmark, qmark))
    da1 = mm_t(dqkv, qkv_w)
    g_qkv = t_mm(a1, dqkv).astype(bf16)
    sums = total(dqkv)
    dres, gain0, shift0 = norm_back(h0, gains[0], da1)
    grad_hidden = swap((dh1 + dres).astype(bf16))

    vb = lax.dynamic_update_slice(jnp.zeros((width,), f32), vb_own, (place,))
    vectors = jnp.stack([gain0, gain1, gain2, gain3, shift0, shift1, shift2, shift3, sums[:width], sums[2 * width :], total(d1), total(dqc), vb, total(d2), total(dm)])
    per = width // n
    vectors = vectors.reshape(15, n, per).transpose(1, 0, 2).reshape(n, 15 * per)
    vectors = jnp.concatenate([vectors, total(du).reshape(n, ff // n)], axis=1)
    long = vectors.shape[1]
    seats = -(-long // reps)
    vectors = jnp.pad(vectors, ((0, 0), (0, seats * reps - long))).reshape(n * reps, seats)
    lines = -(-seats // (8 * width)) * 8
    vectors = jnp.pad(vectors, ((0, 0), (0, lines * width - seats))).reshape(n * reps, lines, width)

    def own_columns(x):
        return lax.dynamic_update_slice(jnp.zeros((x.shape[0], width), x.dtype), x, (jnp.int32(0), place))

    cross = [g_crossq, g_crossout]
    if n == 2:
        cross.append(jnp.concatenate([own_columns(g_k), own_columns(g_v)]))
    cross = reduce_rows(cross)
    crossq_grad, crossout_grad = cross[:2]
    if n == 2:
        kv_grad = cross[2]
    else:
        kv_cols = jnp.concatenate([own_columns(g_k), own_columns(g_v)], axis=1)
        kv_cols = lax.psum_scatter(kv_cols, SHARD, scatter_dimension=1, tiled=True)
        kv_grad = lax.psum(kv_cols, REP).astype(f32)
    got = reduce_rows([g_qkv[:, j * width : (j + 1) * width] for j in range(3)] + [g_selfout], vectors.astype(bf16))
    qkv_grad = jnp.concatenate(got[:3], axis=1)
    selfout_grad = got[3]
    vec = got[4].reshape(reps, lines * width)[:, :seats].reshape(-1)[:long]
    table = vec[: 15 * per].reshape(15, per)
    fc1b_grad = vec[15 * per :]
    return (
        output[None], grad_hidden[None], grad_frames[None],
        table[:4], table[4:8], qkv_grad, selfout_grad, crossq_grad, kv_grad, crossout_grad, fc1_grad, fc2_grad, table[8:15], fc1b_grad,
    )


def solution(mesh):
    reps, n = mesh.devices.shape
    work = Mesh(mesh.devices.reshape(reps // 2, 2, 2, n // 2), ("rz", "core", "ihi", "ilo"))
    rep, inner = ("rz", "core"), ("ihi", "ilo")
    rows, cols = P(inner, None), P(None, inner)
    tokens, features = P(rep, inner, None), P(rep, None, inner)
    weights = (cols, cols, rows, rows, rows, cols, rows, rows, rows, cols, P(inner))
    return jax.shard_map(
        body,
        mesh=work,
        in_specs=(tokens, features, P(rep, None), tokens) + weights,
        out_specs=(tokens, tokens, features) + weights,
        check_vma=False,
    )
```

time: 2180 us -> 1040 us (0.48)
  matrix products: 736 us -> 154 us
  local copies, waits for them, and re-layouts: 476 us -> 101 us
  waiting for transfers between devices: 739 us -> 454 us
  Pallas kernels: 0 us -> 138 us
  other arithmetic: 183 us -> 69.2 us
  blocking collectives: 14 us -> 60.7 us
  starting transfers between devices: 0.95 us -> 38.8 us
    dot_general x189 -> x24, matrix products: 736 us -> 154 us  [the longest x8 69 us: mm(): return jnp.dot(a, b, preferred_element_type=f32)]
    unnamed x23 -> x7, waiting for transfers between devices: 526 us -> 0.11 us
    reduce_scatter x4 -> x3, waiting for transfers between devices: 90.1 us -> 306 us  [reduce_rows(): mine = lax.psum_scatter(flat, SPREAD, scatter_dimension=0, tiled=False)]
    pallas_call x0 -> x4, Pallas kernels: none -> 138 us  [the longest x1 49.5 us: cross_bwd(): pl.pallas_call(kern, grid=(pairs, nq), in_specs=[qs, kspec, kspec, qs, qs...]
    slice x18 -> x19, local copies, waits for them, and re-layouts: 129 us -> 11.6 us  [the longest x8 4.59 us: reduce_rows(): out.append(got[:, at:at + p.shape[1]].reshape(-1, width).astype(f32))]
    convert_element_type x36 -> x15, other arithmetic: 119 us -> 18 us  [the longest x5 7.95 us: reduce_rows(): out.append(got[:, at:at + p.shape[1]].reshape(-1, width).astype(f32))]
    convert_element_type x1, local copies, waits for them, and re-layouts: 79.8 us -> 1.07 us  [body(): part1 = slices(fc1.astype(bf16))]
    ppermute x0 -> x21, waiting for transfers between devices: none -> 77.5 us  [the longest x5 41.7 us: whole(): lax.ppermute(lax.dynamic_slice_in_dim(own, c * half, half), 'ihi', FLIP)]
  transfers between devices with their start and end apart: 19 -> 28, of which waited for: 12 -> 10; matrix products, arithmetic and copies ran while one was open for 25% -> 20% of each run, Pallas kernels for 0% -> 5%
where the time goes in v1:
time: 1040 us; the launch traced here: 1030 us
  waiting for transfers between devices  454 us (44%)
  matrix products  154 us (15%)
  Pallas kernels  138 us (13%)
  local copies, waits for them, and re-layouts  101 us (10%)
  other arithmetic  69.2 us (7%)
  blocking collectives  60.7 us (6%)
  starting transfers between devices  38.8 us (4%)
  between operations  15.9 us (2%)
    reduce_scatter x3, waiting for transfers between devices, reduce_rows(): mine = lax.psum_scatter(flat, SPREAD, scatter_dimension=0, tiled=False)  306 us
    all_gather x3, waiting for transfers between devices, reduce_rows(): got = lax.all_gather(mine, REP, axis=0, tiled=False)  71 us
    dot_general x8, matrix products, mm(): return jnp.dot(a, b, preferred_element_type=f32)  69 us
    pallas_call x1, Pallas kernels, cross_bwd(): pl.pallas_call(kern, grid=(pairs, nq), in_specs=[qs, kspec, kspec, qs, qs...  49.5 us
    dot_general x8, matrix products, mm_t(): lax.dot_general(a, b, (((1,), (1,)), ((), ())), preferred_element_type=f32)  44.1 us
    ppermute x5, waiting for transfers between devices, whole(): lax.ppermute(lax.dynamic_slice_in_dim(own, c * half, half), 'ihi', FLIP)  41.7 us
    dot_general x8, matrix products, t_mm(): lax.dot_general(a, b, (((0,), (0,)), ((), ())), preferred_element_type=f32)  40.9 us
    pallas_call x1, Pallas kernels, self_bwd(): pl.pallas_call(kern, grid=(pairs,), in_specs=part_specs(t) + [spec] * 2 +...  40.2 us
  transfers between devices with their start and end apart: 28, of which 10 were waited for; matrix products, arithmetic and copies ran while one was open for 20% of the time, Pallas kernels for 5%

profile of v1, /device:TPU:1, one launch (start us, length us, event | category | flops | bytes accessed | tf_op | source)
XLA Modules:
  0.0 1031.5 jit_solution(6539468355239179638)
XLA Ops:
  10.1 4.5 collective-permute-start.3
  29.1 32.1 %all-gather = bf16[20,768]{1,0:T(8,128)(2,1)S(1)} all-gather(bf16[20,384]{1,0:T(8,128)(2,1)S(1)} %concatenate.105), channel_id=2, replica_groups=mesh['rz'=8,'core'=2,'ihi'=2,'ilo'=1] {'ihi','ilo'}, dimensions={1}, use_global_device_ids=true | all-gather | bytes 46080 | tf_op jit(solution)/shard_map/all_gather | solution.py:292
  63.7 3.3 collective-permute-start
  69.3 7.3 collective-permute-start.7
  91.1 41.7 %collective-permute-done.1 = bf16[192,2304]{1,0:T(8,128)(2,1)} collective-permute-done((bf16[192,2304]{1,0:T(8,128)(2,1)}, bf16[192,2304]{1,0:T(8,128)(2,1)}, u32[]{:S(2)}, u32[]{:S(2)}) %collective-permute-start.1) | collective-permute-done | bytes 884768 | tf_op jit(solution)/shard_map/ppermute | solution.py:280
  141.3 6.5 add_convert_fusion.1
  147.7 9.9 reshape_reshape.12
  160.6 7.7 all_to_all.20
  171.0 20.4 %shard_map.254 = (bf16[2048,384]{1,0:T(8,128)(2,1)}, f32[3,8,2048]{2,1,0:T(8,128)}) custom-call(bf16[3,2048,384]{2,1,0:T(8,128)(2,1)} %bitcast.89, bf16[3,2048,384]{2,1,0:T(8,128)(2,1)} %bitcast.90, bf16[3,2048,384]{2,1,0:T(8,128)(2,1)} %bitcast.91, bf16[2048,128]{1,0:T(8,128)(2,1)} %get-tuple-element.133.km_ref, bf16[2048,128]{1,0:T(8,128)(2,1)} %get-tuple-element.132.qm_ref), custom_call_target="tpu_custom_call" | custom-call | tf_op jit(solution)/shard_map/pallas_call | solution.py:176
  193.2 5.5 all_to_all.21
  209.9 3.4 convolution_convert_fusion.3.k_ref
  213.3 3.4 add_convert_fusion.2.v_ref
  216.7 27.5 %shard_map.255 = (bf16[1024,768]{1,0:T(8,128)(2,1)}, f32[6,8,1024]{2,1,0:T(8,128)}) custom-call(bf16[1024,768]{1,0:T(8,128)(2,1)} %add_convert_fusion.6.q_ref, bf16[1536,768]{1,0:T(8,128)(2,1)} %convolution_convert_fusion.3.k_ref, bf16[1536,768]{1,0:T(8,128)(2,1)} %add_convert_fusion.2.v_ref), custom_call_target="tpu_custom_call" | custom-call | tf_op jit(solution)/shard_map/pallas_call | solution.py:56
  244.2 3.9 fusion.111
  248.6 3.4 slice.331
  254.7 36.9 %fusion.1 = (f32[1024,3072]{1,0:T(8,128)}, bf16[1024,3072]{1,0:T(8,128)(2,1)}) fusion(f32[3072]{0:T(1024)S(1)} %add.255, bf16[768,768]{1,0:T(8,128)(2,1)S(1)} %bitcast.132, bf16[768,768]{1,0:T(8,128)(2,1)S(1)} %bitcast.134, bf16[768,768]{1,0:T(8,128)(2,1)S(1)} %bitcast.136, bf16[768,768]{1,0:T(8,128)(2,1)S(1)} %bitcast.130, ...), kind=kOutput, calls=%fused_computation.7 | convolution fusion | flops 5062262784 | bytes 26765312 | tf_op jit(solution)/shard_map/dot_general | solution.py:241
  291.7 10.3 fusion.112
  302.6 3.7 fusion.57
  309.0 13.6 %fusion.113 = (bf16[3072]{0:T(1024)(128)(2,1)S(1)}, bf16[1024,3072]{1,0:T(8,128)(2,1)}) fusion(bf16[1024,768]{0,1:T(8,128)(2,1)S(1)} %get-tuple-element.98, bf16[3072,768]{1,0:T(8,128)(2,1)S(1)} %bitcast.113, f32[1024,3072]{1,0:T(8,128)} %get-tuple-element.138, bf16[1024,3072]{1,0:T(8,128)(2,1)} %get-tuple-element.139), kind=kOutput, calls=%fused_computation.269 | convolution fusion | flops 4860146688 | bytes 31463424 | tf_op jit(solution)/shard_map/dot_general | solution.py:245
  322.6 10.1 fusion.116
  332.8 3.6 copy.66
  336.4 4.0 multiply_reduce_fusion
  341.1 4.8 convert_reduce_fusion.4
  348.6 49.5 %shard_map.256 = (bf16[1024,768]{1,0:T(8,128)(2,1)}, bf16[1536,768]{1,0:T(8,128)(2,1)}, bf16[1536,768]{1,0:T(8,128)(2,1)}) custom-call(bf16[1024,768]{1,0:T(8,128)(2,1)} %add_convert_fusion.6.q_ref, bf16[1536,768]{1,0:T(8,128)(2,1)} %convolution_convert_fusion.3.k_ref, bf16[1536,768]{1,0:T(8,128)(2,1)} %add_convert_fusion.2.v_ref, ...), custom_call_target="tpu_custom_call" | custom-call | tf_op jit(solution)/shard_map/pallas_call | solution.py:114
  398.1 4.5 fusion.115
  402.6 3.7 copy.67
  414.0 6.1 all_to_all.22
  420.0 40.2 %shard_map.257 = bf16[3,2048,384]{2,1,0:T(8,128)(2,1)} custom-call(bf16[3,2048,384]{2,1,0:T(8,128)(2,1)} %bitcast.92, bf16[3,2048,384]{2,1,0:T(8,128)(2,1)} %bitcast.93, bf16[3,2048,384]{2,1,0:T(8,128)(2,1)} %bitcast.94, bf16[2048,384]{1,0:T(8,128)(2,1)} %get-tuple-element.21.o_ref, bf16[2048,384]{1,0:T(8,128)(2,1)} %bitcast.101, ...), custom_call_target="tpu_custom_call" | custom-call | tf_op jit(solution)/shard_map/pallas_call | solution.py:217
  460.2 6.6 copy.69
  466.9 9.3 all_to_all.23
  480.4 5.6 fusion.114
  488.3 3.4 constant_dynamic-slice_fusion.1
  493.4 3.9 convolution_convert_fusion.6
  499.1 3.1 fusion.61
  502.4 3.1 fusion.62
  516.7 6.9 convolution_convert_fusion.2
  534.4 8.6 convolution_convert_fusion.1
  547.9 12.1 %convolution_convert_fusion = bf16[3072,768]{1,0:T(8,128)(2,1)S(1)} fusion(bf16[1024,768]{0,1:T(8,128)(2,1)S(1)} %copy-done.42, f32[1024,3072]{1,0:T(8,128)S(1)} %bitcast.148, bf16[1024,3072]{1,0:T(8,128)(2,1)} %get-tuple-element.139), kind=kOutput, calls=%fused_computation.44 | convolution fusion | flops 4843634688 | bytes 25165824 | tf_op jit(solution)/shard_map/dot_general | solution.py:249
  562.5 51.2 %reduce-scatter.6.cloned.1.call-done = bf16[1,96,768]{2,1,0:T(8,128)(2,1)} async-done(((bf16[32,96,768]{2,1,0:T(8,128)(2,1)}), bf16[1,96,768]{2,1,0:T(8,128)(2,1)}) %reduce-scatter.6.cloned.1.call-update) | async-done | bytes 147472 | tf_op jit(solution)/shard_map/reduce_scatter | solution.py:384
  613.8 114.5 %reduce-scatter.4.cloned.1.call-done = bf16[1,104,768]{2,1,0:T(8,128)(2,1)} async-done(((bf16[32,104,768]{2,1,0:T(8,128)(2,1)}), bf16[1,104,768]{2,1,0:T(8,128)(2,1)}) %reduce-scatter.4.cloned.1.call-update) | async-done | bytes 159760 | tf_op jit(solution)/shard_map/reduce_scatter | solution.py:384
  728.3 140.1 %reduce-scatter.8.cloned.1.call-done = bf16[1,192,768]{2,1,0:T(8,128)(2,1)} async-done(((bf16[32,192,768]{2,1,0:T(8,128)(2,1)}), bf16[1,192,768]{2,1,0:T(8,128)(2,1)}) %reduce-scatter.8.cloned.1.call-update) | async-done | bytes 294928 | tf_op jit(solution)/shard_map/reduce_scatter | solution.py:384
  871.7 3.2 add_convert_fusion.3
  886.9 3.4 collective-permute-start.20
  890.3 9.2 collective-permute-done.14
  901.0 15.3 %collective-permute-done.16 = bf16[1024,768]{0,1:T(8,128)(2,1)S(1)} collective-permute-done((bf16[1024,768]{0,1:T(8,128)(2,1)}, bf16[1024,768]{0,1:T(8,128)(2,1)S(1)}, u32[]{:S(2)}, u32[]{:S(2)}) %collective-permute-start.16) | collective-permute-done | bytes 1572896 | tf_op jit(solution)/shard_map/ppermute | solution.py:274
  917.9 10.9 %collective-permute-done.20 = bf16[1500,384]{1,0:T(8,128)(2,1)} collective-permute-done((bf16[1500,384]{1,0:T(8,128)(2,1)}, bf16[1500,384]{1,0:T(8,128)(2,1)}, u32[]{:S(2)}, u32[]{:S(2)}) %collective-permute-start.20) | collective-permute-done | bytes 1152032 | tf_op jit(solution)/shard_map/ppermute | solution.py:274
  934.5 24.2 %all-gather.7.cloned.1.call-done = bf16[16,104,768]{2,1,0:T(8,128)(2,1)} async-done(((bf16[1,104,768]{2,1,0:T(8,128)(2,1)}), bf16[16,104,768]{2,1,0:T(8,128)(2,1)}) %all-gather.7.cloned.1.call-update) | async-done | bytes 2555920 | tf_op jit(solution)/shard_map/all_gather | solution.py:385
  966.6 46.8 %all-gather.11.cloned.1.call-done = bf16[16,192,768]{2,1,0:T(8,128)(2,1)} async-done(((bf16[1,192,768]{2,1,0:T(8,128)(2,1)}), bf16[16,192,768]{2,1,0:T(8,128)(2,1)}) %all-gather.11.cloned.1.call-update) | async-done | bytes 4718608 | tf_op jit(solution)/shard_map/all_gather | solution.py:385
  (402 shorter events, 162.8 us)
Async XLA Ops:
  7.2 241.3 %all-gather.13.cloned.1.call-start = ((), (), s32[]{:S(2)}) async-start(), calls=%async_computation.13 | async-start | bytes 9732096 | tf_op jit(solution)/shard_map/all_gather | solution.py:318
  10.1 603.6 %reduce-scatter.6.cloned.1.call-start = ((), (), s32[]{:S(2)}) async-start(), calls=%async_computation.9 | async-start | bytes 4866048 | tf_op jit(solution)/shard_map/reduce_scatter | solution.py:384
  10.1 53.5 %collective-permute-start.3 = (s32[1,2048]{1,0:T(1,128)}, s32[1,2048]{1,0:T(1,128)S(1)}, u32[]{:S(2)}, u32[]{:S(2)}) collective-permute-start(s32[1,2048]{1,0:T(1,128)} %param.17), channel_id=1, source_target_pairs={{0,0},{1,2},{2,1},{3,3},{4,4},{5,6},{6,5},{7,7},{8,8},{9,10},{10,9... | collective-permute-start | bytes 24584 | tf_op jit(solution)/shard_map/ppermute | solution.py:274
  16.8 45.1 %collective-permute-start.4 = (bf16[192,768]{1,0:T(8,128)(2,1)}, bf16[192,768]{1,0:T(8,128)(2,1)}, u32[]{:S(2)}, u32[]{:S(2)}) collective-permute-start(bf16[192,768]{1,0:T(8,128)(2,1)} %constant_dynamic-slice_fusion.6), channel_id=1, source_target_pairs={{0,1},{1,0},{2,3},{3,2},{4,5},{5,4},{6,7},{7,6},{8,9},{9,8},{10,11... | collective-permute-start | bytes 884744 | tf_op jit(solution)/shard_map/ppermute | solution.py:280
  18.4 48.5 %collective-permute-start.6 = (bf16[192,768]{1,0:T(8,128)(2,1)}, bf16[192,768]{1,0:T(8,128)(2,1)}, u32[]{:S(2)}, u32[]{:S(2)}) collective-permute-start(bf16[192,768]{1,0:T(8,128)(2,1)} %constant_dynamic-slice_fusion.5), channel_id=1, source_target_pairs={{0,1},{1,0},{2,3},{3,2},{4,5},{5,4},{6,7},{7,6},{8,9},{9,8},{10,11... | collective-permute-start | bytes 884744 | tf_op jit(solution)/shard_map/ppermute | solution.py:280
  22.6 58.5 %collective-permute-start.10 = (bf16[384,768]{1,0:T(8,128)(2,1)}, bf16[384,768]{1,0:T(8,128)(2,1)S(1)}, u32[]{:S(2)}, u32[]{:S(2)}) collective-permute-start(bf16[384,768]{1,0:T(8,128)(2,1)} %constant_dynamic-slice_fusion.4), channel_id=1, source_target_pairs={{0,1},{1,0},{2,3},{3,2},{4,5},{5,4},{6,7},{7,6},{8,9},{9,8},{10,11... | collective-permute-start | bytes 1769480 | tf_op jit(solution)/shard_map/ppermute | solution.py:280
  25.4 36.6 %copy-start.36 = (bf16[1,1024,768]{2,1,0:T(8,128)(2,1)S(1)}, bf16[1,1024,768]{2,1,0:T(8,128)(2,1)}, u32[]{:S(2)}) copy-start(bf16[1,1024,768]{2,1,0:T(8,128)(2,1)} %param.15) | copy-start | bytes 4718596
  25.4 43.9 %collective-permute-start.12 = (bf16[192,768]{1,0:T(8,128)(2,1)}, bf16[192,768]{1,0:T(8,128)(2,1)}, u32[]{:S(2)}, u32[]{:S(2)}) collective-permute-start(bf16[192,768]{1,0:T(8,128)(2,1)} %constant_dynamic-slice_fusion.3), channel_id=1, source_target_pairs={{0,1},{1,0},{2,3},{3,2},{4,5},{5,4},{6,7},{7,6},{8,9},{9,8},{10,11... | collective-permute-start | bytes 884744 | tf_op jit(solution)/shard_map/ppermute | solution.py:280
  61.9 78.1 %copy-start.77 = (f32[768]{0:T(1024)}, f32[768]{0:T(1024)S(1)}, u32[]{:S(2)}) copy-start(f32[768]{0:T(1024)S(1)} %get-tuple-element.95) | copy-start | bytes 9220
  61.9 78.1 %copy-start.84 = (f32[768]{0:T(1024)}, f32[768]{0:T(1024)S(1)}, u32[]{:S(2)}) copy-start(f32[768]{0:T(1024)S(1)} %get-tuple-element.94) | copy-start | bytes 9220
  61.9 138.9 %copy-start.73 = (f32[768]{0:T(1024)}, f32[768]{0:T(1024)S(1)}, u32[]{:S(2)}) copy-start(f32[768]{0:T(1024)S(1)} %get-tuple-element.90) | copy-start | bytes 9220
  61.9 138.9 %copy-start.86 = (f32[768]{0:T(1024)}, f32[768]{0:T(1024)S(1)}, u32[]{:S(2)}) copy-start(f32[768]{0:T(1024)S(1)} %get-tuple-element.89) | copy-start | bytes 9220
  61.9 14.6 %collective-permute-start.5 = (bf16[192,768]{1,0:T(8,128)(2,1)}, bf16[192,768]{1,0:T(8,128)(2,1)}, u32[]{:S(2)}, u32[]{:S(2)}) collective-permute-start(bf16[192,768]{1,0:T(8,128)(2,1)} %collective-permute-done.4), channel_id=1, source_target_pairs={{0,2},{2,0},{1,3},{3,1},{4,6},{6,4},{5,7},{7,5},{8,10},{10,8},{9,1... | collective-permute-start | bytes 884744 | tf_op jit(solution)/shard_map/ppermute | solution.py:281
  63.7 73.2 %collective-permute-start = (bf16[1024,768]{0,1:T(8,128)(2,1)}, bf16[1024,768]{0,1:T(8,128)(2,1)S(1)}, u32[]{:S(2)}, u32[]{:S(2)}) collective-permute-start(bf16[1024,768]{0,1:T(8,128)(2,1)} %bitcast.124), channel_id=1, source_target_pairs={{0,0},{1,2},{2,1},{3,3},{4,4},{5,6},{6,5},{7,7},{8,8},{9,10},{10,9... | collective-permute-start | bytes 4718600 | tf_op jit(solution)/shard_map/ppermute | solution.py:274
  66.9 67.6 %collective-permute-start.8 = (bf16[1500,384]{1,0:T(8,128)(2,1)}, bf16[1500,384]{1,0:T(8,128)(2,1)}, u32[]{:S(2)}, u32[]{:S(2)}) collective-permute-start(bf16[1500,384]{1,0:T(8,128)(2,1)} %bitcast.146), channel_id=1, source_target_pairs={{0,0},{1,2},{2,1},{3,3},{4,4},{5,6},{6,5},{7,7},{8,8},{9,10},{10,9... | collective-permute-start | bytes 3456008 | tf_op jit(solution)/shard_map/ppermute | solution.py:274
  69.3 11.0 %collective-permute-start.7 = (bf16[192,768]{1,0:T(8,128)(2,1)}, bf16[192,768]{1,0:T(8,128)(2,1)}, u32[]{:S(2)}, u32[]{:S(2)}) collective-permute-start(bf16[192,768]{1,0:T(8,128)(2,1)} %collective-permute-done.6), channel_id=1, source_target_pairs={{0,2},{2,0},{1,3},{3,1},{4,6},{6,4},{5,7},{7,5},{8,10},{10,8},{9,1... | collective-permute-start | bytes 884744 | tf_op jit(solution)/shard_map/ppermute | solution.py:281
  76.6 56.2 %collective-permute-start.1 = (bf16[192,2304]{1,0:T(8,128)(2,1)}, bf16[192,2304]{1,0:T(8,128)(2,1)}, u32[]{:S(2)}, u32[]{:S(2)}) collective-permute-start(bf16[192,2304]{1,0:T(8,128)(2,1)} %constant_dynamic-slice_fusion.7), channel_id=1, source_target_pairs={{0,1},{1,0},{2,3},{3,2},{4,5},{5,4},{6,7},{7,6},{8,9},{9,8},{10,11... | collective-permute-start | bytes 2654216 | tf_op jit(solution)/shard_map/ppermute | solution.py:280
  80.3 6.6 collective-permute-start.13
  81.1 53.5 %collective-permute-start.11 = (bf16[384,768]{1,0:T(8,128)(2,1)S(1)}, bf16[384,768]{1,0:T(8,128)(2,1)S(1)}, u32[]{:S(2)}, u32[]{:S(2)}) collective-permute-start(bf16[384,768]{1,0:T(8,128)(2,1)S(1)} %collective-permute-done.10), channel_id=1, source_target_pairs={{0,2},{2,0},{1,3},{3,1},{4,6},{6,4},{5,7},{7,5},{8,10},{10,8},{9,1... | collective-permute-start | bytes 1769480 | tf_op jit(solution)/shard_map/ppermute | solution.py:281
  86.9 215.5 %collective-permute-start.15 = (bf16[1024,768]{0,1:T(8,128)(2,1)}, bf16[1024,768]{0,1:T(8,128)(2,1)}, u32[]{:S(2)}, u32[]{:S(2)}) collective-permute-start(bf16[1024,768]{0,1:T(8,128)(2,1)} %bitcast.18), channel_id=1, source_target_pairs={{0,0},{1,2},{2,1},{3,3},{4,4},{5,6},{6,5},{7,7},{8,8},{9,10},{10,9... | collective-permute-start | bytes 4718600 | tf_op jit(solution)/shard_map/ppermute | solution.py:274
  132.8 5.3 collective-permute-start.2
  134.6 71.0 %collective-permute-start.9 = (bf16[1500,384]{1,0:T(8,128)(2,1)}, bf16[1500,384]{1,0:T(8,128)(2,1)}, u32[]{:S(2)}, u32[]{:S(2)}) collective-permute-start(bf16[1500,384]{1,0:T(8,128)(2,1)} %collective-permute-done.8), channel_id=1, source_target_pairs={{0,2},{2,0},{1,3},{3,1},{4,6},{6,4},{5,7},{7,5},{8,10},{10,8},{9,1... | collective-permute-start | bytes 3456008 | tf_op jit(solution)/shard_map/ppermute | solution.py:299
  136.8 61.8 %copy-start.11 = (bf16[1024,768]{0,1:T(8,128)(2,1)}, bf16[1024,768]{0,1:T(8,128)(2,1)S(1)}, u32[]{:S(2)}) copy-start(bf16[1024,768]{0,1:T(8,128)(2,1)S(1)} %collective-permute-done) | copy-start | bytes 4718596
  216.7 27.5 %copy-start.50 = (bf16[384,768]{1,0:T(8,128)(2,1)S(1)}, bf16[384,768]{1,0:T(8,128)(2,1)}, u32[]{:S(2)}) copy-start(bf16[384,768]{1,0:T(8,128)(2,1)} %copy-done.49) | copy-start | bytes 1769476
  216.7 27.5 %copy-start.63 = (bf16[384,768]{1,0:T(8,128)(2,1)S(1)}, bf16[384,768]{1,0:T(8,128)(2,1)}, u32[]{:S(2)}) copy-start(bf16[384,768]{1,0:T(8,128)(2,1)} %maximum_select_fusion.11) | copy-start | bytes 1769476
  254.6 37.0 %copy-start.52 = (bf16[32,24,768]{2,1,0:T(8,128)(2,1)}, bf16[32,24,768]{2,1,0:T(8,128)(2,1)S(1)}, u32[]{:S(2)}) copy-start(bf16[32,24,768]{2,1,0:T(8,128)(2,1)S(1)} %get-tuple-element.103) | copy-start | bytes 3538948
  254.6 37.0 %copy-start.54 = (bf16[32,24,768]{2,1,0:T(8,128)(2,1)}, bf16[32,24,768]{2,1,0:T(8,128)(2,1)S(1)}, u32[]{:S(2)}) copy-start(bf16[32,24,768]{2,1,0:T(8,128)(2,1)S(1)} %get-tuple-element.104) | copy-start | bytes 3538948
  254.6 37.0 %copy-start.56 = (bf16[32,24,768]{2,1,0:T(8,128)(2,1)}, bf16[32,24,768]{2,1,0:T(8,128)(2,1)S(1)}, u32[]{:S(2)}) copy-start(bf16[32,24,768]{2,1,0:T(8,128)(2,1)S(1)} %get-tuple-element.105) | copy-start | bytes 3538948
  254.7 37.0 %copy-start.57 = (bf16[32,24,768]{2,1,0:T(8,128)(2,1)}, bf16[32,24,768]{2,1,0:T(8,128)(2,1)S(1)}, u32[]{:S(2)}) copy-start(bf16[32,24,768]{2,1,0:T(8,128)(2,1)S(1)} %get-tuple-element.106) | copy-start | bytes 3538948
  254.7 37.0 %copy-start.88 = (f32[768]{0:T(1024)S(1)}, f32[768]{0:T(1024)}, u32[]{:S(2)}) copy-start(f32[768]{0:T(1024)} %get-tuple-element.83) | copy-start | bytes 9220
  309.0 13.7 %copy-start.41 = (bf16[1024,768]{0,1:T(8,128)(2,1)}, bf16[1024,768]{0,1:T(8,128)(2,1)S(1)}, u32[]{:S(2)}) copy-start(bf16[1024,768]{0,1:T(8,128)(2,1)S(1)} %get-tuple-element.98) | copy-start | bytes 4718596
  309.0 13.7 %copy-start.53 = (bf16[32,24,768]{2,1,0:T(8,128)(2,1)S(1)}, bf16[32,24,768]{2,1,0:T(8,128)(2,1)}, u32[]{:S(2)}) copy-start(bf16[32,24,768]{2,1,0:T(8,128)(2,1)} %copy-done.52) | copy-start | bytes 3538948
  309.0 13.7 %copy-start.55 = (bf16[32,24,768]{2,1,0:T(8,128)(2,1)S(1)}, bf16[32,24,768]{2,1,0:T(8,128)(2,1)}, u32[]{:S(2)}) copy-start(bf16[32,24,768]{2,1,0:T(8,128)(2,1)} %copy-done.54) | copy-start | bytes 3538948
  348.6 49.5 %copy-start.48 = (bf16[384,768]{1,0:T(8,128)(2,1)S(1)}, bf16[384,768]{1,0:T(8,128)(2,1)}, u32[]{:S(2)}) copy-start(bf16[384,768]{1,0:T(8,128)(2,1)} %copy-done.46) | copy-start | bytes 1769476
  348.6 49.5 %copy-start.62 = (bf16[384,768]{1,0:T(8,128)(2,1)S(1)}, bf16[384,768]{1,0:T(8,128)(2,1)}, u32[]{:S(2)}) copy-start(bf16[384,768]{1,0:T(8,128)(2,1)} %maximum_select_fusion.10) | copy-start | bytes 1769476
  488.3 20.1 %copy-start.5 = (f32[1024,768]{0,1:T(8,128)}, f32[1024,768]{0,1:T(8,128)S(1)}, u32[]{:S(2)}) copy-start(f32[1024,768]{0,1:T(8,128)S(1)} %copy.71) | copy-start | bytes 9437188
  491.8 7.3 collective-permute-start.18
  493.3 9.0 collective-permute-start.17
  508.2 220.0 %reduce-scatter.4.cloned.1.call-start = ((), (), s32[]{:S(2)}) async-start(), calls=%async_computation.7 | async-start | bytes 5271552 | tf_op jit(solution)/shard_map/reduce_scatter | solution.py:384
  533.2 335.3 %reduce-scatter.8.cloned.1.call-start = ((), (), s32[]{:S(2)}) async-start(), calls=%async_computation.11 | async-start | bytes 9732096 | tf_op jit(solution)/shard_map/reduce_scatter | solution.py:384
  562.4 306.0 %copy-start.22 = (bf16[1536,768]{1,0:T(8,128)(2,1)S(1)}, bf16[1536,768]{1,0:T(8,128)(2,1)}, u32[]{:S(2)}) copy-start(bf16[1536,768]{1,0:T(8,128)(2,1)} %maximum_select_fusion.1) | copy-start | bytes 7077892
  562.5 366.4 %all-gather.9.cloned.1.call-start = ((), (), s32[]{:S(2)}) async-start(), calls=%async_computation.10 | async-start | bytes 2506752 | tf_op jit(solution)/shard_map/all_gather | solution.py:385
  613.7 344.9 %all-gather.7.cloned.1.call-start = ((), (), s32[]{:S(2)}) async-start(), calls=%async_computation.8 | async-start | bytes 2715648 | tf_op jit(solution)/shard_map/all_gather | solution.py:385
  728.3 285.1 %all-gather.11.cloned.1.call-start = ((), (), s32[]{:S(2)}) async-start(), calls=%async_computation.12 | async-start | bytes 5013504 | tf_op jit(solution)/shard_map/all_gather | solution.py:385
  875.0 10.5 %collective-permute-start.19 = (bf16[1500,384]{1,0:T(8,128)(2,1)S(1)}, bf16[1500,384]{1,0:T(8,128)(2,1)S(1)}, u32[]{:S(2)}, u32[]{:S(2)}) collective-permute-start(bf16[1500,384]{1,0:T(8,128)(2,1)S(1)} %constant_dynamic-slice_fusion), channel_id=1, source_target_pairs={{0,2},{2,0},{1,3},{3,1},{4,6},{6,4},{5,7},{7,5},{8,10},{10,8},{9,1... | collective-permute-start | bytes 3456008 | tf_op jit(solution)/shard_map/ppermute | solution.py:413
  877.8 21.7 %collective-permute-start.14 = (bf16[1024,768]{0,1:T(8,128)(2,1)S(1)}, bf16[1024,768]{0,1:T(8,128)(2,1)S(1)}, u32[]{:S(2)}, u32[]{:S(2)}) collective-permute-start(bf16[1024,768]{0,1:T(8,128)(2,1)S(1)} %copy-done.40), channel_id=1, source_target_pairs={{0,0},{1,2},{2,1},{3,3},{4,4},{5,6},{6,5},{7,7},{8,8},{9,10},{10,9... | collective-permute-start | bytes 4718600 | tf_op jit(solution)/shard_map/ppermute | solution.py:274
  883.1 33.2 %collective-permute-start.16 = (bf16[1024,768]{0,1:T(8,128)(2,1)}, bf16[1024,768]{0,1:T(8,128)(2,1)S(1)}, u32[]{:S(2)}, u32[]{:S(2)}) collective-permute-start(bf16[1024,768]{0,1:T(8,128)(2,1)} %fusion.51), channel_id=1, source_target_pairs={{0,0},{1,2},{2,1},{3,3},{4,4},{5,6},{6,5},{7,7},{8,8},{9,10},{10,9... | collective-permute-start | bytes 4718600 | tf_op jit(solution)/shard_map/ppermute | solution.py:274
  886.9 41.9 %collective-permute-start.20 = (bf16[1500,384]{1,0:T(8,128)(2,1)}, bf16[1500,384]{1,0:T(8,128)(2,1)}, u32[]{:S(2)}, u32[]{:S(2)}) collective-permute-start(bf16[1500,384]{1,0:T(8,128)(2,1)} %add_convert_fusion.8), channel_id=1, source_target_pairs={{0,0},{1,2},{2,1},{3,3},{4,4},{5,6},{6,5},{7,7},{8,8},{9,10},{10,9... | collective-permute-start | bytes 3456008 | tf_op jit(solution)/shard_map/ppermute | solution.py:274
  (74 other events, 295.9 us)
Sparse Core Ops, SparseCore 0:
  10.9 110.8 all-gather.12
  508.3 105.2 reduce-scatter.5
  620.2 108.0 reduce-scatter.3
  734.0 134.3 reduce-scatter.7
  870.8 43.7 all-gather.8
  916.9 41.7 all-gather.6
  961.2 52.1 all-gather.10

commit v2 on v1

v2 whole, which is shorter than its diff:
```python
import math

import jax
import jax.numpy as jnp
from jax import lax
from jax.experimental import pallas as pl
from jax.experimental.pallas import tpu as pltpu
from jax.sharding import Mesh
from jax.sharding import PartitionSpec as P

HEADS = 12
HD = 64
EPSILON = 1e-05
NEG = -1e30
PROMPT = 1024
REACH = 256
bf16 = jnp.bfloat16
f32 = jnp.float32
FLIP = [(0, 1), (1, 0)]


def mm(a, b):
    return jnp.dot(a, b, preferred_element_type=f32)


def mm_t(a, b):
    return lax.dot_general(a, b, (((1,), (1,)), ((), ())), preferred_element_type=f32)


def t_mm(a, b):
    return lax.dot_general(a, b, (((0,), (0,)), ((), ())), preferred_element_type=f32)


def call(kernel, scalars, args, grid, in_specs, out_specs, out_shape, scratch=(), cost=None):
    spec = pltpu.PrefetchScalarGridSpec(
        num_scalar_prefetch=1, grid=grid, in_specs=in_specs, out_specs=out_specs, scratch_shapes=list(scratch)
    )
    estimate = None
    if cost is not None:
        estimate = pl.CostEstimate(flops=cost, bytes_accessed=1 << 20, transcendentals=0)
    return pl.pallas_call(
        kernel,
        grid_spec=spec,
        out_shape=out_shape,
        cost_estimate=estimate,
        compiler_params=pltpu.CompilerParams(vmem_limit_bytes=60 * 2**20),
    )(scalars, *args)


def shape(dims, kind=bf16):
    return jax.ShapeDtypeStruct(dims, kind)


def half_of(lane, h):
    return (lane < HD) if h == 0 else (lane >= HD)


def delta_of(do, o):
    x = do.astype(f32) * o.astype(f32)
    hi = x.astype(bf16)
    lo = (x - hi.astype(f32)).astype(bf16)
    r = lax.broadcasted_iota(jnp.int32, (8, 128), 0)
    lane = lax.broadcasted_iota(jnp.int32, (8, 128), 1)
    pick = jnp.where((lane // HD) == r, 1.0, 0.0).astype(bf16)
    return mm_t(pick, hi) + mm_t(pick, lo)


def cross_fwd(base, pairs, q, k, v, valid, block=1024):
    tq, tk = q.shape[0], k.shape[0]
    block = min(block, tq)

    def kernel(s_ref, q_ref, k_ref, v_ref, o_ref, l_ref, ks, vts):
        @pl.when(pl.program_id(1) == 0)
        def _():
            low = lax.broadcasted_iota(jnp.int32, (tk, 128), 1)
            row = lax.broadcasted_iota(jnp.int32, (tk, 128), 0)
            bias = jnp.where(row >= valid, NEG, 0.0).astype(bf16)
            one = jnp.ones((tk, 128), bf16)
            for h in range(2):
                ks[h] = jnp.where(half_of(low, h), k_ref[...], bias)
                vts[h] = jnp.where(half_of(low, h), v_ref[...], one).T

        lane = lax.broadcasted_iota(jnp.int32, (block, 128), 1)
        qq = q_ref[...] * bf16(0.125)
        scores = []
        for h in range(2):
            spare = lane == (HD if h == 0 else 0)
            qh = jnp.where(half_of(lane, h), qq, jnp.where(spare, 1.0, 0.0).astype(bf16))
            scores.append(mm_t(ks[h], qh))
        outs = []
        for h, s in enumerate(scores):
            m = jnp.max(s, axis=0, keepdims=True)
            o = mm(vts[h], jnp.exp(s - m).astype(bf16))
            total = o[HD : HD + 1] if h == 0 else o[0:1]
            outs.append(o * (1.0 / total))
            l_ref[0, h : h + 1, :] = m + jnp.log(total)
        sub = lax.broadcasted_iota(jnp.int32, (128, block), 0)
        o_ref[...] = jnp.where(sub < HD, outs[0], outs[1]).T.astype(bf16)

    qspec = pl.BlockSpec((block, 128), lambda p, i, s: (i, s[0] + p))
    kspec = pl.BlockSpec((tk, 128), lambda p, i, s: (0, s[0] + p))
    return call(
        kernel, jnp.reshape(base, (1,)).astype(jnp.int32), (q, k, v), (pairs, tq // block), [qspec, kspec, kspec],
        [pl.BlockSpec((block, 128), lambda p, i, s: (i, p)), pl.BlockSpec((1, 8, block), lambda p, i, s: (p, 0, i))],
        [shape((tq, pairs * 128)), shape((pairs, 8, tq), f32)],
        [pltpu.VMEM((2, tk, 128), bf16), pltpu.VMEM((2, 128, tk), bf16)],
        4 * tq * tk * 256 * pairs,
    )


def cross_bwd(base, pairs, q, k, v, o, do, lse, valid, block=1024):
    tq, tk = q.shape[0], k.shape[0]
    block = min(block, tq)
    steps = tq // block

    def kernel(s_ref, q_ref, k_ref, v_ref, o_ref, do_ref, l_ref, dq_ref, d_ref, ks, kts, dka, dva):
        @pl.when(pl.program_id(1) == 0)
        def _():
            low = lax.broadcasted_iota(jnp.int32, (tk, 128), 1)
            row = lax.broadcasted_iota(jnp.int32, (tk, 128), 0)
            bias = jnp.where(row >= valid, NEG, 0.0).astype(bf16)
            zero = jnp.zeros((tk, 128), bf16)
            for h in range(2):
                ks[h] = jnp.where(half_of(low, h), k_ref[...], bias)
                kts[h] = jnp.where(half_of(low, h), k_ref[...], zero).T
            dka[...] = jnp.zeros((tk, 128), f32)
            dva[...] = jnp.zeros((tk, 128), f32)

        lane = lax.broadcasted_iota(jnp.int32, (block, 128), 1)
        qq = q_ref[...] * bf16(0.125)
        dd = do_ref[...]
        delta = delta_of(dd, o_ref[...])
        zero = jnp.zeros((block, 128), bf16)
        dqt, dk, dv = None, dka[...], dva[...]
        for h in range(2):
            mine = half_of(lane, h)
            spare = lane == (HD if h == 0 else 0)
            qc = jnp.where(mine, qq, zero)
            qs = jnp.where(spare, jnp.ones((block, 128), bf16), qc)
            dh = jnp.where(mine, dd, zero)
            p = jnp.exp(mm_t(ks[h], qs) - l_ref[0, h : h + 1, :])
            ds = (p * (mm_t(v_ref[...], dh) - delta[h : h + 1])).astype(bf16)
            dv = dv + mm(p.astype(bf16), dh)
            dk = dk + mm(ds, qc)
            part = mm(kts[h], ds)
            dqt = part if dqt is None else dqt + part
        dka[...] = dk
        dva[...] = dv
        dq_ref[...] = (dqt * 0.125).T.astype(bf16)

        @pl.when(pl.program_id(1) == steps - 1)
        def _():
            d_ref[0] = dka[...].astype(bf16)
            d_ref[1] = dva[...].astype(bf16)

    mine = pl.BlockSpec((block, 128), lambda p, i, s: (i, p))
    qspec = pl.BlockSpec((block, 128), lambda p, i, s: (i, s[0] + p))
    kspec = pl.BlockSpec((tk, 128), lambda p, i, s: (0, s[0] + p))
    return call(
        kernel, jnp.reshape(base, (1,)).astype(jnp.int32), (q, k, v, o, do, lse), (pairs, steps),
        [qspec, kspec, kspec, mine, mine, pl.BlockSpec((1, 8, block), lambda p, i, s: (p, 0, i))],
        [mine, pl.BlockSpec((2, tk, 128), lambda p, i, s: (0, 0, p))],
        [shape((tq, pairs * 128)), shape((2, tk, pairs * 128))],
        [pltpu.VMEM((2, tk, 128), bf16), pltpu.VMEM((2, 128, tk), bf16), pltpu.VMEM((tk, 128), f32), pltpu.VMEM((tk, 128), f32)],
        2 * tq * tk * 10 * 256 * pairs,
    )


def spans(r0, block):
    if r0 < PROMPT:
        return ([(0, r0)] if r0 else []) + [(r0, r0 + block)]
    left = max(PROMPT, r0 - REACH)
    before = [(0, r0)] if left == PROMPT else [(0, PROMPT), (left, r0)]
    return before + [(r0, r0 + block)]


def seg_marks(seg):
    lane = lax.broadcasted_iota(jnp.int32, (seg.shape[0], 128), 1) % HD
    same = lane == seg[:, None]
    kmark = jnp.where(same, 1.0, 0.0).astype(bf16)
    qmark = jnp.where(same | (lane == 0) | (lane > 8), 0.0, NEG).astype(bf16)
    return kmark, qmark


def half_specs(rows, first=0):
    return [pl.BlockSpec((3, rows, 128), lambda p, s: (0, 0, first + p))] * 2


def self_fwd(first, pairs, place, keep, recv, kmark, qmark, block=512):
    rows, width = keep.shape[1], pairs * 128
    t = 2 * rows

    def kernel(s_ref, a_ref, b_ref, km_ref, qm_ref, o_ref, give_ref, l_ref, qf, ks, vts):
        mine0 = pl.multiple_of(s_ref[0] * rows, rows)
        other0 = pl.multiple_of((1 - s_ref[0]) * rows, rows)
        low = lax.broadcasted_iota(jnp.int32, (rows, 128), 1)
        one = jnp.ones((rows, 128), bf16)
        for ref, at in ((a_ref, mine0), (b_ref, other0)):
            spot = pl.ds(at, rows)
            qf[spot, :] = ref[0] * bf16(0.125)
            for h in range(2):
                ks[h, spot, :] = jnp.where(half_of(low, h), ref[1], km_ref[spot, :])
                vts[h, :, spot] = jnp.where(half_of(low, h), ref[2], one).T
        lane = lax.broadcasted_iota(jnp.int32, (block, 128), 1)
        hide = lax.broadcasted_iota(jnp.int32, (block, block), 0) > lax.broadcasted_iota(jnp.int32, (block, block), 1)
        tasks = [(r0, h) for r0 in range(0, t, block) for h in range(2)]

        def scores(task):
            r0, h = task
            spot = pl.ds(r0, block)
            qs = jnp.where(half_of(lane, h), qf[spot, :], qm_ref[spot, :])
            out = [mm_t(ks[h, pl.ds(a, b - a), :], qs) for a, b in spans(r0, block)]
            out[-1] = jnp.where(hide, NEG, out[-1])
            return out

        now, outs = scores(tasks[0]), [None, None]
        for i, (r0, h) in enumerate(tasks):
            later = scores(tasks[i + 1]) if i + 1 < len(tasks) else None
            m = None
            for s in now:
                top = jnp.max(s, axis=0, keepdims=True)
                m = top if m is None else jnp.maximum(m, top)
            o = None
            for s, (a, b) in zip(now, spans(r0, block)):
                part = mm(vts[h, :, pl.ds(a, b - a)], jnp.exp(s - m).astype(bf16))
                o = part if o is None else o + part
            total = o[HD : HD + 1] if h == 0 else o[0:1]
            l_ref[0, h : h + 1, pl.ds(r0, block)] = m + jnp.log(total)
            outs[h] = o * (1.0 / total)
            if h == 1:
                sub = lax.broadcasted_iota(jnp.int32, (128, block), 0)
                o_ref[pl.ds(r0, block), :] = jnp.where(sub < HD, outs[0], outs[1]).T.astype(bf16)
            now = later
        give_ref[...] = o_ref[pl.ds(other0, rows), :]

    whole = pl.BlockSpec((t, 128), lambda p, s: (0, 0))
    return call(
        kernel, jnp.reshape(place, (1,)).astype(jnp.int32), (keep, recv, kmark, qmark), (pairs,),
        half_specs(rows, first) + [whole, whole],
        [pl.BlockSpec((t, 128), lambda p, s: (0, p)), pl.BlockSpec((rows, 128), lambda p, s: (0, p)), pl.BlockSpec((1, 8, t), lambda p, s: (p, 0, 0))],
        [shape((t, width)), shape((rows, width)), shape((pairs, 8, t), f32)],
        [pltpu.VMEM((t, 128), bf16), pltpu.VMEM((2, t, 128), bf16), pltpu.VMEM((2, 128, t), bf16)],
        2 * t * t * 4 * width,
    )


def self_bwd(first, pairs, place, keep, recv, o, dkeep, drecv, lse, kmark, qmark, block=256):
    rows, width = keep.shape[1], pairs * 128
    t = 2 * rows

    def kernel(s_ref, a_ref, b_ref, o_ref, da_ref, db_ref, l_ref, km_ref, qm_ref, give_ref, keep_ref, qf, df, vf, ks, kts, dqa, dka, dva):
        mine0 = pl.multiple_of(s_ref[0] * rows, rows)
        other0 = pl.multiple_of((1 - s_ref[0]) * rows, rows)
        low = lax.broadcasted_iota(jnp.int32, (rows, 128), 1)
        zero = jnp.zeros((rows, 128), bf16)
        for ref, dref, at in ((a_ref, da_ref, mine0), (b_ref, db_ref, other0)):
            spot = pl.ds(at, rows)
            qf[spot, :] = ref[0] * bf16(0.125)
            df[spot, :] = dref[...]
            vf[spot, :] = ref[2]
            for h in range(2):
                ks[h, spot, :] = jnp.where(half_of(low, h), ref[1], km_ref[spot, :])
                kts[h, :, spot] = jnp.where(half_of(low, h), ref[1], zero).T
        dka[...] = jnp.zeros((t, 128), f32)
        dva[...] = jnp.zeros((t, 128), f32)
        lane = lax.broadcasted_iota(jnp.int32, (block, 128), 1)
        hide = lax.broadcasted_iota(jnp.int32, (block, block), 0) > lax.broadcasted_iota(jnp.int32, (block, block), 1)
        none = jnp.zeros((block, 128), bf16)
        for r0 in range(0, t, block):
            spot = pl.ds(r0, block)
            dd = df[spot, :]
            delta = delta_of(dd, o_ref[spot, :])
            dqt = None
            for h in range(2):
                mine = half_of(lane, h)
                qc = jnp.where(mine, qf[spot, :], none)
                qs = jnp.where(mine, qf[spot, :], qm_ref[spot, :])
                dh = jnp.where(mine, dd, none)
                log_total = l_ref[0, h : h + 1, spot]
                for a, b in spans(r0, block):
                    keys = pl.ds(a, b - a)
                    s = mm_t(ks[h, keys, :], qs)
                    if a == r0:
                        s = jnp.where(hide, NEG, s)
                    p = jnp.exp(s - log_total)
                    ds = (p * (mm_t(vf[keys, :], dh) - delta[h : h + 1])).astype(bf16)
                    dva[keys, :] += mm(p.astype(bf16), dh)
                    dka[keys, :] += mm(ds, qc)
                    part = mm(kts[h, :, keys], ds)
                    dqt = part if dqt is None else dqt + part
            dqa[spot, :] = (dqt * 0.125).T.astype(bf16)
        for out, at in ((give_ref, other0), (keep_ref, mine0)):
            spot = pl.ds(at, rows)
            out[0] = dqa[spot, :]
            out[1] = dka[spot, :].astype(bf16)
            out[2] = dva[spot, :].astype(bf16)

    whole = pl.BlockSpec((t, 128), lambda p, s: (0, 0))
    half = pl.BlockSpec((rows, 128), lambda p, s: (0, first + p))
    return call(
        kernel, jnp.reshape(place, (1,)).astype(jnp.int32), (keep, recv, o, dkeep, drecv, lse, kmark, qmark), (pairs,),
        half_specs(rows, first) + [pl.BlockSpec((t, 128), lambda p, s: (0, p)), half, half, pl.BlockSpec((1, 8, t), lambda p, s: (p, 0, 0)), whole, whole],
        half_specs(rows),
        [shape((3, rows, width))] * 2,
        [pltpu.VMEM((t, 128), bf16)] * 3 + [pltpu.VMEM((2, t, 128), bf16), pltpu.VMEM((2, 128, t), bf16), pltpu.VMEM((t, 128), bf16)]
        + [pltpu.VMEM((t, 128), f32)] * 2,
        2 * t * t * 8 * width,
    )


def norm_stats(rows):
    centered = rows - jnp.mean(rows, axis=-1, keepdims=True)
    inv = lax.rsqrt(jnp.mean(centered * centered, axis=-1, keepdims=True) + EPSILON)
    return centered * inv, inv


def norm(rows, gain, shift):
    return norm_stats(rows)[0] * gain + shift


def norm_back(rows, gain, dy):
    n, inv = norm_stats(rows)
    dn = dy * gain
    dh = inv * (dn - jnp.mean(dn, axis=-1, keepdims=True) - n * jnp.mean(dn * n, axis=-1, keepdims=True))
    return dh, jnp.sum(dy * n, axis=0, keepdims=True), jnp.sum(dy, axis=0, keepdims=True)


ERFC = (
    0.22567585470008253, 0.22566975083164525, 0.20784161289369674, 0.1685452087610459, 0.14142852065437478,
    -0.005612938524279035, 0.1691005263450779, -0.1829144800497475, 0.05026606972001335,
)


def gelu_parts(u):
    bell = jnp.exp(u * u * -0.5)
    t = 1.0 / (1.0 + jnp.abs(u) * (0.4 * math.sqrt(0.5)))
    poly = jnp.full_like(t, ERFC[-1])
    for value in ERFC[-2::-1]:
        poly = poly * t + value
    tail = bell * t * poly * 0.5
    cdf = jnp.where(u < 0.0, tail, 1.0 - tail)
    return u * cdf, cdf + u * bell * (1.0 / math.sqrt(2.0 * math.pi))


def const(dims):
    return pl.BlockSpec(dims, lambda i, s: (0,) * len(dims))


def once(dims):
    return pl.BlockSpec(dims, lambda i, s: (0,) * len(dims), pipeline_mode=pl.Buffered(1))


def tile(rows, width):
    return pl.BlockSpec((rows, width), lambda i, s: (i, 0))


def fill(full, s, own, mine, sib):
    rows = own.shape[0]
    c, h = s[0], s[1]
    full[pl.ds(pl.multiple_of(h * rows, 128), rows), :] = own[...].astype(bf16)
    start = (1 - h) * rows
    full[pl.ds(pl.multiple_of(start + c * (rows // 2), 64), rows // 2), :] = mine[...]
    full[pl.ds(pl.multiple_of(start + (1 - c) * (rows // 2), 64), rows // 2), :] = sib[...]


def weight_specs(weight):
    own, mine, sib = weight
    return [once(own.shape), once(mine.shape), once(sib.shape)]


def full_shape(weight):
    return (2 * weight[0].shape[0], weight[0].shape[1])


def at_core(c, width):
    return pl.ds(pl.multiple_of(c * width, 128), width)


def norm_qkv(s, x_own, x_in, weight, table, rows=512):
    t, width = x_own.shape
    hw = width // 2

    def kernel(s_ref, xo, xi, own, mine, sib, tab, w, a_ref, keep, give):
        @pl.when(pl.program_id(0) == 0)
        def _():
            fill(w, s_ref, own, mine, sib)

        x = jnp.where(s_ref[2] == 1, xo[...].astype(f32), xi[...].astype(f32))
        a = norm(x, tab[0:1], tab[4:5]).astype(bf16)
        a_ref[...] = a
        for j in range(3):
            y = mm(a, w[:, j * width : (j + 1) * width])
            if j != 1:
                y = y + tab[8 + j // 2 : 9 + j // 2]
            low, high = y[:, :hw].astype(bf16), y[:, hw:].astype(bf16)
            first = s_ref[0] == 0
            keep[j] = jnp.where(first, low, high)
            give[j] = jnp.where(first, high, low)

    third = pl.BlockSpec((3, rows, hw), lambda i, s: (0, i, 0))
    dims = full_shape(weight)
    return call(
        kernel, s, (x_own, x_in, *weight, table), (t // rows,),
        [tile(rows, width)] * 2 + weight_specs(weight) + [const(table.shape)],
        [const(dims), tile(rows, width), third, third],
        [shape(dims), shape((t, width)), shape((3, t, hw)), shape((3, t, hw))],
        cost=2 * t * width * 3 * width,
    )


def beside(refs):
    return jnp.concatenate([ref[...] for ref in refs], axis=1) if len(refs) > 1 else refs[0][...]


def self_project(s, ctx, ctx_in, x_own, x_in, w_out, w_q, table, rows=512):
    t, width = x_own.shape
    hw = width // 2
    steps = t // rows
    n = len(ctx)

    def kernel(s_ref, *refs):
        cks, cis = refs[:n], refs[n : 2 * n]
        xo, xi, o1, o2, o3, q1, q2, q3, tab, wo, wq, h_ref, a_ref, qc_ref = refs[2 * n :]

        @pl.when(pl.program_id(0) == 0)
        def _():
            fill(wo, s_ref, o1, o2, o3)
            fill(wq, s_ref, q1, q2, q3)

        c = s_ref[0]
        x = jnp.where(s_ref[2] == 1, xo[...].astype(f32), xi[...].astype(f32))
        h = x + mm(beside(cks), wo[at_core(c, hw), :]) + mm(beside(cis), wo[at_core(1 - c, hw), :]) + tab[10:11]
        h_ref[...] = h
        a = norm(h, tab[1:2], tab[5:6]).astype(bf16)
        a_ref[...] = a
        qc_ref[...] = (mm(a, wq[...]) + tab[11:12]).astype(bf16)

    dims = full_shape(w_out)
    return call(
        kernel, s, (*ctx, *ctx_in, x_own, x_in, *w_out, *w_q, table), (steps,),
        [pl.BlockSpec((rows, part.shape[1]), lambda i, s: (s[0] * steps + i, 0)) for part in ctx]
        + [tile(rows, part.shape[1]) for part in ctx_in] + [tile(rows, width), tile(rows, width)]
        + weight_specs(w_out) + weight_specs(w_q) + [const(table.shape)],
        [const(dims), const(dims), tile(rows, width), tile(rows, width), tile(rows, width)],
        [shape(dims), shape(dims), shape((t, width), f32), shape((t, width)), shape((t, width))],
        cost=4 * t * width * width,
    )


def frame_kv(s, half, twin, weight, table, rows=512):
    count, hw = half.shape
    width = 2 * hw
    steps = -(-count // rows)

    def kernel(s_ref, fa, fb, own, mine, sib, tab, w, k_ref, v_ref):
        @pl.when(pl.program_id(0) == 0)
        def _():
            fill(w, s_ref, own, mine, sib)

        c = s_ref[0]
        live = lax.broadcasted_iota(jnp.int32, (rows, 1), 0) + pl.program_id(0) * rows < count
        for j, out in enumerate((k_ref, v_ref)):
            mine0 = pl.multiple_of(j * width + c * hw, 128)
            other0 = pl.multiple_of(j * width + (1 - c) * hw, 128)
            y = mm(fa[...], w[pl.ds(mine0, hw), :]) + mm(fb[...], w[pl.ds(other0, hw), :])
            if j == 1:
                y = y + tab[12:13]
            out[...] = jnp.where(live, y, 0.0).astype(bf16)

    dims = full_shape(weight)
    return call(
        kernel, s, (half, twin, *weight, table), (steps,),
        [tile(rows, hw)] * 2 + weight_specs(weight) + [const(table.shape)],
        [const(dims), tile(rows, width), tile(rows, width)],
        [shape(dims), shape((steps * rows, width)), shape((steps * rows, width))],
        cost=4 * count * width * width,
    )


def middle(s, h1, c2_keep, c2_give, cot_own, cot_in, w_out, ffw, table, fc1_shift, rows=256):
    t, width = h1.shape
    units = fc1_shift.shape[1] // width
    hw = width // 2
    piece = ffw.shape[2]

    def kernel(s_ref, h1_ref, ck_ref, cg_ref, co, ci, o1, o2, o3, w1, w2, tab, shift, wo, out, a_ref, g_ref, dm_ref, du_ref, d2_ref, dh_ref, dk_ref, dg_ref, vec):
        @pl.when(pl.program_id(0) == 0)
        def _():
            fill(wo, s_ref, o1, o2, o3)
            vec[...] = jnp.zeros(vec.shape, f32)

        def up(h, j):
            at, many = (h * units + j) * (hw // piece), hw // piece
            return w1[at : at + many, 0].reshape(hw, width)

        def down(j):
            many = width // piece
            return w2[j * many : (j + 1) * many, 0].reshape(width, width)

        c = s_ref[0]
        h2 = h1_ref[...] + mm(ck_ref[...], wo[at_core(c, hw), :]) + mm(cg_ref[...], wo[at_core(1 - c, hw), :]) + tab[13:14]
        n2, inv2 = norm_stats(h2)
        a = (n2 * tab[2:3] + tab[6:7]).astype(bf16)
        a_ref[...] = a
        acc = h2 + tab[14:15]
        slopes = []
        for j in range(units):
            cols = slice(j * width, (j + 1) * width)
            u = mm(a[:, :hw], up(0, j)) + mm(a[:, hw:], up(1, j)) + shift[:, cols]
            g, slope = gelu_parts(u.astype(bf16).astype(f32))
            slopes.append(slope)
            g = g.astype(bf16)
            g_ref[:, cols] = g
            acc = acc + mm(g, down(j))
        n3, inv3 = norm_stats(acc)
        out[...] = (n3 * tab[3:4] + tab[7:8]).astype(bf16)

        def back(n, inv, gain, dy):
            dn = dy * gain
            return inv * (dn - jnp.mean(dn, axis=-1, keepdims=True) - n * jnp.mean(dn * n, axis=-1, keepdims=True))

        def total(x):
            return jnp.sum(x, axis=0, keepdims=True)

        dy = jnp.where(s_ref[2] == 1, co[...].astype(f32), ci[...].astype(f32))
        dh3 = back(n3, inv3, tab[3:4], dy)
        dm = dh3.astype(bf16)
        dm_ref[...] = dm
        halves = [None, None]
        for j in range(units):
            cols = slice(j * width, (j + 1) * width)
            du = (slopes[j] * mm_t(dm, down(j))).astype(bf16)
            du_ref[:, cols] = du
            vec[0:1, cols] += total(du.astype(f32))
            for h in range(2):
                part = mm_t(du, up(h, j))
                halves[h] = part if halves[h] is None else halves[h] + part
        da = jnp.concatenate(halves, axis=1)
        dh2 = dh3 + back(n2, inv2, tab[2:3], da)
        d2 = dh2.astype(bf16)
        d2_ref[...] = d2
        dh_ref[...] = dh2
        dk_ref[...] = mm_t(d2, wo[at_core(c, hw), :]).astype(bf16)
        dg_ref[...] = mm_t(d2, wo[at_core(1 - c, hw), :]).astype(bf16)
        rows_of = [total(dm.astype(f32)), total(d2.astype(f32)), total(dy * n3), total(dy), total(da * n2), total(da)]
        for k, value in enumerate(rows_of):
            line, at = 1 + k // 3, (k % 3) * width
            vec[line : line + 1, at : at + width] += value

    dims = full_shape(w_out)
    ff = units * width
    line = tile(rows, width)
    wide, half = tile(rows, ff), tile(rows, hw)
    gathered = [pl.BlockSpec((32, 1, piece, width), lambda i, s, k=k: (0, k, 0, 0), pipeline_mode=pl.Buffered(1)) for k in range(2)]
    return call(
        kernel, s, (h1, c2_keep, c2_give, cot_own, cot_in, *w_out, ffw, ffw, table, fc1_shift), (t // rows,),
        [line, half, half, line, line] + weight_specs(w_out) + gathered + [const(table.shape), const(fc1_shift.shape)],
        [const(dims), line, line, wide, line, wide, line, line, half, half, const((8, ff))],
        [shape(dims), shape((t, width)), shape((t, width)), shape((t, ff)), shape((t, width)), shape((t, ff)), shape((t, width)),
         shape((t, width), f32), shape((t, hw)), shape((t, hw)), shape((8, ff), f32)],
        cost=8 * t * width * ff + 4 * t * width * width,
    )


def ff_grads(s, a, du, g, dm):
    t, width = a.shape
    hw = width // 2
    ff = du.shape[1]
    units = ff // width
    piece = hw * units // 16

    def kernel(s_ref, a_ref, du_ref, g_ref, dm_ref, out):
        step = pl.program_id(0)

        @pl.when(step < 2 * units)
        def _():
            out[...] = t_mm(a_ref[...], du_ref[...]).astype(bf16).reshape(out.shape)

        @pl.when(step >= 2 * units)
        def _():
            out[...] = t_mm(g_ref[...], dm_ref[...]).astype(bf16).reshape(out.shape)

    n1 = 2 * units
    many = hw // piece
    return call(
        kernel, s, (a, du, g, dm), (2 * n1,),
        [pl.BlockSpec((t, hw), lambda i, s: (0, jnp.minimum(i // units, 1))),
         pl.BlockSpec((t, width), lambda i, s: (0, jnp.where(i < n1, i % units, units - 1))),
         pl.BlockSpec((t, hw), lambda i, s: (0, jnp.maximum(i - n1, 0))),
         pl.BlockSpec((t, width), lambda i, s: (0, 0))],
        pl.BlockSpec((many, 1, piece, width), lambda i, s: (jnp.where(i < n1, i, i - n1), jnp.where(i < n1, 0, 1), 0, 0)),
        shape((32, 2, piece, width)),
        cost=4 * t * width * ff,
    )


def cross_back(s, dq_keep, dq_give, h1, dh2, w_q, w_out, table, rows=512):
    t, width = h1.shape
    hw = width // 2

    def kernel(s_ref, dk_ref, dg_ref, h_ref, dh2_ref, wq, wo, tab, dh_ref, d1_ref, keep, give, vec):
        @pl.when(pl.program_id(0) == 0)
        def _():
            vec[...] = jnp.zeros(vec.shape, f32)

        c = s_ref[0]
        da = mm_t(dk_ref[...], wq[:, at_core(c, hw)]) + mm_t(dg_ref[...], wq[:, at_core(1 - c, hw)])
        dres, dgain, dshift = norm_back(h_ref[...], tab[1:2], da)
        dh1 = dh2_ref[...] + dres
        dh_ref[...] = dh1
        d1 = dh1.astype(bf16)
        d1_ref[...] = d1
        keep[...] = mm_t(d1, wo[at_core(c, hw), :]).astype(bf16)
        give[...] = mm_t(d1, wo[at_core(1 - c, hw), :]).astype(bf16)
        vec[0:1] += dgain
        vec[1:2] += dshift
        vec[2:3] += jnp.sum(d1.astype(f32), axis=0, keepdims=True)
        vec[3:4, at_core(c, hw)] += jnp.sum(dk_ref[...].astype(f32), axis=0, keepdims=True)
        vec[3:4, at_core(1 - c, hw)] += jnp.sum(dg_ref[...].astype(f32), axis=0, keepdims=True)

    line, half = tile(rows, width), tile(rows, hw)
    return call(
        kernel, s, (dq_keep, dq_give, h1, dh2, w_q, w_out, table), (t // rows,),
        [half, half, line, line, once(w_q.shape), once(w_out.shape), const(table.shape)],
        [line, line, half, half, const((8, width))],
        [shape((t, width), f32), shape((t, width)), shape((t, hw)), shape((t, hw)), shape((8, width), f32)],
        cost=4 * t * width * width,
    )


def frame_back(s, keep, recv, half, twin, weight, rows=512):
    count, hw = half.shape
    width = 2 * hw
    steps = -(-count // rows)

    def kernel(s_ref, ka, kb, fa, fb, w, fkeep, fgive, xkeep, xgive, vec, acc):
        @pl.when(pl.program_id(0) == 0)
        def _():
            vec[...] = jnp.zeros(vec.shape, f32)
            acc[...] = jnp.zeros(acc.shape, f32)

        c, h = s_ref[0], s_ref[1]
        live = lax.broadcasted_iota(jnp.int32, (rows, 1), 0) + pl.program_id(0) * rows < count
        zero = jnp.zeros((rows, hw), bf16)
        f_mine = jnp.where(live, fa[...], zero)
        f_other = jnp.where(live, fb[...], zero)
        back = None
        for j in range(2):
            d = (ka[j].astype(f32) + kb[j].astype(f32)).astype(bf16)
            part = mm_t(d, w[j * width : (j + 1) * width, at_core(c, hw)])
            back = part if back is None else back + part
            acc[j, at_core(c, hw), :] += t_mm(f_mine, d)
            acc[j, at_core(1 - c, hw), :] += t_mm(f_other, d)
            if j == 1:
                vec[0:1] += jnp.sum(d.astype(f32), axis=0, keepdims=True)
        low, high = back[:, :hw].astype(bf16), back[:, hw:].astype(bf16)
        fkeep[...] = jnp.where(c == 0, low, high)
        fgive[...] = jnp.where(c == 0, high, low)

        @pl.when(pl.program_id(0) == steps - 1)
        def _():
            xkeep[...] = acc[h].astype(bf16)
            xgive[...] = acc[1 - h].astype(bf16)

    pair = pl.BlockSpec((2, rows, hw), lambda i, s: (0, i, 0))
    strip = tile(rows, hw)
    return call(
        kernel, s, (keep, recv, half, twin, weight), (steps,),
        [pair, pair, strip, strip, once(weight.shape)],
        [strip, strip, const((width, hw)), const((width, hw)), const((8, hw))],
        [shape((count, hw)), shape((count, hw)), shape((width, hw)), shape((width, hw)), shape((8, hw), f32)],
        [pltpu.VMEM((2, width, hw), f32)],
        cost=8 * count * width * width,
    )


def give_grads(s, c2_keep, c2_give, d2, a2, dq_give):
    t, width = d2.shape
    hw = width // 2

    def kernel(s_ref, k_ref, g_ref, d_ref, a_ref, q_ref, out):
        c = s_ref[0]
        out[0, at_core(c, hw), :] = t_mm(k_ref[...], d_ref[...]).astype(bf16)
        out[0, at_core(1 - c, hw), :] = t_mm(g_ref[...], d_ref[...]).astype(bf16)
        out[1] = t_mm(a_ref[...], q_ref[...]).astype(bf16)

    half = const((t, hw))
    return call(
        kernel, s, (c2_keep, c2_give, d2, a2, dq_give), (1,),
        [half, half, pl.BlockSpec((t, hw), lambda i, s: (0, 1 - s[0])), const((t, width)), half],
        const((2, width, hw)), shape((2, width, hw)), cost=4 * t * width * hw,
    )


def give_grad_out(s, ctx, ctx_in, d1):
    t, width = d1.shape
    hw = width // 2
    n = len(ctx)

    def kernel(s_ref, *refs):
        d_ref, out = refs[2 * n :]
        c = s_ref[0]
        out[at_core(c, hw), :] = t_mm(beside(refs[:n]), d_ref[...]).astype(bf16)
        out[at_core(1 - c, hw), :] = t_mm(beside(refs[n : 2 * n]), d_ref[...]).astype(bf16)

    return call(
        kernel, s, (*ctx, *ctx_in, d1), (1,),
        [pl.BlockSpec((t, part.shape[1]), lambda i, s: (s[0], 0)) for part in ctx] + [const(part.shape) for part in ctx_in]
        + [pl.BlockSpec((t, hw), lambda i, s: (0, 1 - s[0]))],
        const((width, hw)), shape((width, hw)), cost=2 * t * width * hw,
    )


def keep_grads(s, c2_keep, c2_give, d2, a2, dq_keep, ctx, ctx_in, d1, pair_in, out_in, kv_keep, kv_give):
    t, width = d2.shape
    hw = width // 2
    n = len(ctx)

    def kernel(s_ref, ck, cg, d2_ref, a_ref, q_ref, *refs):
        d1_ref, p_ref, o_ref, kk, kg, xgive, xkeep = refs[2 * n :]
        c, h = s_ref[0], s_ref[1]
        same = c == h
        for out, shard, kv in ((xgive, 1 - h, kg), (xkeep, h, kk)):
            rows = at_core(shard, hw)
            out[1] = (t_mm(a_ref[:, rows], q_ref[...]) + p_ref[1, rows, :].astype(f32)).astype(bf16)
            out[3] = kv[:hw]
            out[4] = kv[hw:]
        for k, lefts, right, extra in ((0, (ck[...], cg[...]), d2_ref, p_ref.at[0]), (2, (beside(refs[:n]), beside(refs[n : 2 * n])), d1_ref, o_ref)):
            own_rows = t_mm(lefts[0], right[...]) + extra[at_core(c, hw), :].astype(f32)
            far_rows = t_mm(lefts[1], right[...]) + extra[at_core(1 - c, hw), :].astype(f32)
            xkeep[k] = jnp.where(same, own_rows, far_rows).astype(bf16)
            xgive[k] = jnp.where(same, far_rows, own_rows).astype(bf16)

    cols, half = pl.BlockSpec((t, hw), lambda i, s: (0, s[0])), const((t, hw))
    five = (5, hw, hw)
    return call(
        kernel, s, (c2_keep, c2_give, d2, a2, dq_keep, *ctx, *ctx_in, d1, pair_in, out_in, kv_keep, kv_give), (1,),
        [half, half, cols, const((t, width)), half]
        + [pl.BlockSpec((t, part.shape[1]), lambda i, s: (s[0], 0)) for part in ctx] + [const(part.shape) for part in ctx_in]
        + [cols, const((2, width, hw)), const((width, hw)), const((width, hw)), const((width, hw))],
        [const(five), const(five)], [shape(five), shape(five)], cost=6 * t * width * hw,
    )


def split_y(s, keep, got):
    b, rows, cols = keep.shape
    half = rows // 2

    def kernel(s_ref, k_ref, g_ref, give, mine):
        for out, y in ((give, 1 - s_ref[4]), (mine, s_ref[4])):
            at = pl.ds(pl.multiple_of(y * half, 64), half)
            out[...] = (k_ref[:, at, :].astype(f32) + g_ref[:, at, :].astype(f32)).astype(bf16)

    dims = (b, half, cols)
    return call(kernel, s, (keep, got), (1,), [const(keep.shape)] * 2, [const(dims)] * 2, [shape(dims)] * 2)


def split_z(s, keep, got):
    b, rows, cols = keep.shape
    part = rows // 4

    def kernel(s_ref, k_ref, g_ref, *outs):
        for d, out in enumerate(outs):
            at = pl.ds(pl.multiple_of(s_ref[5 + d] * part, 16), part)
            out[...] = (k_ref[:, at, :].astype(f32) + g_ref[:, at, :].astype(f32)).astype(bf16)

    dims = (b, part, cols)
    return call(kernel, s, (keep, got), (1,), [const(keep.shape)] * 2, [const(dims)] * 4, [shape(dims)] * 4)


def sum_four(s, parts, vectors=()):
    b, part, cols = parts[0].shape

    def kernel(s_ref, p0, p1, p2, p3, *refs):
        out = refs[-1]
        total = (p0[...].astype(f32) + p1[...].astype(f32)) + (p2[...].astype(f32) + p3[...].astype(f32))
        out[0:b] = total.astype(bf16)
        if vectors:
            v = refs[0][...] + refs[1][...]
            high = v.astype(bf16).astype(f32)
            out[b] = jnp.concatenate([high, v - high], axis=0).astype(bf16)

    dims = (b + (1 if vectors else 0), part, cols)
    return call(
        kernel, s, (*parts, *vectors), (1,), [const(parts[0].shape)] * 4 + [const(v.shape) for v in vectors], const(dims), shape(dims)
    )


def pack_vectors(s, last, cross, mid, kv):
    width = last.shape[1]
    hw = width // 2
    units = mid.shape[1] // width

    def kernel(s_ref, l_ref, c_ref, m_ref, k_ref, give, mine):
        def line(ref, row, at=0):
            return ref[row : row + 1, at : at + width]

        zero = jnp.zeros((1, hw), f32)
        first = s_ref[0] == 0
        kv_row = jnp.concatenate([jnp.where(first, k_ref[0:1], zero), jnp.where(first, zero, k_ref[0:1])], axis=1)
        rows = [
            line(l_ref, 0), line(c_ref, 0), line(m_ref, 2, width), line(m_ref, 1, 2 * width),
            line(l_ref, 1), line(c_ref, 1), line(m_ref, 2, 2 * width), line(m_ref, 2),
            line(l_ref, 2), line(l_ref, 3), line(c_ref, 2), line(c_ref, 3), kv_row, line(m_ref, 1, width), line(m_ref, 1),
        ]
        halves = []
        for h in range(2):
            own = [row[:, h * hw : (h + 1) * hw] for row in rows]
            own += [m_ref[0:1, (h * units + j) * hw : (h * units + j + 1) * hw] for j in range(units)]
            halves.append(jnp.concatenate(own + [zero] * (24 - len(own)), axis=0))
        give[...] = jnp.where(s_ref[1] == 0, halves[1], halves[0])
        mine[...] = jnp.where(s_ref[1] == 0, halves[0], halves[1])

    return call(
        kernel, s, (last, cross, mid, kv), (1,), [const(x.shape) for x in (last, cross, mid, kv)],
        [const((24, hw))] * 2, [shape((24, hw), f32)] * 2,
    )


def join_z(s, parts):
    b, part, cols = parts[0].shape

    def kernel(s_ref, p0, p1, p2, p3, out):
        for d, ref in enumerate((p0, p1, p2, p3)):
            out[:, pl.ds(pl.multiple_of(s_ref[5 + d] * part, 16), part), :] = ref[...]

    dims = (b, 4 * part, cols)
    return call(kernel, s, parts, (1,), [const(parts[0].shape)] * 4, const(dims), shape(dims))


def spread_out(s, groups, outs, vectors=False):
    hw = 384

    def kernel(s_ref, *refs):
        results = refs[4 * len(groups) :]
        for n, (parts, spots) in enumerate(groups):
            b, half, cols = parts[0].shape
            for k, ref in enumerate(refs[4 * n : 4 * n + 4]):
                y = s_ref[4] if k % 2 == 0 else 1 - s_ref[4]
                core = s_ref[0] if k < 2 else 1 - s_ref[0]
                for block, (which, row, col) in enumerate(spots):
                    at_row = pl.multiple_of(row + y * half, 64)
                    at_col = pl.multiple_of(col + core * hw, 128)
                    results[which][pl.ds(at_row, half), pl.ds(at_col, cols)] = ref[block].astype(f32)
        if vectors:
            total = None
            for ref in refs[:4]:
                rows = ref[ref.shape[0] - 1].astype(f32)
                for z in range(4):
                    part = rows[48 * z : 48 * z + 48]
                    total = part if total is None else total + part
            results[-1][...] = total[0:24] + total[24:48]

    parts = [part for group, _ in groups for part in group]
    return call(kernel, s, parts, (1,), [const(part.shape) for part in parts], [const(d) for d in outs], [shape(d, f32) for d in outs])


def spread_ff(s, got):
    reps, _, per, width = got.shape
    units = 4
    rows = reps // units * per

    def kernel(s_ref, g_ref, one, two):
        one[...] = g_ref[:, 0].reshape(rows, width).astype(f32)
        two[...] = g_ref[:, 1].reshape(rows, width).astype(f32)

    return call(
        kernel, s, (got,), (units,), [pl.BlockSpec((reps // units, 2, per, width), lambda i, s: (i, 0, 0, 0))],
        [pl.BlockSpec((rows, width), lambda i, s: (0, i)), pl.BlockSpec((rows, width), lambda i, s: (i, 0))],
        [shape((rows, units * width), f32), shape((units * rows, width), f32)],
    )


def qkv_grad(s, a_own, a_sib, keep, give):
    t, width = a_own.shape
    hw = width // 2
    n = len(keep)

    def kernel(s_ref, ao, ai, *refs):
        xgive, xkeep = refs[2 * n :]
        k, g = (jnp.concatenate([ref[0] for ref in part], axis=1) for part in (refs[:n], refs[n : 2 * n]))
        for out, shard in ((xgive, 1 - s_ref[1]), (xkeep, s_ref[1])):
            rows = at_core(shard, hw)
            out[0] = (t_mm(ao[:, rows], k) + t_mm(ai[:, rows], g)).astype(bf16)

    out = pl.BlockSpec((1, hw, hw), lambda i, s: (i, 0, 0))
    return call(
        kernel, s, (a_own, a_sib, *keep, *give), (3,),
        [once((t, width)), once((t, width))] + [pl.BlockSpec((1, t, part.shape[2]), lambda i, s: (i, 0, 0)) for part in (*keep, *give)],
        [out, out], [shape((3, hw, hw))] * 2, cost=12 * t * width * hw,
    )


def last_rows(s, keep, recv, x_own, x_in, dh1, weight, table, rows=512):
    t, width = x_own.shape
    hw = width // 2
    n = len(keep)

    def kernel(s_ref, *refs):
        xo, xi, dh, w, tab, out, vec = refs[2 * n :]

        @pl.when(pl.program_id(0) == 0)
        def _():
            vec[...] = jnp.zeros(vec.shape, f32)

        c = s_ref[0]
        da = None
        for j in range(3):
            for parts, core in ((refs[:n], c), (refs[n : 2 * n], 1 - c)):
                d = jnp.concatenate([part[j] for part in parts], axis=1)
                at = pl.multiple_of(j * width + core * hw, 128)
                part = mm_t(d, w[:, pl.ds(at, hw)])
                da = part if da is None else da + part
                if j != 1:
                    line = 2 + j // 2
                    vec[line : line + 1, at_core(core, hw)] += jnp.sum(d.astype(f32), axis=0, keepdims=True)
        x = jnp.where(s_ref[2] == 1, xo[...].astype(f32), xi[...].astype(f32))
        dres, dgain, dshift = norm_back(x, tab[0:1], da)
        out[...] = (dh[...] + dres).astype(bf16)
        vec[0:1] += dgain
        vec[1:2] += dshift

    line = tile(rows, width)
    return call(
        kernel, s, (*keep, *recv, x_own, x_in, dh1, weight, table), (t // rows,),
        [pl.BlockSpec((3, rows, part.shape[2]), lambda i, s: (0, i, 0)) for part in (*keep, *recv)]
        + [line, line, line, once(weight.shape), const(table.shape)],
        [line, const((8, width))], [shape((t, width)), shape((8, width), f32)],
        cost=6 * t * width * width,
    )


EVERY = ("z", "y", "core", "x")
SPREAD2 = ("x", "z", "y", "core")
REP2 = ("z", "y", "core")
SWAP = [(1, 2), (2, 1)]


def tie(*values):
    return lax.optimization_barrier(values)


def across_z(x, d):
    return lax.ppermute(x, "z", [(j, j ^ d) for j in range(4)])


def across(x, axis):
    return lax.ppermute(x, axis, FLIP)


def body_pair(hidden, frames, segment, cotangent, norm_gain, norm_bias, self_qkv, self_out, cross_q, cross_kv, cross_out, fc1, fc2, proj_bias, fc1_bias):
    c, h = lax.axis_index("core"), lax.axis_index("x")
    y_at, z_at = lax.axis_index("y"), lax.axis_index("z")
    stay = c == h
    s = jnp.stack([c, h, stay.astype(jnp.int32), jnp.int32(0), y_at, z_at, z_at ^ 1, z_at ^ 2, z_at ^ 3]).astype(jnp.int32)
    rep_at = lax.axis_index(REP2)
    reps = lax.axis_size(REP2)
    width = self_out.shape[1]
    hw = width // 2
    ff = fc1.shape[1]
    units = ff // width
    pairs = hw // 128

    def swap(x):
        return lax.ppermute(x, ("core", "x"), SWAP)

    def sibling(x):
        return across(x, "core")

    def near(own):
        half = own.shape[0] // 2
        return across(lax.dynamic_slice_in_dim(own, c * half, half).astype(bf16), "x")

    x_own = hidden[0]
    small = jnp.concatenate([norm_gain, norm_bias, proj_bias, fc1_bias.reshape(units, hw), jnp.zeros((1, hw), f32)]).astype(bf16)
    small_in = across(small, "x")
    qkv_near = near(self_qkv)
    x_in = swap(x_own)
    seg = jnp.where(stay, segment, swap(segment))[0]
    per = hw * units // reps
    small = jnp.where(h == 0, jnp.stack([small, small_in]), jnp.stack([small_in, small])).astype(f32)
    table = jnp.concatenate([small[0, :16], small[1, :16]], axis=1)
    fc1_shift = small[:, 15:19].reshape(1, ff)
    kmark, qmark = seg_marks(seg)
    deep = hw // per
    part1 = lax.dynamic_slice(fc1, (rep_at % deep * per, rep_at // deep * width), (per, width))
    part2 = lax.dynamic_slice_in_dim(fc2, rep_at * per, per)
    slot = jnp.concatenate([part1, part2]).astype(bf16)
    x_in, slot, kmark, qmark, frames, cross_kv = tie(x_in, slot, kmark, qmark, frames, cross_kv)
    ffw = lax.all_gather(slot, SPREAD2, axis=0, tiled=False).reshape(2 * reps, 2, per, width)
    f_own = frames[0]
    f_in = swap(f_own)
    kv_near = near(cross_kv)
    w_qkv, a1, keep, give = norm_qkv(s, x_own, x_in, (self_qkv, qkv_near, sibling(qkv_near)), table)
    recv = sibling(give)

    many = pairs - 1
    ctx_a, give_a, lse_a = self_fwd(0, many, c, keep, recv, kmark, qmark)
    give_a, f_in, kv_near, keep, recv = tie(give_a, f_in, kv_near, keep, recv)
    half = jnp.where(stay, f_own, f_in)
    twin = sibling(half)
    kv_sib = sibling(kv_near)
    in_a = sibling(give_a)
    half, self_out, cross_q = tie(half, self_out, cross_q)
    out_near, q_near = near(self_out), near(cross_q)
    out_near, cross_out, cotangent = tie(out_near, cross_out, cotangent)
    co_near = near(cross_out)
    cot_in = swap(cotangent[0])
    ctx_b, give_b, lse_b = self_fwd(many, 1, c, keep, recv, kmark, qmark)
    in_b = sibling(give_b)
    w_kv, kc, vc = frame_kv(s, half, twin, (cross_kv, kv_near, kv_sib), table)
    kc, out_near, q_near = tie(kc, out_near, q_near)
    ctx, ctx_in = (ctx_a, ctx_b), (in_a, in_b)
    w_out, w_q, h1, a2, qc = self_project(
        s, ctx, ctx_in, x_own, x_in, (self_out, out_near, sibling(out_near)), (cross_q, q_near, sibling(q_near)), table
    )
    count = half.shape[0]
    own_pairs, far_pairs = c * pairs, (1 - c) * pairs
    c2_give, cross_lse_give = cross_fwd(far_pairs, pairs, qc, kc, vc, count)
    c2_give, co_near, qc = tie(c2_give, co_near, qc)
    co_sib = sibling(co_near)
    c2_keep, cross_lse_keep = cross_fwd(own_pairs, pairs, qc, kc, vc, count)
    w_co, out, a3, g, dm, du, d2, dh2, dc2_keep, dc2_give, vec_mid = middle(
        s, h1, c2_keep, c2_give, cotangent[0], cot_in, (cross_out, co_near, co_sib), ffw, table, fc1_shift,
    )

    packed = ff_grads(s, a3, du, g, dm)
    dc2_give, packed, out, a1_out = tie(dc2_give, packed, out, a1)
    ff_mine = lax.psum_scatter(packed.reshape(2 * reps, 2 * per, width), SPREAD2, scatter_dimension=0, tiled=False)
    out_in = swap(out)
    a1_sib = sibling(a1_out)
    dq_give, dkv_give = cross_bwd(far_pairs, pairs, qc, kc, vc, c2_give, dc2_give, cross_lse_give, count)
    dkv_give, dq_give = tie(dkv_give, dq_give)
    dkv_in = sibling(dkv_give)
    pair_give = give_grads(s, c2_keep, c2_give, d2, a2, dq_give)
    pair_give, dc2_keep = tie(pair_give, dc2_keep)
    pair_in = sibling(pair_give)
    dq_keep, dkv_keep = cross_bwd(own_pairs, pairs, qc, kc, vc, c2_keep, dc2_keep, cross_lse_keep, count)
    dq_keep, out_in, dkv_in, a1_sib, pair_in = tie(dq_keep, out_in, dkv_in, a1_sib, pair_in)
    dh1, d1, dctx_keep, dctx_give, vec_cross = cross_back(s, dq_keep, dq_give, h1, dh2, w_q, w_out, table)
    dctx_give, d1 = tie(dctx_give, d1)
    dctx_in = sibling(dctx_give)
    so_give = give_grad_out(s, ctx, ctx_in, d1)
    so_give, dkv_keep = tie(so_give, dkv_keep)
    so_in = sibling(so_give)
    fkeep, fgive, kv_xkeep, kv_xgive, vec_kv = frame_back(s, dkv_keep, dkv_in, half, twin, w_kv)
    fgive, kv_xgive = tie(fgive, kv_xgive)
    fr_in = sibling(fgive)
    xgive, xkeep = keep_grads(s, c2_keep, c2_give, d2, a2, dq_keep, ctx, ctx_in, d1, pair_in, so_in, kv_xkeep, kv_xgive)
    xgive, fr_in, fkeep = tie(xgive, fr_in, fkeep)
    got_x = across(xgive, "x")
    fr_own = (fkeep.astype(f32) + fr_in.astype(f32)).astype(bf16)
    fr_own, dctx_keep = tie(fr_own, dctx_keep)
    fr_swapped = swap(fr_own)

    def send_z(pieces):
        return (pieces[0],) + tuple(across_z(pieces[d], d) for d in (1, 2, 3))

    def gather_z(piece):
        return (piece,) + tuple(across_z(piece, d) for d in (1, 2, 3))

    bg_a, bk_a = self_bwd(0, many, c, keep, recv, ctx_a, dctx_keep, dctx_in, lse_a, kmark, qmark)
    bg_a, bk_a, got_x, keep, ff_mine = tie(bg_a, bk_a, got_x, keep, ff_mine)
    ff_got = lax.all_gather(ff_mine, REP2, axis=0, tiled=False)
    bi_a = sibling(bg_a)
    m_ygive, m_ykeep = split_y(s, xkeep, got_x)
    m_ygive, keep = tie(m_ygive, keep)
    m_y = across(m_ygive, "y")
    bg_b, bk_b = self_bwd(many, 1, c, keep, recv, ctx_b, dctx_keep, dctx_in, lse_b, kmark, qmark)
    bg_b, bk_b, m_y, fr_swapped = tie(bg_b, bk_b, m_y, fr_swapped)
    bi_b = sibling(bg_b)
    m_four = split_z(s, m_ykeep, m_y)
    bk_b, *m_four = tie(bk_b, *m_four)
    m_z = send_z(m_four)
    q_xgive, q_xkeep = qkv_grad(s, a1, a1_sib, (bk_a, bk_b), (bg_a, bg_b))
    q_xgive, q_xkeep, dh1 = tie(q_xgive, q_xkeep, dh1)
    q_x = across(q_xgive, "x")
    grad_hidden, vec_last = last_rows(s, (bk_a, bk_b), (bi_a, bi_b), x_own, x_in, dh1, w_qkv, table)
    v_give, v_mine = pack_vectors(s, vec_last, vec_cross, vec_mid, vec_kv)
    v_got = across(v_give, "x")
    v_mine, *m_z = tie(v_mine, *m_z)
    m_all = gather_z(sum_four(s, m_z))
    q_x, *m_all = tie(q_x, *m_all)
    q_ygive, q_ykeep = split_y(s, q_xkeep, q_x)
    q_ygive, grad_hidden, *m_all = tie(q_ygive, grad_hidden, *m_all)
    q_y = across(q_ygive, "y")
    hid_in = swap(grad_hidden)
    m_own = join_z(s, m_all)
    m_own, q_y = tie(m_own, q_y)
    m_far = across(m_own, "y")
    q_four = split_z(s, q_ykeep, q_y)
    q_z = send_z(q_four)
    q_own = join_z(s, gather_z(sum_four(s, q_z, (v_mine, v_got))))
    q_far = across(q_own, "y")

    def quarters(own, far):
        return own, far, sibling(own), sibling(far)

    spots = ((0, 0, 0), (1, 0, 0), (2, 0, 0), (3, 0, 0), (3, hw, 0))
    crossout_grad, crossq_grad, selfout_grad, kv_grad = spread_out(s, ((quarters(m_own, m_far), spots),), ((hw, width),) * 3 + ((width, width),))
    first = tuple((0, 0, j * width) for j in range(3))
    qkv_grad_out, mine = spread_out(s, ((quarters(q_own, q_far), first),), ((hw, 3 * width), (24, hw)), True)
    fc1_grad, fc2_grad = spread_ff(s, ff_got.reshape(reps, 2, per, width))

    output = jnp.where(stay, out, out_in)
    grad_hidden = jnp.where(stay, grad_hidden, hid_in)
    grad_frames = jnp.where(stay, fr_own, fr_swapped)
    return (
        output[None], grad_hidden[None], grad_frames[None], mine[:4], mine[4:8],
        qkv_grad_out, selfout_grad, crossq_grad, kv_grad, crossout_grad, fc1_grad, fc2_grad, mine[8:15], mine[15:19].reshape(-1),
    )


GROUP = ("core", "ilo")
SHARD = ("ihi", "ilo")
REP = ("rz", "core")
SPREAD = ("ihi", "ilo", "rz", "core")


def body_general(hidden, frames, segment, cotangent, norm_gain, norm_bias, self_qkv, self_out, cross_q, cross_kv, cross_out, fc1, fc2, proj_bias, fc1_bias):
    c = lax.axis_index("core")
    hi = lax.axis_index("ihi")
    n = lax.axis_size("core") * lax.axis_size("ilo")
    reps = lax.axis_size("rz") * lax.axis_size("core")
    rep_at = lax.axis_index(REP)
    width = self_out.shape[1]
    ff = fc1.shape[1]

    def swap(x):
        return lax.ppermute(x, ("core", "ihi"), [(0, 0), (1, 2), (2, 1), (3, 3)])

    def whole(own):
        if n != 2:
            return lax.all_gather(own, SHARD, axis=0, tiled=True)
        half = own.shape[0] // 2
        mine = lax.ppermute(lax.dynamic_slice_in_dim(own, c * half, half), "ihi", FLIP)
        sib = lax.ppermute(mine, "core", FLIP)
        other = jnp.where(c == 0, jnp.concatenate([mine, sib]), jnp.concatenate([sib, mine]))
        return jnp.where(hi == 0, jnp.concatenate([own, other]), jnp.concatenate([other, own]))

    def slices(own):
        rows = own.shape[0] // reps
        return lax.dynamic_slice_in_dim(own, rep_at * rows, rows)

    rows_in = swap(hidden[0])
    qkv_w = whole(self_qkv.astype(bf16))
    small = jnp.concatenate([norm_gain.astype(bf16), norm_bias.astype(bf16), proj_bias.astype(bf16), fc1_bias.astype(bf16).reshape(-1, norm_gain.shape[1]), jnp.zeros((1, norm_gain.shape[1]), bf16)])
    small = lax.all_gather(small, SHARD, axis=1, tiled=False).astype(f32)
    table = small[:15].reshape(15, width)
    gains, shifts, biases = table[:4], table[4:8], table[8:15]
    fc1_shift = small[15:19].transpose(1, 0, 2).reshape(ff)
    seg = swap(segment)[0]
    frames_half = swap(frames[0])
    if n == 2:
        twin = lax.ppermute(frames_half, "core", FLIP)
        frame_rows = jnp.concatenate([jnp.where(c == 0, frames_half, twin), jnp.where(c == 0, twin, frames_half)], axis=1)
    else:
        frame_rows = lax.all_gather(frames_half, GROUP, axis=1, tiled=True)
    selfout_w = whole(self_out.astype(bf16))
    crossq_w = whole(cross_q.astype(bf16))
    kv_w = whole(cross_kv.astype(bf16)) if n == 2 else None
    if n == 2:
        k_w, v_w = kv_w[:width], kv_w[width:]
    else:
        kv_w = lax.all_gather(cross_kv.astype(bf16), SHARD, axis=1, tiled=True)
        k_w, v_w = kv_w[:, :width], kv_w[:, width:]
    crossout_w = whole(cross_out.astype(bf16))
    cot = swap(cotangent[0])
    units = ff // width
    part1 = slices(fc1.astype(bf16))
    part2 = slices(fc2.astype(bf16))
    few = part1.shape[0]
    parts = jnp.concatenate([part1[:, j * width : (j + 1) * width] for j in range(units)] + [part2])
    ffw = lax.all_gather(parts, SPREAD, axis=0, tiled=False)
    fc1_w = jnp.concatenate([ffw[:, j * few : (j + 1) * few].reshape(width, width) for j in range(units)], axis=1)
    fc2_w = ffw[:, units * few :].reshape(ff, width)

    own_rows = rows_in.shape[0]
    hw = -(-HEADS // n)
    padded = hw * n * HD - width

    lanes = hw * HD

    def to_heads(x):
        x = x.reshape(own_rows, -1, width)
        if padded:
            x = jnp.pad(x, ((0, 0), (0, 0), (0, padded)))
        x = x.reshape(own_rows, -1, n, lanes).transpose(1, 2, 0, 3)
        x = lax.all_to_all(x, GROUP, 1, 1, tiled=True)
        return x.reshape(-1, n * own_rows, lanes)

    def to_tokens(x):
        x = lax.all_to_all(x.reshape(-1, n, own_rows, lanes), GROUP, 1, 1, tiled=True)
        return x.transpose(2, 0, 1, 3).reshape(own_rows, -1, n * lanes)[:, :, :width].reshape(own_rows, -1)

    h0 = rows_in.astype(f32)
    a1 = norm(h0, gains[0], shifts[0]).astype(bf16)
    zeros_row = jnp.zeros((width,), f32)
    qkv = (mm(a1, qkv_w) + jnp.concatenate([biases[0], zeros_row, biases[1]])).astype(bf16)
    heads = to_heads(qkv)
    kmark, qmark = seg_marks(seg)
    mid = heads.shape[1] // 2
    first = jnp.int32(0)
    ctx, _, self_lse = self_fwd(0, lanes // 128, first, heads[:, :mid], heads[:, mid:], kmark, qmark)
    c1 = to_tokens(ctx)
    h1 = h0 + mm(c1, selfout_w) + biases[2]
    a2 = norm(h1, gains[1], shifts[1]).astype(bf16)
    qc = (mm(a2, crossq_w) + biases[3]).astype(bf16)
    count = frame_rows.shape[0]
    pad = -count % 256
    frame_pad = jnp.pad(frame_rows, ((0, pad), (0, 0)))
    kc = mm(frame_pad, k_w).astype(bf16)
    live = lax.broadcasted_iota(jnp.int32, (count + pad, 1), 0) < count
    vc = (mm(frame_pad, v_w) + jnp.where(live, biases[4], 0.0)).astype(bf16)
    c2, cross_lse = cross_fwd(first, width // 128, qc, kc, vc, count)
    h2 = h1 + mm(c2, crossout_w) + biases[5]
    a3 = norm(h2, gains[2], shifts[2]).astype(bf16)
    u = (mm(a3, fc1_w) + fc1_shift).astype(bf16)
    uf = u.astype(f32)
    g, slope = gelu_parts(uf)
    g = g.astype(bf16)
    h3 = h2 + mm(g, fc2_w) + biases[6]
    output = norm(h3, gains[3], shifts[3]).astype(bf16)
    output = swap(output)

    def total(x):
        return jnp.sum(x.astype(f32), axis=0)

    dh3, gain3, shift3 = norm_back(h3, gains[3], cot.astype(f32))
    dm = dh3.astype(bf16)
    g_fc2 = t_mm(g, dm).astype(bf16)
    du = (slope * mm_t(dm, fc2_w)).astype(bf16)
    g_fc1 = t_mm(a3, du).astype(bf16)

    def reduce_rows(parts, extra=None):
        total = n * reps
        cut = [p.reshape(total, -1, width) for p in parts]
        if extra is not None:
            cut.append(extra)
        flat = jnp.concatenate(cut, axis=1)
        mine = lax.psum_scatter(flat, SPREAD, scatter_dimension=0, tiled=False)
        got = lax.all_gather(mine, REP, axis=0, tiled=False)
        out, at = [], 0
        for p in cut:
            out.append(got[:, at : at + p.shape[1]].reshape(-1, width).astype(f32))
            at += p.shape[1]
        return out

    ff_grads = reduce_rows([g_fc1[:, j * width : (j + 1) * width] for j in range(units)] + [g_fc2])
    fc1_grad = jnp.concatenate(ff_grads[:units], axis=1)
    fc2_grad = ff_grads[units]

    da3 = mm_t(du, fc1_w)
    dres, gain2, shift2 = norm_back(h2, gains[2], da3)
    dh2 = dh3 + dres
    d2 = dh2.astype(bf16)
    g_crossout = t_mm(c2, d2).astype(bf16)
    dc2 = mm_t(d2, crossout_w).astype(bf16)
    dqc, (dkc, dvc) = cross_bwd(first, width // 128, qc, kc, vc, c2, dc2, cross_lse, count)
    share = width // n

    def sum_columns(x):
        return lax.psum_scatter(x, GROUP, scatter_dimension=1, tiled=True)

    if n == 2:

        def sum_columns(x):
            give = lax.dynamic_slice_in_dim(x, (1 - c) * share, share, axis=1)
            keep = lax.dynamic_slice_in_dim(x, c * share, share, axis=1)
            return (keep.astype(f32) + lax.ppermute(give, "core", FLIP).astype(f32)).astype(bf16)

    dk_own = sum_columns(dkc)[:count]
    dv_own = sum_columns(dvc)[:count]
    place = lax.axis_index(GROUP) * share
    kw_own = lax.dynamic_slice_in_dim(k_w, place, share, axis=1)
    vw_own = lax.dynamic_slice_in_dim(v_w, place, share, axis=1)
    dframe = (mm_t(dk_own, kw_own) + mm_t(dv_own, vw_own)).astype(bf16)
    grad_frames = swap(sum_columns(dframe))
    g_k = t_mm(frame_rows, dk_own).astype(bf16)
    g_v = t_mm(frame_rows, dv_own).astype(bf16)
    vb_own = jnp.sum(dv_own.astype(f32), axis=0)

    g_crossq = t_mm(a2, dqc).astype(bf16)
    da2 = mm_t(dqc, crossq_w)
    dres, gain1, shift1 = norm_back(h1, gains[1], da2)
    dh1 = dh2 + dres
    d1 = dh1.astype(bf16)
    g_selfout = t_mm(c1, d1).astype(bf16)
    dctx = mm_t(d1, selfout_w).astype(bf16)
    dctx = to_heads(dctx)[0]
    late, early = self_bwd(0, lanes // 128, first, heads[:, :mid], heads[:, mid:], ctx, dctx[:mid], dctx[mid:], self_lse, kmark, qmark)
    dqkv = to_tokens(jnp.concatenate([early, late], axis=1))
    da1 = mm_t(dqkv, qkv_w)
    g_qkv = t_mm(a1, dqkv).astype(bf16)
    sums = total(dqkv)
    dres, gain0, shift0 = norm_back(h0, gains[0], da1)
    grad_hidden = swap((dh1 + dres).astype(bf16))

    vb = lax.dynamic_update_slice(jnp.zeros((width,), f32), vb_own, (place,))
    vectors = jnp.stack([gain0[0], gain1[0], gain2[0], gain3[0], shift0[0], shift1[0], shift2[0], shift3[0], sums[:width], sums[2 * width :], total(d1), total(dqc), vb, total(d2), total(dm)])
    per = width // n
    vectors = vectors.reshape(15, n, per).transpose(1, 0, 2).reshape(n, 15 * per)
    vectors = jnp.concatenate([vectors, total(du).reshape(n, ff // n)], axis=1)
    long = vectors.shape[1]
    seats = -(-long // reps)
    vectors = jnp.pad(vectors, ((0, 0), (0, seats * reps - long))).reshape(n * reps, seats)
    lines = -(-seats // (8 * width)) * 8
    vectors = jnp.pad(vectors, ((0, 0), (0, lines * width - seats))).reshape(n * reps, lines, width)

    def own_columns(x):
        return lax.dynamic_update_slice(jnp.zeros((x.shape[0], width), x.dtype), x, (jnp.int32(0), place))

    cross = [g_crossq, g_crossout]
    if n == 2:
        cross.append(jnp.concatenate([own_columns(g_k), own_columns(g_v)]))
    cross = reduce_rows(cross)
    crossq_grad, crossout_grad = cross[:2]
    if n == 2:
        kv_grad = cross[2]
    else:
        kv_cols = jnp.concatenate([own_columns(g_k), own_columns(g_v)], axis=1)
        kv_cols = lax.psum_scatter(kv_cols, SHARD, scatter_dimension=1, tiled=True)
        kv_grad = lax.psum(kv_cols, REP).astype(f32)
    got = reduce_rows([g_qkv[:, j * width : (j + 1) * width] for j in range(3)] + [g_selfout], vectors.astype(bf16))
    qkv_grad = jnp.concatenate(got[:3], axis=1)
    selfout_grad = got[3]
    vec = got[4].reshape(reps, lines * width)[:, :seats].reshape(-1)[:long]
    table = vec[: 15 * per].reshape(15, per)
    fc1b_grad = vec[15 * per :]
    return (
        output[None], grad_hidden[None], grad_frames[None],
        table[:4], table[4:8], qkv_grad, selfout_grad, crossq_grad, kv_grad, crossout_grad, fc1_grad, fc2_grad, table[8:15], fc1b_grad,
    )


def solution(mesh):
    reps, n = mesh.devices.shape
    paired = (reps, n) == (16, 2)
    if paired:
        work = Mesh(mesh.devices.reshape(4, 2, 2, 2), EVERY)
        rep, inner = REP2, ("x",)
    else:
        work = Mesh(mesh.devices.reshape(reps // 2, 2, 2, n // 2), ("rz", "core", "ihi", "ilo"))
        rep, inner = REP, SHARD
    rows, cols = P(inner, None), P(None, inner)
    tokens, features = P(rep, inner, None), P(rep, None, inner)
    weights = (cols, cols, rows, rows, rows, cols, rows, rows, rows, cols, P(inner))
    return jax.shard_map(
        body_pair if paired else body_general,
        mesh=work,
        in_specs=(tokens, features, P(rep, None), tokens) + weights,
        out_specs=(tokens, tokens, features) + weights,
        check_vma=False,
    )
```

time: 1040 us -> 618 us (0.59)
  waiting for transfers between devices: 454 us -> 127 us
  Pallas kernels: 138 us -> 364 us
  matrix products: 154 us -> 0 us
  local copies, waits for them, and re-layouts: 101 us -> 27.3 us
  blocking collectives: 60.7 us -> 0 us
  other arithmetic: 69.2 us -> 12.5 us
  starting transfers between devices: 38.8 us -> 62.1 us
    reduce_scatter x3 -> x1, waiting for transfers between devices: 306 us -> 0.01 us  [body_pair(): lax.psum_scatter(packed.reshape(2 * reps, 2 * per, width), SPREAD2, scatt...]
    pallas_call x4 -> x32, Pallas kernels: 138 us -> 364 us  [call(): pl.pallas_call(kernel, grid_spec=spec, out_shape=out_shape, cost_estimate...]
    dot_general x24 -> x0, matrix products: 154 us -> none  [the longest x8 69 us: mm(): return jnp.dot(a, b, preferred_element_type=f32)]
    all_gather x4 -> x2, waiting for transfers between devices: 71 us -> 0.02 us  [the longest x1 0.02 us: body_pair(): lax.all_gather(slot, SPREAD2, axis=0, tiled=False)]
    ppermute x21 -> x53, waiting for transfers between devices: 77.5 us -> 127 us  [the longest x34 81.9 us: across(): return lax.ppermute(x, axis, FLIP)]
    all_gather x1 -> x0, blocking collectives: 32.1 us -> none  [body(): small = lax.all_gather(small, SHARD, axis=1, tiled=False).astype(f32)]
    reduce_sum x15 -> x0, other arithmetic: 30.8 us -> none  [the longest x5 13.8 us: total(): return jnp.sum(x.astype(f32), axis=0)]
    all_to_all x4 -> x0, blocking collectives: 28.6 us -> none  [the longest x2 14.8 us: to_tokens(): lax.all_to_all(x.reshape(-1, n, own_rows, lanes), GROUP, 1, 1, tiled=True)]
  transfers between devices with their start and end apart: 28 -> 56, of which waited for: 10 -> 17; matrix products, arithmetic and copies ran while one was open for 20% -> 4% of each run, Pallas kernels for 5% -> 46%
where the time goes in v2:
time: 618 us; the launch traced here: 608 us
  Pallas kernels  364 us (59%)
  waiting for transfers between devices  127 us (21%)
  starting transfers between devices  62.1 us (10%)
  local copies, waits for them, and re-layouts  27.3 us (4%)
  between operations  14.9 us (2%)
  other arithmetic  12.5 us (2%)
    pallas_call x32, Pallas kernels, call(): pl.pallas_call(kernel, grid_spec=spec, out_shape=out_shape, cost_estimate...  364 us
    ppermute x34, waiting for transfers between devices, across(): return lax.ppermute(x, axis, FLIP)  81.9 us
    ppermute x12, waiting for transfers between devices, across_z(): return lax.ppermute(x, 'z', [(j, j ^ d) for j in range(4)])  31.8 us
    ppermute x7, starting transfers between devices, swap(): return lax.ppermute(x, ('core', 'x'), SWAP)  23.2 us
    ppermute x34, starting transfers between devices, across(): return lax.ppermute(x, axis, FLIP)  21.1 us
    ppermute x12, starting transfers between devices, across_z(): return lax.ppermute(x, 'z', [(j, j ^ d) for j in range(4)])  17.7 us
    ppermute x7, waiting for transfers between devices, swap(): return lax.ppermute(x, ('core', 'x'), SWAP)  13.7 us
    unnamed x92, local copies, waits for them, and re-layouts  13.6 us
  transfers between devices with their start and end apart: 56, of which 17 were waited for; matrix products, arithmetic and copies ran while one was open for 4% of the time, Pallas kernels for 46%

profile of v2, /device:TPU:1, one launch (start us, length us, event | category | flops | bytes accessed | tf_op | source)
XLA Modules:
  0.0 608.2 jit_solution(15371672410280122605)
XLA Ops:
  7.2 4.5 collective-permute-start
  16.4 13.7 %collective-permute-done.1 = s32[1,2048]{1,0:T(1,128)S(1)} collective-permute-done((s32[1,2048]{1,0:T(1,128)}, s32[1,2048]{1,0:T(1,128)S(1)}, u32[]{:S(2)}, u32[]{:S(2)}) %collective-permute-start.1) | collective-permute-done | bytes 8224 | tf_op jit(solution)/shard_map/ppermute | solution.py:965
  35.4 21.6 %collective-permute-done.2.mine = bf16[192,2304]{1,0:T(8,128)(2,1)} collective-permute-done((bf16[192,2304]{1,0:T(8,128)(2,1)S(1)}, bf16[192,2304]{1,0:T(8,128)(2,1)}, u32[]{:S(2)}, u32[]{:S(2)}) %collective-permute-start.2) | collective-permute-done | bytes 884768 | tf_op jit(solution)/shard_map/ppermute | solution.py:948
  60.5 10.4 %shard_map.254 = (bf16[768,2304]{1,0:T(8,128)(2,1)}, bf16[1024,768]{1,0:T(8,128)(2,1)}, bf16[3,1024,384]{2,1,0:T(8,128)(2,1)}, bf16[3,1024,384]{2,1,0:T(8,128)(2,1)}) custom-call(s32[9]{0:T(128)} %stack.51.s_ref, bf16[1024,768]{1,0:T(8,128)(2,1)} %bitcast.38, bf16[1024,768]{1,0:T(8,128)(2,1)} %copy-done, f32[384,2304]{1,0:T(8,128)} %own.1, ...), custom_call_target="tpu_custom_call" | custom-call | flops 3623878656 | bytes 1048576 | tf_op jit(solution)/shard_map/pallas_call | solution.py:41
  75.7 15.4 %shard_map.255 = (bf16[2048,256]{1,0:T(8,128)(2,1)}, bf16[1024,256]{1,0:T(8,128)(2,1)}, f32[2,8,2048]{2,1,0:T(8,128)}) custom-call(s32[1]{0:T(128)} %bitcast.s_ref, bf16[3,1024,384]{2,1,0:T(8,128)(2,1)} %get-tuple-element.270.a_ref, bf16[3,1024,384]{2,1,0:T(8,128)(2,1)} %collective-permute-done.5.b_ref, bf16[2048,128]{1,0:T(8,128)(2,1)} %get-tuple-element.179.km_ref, ...), custom_call_target="tpu_custom_call" | custom-call | flops 8589934592 | bytes 1048576 | tf_op jit(solution)/shard_map/pallas_call | solution.py:41
  91.1 24.6 %collective-permute-done.7.mine = bf16[384,768]{1,0:T(8,128)(2,1)} collective-permute-done((bf16[384,768]{1,0:T(8,128)(2,1)S(1)}, bf16[384,768]{1,0:T(8,128)(2,1)}, u32[]{:S(2)}, u32[]{:S(2)}) %collective-permute-start.7) | collective-permute-done | bytes 589856 | tf_op jit(solution)/shard_map/ppermute | solution.py:948
  115.8 3.1 collective-permute-start.10
  123.5 4.8 collective-permute-done.12.refs_7_
  128.3 3.8 collective-permute-start.17
  134.0 10.1 %shard_map.257 = (bf16[1536,768]{1,0:T(8,128)(2,1)}, bf16[1536,768]{1,0:T(8,128)(2,1)}, bf16[1536,768]{1,0:T(8,128)(2,1)}) custom-call(s32[9]{0:T(128)} %stack.51.s_ref, bf16[1500,384]{1,0:T(8,128)(2,1)} %copy-done.9, bf16[1500,384]{1,0:T(8,128)(2,1)} %copy-done.41, f32[768,768]{1,0:T(8,128)} %own.2, bf16[384,768]{1,0:T(8,128)(2,1)} %collective-permute-done.7.mine, ...), custom_call_target="tpu_custom_call" | custom-call | flops 3538944000 | bytes 1048576 | tf_op jit(solution)/shard_map/pallas_call | solution.py:41
  144.7 8.9 %shard_map.256 = (bf16[2048,128]{1,0:T(8,128)(2,1)}, bf16[1024,128]{1,0:T(8,128)(2,1)}, f32[1,8,2048]{2,1,0:T(8,128)}) custom-call(s32[1]{0:T(128)} %bitcast.s_ref, bf16[3,1024,384]{2,1,0:T(8,128)(2,1)} %get-tuple-element.270.a_ref, bf16[3,1024,384]{2,1,0:T(8,128)(2,1)} %collective-permute-done.5.b_ref, bf16[2048,128]{1,0:T(8,128)(2,1)} %get-tuple-element.179.km_ref, ...), custom_call_target="tpu_custom_call" | custom-call | flops 4294967296 | bytes 1048576 | tf_op jit(solution)/shard_map/pallas_call | solution.py:41
  156.7 9.8 %shard_map.258 = (bf16[768,768]{1,0:T(8,128)(2,1)}, bf16[768,768]{1,0:T(8,128)(2,1)}, f32[1024,768]{1,0:T(8,128)}, bf16[1024,768]{1,0:T(8,128)(2,1)}, bf16[1024,768]{1,0:T(8,128)(2,1)}) custom-call(s32[9]{0:T(128)} %stack.51.s_ref, bf16[2048,256]{1,0:T(8,128)(2,1)} %get-tuple-element.181.refs_0_.o_ref, bf16[2048,128]{1,0:T(8,128)(2,1)} %get-tuple-element.187.refs_1_.o_ref, ...), custom_call_target="tpu_custom_call" | custom-call | flops 2415919104 | bytes 1048576 | tf_op jit(solution)/shard_map/pallas_call | solution.py:41
  166.5 15.3 %shard_map.259 = (bf16[1024,384]{1,0:T(8,128)(2,1)}, f32[3,8,1024]{2,1,0:T(8,128)}) custom-call(s32[1]{0:T(128)} %bitcast.18.s_ref, bf16[1024,768]{1,0:T(8,128)(2,1)} %get-tuple-element.205.q_ref, bf16[1536,768]{1,0:T(8,128)(2,1)} %get-tuple-element.201.k_ref, bf16[1536,768]{1,0:T(8,128)(2,1)} %get-tuple-element.202.v_ref), custom_call_target="tpu_custom_call" | custom-call | flops 4831838208 | bytes 1048576 | tf_op jit(solution)/shard_map/pallas_call | solution.py:41
  182.1 14.8 %shard_map.260 = (bf16[1024,384]{1,0:T(8,128)(2,1)}, f32[3,8,1024]{2,1,0:T(8,128)}) custom-call(s32[1]{0:T(128)} %bitcast.17.s_ref, bf16[1024,768]{1,0:T(8,128)(2,1)} %get-tuple-element.205.q_ref, bf16[1536,768]{1,0:T(8,128)(2,1)} %get-tuple-element.201.k_ref, bf16[1536,768]{1,0:T(8,128)(2,1)} %get-tuple-element.202.v_ref), custom_call_target="tpu_custom_call" | custom-call | flops 4831838208 | bytes 1048576 | tf_op jit(solution)/shard_map/pallas_call | solution.py:41
  197.6 54.5 %shard_map.261 = (bf16[768,768]{1,0:T(8,128)(2,1)}, bf16[1024,768]{1,0:T(8,128)(2,1)}, bf16[1024,768]{1,0:T(8,128)(2,1)}, bf16[1024,3072]{1,0:T(8,128)(2,1)}, bf...) custom-call(s32[9]{0:T(128)} %stack.51.s_ref, ...), custom_call_target="tpu_custom_call" | custom-call | flops 21743271936 | bytes 1048576 | tf_op jit(solution)/shard_map/pallas_call | solution.py:41
  252.1 22.8 %shard_map.262 = bf16[32,2,96,768]{3,2,1,0:T(8,128)(2,1)} custom-call(s32[9]{0:T(128)} %stack.51.s_ref, bf16[1024,768]{1,0:T(8,128)(2,1)} %get-tuple-element.212.a_ref, bf16[1024,3072]{1,0:T(8,128)(2,1)} %get-tuple-element.213.du_ref, bf16[1024,3072]{1,0:T(8,128)(2,1)} %get-tuple-element.214.g_ref, bf16[1024,768]{1,0:T(8,128)(2,1)} %get-tuple-element.215.dm_ref), custom_call_target="tpu_custom_call" | custom-call | flops 9663676416 | bytes 1048576 | tf_op jit(solution)/shard_map/pallas_call | solution.py:41
  276.3 3.6 collective-permute-start.19
  279.8 25.9 %shard_map.263 = (bf16[1024,384]{1,0:T(8,128)(2,1)}, bf16[2,1536,384]{2,1,0:T(8,128)(2,1)}) custom-call(s32[1]{0:T(128)} %bitcast.18.s_ref, bf16[1024,768]{1,0:T(8,128)(2,1)} %get-tuple-element.205.q_ref, bf16[1536,768]{1,0:T(8,128)(2,1)} %get-tuple-element.201.k_ref, bf16[1536,768]{1,0:T(8,128)(2,1)} %get-tuple-element.202.v_ref, ...), custom_call_target="tpu_custom_call" | custom-call | flops 24159191040 | bytes 1048576 | tf_op jit(solution)/shard_map/pallas_call | solution.py:41
  305.8 6.0 shard_map.264
  312.3 26.2 %shard_map.265 = (bf16[1024,384]{1,0:T(8,128)(2,1)}, bf16[2,1536,384]{2,1,0:T(8,128)(2,1)}) custom-call(s32[1]{0:T(128)} %bitcast.17.s_ref, bf16[1024,768]{1,0:T(8,128)(2,1)} %get-tuple-element.205.q_ref, bf16[1536,768]{1,0:T(8,128)(2,1)} %get-tuple-element.201.k_ref, bf16[1536,768]{1,0:T(8,128)(2,1)} %get-tuple-element.202.v_ref, ...), custom_call_target="tpu_custom_call" | custom-call | flops 24159191040 | bytes 1048576 | tf_op jit(solution)/shard_map/pallas_call | solution.py:41
  338.6 10.8 %shard_map.266 = (f32[1024,768]{1,0:T(8,128)}, bf16[1024,768]{1,0:T(8,128)(2,1)}, bf16[1024,384]{1,0:T(8,128)(2,1)}, bf16[1024,384]{1,0:T(8,128)(2,1)}, f32[8,768]{1,0:T(8,128)}) custom-call(s32[9]{0:T(128)} %stack.51.s_ref, bf16[1024,384]{1,0:T(8,128)(2,1)} %get-tuple-element.235.dk_ref.q_ref, bf16[1024,384]{1,0:T(8,128)(2,1)} %get-tuple-element.225.q_ref.dg_ref, ...), custom_call_target="tpu_custom_call" | custom-call | flops 2415919104 | bytes 1048576 | tf_op jit(solution)/shard_map/pallas_call | solution.py:41
  349.4 4.1 shard_map.267
  353.5 10.6 %shard_map.268 = (bf16[1500,384]{1,0:T(8,128)(2,1)}, bf16[1500,384]{1,0:T(8,128)(2,1)}, bf16[768,384]{1,0:T(8,128)(2,1)}, bf16[768,384]{1,0:T(8,128)(2,1)}, f32[8,384]{1,0:T(8,128)}) custom-call(s32[9]{0:T(128)} %stack.51.s_ref, bf16[2,1536,384]{2,1,0:T(8,128)(2,1)} %get-tuple-element.245.ka, bf16[2,1536,384]{2,1,0:T(8,128)(2,1)} %collective-permute-done.20.kb, ...), custom_call_target="tpu_custom_call" | custom-call | flops 7077888000 | bytes 1048576 | tf_op jit(solution)/shard_map/pallas_call | solution.py:41
  364.8 3.6 collective-permute-done.23.refs_6_
  369.2 8.9 %shard_map.269 = (bf16[5,384,384]{2,1,0:T(8,128)(2,1)}, bf16[5,384,384]{2,1,0:T(8,128)(2,1)}) custom-call(s32[9]{0:T(128)} %stack.51.s_ref, bf16[1024,384]{1,0:T(8,128)(2,1)} %get-tuple-element.206.ck_ref.k_ref.o_ref.ck, bf16[1024,384]{1,0:T(8,128)(2,1)} %get-tuple-element.207.cg_ref.o_ref.g_ref.cg, bf16[1024,768]{1,0:T(8,128)(2,1)} %get-tuple-element.219.d_ref.d2_ref, ...), custom_call_target="tpu_custom_call" | custom-call | flops 1811939328 | bytes 1048576 | tf_op jit(solution)/shard_map/pallas_call | solution.py:41
  381.3 29.3 %shard_map.270 = (bf16[3,1024,256]{2,1,0:T(8,128)(2,1)}, bf16[3,1024,256]{2,1,0:T(8,128)(2,1)}) custom-call(s32[1]{0:T(128)} %bitcast.s_ref, bf16[3,1024,384]{2,1,0:T(8,128)(2,1)} %get-tuple-element.270.a_ref, bf16[3,1024,384]{2,1,0:T(8,128)(2,1)} %collective-permute-done.5.b_ref, bf16[2048,256]{1,0:T(8,128)(2,1)} %get-tuple-element.181.refs_0_.o_ref, ...), custom_call_target="tpu_custom_call" | custom-call | flops 17179869184 | bytes 1048576 | tf_op jit(solution)/shard_map/pallas_call | solution.py:41
  410.6 6.3 %collective-permute-done.26.g_ref = bf16[5,384,384]{2,1,0:T(8,128)(2,1)} collective-permute-done((bf16[5,384,384]{2,1,0:T(8,128)(2,1)}, bf16[5,384,384]{2,1,0:T(8,128)(2,1)}, u32[]{:S(2)}, u32[]{:S(2)}) %collective-permute-start.26) | collective-permute-done | bytes 1474592 | tf_op jit(solution)/shard_map/ppermute | solution.py:948
  417.0 3.2 collective-permute-start.28
  420.2 3.8 shard_map.271
  425.6 16.2 %shard_map.272 = (bf16[3,1024,128]{2,1,0:T(8,128)(2,1)}, bf16[3,1024,128]{2,1,0:T(8,128)(2,1)}) custom-call(s32[1]{0:T(128)} %bitcast.s_ref, bf16[3,1024,384]{2,1,0:T(8,128)(2,1)} %get-tuple-element.270.a_ref, bf16[3,1024,384]{2,1,0:T(8,128)(2,1)} %collective-permute-done.5.b_ref, bf16[2048,128]{1,0:T(8,128)(2,1)} %get-tuple-element.187.refs_1_.o_ref, ...), custom_call_target="tpu_custom_call" | custom-call | flops 8589934592 | bytes 1048576 | tf_op jit(solution)/shard_map/pallas_call | solution.py:41
  441.8 3.9 collective-permute-done.27.g_ref
  447.2 3.1 shard_map.273
  450.3 9.6 %shard_map.274 = (bf16[3,384,384]{2,1,0:T(8,128)(2,1)}, bf16[3,384,384]{2,1,0:T(8,128)(2,1)}) custom-call(s32[9]{0:T(128)} %stack.51.s_ref, bf16[1024,768]{1,0:T(8,128)(2,1)} %get-tuple-element.231.ao, bf16[1024,768]{1,0:T(8,128)(2,1)} %collective-permute-done.21.ai, bf16[3,1024,256]{2,1,0:T(8,128)(2,1)} %get-tuple-element.265.refs_0_, ...), custom_call_target="tpu_custom_call" | custom-call | flops 3623878656 | bytes 1048576 | tf_op jit(solution)/shard_map/pallas_call | solution.py:41
  464.5 12.2 %shard_map.275 = (bf16[1024,768]{1,0:T(8,128)(2,1)}, f32[8,768]{1,0:T(8,128)}) custom-call(s32[9]{0:T(128)} %stack.51.s_ref, bf16[3,1024,256]{2,1,0:T(8,128)(2,1)} %get-tuple-element.265.refs_0_, bf16[3,1024,128]{2,1,0:T(8,128)(2,1)} %get-tuple-element.283.refs_1_, bf16[3,1024,256]{2,1,0:T(8,128)(2,1)} %collective-permute-done.30.refs_2_, ...), custom_call_target="tpu_custom_call" | custom-call | flops 3623878656 | bytes 1048576 | tf_op jit(solution)/shard_map/pallas_call | solution.py:41
  479.1 5.3 collective-permute-done.34.p3
  489.1 3.7 collective-permute-start.36
  492.8 2.8 collective-permute-done.37.p3
  495.5 12.6 %collective-permute-done.36.p2 = bf16[5,48,384]{2,1,0:T(8,128)(2,1)S(1)} collective-permute-done((bf16[5,48,384]{2,1,0:T(8,128)(2,1)}, bf16[5,48,384]{2,1,0:T(8,128)(2,1)S(1)}, u32[]{:S(2)}, u32[]{:S(2)}) %collective-permute-start.36) | collective-permute-done | bytes 184352 | tf_op jit(solution)/shard_map/ppermute | solution.py:944
  508.1 3.1 shard_map.278
  511.7 4.0 collective-permute-start.38
  515.8 2.8 shard_map.279.refs_0_
  518.6 4.1 collective-permute-done.39.g_ref
  543.6 10.0 %collective-permute-done.45.p2 = bf16[4,48,384]{2,1,0:T(8,128)(2,1)S(1)} collective-permute-done((bf16[4,48,384]{2,1,0:T(8,128)(2,1)}, bf16[4,48,384]{2,1,0:T(8,128)(2,1)S(1)}, u32[]{:S(2)}, u32[]{:S(2)}) %collective-permute-start.45) | collective-permute-done | bytes 147488 | tf_op jit(solution)/shard_map/ppermute | solution.py:944
  562.6 8.2 %collective-permute-done.47.refs_1_ = bf16[4,192,384]{2,1,0:T(8,128)(2,1)S(1)} collective-permute-done((bf16[4,192,384]{2,1,0:T(8,128)(2,1)}, bf16[4,192,384]{2,1,0:T(8,128)(2,1)S(1)}, u32[]{:S(2)}, u32[]{:S(2)}) %collective-permute-start.47) | collective-permute-done | bytes 589856 | tf_op jit(solution)/shard_map/ppermute | solution.py:948
  570.8 2.8 collective-permute-start.49
  579.6 4.3 shard_map.283
  588.9 5.3 shard_map.284
  594.2 7.0 %shard_map.285 = (f32[384,3072]{1,0:T(8,128)}, f32[1536,768]{1,0:T(8,128)}) custom-call(s32[9]{0:T(128)} %stack.51.s_ref, bf16[16,2,96,768]{3,2,1,0:T(8,128)(2,1)} %bitcast.41), custom_call_target="tpu_custom_call" | custom-call | tf_op jit(solution)/shard_map/pallas_call | solution.py:41
  (230 shorter events, 91.8 us)
Async XLA Ops:
  7.2 189.8 %all-gather.5.cloned.1.call-start = ((), (), s32[]{:S(2)}) async-start(), calls=%async_computation.2 | async-start | bytes 9732096 | tf_op jit(solution)/shard_map/all_gather | solution.py:990
  7.2 24.2 %collective-permute-start = (bf16[1024,768]{1,0:T(8,128)(2,1)}, bf16[1024,768]{1,0:T(8,128)(2,1)S(1)}, u32[]{:S(2)}, u32[]{:S(2)}) collective-permute-start(bf16[1024,768]{1,0:T(8,128)(2,1)} %bitcast.37), channel_id=1, source_target_pairs={{1,2},{2,1},{5,6},{6,5},{9,10},{10,9},{13,14},{14,13},{17,18},{18,... | collective-permute-start | bytes 4718600 | tf_op jit(solution)/shard_map/ppermute | solution.py:965
  11.7 18.4 %collective-permute-start.1 = (s32[1,2048]{1,0:T(1,128)}, s32[1,2048]{1,0:T(1,128)S(1)}, u32[]{:S(2)}, u32[]{:S(2)}) collective-permute-start(s32[1,2048]{1,0:T(1,128)} %param.17), channel_id=1, source_target_pairs={{1,2},{2,1},{5,6},{6,5},{9,10},{10,9},{13,14},{14,13},{17,18},{18,... | collective-permute-start | bytes 24584 | tf_op jit(solution)/shard_map/ppermute | solution.py:965
  31.4 385.5 %reduce-scatter.2.cloned.1.call-start = ((), (), s32[]{:S(2)}) async-start(), calls=%async_computation.1 | async-start | bytes 9732096 | tf_op jit(solution)/shard_map/reduce_scatter | solution.py:1029
  33.6 23.4 %collective-permute-start.2 = (bf16[192,2304]{1,0:T(8,128)(2,1)S(1)}, bf16[192,2304]{1,0:T(8,128)(2,1)}, u32[]{:S(2)}, u32[]{:S(2)}) collective-permute-start(bf16[192,2304]{1,0:T(8,128)(2,1)S(1)} %dynamic-slice_convert_fusion), channel_id=1, source_target_pairs={{0,1},{1,0},{2,3},{3,2},{4,5},{5,4},{6,7},{7,6},{8,9},{9,8},{10,11... | collective-permute-start | bytes 2654216 | tf_op jit(solution)/shard_map/ppermute | solution.py:948
  33.9 25.0 %collective-permute-start.4 = (bf16[20,384]{1,0:T(8,128)(2,1)S(1)}, bf16[20,384]{1,0:T(8,128)(2,1)S(1)}, u32[]{:S(2)}, u32[]{:S(2)}) collective-permute-start(bf16[20,384]{1,0:T(8,128)(2,1)S(1)} %concatenate.35), channel_id=1, source_target_pairs={{0,1},{1,0},{2,3},{3,2},{4,5},{5,4},{6,7},{7,6},{8,9},{9,8},{10,11... | collective-permute-start | bytes 46088 | tf_op jit(solution)/shard_map/ppermute | solution.py:948
  71.1 44.5 %collective-permute-start.6 = (bf16[1500,384]{1,0:T(8,128)(2,1)S(1)}, bf16[1500,384]{1,0:T(8,128)(2,1)S(1)}, u32[]{:S(2)}, u32[]{:S(2)}) collective-permute-start(bf16[1500,384]{1,0:T(8,128)(2,1)S(1)} %bitcast.42), channel_id=1, source_target_pairs={{1,2},{2,1},{5,6},{6,5},{9,10},{10,9},{13,14},{14,13},{17,18},{18,... | collective-permute-start | bytes 3456008 | tf_op jit(solution)/shard_map/ppermute | solution.py:965
  74.7 41.0 %collective-permute-start.7 = (bf16[384,768]{1,0:T(8,128)(2,1)S(1)}, bf16[384,768]{1,0:T(8,128)(2,1)}, u32[]{:S(2)}, u32[]{:S(2)}) collective-permute-start(bf16[384,768]{1,0:T(8,128)(2,1)S(1)} %dynamic-slice_convert_fusion.1), channel_id=1, source_target_pairs={{0,1},{1,0},{2,3},{3,2},{4,5},{5,4},{6,7},{7,6},{8,9},{9,8},{10,11... | collective-permute-start | bytes 1769480 | tf_op jit(solution)/shard_map/ppermute | solution.py:948
  115.8 16.4 %collective-permute-start.10 = (bf16[1500,384]{1,0:T(8,128)(2,1)S(1)}, bf16[1500,384]{1,0:T(8,128)(2,1)S(1)}, u32[]{:S(2)}, u32[]{:S(2)}) collective-permute-start(bf16[1500,384]{1,0:T(8,128)(2,1)S(1)} %broadcast_select_fusion.fa), channel_id=1, source_target_pairs={{0,2},{2,0},{1,3},{3,1},{4,6},{6,4},{5,7},{7,5},{8,10},{10,8},{9,1... | collective-permute-start | bytes 3456008 | tf_op jit(solution)/shard_map/ppermute | solution.py:948
  118.9 13.2 %collective-permute-start.11 = (bf16[384,768]{1,0:T(8,128)(2,1)}, bf16[384,768]{1,0:T(8,128)(2,1)S(1)}, u32[]{:S(2)}, u32[]{:S(2)}) collective-permute-start(bf16[384,768]{1,0:T(8,128)(2,1)} %collective-permute-done.7.mine), channel_id=1, source_target_pairs={{0,2},{2,0},{1,3},{3,1},{4,6},{6,4},{5,7},{7,5},{8,10},{10,8},{9,1... | collective-permute-start | bytes 1769480 | tf_op jit(solution)/shard_map/ppermute | solution.py:948
  120.1 8.2 %collective-permute-start.12 = (bf16[192,768]{1,0:T(8,128)(2,1)S(1)}, bf16[192,768]{1,0:T(8,128)(2,1)S(1)}, u32[]{:S(2)}, u32[]{:S(2)}) collective-permute-start(bf16[192,768]{1,0:T(8,128)(2,1)S(1)} %dynamic-slice_convert_fusion.4), channel_id=1, source_target_pairs={{0,1},{1,0},{2,3},{3,2},{4,5},{5,4},{6,7},{7,6},{8,9},{9,8},{10,11... | collective-permute-start | bytes 884744 | tf_op jit(solution)/shard_map/ppermute | solution.py:948
  120.2 35.5 %collective-permute-start.8 = (bf16[1024,256]{1,0:T(8,128)(2,1)}, bf16[1024,256]{1,0:T(8,128)(2,1)S(1)}, u32[]{:S(2)}, u32[]{:S(2)}) collective-permute-start(bf16[1024,256]{1,0:T(8,128)(2,1)} %get-tuple-element.188), channel_id=1, source_target_pairs={{0,2},{2,0},{1,3},{3,1},{4,6},{6,4},{5,7},{7,5},{8,10},{10,8},{9,1... | collective-permute-start | bytes 1572872 | tf_op jit(solution)/shard_map/ppermute | solution.py:948
  121.9 22.2 %collective-permute-start.13 = (bf16[192,768]{1,0:T(8,128)(2,1)S(1)}, bf16[192,768]{1,0:T(8,128)(2,1)S(1)}, u32[]{:S(2)}, u32[]{:S(2)}) collective-permute-start(bf16[192,768]{1,0:T(8,128)(2,1)S(1)} %dynamic-slice_convert_fusion.3), channel_id=1, source_target_pairs={{0,1},{1,0},{2,3},{3,2},{4,5},{5,4},{6,7},{7,6},{8,9},{9,8},{10,11... | collective-permute-start | bytes 884744 | tf_op jit(solution)/shard_map/ppermute | solution.py:948
  128.3 68.6 %collective-permute-start.17 = (bf16[1024,768]{1,0:T(8,128)(2,1)}, bf16[1024,768]{1,0:T(8,128)(2,1)}, u32[]{:S(2)}, u32[]{:S(2)}) collective-permute-start(bf16[1024,768]{1,0:T(8,128)(2,1)} %bitcast.19.co), channel_id=1, source_target_pairs={{1,2},{2,1},{5,6},{6,5},{9,10},{10,9},{13,14},{14,13},{17,18},{18,... | collective-permute-start | bytes 4718600 | tf_op jit(solution)/shard_map/ppermute | solution.py:965
  144.1 11.6 %collective-permute-start.14 = (bf16[192,768]{1,0:T(8,128)(2,1)S(1)}, bf16[192,768]{1,0:T(8,128)(2,1)S(1)}, u32[]{:S(2)}, u32[]{:S(2)}) collective-permute-start(bf16[192,768]{1,0:T(8,128)(2,1)S(1)} %collective-permute-done.12.refs_7_), channel_id=1, source_target_pairs={{0,2},{2,0},{1,3},{3,1},{4,6},{6,4},{5,7},{7,5},{8,10},{10,8},{9,1... | collective-permute-start | bytes 884744 | tf_op jit(solution)/shard_map/ppermute | solution.py:948
  144.5 11.3 %collective-permute-start.15 = (bf16[192,768]{1,0:T(8,128)(2,1)S(1)}, bf16[192,768]{1,0:T(8,128)(2,1)S(1)}, u32[]{:S(2)}, u32[]{:S(2)}) collective-permute-start(bf16[192,768]{1,0:T(8,128)(2,1)S(1)} %collective-permute-done.13.refs_10_), channel_id=1, source_target_pairs={{0,2},{2,0},{1,3},{3,1},{4,6},{6,4},{5,7},{7,5},{8,10},{10,8},{9,1... | collective-permute-start | bytes 884744 | tf_op jit(solution)/shard_map/ppermute | solution.py:948
  155.6 26.2 %collective-permute-start.16 = (bf16[192,768]{1,0:T(8,128)(2,1)S(1)}, bf16[192,768]{1,0:T(8,128)(2,1)S(1)}, u32[]{:S(2)}, u32[]{:S(2)}) collective-permute-start(bf16[192,768]{1,0:T(8,128)(2,1)S(1)} %dynamic-slice_convert_fusion.2), channel_id=1, source_target_pairs={{0,1},{1,0},{2,3},{3,2},{4,5},{5,4},{6,7},{7,6},{8,9},{9,8},{10,11... | collective-permute-start | bytes 884744 | tf_op jit(solution)/shard_map/ppermute | solution.py:948
  181.8 15.1 %collective-permute-start.18 = (bf16[192,768]{1,0:T(8,128)(2,1)S(1)}, bf16[192,768]{1,0:T(8,128)(2,1)S(1)}, u32[]{:S(2)}, u32[]{:S(2)}) collective-permute-start(bf16[192,768]{1,0:T(8,128)(2,1)S(1)} %collective-permute-done.16.o2), channel_id=1, source_target_pairs={{0,2},{2,0},{1,3},{3,1},{4,6},{6,4},{5,7},{7,5},{8,10},{10,8},{9,1... | collective-permute-start | bytes 884744 | tf_op jit(solution)/shard_map/ppermute | solution.py:948
  274.9 319.3 %all-gather.7.cloned.1.call-start = ((), (), s32[]{:S(2)}) async-start(), calls=%async_computation.3 | async-start | bytes 5013504 | tf_op jit(solution)/shard_map/all_gather | solution.py:1064
  274.9 63.6 %collective-permute-start.21 = (bf16[1024,768]{1,0:T(8,128)(2,1)}, bf16[1024,768]{1,0:T(8,128)(2,1)}, u32[]{:S(2)}, u32[]{:S(2)}) collective-permute-start(bf16[1024,768]{1,0:T(8,128)(2,1)} %get-tuple-element.231.ao), channel_id=1, source_target_pairs={{0,2},{2,0},{1,3},{3,1},{4,6},{6,4},{5,7},{7,5},{8,10},{10,8},{9,1... | collective-permute-start | bytes 4718600 | tf_op jit(solution)/shard_map/ppermute | solution.py:948
  276.3 62.3 %collective-permute-start.19 = (bf16[1024,768]{1,0:T(8,128)(2,1)S(1)}, bf16[1024,768]{1,0:T(8,128)(2,1)S(1)}, u32[]{:S(2)}, u32[]{:S(2)}) collective-permute-start(bf16[1024,768]{1,0:T(8,128)(2,1)S(1)} %copy-done.5), channel_id=1, source_target_pairs={{1,2},{2,1},{5,6},{6,5},{9,10},{10,9},{13,14},{14,13},{17,18},{18,... | collective-permute-start | bytes 4718600 | tf_op jit(solution)/shard_map/ppermute | solution.py:965
  305.7 32.8 %collective-permute-start.20 = (bf16[2,1536,384]{2,1,0:T(8,128)(2,1)}, bf16[2,1536,384]{2,1,0:T(8,128)(2,1)}, u32[]{:S(2)}, u32[]{:S(2)}) collective-permute-start(bf16[2,1536,384]{2,1,0:T(8,128)(2,1)} %get-tuple-element.230), channel_id=1, source_target_pairs={{0,2},{2,0},{1,3},{3,1},{4,6},{6,4},{5,7},{7,5},{8,10},{10,8},{9,1... | collective-permute-start | bytes 7077896 | tf_op jit(solution)/shard_map/ppermute | solution.py:948
  311.8 26.7 %collective-permute-start.22 = (bf16[2,768,384]{2,1,0:T(8,128)(2,1)}, bf16[2,768,384]{2,1,0:T(8,128)(2,1)}, u32[]{:S(2)}, u32[]{:S(2)}) collective-permute-start(bf16[2,768,384]{2,1,0:T(8,128)(2,1)} %shard_map.264), channel_id=1, source_target_pairs={{0,2},{2,0},{1,3},{3,1},{4,6},{6,4},{5,7},{7,5},{8,10},{10,8},{9,1... | collective-permute-start | bytes 3538952 | tf_op jit(solution)/shard_map/ppermute | solution.py:948
  364.2 14.0 %collective-permute-start.24 = (bf16[1500,384]{1,0:T(8,128)(2,1)}, bf16[1500,384]{1,0:T(8,128)(2,1)S(1)}, u32[]{:S(2)}, u32[]{:S(2)}) collective-permute-start(bf16[1500,384]{1,0:T(8,128)(2,1)} %get-tuple-element.253), channel_id=1, source_target_pairs={{0,2},{2,0},{1,3},{3,1},{4,6},{6,4},{5,7},{7,5},{8,10},{10,8},{9,1... | collective-permute-start | bytes 3456008 | tf_op jit(solution)/shard_map/ppermute | solution.py:948
  364.7 16.6 %collective-permute-start.25 = (bf16[1024,384]{1,0:T(8,128)(2,1)}, bf16[1024,384]{1,0:T(8,128)(2,1)}, u32[]{:S(2)}, u32[]{:S(2)}) collective-permute-start(bf16[1024,384]{1,0:T(8,128)(2,1)} %get-tuple-element.259), channel_id=1, source_target_pairs={{0,2},{2,0},{1,3},{3,1},{4,6},{6,4},{5,7},{7,5},{8,10},{10,8},{9,1... | collective-permute-start | bytes 2359304 | tf_op jit(solution)/shard_map/ppermute | solution.py:948
  381.0 35.9 %collective-permute-start.26 = (bf16[5,384,384]{2,1,0:T(8,128)(2,1)}, bf16[5,384,384]{2,1,0:T(8,128)(2,1)}, u32[]{:S(2)}, u32[]{:S(2)}) collective-permute-start(bf16[5,384,384]{2,1,0:T(8,128)(2,1)} %get-tuple-element.263), channel_id=1, source_target_pairs={{0,1},{1,0},{2,3},{3,2},{4,5},{5,4},{6,7},{7,6},{8,9},{9,8},{10,11... | collective-permute-start | bytes 4423688 | tf_op jit(solution)/shard_map/ppermute | solution.py:948
  417.0 24.8 %collective-permute-start.28 = (bf16[1500,384]{1,0:T(8,128)(2,1)S(1)}, bf16[1500,384]{1,0:T(8,128)(2,1)}, u32[]{:S(2)}, u32[]{:S(2)}) collective-permute-start(bf16[1500,384]{1,0:T(8,128)(2,1)S(1)} %add_convert_fusion), channel_id=1, source_target_pairs={{1,2},{2,1},{5,6},{6,5},{9,10},{10,9},{13,14},{14,13},{17,18},{18,... | collective-permute-start | bytes 3456008 | tf_op jit(solution)/shard_map/ppermute | solution.py:965
  424.0 21.7 %collective-permute-start.27 = (bf16[5,192,384]{2,1,0:T(8,128)(2,1)}, bf16[5,192,384]{2,1,0:T(8,128)(2,1)S(1)}, u32[]{:S(2)}, u32[]{:S(2)}) collective-permute-start(bf16[5,192,384]{2,1,0:T(8,128)(2,1)} %get-tuple-element.274), channel_id=1, source_target_pairs={{0,4},{4,0},{1,5},{5,1},{2,6},{6,2},{3,7},{7,3},{8,12},{12,8},{9,1... | collective-permute-start | bytes 2211848 | tf_op jit(solution)/shard_map/ppermute | solution.py:948
  425.5 38.5 %collective-permute-start.30 = (bf16[3,1024,256]{2,1,0:T(8,128)(2,1)}, bf16[3,1024,256]{2,1,0:T(8,128)(2,1)}, u32[]{:S(2)}, u32[]{:S(2)}) collective-permute-start(bf16[3,1024,256]{2,1,0:T(8,128)(2,1)} %get-tuple-element.284.refs_2_), channel_id=1, source_target_pairs={{0,2},{2,0},{1,3},{3,1},{4,6},{6,4},{5,7},{7,5},{8,10},{10,8},{9,1... | collective-permute-start | bytes 4718600 | tf_op jit(solution)/shard_map/ppermute | solution.py:948
  446.5 17.1 %collective-permute-start.31 = (bf16[3,1024,128]{2,1,0:T(8,128)(2,1)}, bf16[3,1024,128]{2,1,0:T(8,128)(2,1)S(1)}, u32[]{:S(2)}, u32[]{:S(2)}) collective-permute-start(bf16[3,1024,128]{2,1,0:T(8,128)(2,1)} %get-tuple-element.285.refs_3_), channel_id=1, source_target_pairs={{0,2},{2,0},{1,3},{3,1},{4,6},{6,4},{5,7},{7,5},{8,10},{10,8},{9,1... | collective-permute-start | bytes 2359304 | tf_op jit(solution)/shard_map/ppermute | solution.py:948
  459.9 32.8 %collective-permute-start.29 = (bf16[3,384,384]{2,1,0:T(8,128)(2,1)}, bf16[3,384,384]{2,1,0:T(8,128)(2,1)}, u32[]{:S(2)}, u32[]{:S(2)}) collective-permute-start(bf16[3,384,384]{2,1,0:T(8,128)(2,1)} %get-tuple-element.290), channel_id=1, source_target_pairs={{0,1},{1,0},{2,3},{3,2},{4,5},{5,4},{6,7},{7,6},{8,9},{9,8},{10,11... | collective-permute-start | bytes 2654216 | tf_op jit(solution)/shard_map/ppermute | solution.py:948
  459.9 19.1 %collective-permute-start.32 = (bf16[5,48,384]{2,1,0:T(8,128)(2,1)}, bf16[5,48,384]{2,1,0:T(8,128)(2,1)S(1)}, u32[]{:S(2)}, u32[]{:S(2)}) collective-permute-start(bf16[5,48,384]{2,1,0:T(8,128)(2,1)} %get-tuple-element.299), channel_id=1, source_target_pairs={{0,8},{8,0},{16,24},{24,16},{1,9},{9,1},{17,25},{25,17},{2,10},{10... | collective-permute-start | bytes 552968 | tf_op jit(solution)/shard_map/ppermute | solution.py:944
  461.9 17.2 %collective-permute-start.33 = (bf16[5,48,384]{2,1,0:T(8,128)(2,1)}, bf16[5,48,384]{2,1,0:T(8,128)(2,1)S(1)}, u32[]{:S(2)}, u32[]{:S(2)}) collective-permute-start(bf16[5,48,384]{2,1,0:T(8,128)(2,1)} %get-tuple-element.300), channel_id=1, source_target_pairs={{0,16},{8,24},{16,0},{24,8},{1,17},{9,25},{17,1},{25,9},{2,18},{10... | collective-permute-start | bytes 552968 | tf_op jit(solution)/shard_map/ppermute | solution.py:944
  463.7 20.8 %collective-permute-start.34 = (bf16[5,48,384]{2,1,0:T(8,128)(2,1)}, bf16[5,48,384]{2,1,0:T(8,128)(2,1)S(1)}, u32[]{:S(2)}, u32[]{:S(2)}) collective-permute-start(bf16[5,48,384]{2,1,0:T(8,128)(2,1)} %get-tuple-element.301), channel_id=1, source_target_pairs={{0,24},{8,16},{16,8},{24,0},{1,25},{9,17},{17,9},{25,1},{2,26},{10... | collective-permute-start | bytes 552968 | tf_op jit(solution)/shard_map/ppermute | solution.py:944
  489.1 19.1 %collective-permute-start.36 = (bf16[5,48,384]{2,1,0:T(8,128)(2,1)}, bf16[5,48,384]{2,1,0:T(8,128)(2,1)S(1)}, u32[]{:S(2)}, u32[]{:S(2)}) collective-permute-start(bf16[5,48,384]{2,1,0:T(8,128)(2,1)} %shard_map.277.p0), channel_id=1, source_target_pairs={{0,16},{8,24},{16,0},{24,8},{1,17},{9,25},{17,1},{25,9},{2,18},{10... | collective-permute-start | bytes 552968 | tf_op jit(solution)/shard_map/ppermute | solution.py:944
  492.8 15.4 %collective-permute-start.35 = (bf16[5,48,384]{2,1,0:T(8,128)(2,1)}, bf16[5,48,384]{2,1,0:T(8,128)(2,1)S(1)}, u32[]{:S(2)}, u32[]{:S(2)}) collective-permute-start(bf16[5,48,384]{2,1,0:T(8,128)(2,1)} %shard_map.277.p0), channel_id=1, source_target_pairs={{0,8},{8,0},{16,24},{24,16},{1,9},{9,1},{17,25},{25,17},{2,10},{10... | collective-permute-start | bytes 552968 | tf_op jit(solution)/shard_map/ppermute | solution.py:944
  511.3 11.5 %collective-permute-start.39 = (bf16[3,192,384]{2,1,0:T(8,128)(2,1)}, bf16[3,192,384]{2,1,0:T(8,128)(2,1)S(1)}, u32[]{:S(2)}, u32[]{:S(2)}) collective-permute-start(bf16[3,192,384]{2,1,0:T(8,128)(2,1)} %get-tuple-element.320), channel_id=1, source_target_pairs={{0,4},{4,0},{1,5},{5,1},{2,6},{6,2},{3,7},{7,3},{8,12},{12,8},{9,1... | collective-permute-start | bytes 1327112 | tf_op jit(solution)/shard_map/ppermute | solution.py:948
  511.7 64.2 %collective-permute-start.38 = (bf16[1024,768]{1,0:T(8,128)(2,1)}, bf16[1024,768]{1,0:T(8,128)(2,1)}, u32[]{:S(2)}, u32[]{:S(2)}) collective-permute-start(bf16[1024,768]{1,0:T(8,128)(2,1)} %get-tuple-element.313), channel_id=1, source_target_pairs={{1,2},{2,1},{5,6},{6,5},{9,10},{10,9},{13,14},{14,13},{17,18},{18,... | collective-permute-start | bytes 4718600 | tf_op jit(solution)/shard_map/ppermute | solution.py:965
  526.1 8.4 %collective-permute-start.40 = (bf16[3,48,384]{2,1,0:T(8,128)(2,1)}, bf16[3,48,384]{2,1,0:T(8,128)(2,1)S(1)}, u32[]{:S(2)}, u32[]{:S(2)}) collective-permute-start(bf16[3,48,384]{2,1,0:T(8,128)(2,1)} %get-tuple-element.323), channel_id=1, source_target_pairs={{0,8},{8,0},{16,24},{24,16},{1,9},{9,1},{17,25},{25,17},{2,10},{10... | collective-permute-start | bytes 331784 | tf_op jit(solution)/shard_map/ppermute | solution.py:944
  526.1 8.4 %collective-permute-start.41 = (bf16[3,48,384]{2,1,0:T(8,128)(2,1)}, bf16[3,48,384]{2,1,0:T(8,128)(2,1)S(1)}, u32[]{:S(2)}, u32[]{:S(2)}) collective-permute-start(bf16[3,48,384]{2,1,0:T(8,128)(2,1)} %get-tuple-element.324), channel_id=1, source_target_pairs={{0,16},{8,24},{16,0},{24,8},{1,17},{9,25},{17,1},{25,9},{2,18},{10... | collective-permute-start | bytes 331784 | tf_op jit(solution)/shard_map/ppermute | solution.py:944
  533.7 28.4 %collective-permute-start.50 = (bf16[5,192,384]{2,1,0:T(8,128)(2,1)}, bf16[5,192,384]{2,1,0:T(8,128)(2,1)}, u32[]{:S(2)}, u32[]{:S(2)}) collective-permute-start(bf16[5,192,384]{2,1,0:T(8,128)(2,1)} %shard_map.279.refs_0_), channel_id=1, source_target_pairs={{0,4},{4,0},{1,5},{5,1},{2,6},{6,2},{3,7},{7,3},{8,12},{12,8},{9,1... | collective-permute-start | bytes 2211848 | tf_op jit(solution)/shard_map/ppermute | solution.py:948
  540.3 13.3 %collective-permute-start.45 = (bf16[4,48,384]{2,1,0:T(8,128)(2,1)}, bf16[4,48,384]{2,1,0:T(8,128)(2,1)S(1)}, u32[]{:S(2)}, u32[]{:S(2)}) collective-permute-start(bf16[4,48,384]{2,1,0:T(8,128)(2,1)} %shard_map.281.p0), channel_id=1, source_target_pairs={{0,16},{8,24},{16,0},{24,8},{1,17},{9,25},{17,1},{25,9},{2,18},{10... | collective-permute-start | bytes 442376 | tf_op jit(solution)/shard_map/ppermute | solution.py:944
  542.6 11.0 %collective-permute-start.44 = (bf16[4,48,384]{2,1,0:T(8,128)(2,1)}, bf16[4,48,384]{2,1,0:T(8,128)(2,1)S(1)}, u32[]{:S(2)}, u32[]{:S(2)}) collective-permute-start(bf16[4,48,384]{2,1,0:T(8,128)(2,1)} %shard_map.281.p0), channel_id=1, source_target_pairs={{0,8},{8,0},{16,24},{24,16},{1,9},{9,1},{17,25},{25,17},{2,10},{10... | collective-permute-start | bytes 442376 | tf_op jit(solution)/shard_map/ppermute | solution.py:944
  557.6 13.2 %collective-permute-start.47 = (bf16[4,192,384]{2,1,0:T(8,128)(2,1)}, bf16[4,192,384]{2,1,0:T(8,128)(2,1)S(1)}, u32[]{:S(2)}, u32[]{:S(2)}) collective-permute-start(bf16[4,192,384]{2,1,0:T(8,128)(2,1)} %shard_map.282.refs_0_), channel_id=1, source_target_pairs={{0,4},{4,0},{1,5},{5,1},{2,6},{6,2},{3,7},{7,3},{8,12},{12,8},{9,1... | collective-permute-start | bytes 1769480 | tf_op jit(solution)/shard_map/ppermute | solution.py:948
  561.4 25.8 %collective-permute-start.51 = (bf16[5,192,384]{2,1,0:T(8,128)(2,1)S(1)}, bf16[5,192,384]{2,1,0:T(8,128)(2,1)S(1)}, u32[]{:S(2)}, u32[]{:S(2)}) collective-permute-start(bf16[5,192,384]{2,1,0:T(8,128)(2,1)S(1)} %copy-done.2), channel_id=1, source_target_pairs={{0,2},{2,0},{1,3},{3,1},{4,6},{6,4},{5,7},{7,5},{8,10},{10,8},{9,1... | collective-permute-start | bytes 2211848 | tf_op jit(solution)/shard_map/ppermute | solution.py:948
  562.1 16.7 %collective-permute-start.48 = (bf16[4,192,384]{2,1,0:T(8,128)(2,1)S(1)}, bf16[4,192,384]{2,1,0:T(8,128)(2,1)S(1)}, u32[]{:S(2)}, u32[]{:S(2)}) collective-permute-start(bf16[4,192,384]{2,1,0:T(8,128)(2,1)S(1)} %copy-done.4), channel_id=1, source_target_pairs={{0,2},{2,0},{1,3},{3,1},{4,6},{6,4},{5,7},{7,5},{8,10},{10,8},{9,1... | collective-permute-start | bytes 1769480 | tf_op jit(solution)/shard_map/ppermute | solution.py:948
  562.1 25.0 %collective-permute-start.52 = (bf16[5,192,384]{2,1,0:T(8,128)(2,1)}, bf16[5,192,384]{2,1,0:T(8,128)(2,1)S(1)}, u32[]{:S(2)}, u32[]{:S(2)}) collective-permute-start(bf16[5,192,384]{2,1,0:T(8,128)(2,1)} %collective-permute-done.50.refs_1_), channel_id=1, source_target_pairs={{0,2},{2,0},{1,3},{3,1},{4,6},{6,4},{5,7},{7,5},{8,10},{10,8},{9,1... | collective-permute-start | bytes 2211848 | tf_op jit(solution)/shard_map/ppermute | solution.py:948
  570.8 8.8 %collective-permute-start.49 = (bf16[4,192,384]{2,1,0:T(8,128)(2,1)S(1)}, bf16[4,192,384]{2,1,0:T(8,128)(2,1)}, u32[]{:S(2)}, u32[]{:S(2)}) collective-permute-start(bf16[4,192,384]{2,1,0:T(8,128)(2,1)S(1)} %collective-permute-done.47.refs_1_), channel_id=1, source_target_pairs={{0,2},{2,0},{1,3},{3,1},{4,6},{6,4},{5,7},{7,5},{8,10},{10,8},{9,1... | collective-permute-start | bytes 1769480 | tf_op jit(solution)/shard_map/ppermute | solution.py:948
  (54 other events, 281.8 us)
Sparse Core Ops, SparseCore 0:
  31.6 96.2 all-gather.4
  275.0 140.9 reduce-scatter.1
  418.6 67.8 all-gather.6

commit v3 on v2

--- a/solution.py
+++ b/solution.py
@@ -37,7 +37,7 @@
     )
     estimate = None
     if cost is not None:
-        estimate = pl.CostEstimate(flops=cost, bytes_accessed=1 << 20, transcendentals=0)
+        estimate = pl.CostEstimate(flops=cost // 10, bytes_accessed=1 << 20, transcendentals=0)
     return pl.pallas_call(
         kernel,
         grid_spec=spec,
@@ -244,7 +244,7 @@
     )
 
 
-def self_bwd(first, pairs, place, keep, recv, o, dkeep, drecv, lse, kmark, qmark, block=256):
+def self_bwd(first, pairs, seat, place, keep, recv, o, dkeep, drecv, lse, kmark, qmark, block=256):
     rows, width = keep.shape[1], pairs * 128
     t = 2 * rows
 
@@ -299,7 +299,8 @@
     half = pl.BlockSpec((rows, 128), lambda p, s: (0, first + p))
     return call(
         kernel, jnp.reshape(place, (1,)).astype(jnp.int32), (keep, recv, o, dkeep, drecv, lse, kmark, qmark), (pairs,),
-        half_specs(rows, first) + [pl.BlockSpec((t, 128), lambda p, s: (0, p)), half, half, pl.BlockSpec((1, 8, t), lambda p, s: (p, 0, 0)), whole, whole],
+        half_specs(rows, first)
+        + [pl.BlockSpec((t, 128), lambda p, s: (0, seat + p)), half, half, pl.BlockSpec((1, 8, t), lambda p, s: (seat + p, 0, 0)), whole, whole],
         half_specs(rows),
         [shape((3, rows, width))] * 2,
         [pltpu.VMEM((t, 128), bf16)] * 3 + [pltpu.VMEM((2, t, 128), bf16), pltpu.VMEM((2, 128, t), bf16), pltpu.VMEM((t, 128), bf16)]
@@ -363,9 +364,19 @@
     full[pl.ds(pl.multiple_of(start + (1 - c) * (rows // 2), 64), rows // 2), :] = sib[...]
 
 
+def picked(part):
+    if not isinstance(part, tuple):
+        return once(part.shape)
+    stack, which = part
+    return pl.BlockSpec((None, *stack.shape[1:]), lambda i, s: (which, 0, 0), pipeline_mode=pl.Buffered(1))
+
+
 def weight_specs(weight):
-    own, mine, sib = weight
-    return [once(own.shape), once(mine.shape), once(sib.shape)]
+    return [picked(part) for part in weight]
+
+
+def arrays(weight):
+    return [part[0] if isinstance(part, tuple) else part for part in weight]
 
 
 def full_shape(weight):
@@ -437,7 +448,7 @@
 
     dims = full_shape(w_out)
     return call(
-        kernel, s, (*ctx, *ctx_in, x_own, x_in, *w_out, *w_q, table), (steps,),
+        kernel, s, (*ctx, *ctx_in, x_own, x_in, *arrays(w_out), *arrays(w_q), table), (steps,),
         [pl.BlockSpec((rows, part.shape[1]), lambda i, s: (s[0] * steps + i, 0)) for part in ctx]
         + [tile(rows, part.shape[1]) for part in ctx_in] + [tile(rows, width), tile(rows, width)]
         + weight_specs(w_out) + weight_specs(w_q) + [const(table.shape)],
@@ -477,25 +488,34 @@
     )
 
 
-def middle(s, h1, c2_keep, c2_give, cot_own, cot_in, w_out, ffw, table, fc1_shift, rows=256):
+def middle(s, h1, c2_keep, c2_give, cot_own, cot_in, w_out, ff_own, ff_far, table, fc1_shift, rows=256):
     t, width = h1.shape
     units = fc1_shift.shape[1] // width
     hw = width // 2
-    piece = ffw.shape[2]
-
-    def kernel(s_ref, h1_ref, ck_ref, cg_ref, co, ci, o1, o2, o3, w1, w2, tab, shift, wo, out, a_ref, g_ref, dm_ref, du_ref, d2_ref, dh_ref, dk_ref, dg_ref, vec):
+    pieces, piece = ff_own[0].shape[:2]
+
+    def kernel(s_ref, h1_ref, ck_ref, cg_ref, co, ci, o1, o2, o3, own1, own2, far, tab, shift, wo, out, a_ref, g_ref, dm_ref, du_ref, d2_ref, dh_ref, dk_ref, dg_ref, vec, w1, w2, sems):
+        def moves():
+            for k, (dst, own) in enumerate(((w1, own1), (w2, own2))):
+                yield pltpu.make_async_copy(own, dst.at[pl.ds(s_ref[1] * pieces, pieces)], sems.at[2 * k])
+                yield pltpu.make_async_copy(far.at[:, k], dst.at[pl.ds((1 - s_ref[1]) * pieces, pieces)], sems.at[2 * k + 1])
+
         @pl.when(pl.program_id(0) == 0)
         def _():
+            for move in moves():
+                move.start()
             fill(wo, s_ref, o1, o2, o3)
             vec[...] = jnp.zeros(vec.shape, f32)
+            for move in moves():
+                move.wait()
 
         def up(h, j):
             at, many = (h * units + j) * (hw // piece), hw // piece
-            return w1[at : at + many, 0].reshape(hw, width)
+            return w1[at : at + many].reshape(hw, width)
 
         def down(j):
             many = width // piece
-            return w2[j * many : (j + 1) * many, 0].reshape(width, width)
+            return w2[j * many : (j + 1) * many].reshape(width, width)
 
         c = s_ref[0]
         h2 = h1_ref[...] + mm(ck_ref[...], wo[at_core(c, hw), :]) + mm(cg_ref[...], wo[at_core(1 - c, hw), :]) + tab[13:14]
@@ -504,14 +524,19 @@
         a_ref[...] = a
         acc = h2 + tab[14:15]
         slopes = []
+
+        def climb(j):
+            return mm(a[:, :hw], up(0, j)) + mm(a[:, hw:], up(1, j)) + shift[:, j * width : (j + 1) * width]
+
+        u = climb(0)
         for j in range(units):
-            cols = slice(j * width, (j + 1) * width)
-            u = mm(a[:, :hw], up(0, j)) + mm(a[:, hw:], up(1, j)) + shift[:, cols]
+            u_next = climb(j + 1) if j + 1 < units else None
             g, slope = gelu_parts(u.astype(bf16).astype(f32))
             slopes.append(slope)
             g = g.astype(bf16)
-            g_ref[:, cols] = g
+            g_ref[:, j * width : (j + 1) * width] = g
             acc = acc + mm(g, down(j))
+            u = u_next
         n3, inv3 = norm_stats(acc)
         out[...] = (n3 * tab[3:4] + tab[7:8]).astype(bf16)
 
@@ -527,9 +552,12 @@
         dm = dh3.astype(bf16)
         dm_ref[...] = dm
         halves = [None, None]
+        dg = mm_t(dm, down(0))
         for j in range(units):
             cols = slice(j * width, (j + 1) * width)
-            du = (slopes[j] * mm_t(dm, down(j))).astype(bf16)
+            dg_next = mm_t(dm, down(j + 1)) if j + 1 < units else None
+            du = (slopes[j] * dg).astype(bf16)
+            dg = dg_next
             du_ref[:, cols] = du
             vec[0:1, cols] += total(du.astype(f32))
             for h in range(2):
@@ -551,13 +579,14 @@
     ff = units * width
     line = tile(rows, width)
     wide, half = tile(rows, ff), tile(rows, hw)
-    gathered = [pl.BlockSpec((32, 1, piece, width), lambda i, s, k=k: (0, k, 0, 0), pipeline_mode=pl.Buffered(1)) for k in range(2)]
-    return call(
-        kernel, s, (h1, c2_keep, c2_give, cot_own, cot_in, *w_out, ffw, ffw, table, fc1_shift), (t // rows,),
-        [line, half, half, line, line] + weight_specs(w_out) + gathered + [const(table.shape), const(fc1_shift.shape)],
+    away = pl.BlockSpec(memory_space=pl.ANY)
+    return call(
+        kernel, s, (h1, c2_keep, c2_give, cot_own, cot_in, *arrays(w_out), *ff_own, ff_far, table, fc1_shift), (t // rows,),
+        [line, half, half, line, line] + weight_specs(w_out) + [away] * 3 + [const(table.shape), const(fc1_shift.shape)],
         [const(dims), line, line, wide, line, wide, line, line, half, half, const((8, ff))],
         [shape(dims), shape((t, width)), shape((t, width)), shape((t, ff)), shape((t, width)), shape((t, ff)), shape((t, width)),
          shape((t, width), f32), shape((t, hw)), shape((t, hw)), shape((8, ff), f32)],
+        [pltpu.VMEM((2 * pieces, piece, width), bf16)] * 2 + [pltpu.SemaphoreType.DMA((4,))],
         cost=8 * t * width * ff + 4 * t * width * width,
     )
 
@@ -568,28 +597,26 @@
     ff = du.shape[1]
     units = ff // width
     piece = hw * units // 16
-
-    def kernel(s_ref, a_ref, du_ref, g_ref, dm_ref, out):
-        step = pl.program_id(0)
-
-        @pl.when(step < 2 * units)
+    many = hw // piece
+
+    def kernel(s_ref, a_ref, du_ref, g0, g1, dm_ref, out):
+        @pl.when(pl.program_id(0) < units)
         def _():
-            out[...] = t_mm(a_ref[...], du_ref[...]).astype(bf16).reshape(out.shape)
-
-        @pl.when(step >= 2 * units)
+            for h in range(2):
+                out[h] = t_mm(a_ref[:, h * hw : (h + 1) * hw], du_ref[...]).astype(bf16).reshape(out.shape[1:])
+
+        @pl.when(pl.program_id(0) >= units)
         def _():
-            out[...] = t_mm(g_ref[...], dm_ref[...]).astype(bf16).reshape(out.shape)
-
-    n1 = 2 * units
-    many = hw // piece
-    return call(
-        kernel, s, (a, du, g, dm), (2 * n1,),
-        [pl.BlockSpec((t, hw), lambda i, s: (0, jnp.minimum(i // units, 1))),
-         pl.BlockSpec((t, width), lambda i, s: (0, jnp.where(i < n1, i % units, units - 1))),
-         pl.BlockSpec((t, hw), lambda i, s: (0, jnp.maximum(i - n1, 0))),
-         pl.BlockSpec((t, width), lambda i, s: (0, 0))],
-        pl.BlockSpec((many, 1, piece, width), lambda i, s: (jnp.where(i < n1, i, i - n1), jnp.where(i < n1, 0, 1), 0, 0)),
-        shape((32, 2, piece, width)),
+            for h, ref in enumerate((g0, g1)):
+                out[h] = t_mm(ref[...], dm_ref[...]).astype(bf16).reshape(out.shape[1:])
+
+    return call(
+        kernel, s, (a, du, g, g, dm), (2 * units,),
+        [once((t, width)), pl.BlockSpec((t, width), lambda i, s: (0, jnp.minimum(i, units - 1))),
+         pl.BlockSpec((t, hw), lambda i, s: (0, jnp.maximum(i - units, 0))),
+         pl.BlockSpec((t, hw), lambda i, s: (0, units + jnp.maximum(i - units, 0))), once((t, width))],
+        pl.BlockSpec((2, many, 1, piece, width), lambda i, s: (0, i % units, i // units, 0, 0)),
+        shape((2, 16, 2, piece, width)),
         cost=4 * t * width * ff,
     )
 
@@ -711,48 +738,69 @@
     )
 
 
-def keep_grads(s, c2_keep, c2_give, d2, a2, dq_keep, ctx, ctx_in, d1, pair_in, out_in, kv_keep, kv_give):
+def keep_grads(s, c2_keep, c2_give, d2, a2, dq_keep, pair_in, kv_keep, kv_give):
     t, width = d2.shape
     hw = width // 2
-    n = len(ctx)
-
-    def kernel(s_ref, ck, cg, d2_ref, a_ref, q_ref, *refs):
-        d1_ref, p_ref, o_ref, kk, kg, xgive, xkeep = refs[2 * n :]
+
+    def kernel(s_ref, ck, cg, d2_ref, a_ref, q_ref, p_ref, kk, kg, xgive, xkeep):
         c, h = s_ref[0], s_ref[1]
-        same = c == h
         for out, shard, kv in ((xgive, 1 - h, kg), (xkeep, h, kk)):
             rows = at_core(shard, hw)
             out[1] = (t_mm(a_ref[:, rows], q_ref[...]) + p_ref[1, rows, :].astype(f32)).astype(bf16)
-            out[3] = kv[:hw]
-            out[4] = kv[hw:]
-        for k, lefts, right, extra in ((0, (ck[...], cg[...]), d2_ref, p_ref.at[0]), (2, (beside(refs[:n]), beside(refs[n : 2 * n])), d1_ref, o_ref)):
-            own_rows = t_mm(lefts[0], right[...]) + extra[at_core(c, hw), :].astype(f32)
-            far_rows = t_mm(lefts[1], right[...]) + extra[at_core(1 - c, hw), :].astype(f32)
-            xkeep[k] = jnp.where(same, own_rows, far_rows).astype(bf16)
-            xgive[k] = jnp.where(same, far_rows, own_rows).astype(bf16)
+            out[2] = kv[:hw]
+            out[3] = kv[hw:]
+        own_rows = t_mm(ck[...], d2_ref[...]) + p_ref[0, at_core(c, hw), :].astype(f32)
+        far_rows = t_mm(cg[...], d2_ref[...]) + p_ref[0, at_core(1 - c, hw), :].astype(f32)
+        xkeep[0] = jnp.where(c == h, own_rows, far_rows).astype(bf16)
+        xgive[0] = jnp.where(c == h, far_rows, own_rows).astype(bf16)
 
     cols, half = pl.BlockSpec((t, hw), lambda i, s: (0, s[0])), const((t, hw))
-    five = (5, hw, hw)
-    return call(
-        kernel, s, (c2_keep, c2_give, d2, a2, dq_keep, *ctx, *ctx_in, d1, pair_in, out_in, kv_keep, kv_give), (1,),
-        [half, half, cols, const((t, width)), half]
-        + [pl.BlockSpec((t, part.shape[1]), lambda i, s: (s[0], 0)) for part in ctx] + [const(part.shape) for part in ctx_in]
-        + [cols, const((2, width, hw)), const((width, hw)), const((width, hw)), const((width, hw))],
-        [const(five), const(five)], [shape(five), shape(five)], cost=6 * t * width * hw,
-    )
-
-
-def split_y(s, keep, got):
-    b, rows, cols = keep.shape
-    half = rows // 2
-
-    def kernel(s_ref, k_ref, g_ref, give, mine):
+    four = (4, hw, hw)
+    return call(
+        kernel, s, (c2_keep, c2_give, d2, a2, dq_keep, pair_in, kv_keep, kv_give), (1,),
+        [half, half, cols, const((t, width)), half, const((2, width, hw)), const((width, hw)), const((width, hw))],
+        [const(four), const(four)], [shape(four), shape(four)], cost=4 * t * width * hw,
+    )
+
+
+def keep_grad_out(s, ctx, ctx_in, d1, out_in):
+    t, width = d1.shape
+    hw = width // 2
+    n = len(ctx)
+
+    def kernel(s_ref, *refs):
+        d1_ref, o_ref, xgive, xkeep = refs[2 * n :]
+        c, h = s_ref[0], s_ref[1]
+        own_rows = t_mm(beside(refs[:n]), d1_ref[...]) + o_ref[at_core(c, hw), :].astype(f32)
+        far_rows = t_mm(beside(refs[n : 2 * n]), d1_ref[...]) + o_ref[at_core(1 - c, hw), :].astype(f32)
+        xkeep[0] = jnp.where(c == h, own_rows, far_rows).astype(bf16)
+        xgive[0] = jnp.where(c == h, far_rows, own_rows).astype(bf16)
+
+    one = (1, hw, hw)
+    return call(
+        kernel, s, (*ctx, *ctx_in, d1, out_in), (1,),
+        [pl.BlockSpec((t, part.shape[1]), lambda i, s: (s[0], 0)) for part in ctx] + [const(part.shape) for part in ctx_in]
+        + [pl.BlockSpec((t, hw), lambda i, s: (0, s[0])), const((width, hw))],
+        [const(one), const(one)], [shape(one), shape(one)], cost=2 * t * width * hw,
+    )
+
+
+def split_y(s, keeps, gots):
+    _, rows, cols = keeps[0].shape
+    half, n = rows // 2, len(keeps)
+    counts = [k.shape[0] for k in keeps]
+
+    def kernel(s_ref, *refs):
+        give, mine = refs[2 * n :]
         for out, y in ((give, 1 - s_ref[4]), (mine, s_ref[4])):
-            at = pl.ds(pl.multiple_of(y * half, 64), half)
-            out[...] = (k_ref[:, at, :].astype(f32) + g_ref[:, at, :].astype(f32)).astype(bf16)
-
-    dims = (b, half, cols)
-    return call(kernel, s, (keep, got), (1,), [const(keep.shape)] * 2, [const(dims)] * 2, [shape(dims)] * 2)
+            rows_at = pl.ds(pl.multiple_of(y * half, 64), half)
+            at = 0
+            for k_ref, g_ref, count in zip(refs[:n], refs[n : 2 * n], counts):
+                out[at : at + count] = (k_ref[:, rows_at, :].astype(f32) + g_ref[:, rows_at, :].astype(f32)).astype(bf16)
+                at += count
+
+    dims = (sum(counts), half, cols)
+    return call(kernel, s, (*keeps, *gots), (1,), [const(k.shape) for k in (*keeps, *gots)], [const(dims)] * 2, [shape(dims)] * 2)
 
 
 def split_z(s, keep, got):
@@ -871,23 +919,20 @@
     )
 
 
-def qkv_grad(s, a_own, a_sib, keep, give):
+def qkv_grad(s, a_own, a_sib, keep, give, mine):
     t, width = a_own.shape
     hw = width // 2
     n = len(keep)
 
     def kernel(s_ref, ao, ai, *refs):
-        xgive, xkeep = refs[2 * n :]
         k, g = (jnp.concatenate([ref[0] for ref in part], axis=1) for part in (refs[:n], refs[n : 2 * n]))
-        for out, shard in ((xgive, 1 - s_ref[1]), (xkeep, s_ref[1])):
-            rows = at_core(shard, hw)
-            out[0] = (t_mm(ao[:, rows], k) + t_mm(ai[:, rows], g)).astype(bf16)
-
-    out = pl.BlockSpec((1, hw, hw), lambda i, s: (i, 0, 0))
+        refs[-1][0] = (t_mm(ao[...], k) + t_mm(ai[...], g)).astype(bf16)
+
+    cols = pl.BlockSpec((t, hw), lambda i, s: (0, s[1] if mine else 1 - s[1]))
     return call(
         kernel, s, (a_own, a_sib, *keep, *give), (3,),
-        [once((t, width)), once((t, width))] + [pl.BlockSpec((1, t, part.shape[2]), lambda i, s: (i, 0, 0)) for part in (*keep, *give)],
-        [out, out], [shape((3, hw, hw))] * 2, cost=12 * t * width * hw,
+        [cols, cols] + [pl.BlockSpec((1, t, part.shape[2]), lambda i, s: (i, 0, 0)) for part in (*keep, *give)],
+        pl.BlockSpec((1, hw, hw), lambda i, s: (i, 0, 0)), shape((3, hw, hw)), cost=6 * t * width * hw,
     )
 
 
@@ -982,46 +1027,46 @@
     table = jnp.concatenate([small[0, :16], small[1, :16]], axis=1)
     fc1_shift = small[:, 15:19].reshape(1, ff)
     kmark, qmark = seg_marks(seg)
-    deep = hw // per
-    part1 = lax.dynamic_slice(fc1, (rep_at % deep * per, rep_at // deep * width), (per, width))
-    part2 = lax.dynamic_slice_in_dim(fc2, rep_at * per, per)
-    slot = jnp.concatenate([part1, part2]).astype(bf16)
-    x_in, slot, kmark, qmark, frames, cross_kv = tie(x_in, slot, kmark, qmark, frames, cross_kv)
-    ffw = lax.all_gather(slot, SPREAD2, axis=0, tiled=False).reshape(2 * reps, 2, per, width)
+    own1 = jnp.concatenate([fc1[:, j * width : (j + 1) * width] for j in range(units)]).astype(bf16).reshape(reps, per, width)
+    own2 = fc2.astype(bf16).reshape(reps, per, width)
+    slot = jnp.stack([lax.dynamic_index_in_dim(own1, rep_at, keepdims=False), lax.dynamic_index_in_dim(own2, rep_at, keepdims=False)])
+    part = hw // 2
+    squares = jnp.stack([lax.dynamic_slice_in_dim(w, c * part, part) for w in (self_out, cross_q, cross_out)]).astype(bf16)
+    kv_part = lax.dynamic_slice_in_dim(cross_kv, c * hw, hw).astype(bf16)
+    x_in, kmark, qmark, squares, kv_part, frames, own1, own2, slot = tie(x_in, kmark, qmark, squares, kv_part, frames, own1, own2, slot)
+    slot = across(slot, "x")
+    squares_near = across(squares, "x")
     f_own = frames[0]
     f_in = swap(f_own)
-    kv_near = near(cross_kv)
+    kv_near = across(kv_part, "x")
     w_qkv, a1, keep, give = norm_qkv(s, x_own, x_in, (self_qkv, qkv_near, sibling(qkv_near)), table)
+    give, slot = tie(give, slot)
     recv = sibling(give)
+    ff_far = lax.all_gather(slot, REP2, axis=0, tiled=False)
 
     many = pairs - 1
     ctx_a, give_a, lse_a = self_fwd(0, many, c, keep, recv, kmark, qmark)
-    give_a, f_in, kv_near, keep, recv = tie(give_a, f_in, kv_near, keep, recv)
+    give_a, keep, recv, squares_near, cotangent = tie(give_a, keep, recv, squares_near, cotangent)
+    cot_in = swap(cotangent[0])
+    squares_sib = sibling(squares_near)
+    w_out, w_q, w_co = (
+        (w, (squares_near, k), (squares_sib, k)) for k, w in enumerate((self_out, cross_q, cross_out))
+    )
+    in_a = sibling(give_a)
+    ctx_b, give_b, lse_b = self_fwd(many, 1, c, keep, recv, kmark, qmark)
+    in_b = sibling(give_b)
+    ctx, ctx_in = (ctx_a, ctx_b), (in_a, in_b)
+    w_out, w_q, h1, a2, qc = self_project(s, ctx, ctx_in, x_own, x_in, w_out, w_q, table)
+    qc, f_in, kv_near = tie(qc, f_in, kv_near)
     half = jnp.where(stay, f_own, f_in)
     twin = sibling(half)
-    kv_sib = sibling(kv_near)
-    in_a = sibling(give_a)
-    half, self_out, cross_q = tie(half, self_out, cross_q)
-    out_near, q_near = near(self_out), near(cross_q)
-    out_near, cross_out, cotangent = tie(out_near, cross_out, cotangent)
-    co_near = near(cross_out)
-    cot_in = swap(cotangent[0])
-    ctx_b, give_b, lse_b = self_fwd(many, 1, c, keep, recv, kmark, qmark)
-    in_b = sibling(give_b)
-    w_kv, kc, vc = frame_kv(s, half, twin, (cross_kv, kv_near, kv_sib), table)
-    kc, out_near, q_near = tie(kc, out_near, q_near)
-    ctx, ctx_in = (ctx_a, ctx_b), (in_a, in_b)
-    w_out, w_q, h1, a2, qc = self_project(
-        s, ctx, ctx_in, x_own, x_in, (self_out, out_near, sibling(out_near)), (cross_q, q_near, sibling(q_near)), table
-    )
+    w_kv, kc, vc = frame_kv(s, half, twin, (cross_kv, kv_near, sibling(kv_near)), table)
     count = half.shape[0]
     own_pairs, far_pairs = c * pairs, (1 - c) * pairs
     c2_give, cross_lse_give = cross_fwd(far_pairs, pairs, qc, kc, vc, count)
-    c2_give, co_near, qc = tie(c2_give, co_near, qc)
-    co_sib = sibling(co_near)
     c2_keep, cross_lse_keep = cross_fwd(own_pairs, pairs, qc, kc, vc, count)
-    w_co, out, a3, g, dm, du, d2, dh2, dc2_keep, dc2_give, vec_mid = middle(
-        s, h1, c2_keep, c2_give, cotangent[0], cot_in, (cross_out, co_near, co_sib), ffw, table, fc1_shift,
+    _, out, a3, g, dm, du, d2, dh2, dc2_keep, dc2_give, vec_mid = middle(
+        s, h1, c2_keep, c2_give, cotangent[0], cot_in, w_co, (own1, own2), ff_far, table, fc1_shift,
     )
 
     packed = ff_grads(s, a3, du, g, dm)
@@ -1037,21 +1082,24 @@
     pair_in = sibling(pair_give)
     dq_keep, dkv_keep = cross_bwd(own_pairs, pairs, qc, kc, vc, c2_keep, dc2_keep, cross_lse_keep, count)
     dq_keep, out_in, dkv_in, a1_sib, pair_in = tie(dq_keep, out_in, dkv_in, a1_sib, pair_in)
+    fkeep, fgive, kv_xkeep, kv_xgive, vec_kv = frame_back(s, dkv_keep, dkv_in, half, twin, w_kv)
+    fgive, dq_keep = tie(fgive, dq_keep)
+    fr_in = sibling(fgive)
+    xgive, xkeep = keep_grads(s, c2_keep, c2_give, d2, a2, dq_keep, pair_in, kv_xkeep, kv_xgive)
+    xgive, dq_keep = tie(xgive, dq_keep)
+    got_x = across(xgive, "x")
     dh1, d1, dctx_keep, dctx_give, vec_cross = cross_back(s, dq_keep, dq_give, h1, dh2, w_q, w_out, table)
     dctx_give, d1 = tie(dctx_give, d1)
     dctx_in = sibling(dctx_give)
     so_give = give_grad_out(s, ctx, ctx_in, d1)
-    so_give, dkv_keep = tie(so_give, dkv_keep)
+    so_give, fr_in, fkeep = tie(so_give, fr_in, fkeep)
     so_in = sibling(so_give)
-    fkeep, fgive, kv_xkeep, kv_xgive, vec_kv = frame_back(s, dkv_keep, dkv_in, half, twin, w_kv)
-    fgive, kv_xgive = tie(fgive, kv_xgive)
-    fr_in = sibling(fgive)
-    xgive, xkeep = keep_grads(s, c2_keep, c2_give, d2, a2, dq_keep, ctx, ctx_in, d1, pair_in, so_in, kv_xkeep, kv_xgive)
-    xgive, fr_in, fkeep = tie(xgive, fr_in, fkeep)
-    got_x = across(xgive, "x")
     fr_own = (fkeep.astype(f32) + fr_in.astype(f32)).astype(bf16)
     fr_own, dctx_keep = tie(fr_own, dctx_keep)
     fr_swapped = swap(fr_own)
+    so_xgive, so_xkeep = keep_grad_out(s, ctx, ctx_in, d1, so_in)
+    so_xgive, dctx_keep = tie(so_xgive, dctx_keep)
+    so_x = across(so_xgive, "x")
 
     def send_z(pieces):
         return (pieces[0],) + tuple(across_z(pieces[d], d) for d in (1, 2, 3))
@@ -1059,52 +1107,61 @@
     def gather_z(piece):
         return (piece,) + tuple(across_z(piece, d) for d in (1, 2, 3))
 
-    bg_a, bk_a = self_bwd(0, many, c, keep, recv, ctx_a, dctx_keep, dctx_in, lse_a, kmark, qmark)
-    bg_a, bk_a, got_x, keep, ff_mine = tie(bg_a, bk_a, got_x, keep, ff_mine)
+    bg1, bk1 = self_bwd(0, 1, 0, c, keep, recv, ctx_a, dctx_keep, dctx_in, lse_a, kmark, qmark)
+    bg1, bk1, keep = tie(bg1, bk1, keep)
+    bi1 = sibling(bg1)
+    bg2, bk2 = self_bwd(1, 1, 1, c, keep, recv, ctx_a, dctx_keep, dctx_in, lse_a, kmark, qmark)
+    bg2, bk2, got_x, so_x, keep, bi1, fr_swapped = tie(bg2, bk2, got_x, so_x, keep, bi1, fr_swapped)
+    bi2 = sibling(bg2)
+    m_ygive, m_ykeep = split_y(s, (xkeep, so_xkeep), (got_x, so_x))
+    m_ygive, keep, ff_mine = tie(m_ygive, keep, ff_mine)
+    m_y = across(m_ygive, "y")
     ff_got = lax.all_gather(ff_mine, REP2, axis=0, tiled=False)
-    bi_a = sibling(bg_a)
-    m_ygive, m_ykeep = split_y(s, xkeep, got_x)
-    m_ygive, keep = tie(m_ygive, keep)
-    m_y = across(m_ygive, "y")
-    bg_b, bk_b = self_bwd(many, 1, c, keep, recv, ctx_b, dctx_keep, dctx_in, lse_b, kmark, qmark)
-    bg_b, bk_b, m_y, fr_swapped = tie(bg_b, bk_b, m_y, fr_swapped)
-    bi_b = sibling(bg_b)
-    m_four = split_z(s, m_ykeep, m_y)
-    bk_b, *m_four = tie(bk_b, *m_four)
-    m_z = send_z(m_four)
-    q_xgive, q_xkeep = qkv_grad(s, a1, a1_sib, (bk_a, bk_b), (bg_a, bg_b))
-    q_xgive, q_xkeep, dh1 = tie(q_xgive, q_xkeep, dh1)
+    bg3, bk3 = self_bwd(2, 1, 0, c, keep, recv, ctx_b, dctx_keep, dctx_in, lse_b, kmark, qmark)
+    bg3, bk3, m_y, bi2 = tie(bg3, bk3, m_y, bi2)
+    bi3 = sibling(bg3)
+    q_xgive = qkv_grad(s, a1, a1_sib, (bk1, bk2, bk3), (bg1, bg2, bg3), False)
+    q_xgive, m_y = tie(q_xgive, m_y)
     q_x = across(q_xgive, "x")
-    grad_hidden, vec_last = last_rows(s, (bk_a, bk_b), (bi_a, bi_b), x_own, x_in, dh1, w_qkv, table)
+    m_z = split_z(s, m_ykeep, m_y)
+    bk3, dh1, *m_z = tie(bk3, dh1, *m_z)
+    m_z = send_z(m_z)
+    q_xkeep = qkv_grad(s, a1, a1_sib, (bk1, bk2, bk3), (bg1, bg2, bg3), True)
+    grad_hidden, vec_last = last_rows(s, (bk1, bk2, bk3), (bi1, bi2, bi3), x_own, x_in, dh1, w_qkv, table)
+    vec_last, *m_z = tie(vec_last, *m_z)
+    m_all = gather_z(sum_four(s, m_z))
     v_give, v_mine = pack_vectors(s, vec_last, vec_cross, vec_mid, vec_kv)
     v_got = across(v_give, "x")
-    v_mine, *m_z = tie(v_mine, *m_z)
-    m_all = gather_z(sum_four(s, m_z))
-    q_x, *m_all = tie(q_x, *m_all)
-    q_ygive, q_ykeep = split_y(s, q_xkeep, q_x)
-    q_ygive, grad_hidden, *m_all = tie(q_ygive, grad_hidden, *m_all)
+    v_mine, q_x = tie(v_mine, q_x)
+    q_ygive, q_ykeep = split_y(s, (q_xkeep,), (q_x,))
+    q_ygive, grad_hidden = tie(q_ygive, grad_hidden)
     q_y = across(q_ygive, "y")
     hid_in = swap(grad_hidden)
-    m_own = join_z(s, m_all)
-    m_own, q_y = tie(m_own, q_y)
+    q_four = split_z(s, q_ykeep, q_y)
+    *q_four, m_first = tie(*q_four, m_all[0])
+    q_z = send_z(q_four)
+    m_own = join_z(s, (m_first, *m_all[1:]))
     m_far = across(m_own, "y")
-    q_four = split_z(s, q_ykeep, q_y)
-    q_z = send_z(q_four)
-    q_own = join_z(s, gather_z(sum_four(s, q_z, (v_mine, v_got))))
+    fc1_grad, fc2_grad = spread_ff(s, ff_got.reshape(reps, 2, per, width))
+    m_own_sib = sibling(m_own)
+    output = jnp.where(stay, out, out_in)
+    fc1_grad, fc2_grad, output, *q_z = tie(fc1_grad, fc2_grad, output, *q_z)
+    q_piece = sum_four(s, q_z, (v_mine, v_got))
+    q_piece, m_far = tie(q_piece, m_far)
+    q_all = gather_z(q_piece)
+    spots = ((0, 0, 0), (1, 0, 0), (3, 0, 0), (3, hw, 0), (2, 0, 0))
+    crossout_grad, crossq_grad, selfout_grad, kv_grad = spread_out(
+        s, (((m_own, m_far, m_own_sib, sibling(m_far)), spots),), ((hw, width),) * 3 + ((width, width),)
+    )
+    grad_frames = jnp.where(stay, fr_own, fr_swapped)
+    grad_hidden = jnp.where(stay, grad_hidden, hid_in)
+    crossout_grad, grad_frames, grad_hidden, *q_all = tie(crossout_grad, grad_frames, grad_hidden, *q_all)
+    q_own = join_z(s, q_all)
     q_far = across(q_own, "y")
-
-    def quarters(own, far):
-        return own, far, sibling(own), sibling(far)
-
-    spots = ((0, 0, 0), (1, 0, 0), (2, 0, 0), (3, 0, 0), (3, hw, 0))
-    crossout_grad, crossq_grad, selfout_grad, kv_grad = spread_out(s, ((quarters(m_own, m_far), spots),), ((hw, width),) * 3 + ((width, width),))
+    q_own_sib = sibling(q_own)
     first = tuple((0, 0, j * width) for j in range(3))
-    qkv_grad_out, mine = spread_out(s, ((quarters(q_own, q_far), first),), ((hw, 3 * width), (24, hw)), True)
-    fc1_grad, fc2_grad = spread_ff(s, ff_got.reshape(reps, 2, per, width))
-
-    output = jnp.where(stay, out, out_in)
-    grad_hidden = jnp.where(stay, grad_hidden, hid_in)
-    grad_frames = jnp.where(stay, fr_own, fr_swapped)
+    qkv_grad_out, mine = spread_out(s, (((q_own, q_far, q_own_sib, sibling(q_far)), first),), ((hw, 3 * width), (24, hw)), True)
+
     return (
         output[None], grad_hidden[None], grad_frames[None], mine[:4], mine[4:8],
         qkv_grad_out, selfout_grad, crossq_grad, kv_grad, crossout_grad, fc1_grad, fc2_grad, mine[8:15], mine[15:19].reshape(-1),
@@ -1288,7 +1345,7 @@
     g_selfout = t_mm(c1, d1).astype(bf16)
     dctx = mm_t(d1, selfout_w).astype(bf16)
     dctx = to_heads(dctx)[0]
-    late, early = self_bwd(0, lanes // 128, first, heads[:, :mid], heads[:, mid:], ctx, dctx[:mid], dctx[mid:], self_lse, kmark, qmark)
+    late, early = self_bwd(0, lanes // 128, 0, first, heads[:, :mid], heads[:, mid:], ctx, dctx[:mid], dctx[mid:], self_lse, kmark, qmark)
     dqkv = to_tokens(jnp.concatenate([early, late], axis=1))
     da1 = mm_t(dqkv, qkv_w)
     g_qkv = t_mm(a1, dqkv).astype(bf16)

time: 618 us -> 565 us (0.914)
  waiting for transfers between devices: 127 us -> 62 us
  other arithmetic: 12.5 us -> 22.7 us
    ppermute x34 -> x33, waiting for transfers between devices: 81.9 us -> 27 us  [across(): return lax.ppermute(x, axis, FLIP)]
    ppermute x12, waiting for transfers between devices: 31.8 us -> 20.2 us  [across_z(): return lax.ppermute(x, 'z', [(j, j ^ d) for j in range(4)])]
    select_n x0 -> x3, other arithmetic: none -> 8.27 us  [the longest x1 2.76 us: body_pair(): output = jnp.where(stay, out, out_in)]
    broadcast_in_dim x3 -> x0, other arithmetic: 7.88 us -> none  [the longest x1 2.77 us: body_pair(): grad_hidden[None]]
    another operation x4 -> x7, other arithmetic: 0.02 us -> 7.4 us
    unnamed x92 -> x114, local copies, waits for them, and re-layouts: 13.6 us -> 18.2 us
    pallas_call x32 -> x35, Pallas kernels: 364 us -> 366 us  [call(): pl.pallas_call(kernel, grid_spec=spec, out_shape=out_shape, cost_estimate...]
    ppermute x34 -> x33, starting transfers between devices: 21.1 us -> 21 us  [across(): return lax.ppermute(x, axis, FLIP)]
  transfers between devices with their start and end apart: 56 -> 55, of which waited for: 17 -> 14; matrix products, arithmetic and copies ran while one was open for 4% -> 6% of each run, Pallas kernels for 46% -> 52%
where the time goes in v3:
time: 565 us; the launch traced here: 558 us
  Pallas kernels  366 us (65%)
  waiting for transfers between devices  62 us (11%)
  starting transfers between devices  59.9 us (11%)
  local copies, waits for them, and re-layouts  32.9 us (6%)
  other arithmetic  22.7 us (4%)
  between operations  14.6 us (3%)
    pallas_call x35, Pallas kernels, call(): pl.pallas_call(kernel, grid_spec=spec, out_shape=out_shape, cost_estimate...  366 us
    ppermute x33, waiting for transfers between devices, across(): return lax.ppermute(x, axis, FLIP)  27 us
    ppermute x7, starting transfers between devices, swap(): return lax.ppermute(x, ('core', 'x'), SWAP)  23.8 us
    ppermute x33, starting transfers between devices, across(): return lax.ppermute(x, axis, FLIP)  21 us
    ppermute x12, waiting for transfers between devices, across_z(): return lax.ppermute(x, 'z', [(j, j ^ d) for j in range(4)])  20.2 us
    unnamed x114, local copies, waits for them, and re-layouts  18.2 us
    ppermute x12, starting transfers between devices, across_z(): return lax.ppermute(x, 'z', [(j, j ^ d) for j in range(4)])  15 us
    ppermute x7, waiting for transfers between devices, swap(): return lax.ppermute(x, ('core', 'x'), SWAP)  14.8 us
  transfers between devices with their start and end apart: 55, of which 14 were waited for; matrix products, arithmetic and copies ran while one was open for 6% of the time, Pallas kernels for 52%

profile of v3, /device:TPU:1, one launch (start us, length us, event | category | flops | bytes accessed | tf_op | source)
XLA Modules:
  0.0 558.1 jit_solution(10644472484922982315)
XLA Ops:
  7.3 4.6 collective-permute-start.1
  22.7 2.8 convert.51
  41.1 14.8 %collective-permute-done.xi.refs_5_.refs_7_ = bf16[1024,768]{1,0:T(8,128)(2,1)S(1)} collective-permute-done((bf16[1024,768]{1,0:T(8,128)(2,1)S(1)}, bf16[1024,768]{1,0:T(8,128)(2,1)S(1)}, u32[]{:S(2)}, u32[]{:S(2)}) %collective-permute-start) | collective-permute-done | bytes 1572896 | tf_op jit(solution)/shard_map/ppermute | solution.py:1010
  57.0 10.2 %shard_map.254 = (bf16[768,2304]{1,0:T(8,128)(2,1)}, bf16[1024,768]{1,0:T(8,128)(2,1)}, bf16[3,1024,384]{2,1,0:T(8,128)(2,1)}, bf16[3,1024,384]{2,1,0:T(8,128)(2,1)}) custom-call(s32[9]{0:T(128)} %stack.72.s_ref, bf16[1024,768]{1,0:T(8,128)(2,1)} %bitcast.42, bf16[1024,768]{1,0:T(8,128)(2,1)} %copy-done.2, f32[384,2304]{1,0:T(8,128)} %own.2, ...), custom_call_target="tpu_custom_call" | custom-call | flops 362387872 | bytes 1048576 | tf_op jit(solution)/shard_map/pallas_call | solution.py:41
  69.4 3.6 collective-permute-start.11
  75.0 15.6 %shard_map.255 = (bf16[2048,256]{1,0:T(8,128)(2,1)}, bf16[1024,256]{1,0:T(8,128)(2,1)}, f32[2,8,2048]{2,1,0:T(8,128)}) custom-call(s32[1]{0:T(128)} %bitcast.s_ref, bf16[3,1024,384]{2,1,0:T(8,128)(2,1)} %get-tuple-element.298.a_ref, bf16[3,1024,384]{2,1,0:T(8,128)(2,1)} %copy-done, bf16[2048,128]{1,0:T(8,128)(2,1)} %get-tuple-element.199.km_ref, ...), custom_call_target="tpu_custom_call" | custom-call | flops 858993472 | bytes 1048576 | tf_op jit(solution)/shard_map/pallas_call | solution.py:41
  92.5 8.9 %shard_map.256 = (bf16[2048,128]{1,0:T(8,128)(2,1)}, bf16[1024,128]{1,0:T(8,128)(2,1)}, f32[1,8,2048]{2,1,0:T(8,128)}) custom-call(s32[1]{0:T(128)} %bitcast.s_ref, bf16[3,1024,384]{2,1,0:T(8,128)(2,1)} %get-tuple-element.298.a_ref, bf16[3,1024,384]{2,1,0:T(8,128)(2,1)} %copy-done, bf16[2048,128]{1,0:T(8,128)(2,1)} %get-tuple-element.199.km_ref, ...), custom_call_target="tpu_custom_call" | custom-call | flops 429496736 | bytes 1048576 | tf_op jit(solution)/shard_map/pallas_call | solution.py:41
  103.2 2.7 collective-permute-start.15
  107.0 10.5 %shard_map.257 = (bf16[768,768]{1,0:T(8,128)(2,1)}, bf16[768,768]{1,0:T(8,128)(2,1)}, f32[1024,768]{1,0:T(8,128)}, bf16[1024,768]{1,0:T(8,128)(2,1)}, bf16[1024,768]{1,0:T(8,128)(2,1)}) custom-call(s32[9]{0:T(128)} %stack.72.s_ref, bf16[2048,256]{1,0:T(8,128)(2,1)} %get-tuple-element.201.refs_0_.o_ref, bf16[2048,128]{1,0:T(8,128)(2,1)} %get-tuple-element.206.refs_1_.o_ref, ...), custom_call_target="tpu_custom_call" | custom-call | flops 241591904 | bytes 1048576 | tf_op jit(solution)/shard_map/pallas_call | solution.py:41
  120.1 2.7 collective-permute-done.14.sib
  124.6 10.1 %shard_map.258 = (bf16[1536,768]{1,0:T(8,128)(2,1)}, bf16[1536,768]{1,0:T(8,128)(2,1)}, bf16[1536,768]{1,0:T(8,128)(2,1)}) custom-call(s32[9]{0:T(128)} %stack.72.s_ref, bf16[1500,384]{1,0:T(8,128)(2,1)} %copy-done.3, bf16[1500,384]{1,0:T(8,128)(2,1)} %copy-done.10, f32[768,768]{1,0:T(8,128)} %own.3, bf16[384,768]{1,0:T(8,128)(2,1)} %collective-permute-done.12.mine, ...), custom_call_target="tpu_custom_call" | custom-call | flops 353894400 | bytes 1048576 | tf_op jit(solution)/shard_map/pallas_call | solution.py:41
  134.7 14.8 %shard_map.260 = (bf16[1024,384]{1,0:T(8,128)(2,1)}, f32[3,8,1024]{2,1,0:T(8,128)}) custom-call(s32[1]{0:T(128)} %bitcast.23.s_ref, bf16[1024,768]{1,0:T(8,128)(2,1)} %get-tuple-element.213.q_ref, bf16[1536,768]{1,0:T(8,128)(2,1)} %get-tuple-element.216.k_ref, bf16[1536,768]{1,0:T(8,128)(2,1)} %get-tuple-element.217.v_ref), custom_call_target="tpu_custom_call" | custom-call | flops 483183808 | bytes 1048576 | tf_op jit(solution)/shard_map/pallas_call | solution.py:41
  149.6 14.8 %shard_map.259 = (bf16[1024,384]{1,0:T(8,128)(2,1)}, f32[3,8,1024]{2,1,0:T(8,128)}) custom-call(s32[1]{0:T(128)} %bitcast.8.s_ref, bf16[1024,768]{1,0:T(8,128)(2,1)} %get-tuple-element.213.q_ref, bf16[1536,768]{1,0:T(8,128)(2,1)} %get-tuple-element.216.k_ref, bf16[1536,768]{1,0:T(8,128)(2,1)} %get-tuple-element.217.v_ref), custom_call_target="tpu_custom_call" | custom-call | flops 483183808 | bytes 1048576 | tf_op jit(solution)/shard_map/pallas_call | solution.py:41
  164.4 51.7 %shard_map.261 = (bf16[768,768]{1,0:T(8,128)(2,1)}, bf16[1024,768]{1,0:T(8,128)(2,1)}, bf16[1024,768]{1,0:T(8,128)(2,1)}, bf16[1024,3072]{1,0:T(8,128)(2,1)}, bf...) custom-call(s32[9]{0:T(128)} %stack.72.s_ref, ...), custom_call_target="tpu_custom_call" | custom-call | flops 2174327296 | bytes 1048576 | tf_op jit(solution)/shard_map/pallas_call | solution.py:41
  216.1 17.4 %shard_map.262 = bf16[2,16,2,96,768]{4,3,2,1,0:T(8,128)(2,1)} custom-call(s32[9]{0:T(128)} %stack.72.s_ref, bf16[1024,768]{1,0:T(8,128)(2,1)} %get-tuple-element.228.a_ref, bf16[1024,3072]{1,0:T(8,128)(2,1)} %get-tuple-element.229.du_ref, bf16[1024,3072]{1,0:T(8,128)(2,1)} %get-tuple-element.230.g0.g1, bf16[1024,3072]{1,0:T(8,128)(2,1)} %get-tuple-element.230.g0.g1, ...), custom_call_target="tpu_custom_call" | custom-call | flops 966367616 | bytes 1048576 | tf_op jit(solution)/shard_map/pallas_call | solution.py:41
  233.6 26.1 %shard_map.263 = (bf16[1024,384]{1,0:T(8,128)(2,1)}, bf16[2,1536,384]{2,1,0:T(8,128)(2,1)}) custom-call(s32[1]{0:T(128)} %bitcast.23.s_ref, bf16[1024,768]{1,0:T(8,128)(2,1)} %get-tuple-element.213.q_ref, bf16[1536,768]{1,0:T(8,128)(2,1)} %get-tuple-element.216.k_ref, bf16[1536,768]{1,0:T(8,128)(2,1)} %get-tuple-element.217.v_ref, ...), custom_call_target="tpu_custom_call" | custom-call | flops 2415919104 | bytes 1048576 | tf_op jit(solution)/shard_map/pallas_call | solution.py:41
  260.2 3.4 collective-permute-start.16
  263.6 5.8 %shard_map.264 = bf16[2,768,384]{2,1,0:T(8,128)(2,1)} custom-call(s32[9]{0:T(128)} %stack.72.s_ref, bf16[1024,384]{1,0:T(8,128)(2,1)} %get-tuple-element.218.ck_ref.k_ref.o_ref.ck, bf16[1024,384]{1,0:T(8,128)(2,1)} %get-tuple-element.219.cg_ref.o_ref.g_ref.cg, bf16[1024,768]{1,0:T(8,128)(2,1)} %get-tuple-element.225.d_ref.d2_ref, ...), custom_call_target="tpu_custom_call" | custom-call | flops 120795952 | bytes 1048576 | tf_op jit(solution)/shard_map/pallas_call | solution.py:41
  269.4 26.2 %shard_map.265 = (bf16[1024,384]{1,0:T(8,128)(2,1)}, bf16[2,1536,384]{2,1,0:T(8,128)(2,1)}) custom-call(s32[1]{0:T(128)} %bitcast.8.s_ref, bf16[1024,768]{1,0:T(8,128)(2,1)} %get-tuple-element.213.q_ref, bf16[1536,768]{1,0:T(8,128)(2,1)} %get-tuple-element.216.k_ref, bf16[1536,768]{1,0:T(8,128)(2,1)} %get-tuple-element.217.v_ref, ...), custom_call_target="tpu_custom_call" | custom-call | flops 2415919104 | bytes 1048576 | tf_op jit(solution)/shard_map/pallas_call | solution.py:41
  297.0 10.6 %shard_map.266 = (bf16[1500,384]{1,0:T(8,128)(2,1)}, bf16[1500,384]{1,0:T(8,128)(2,1)}, bf16[768,384]{1,0:T(8,128)(2,1)}, bf16[768,384]{1,0:T(8,128)(2,1)}, f32[8,384]{1,0:T(8,128)}) custom-call(s32[9]{0:T(128)} %stack.72.s_ref, bf16[2,1536,384]{2,1,0:T(8,128)(2,1)} %get-tuple-element.242.ka, bf16[2,1536,384]{2,1,0:T(8,128)(2,1)} %copy-done.18, ...), custom_call_target="tpu_custom_call" | custom-call | flops 707788800 | bytes 1048576 | tf_op jit(solution)/shard_map/pallas_call | solution.py:41
  308.1 7.1 %shard_map.267 = (bf16[4,384,384]{2,1,0:T(8,128)(2,1)}, bf16[4,384,384]{2,1,0:T(8,128)(2,1)}) custom-call(s32[9]{0:T(128)} %stack.72.s_ref, bf16[1024,384]{1,0:T(8,128)(2,1)} %get-tuple-element.218.ck_ref.k_ref.o_ref.ck, bf16[1024,384]{1,0:T(8,128)(2,1)} %get-tuple-element.219.cg_ref.o_ref.g_ref.cg, bf16[1024,768]{1,0:T(8,128)(2,1)} %get-tuple-element.225.d_ref.d2_ref, ...), custom_call_target="tpu_custom_call" | custom-call | flops 120795952 | bytes 1048576 | tf_op jit(solution)/shard_map/pallas_call | solution.py:41
  315.2 10.9 %shard_map.268 = (f32[1024,768]{1,0:T(8,128)}, bf16[1024,768]{1,0:T(8,128)(2,1)}, bf16[1024,384]{1,0:T(8,128)(2,1)}, bf16[1024,384]{1,0:T(8,128)(2,1)}, f32[8,768]{1,0:T(8,128)}) custom-call(s32[9]{0:T(128)} %stack.72.s_ref, bf16[1024,384]{1,0:T(8,128)(2,1)} %get-tuple-element.258.q_ref.dk_ref, bf16[1024,384]{1,0:T(8,128)(2,1)} %get-tuple-element.238.q_ref.dg_ref, ...), custom_call_target="tpu_custom_call" | custom-call | flops 241591904 | bytes 1048576 | tf_op jit(solution)/shard_map/pallas_call | solution.py:41
  326.8 4.2 shard_map.269
  334.2 3.3 collective-permute-start.26
  337.5 4.3 shard_map.270
  342.8 16.0 %shard_map.271 = (bf16[3,1024,128]{2,1,0:T(8,128)(2,1)}, bf16[3,1024,128]{2,1,0:T(8,128)(2,1)}) custom-call(s32[1]{0:T(128)} %bitcast.s_ref, bf16[3,1024,384]{2,1,0:T(8,128)(2,1)} %get-tuple-element.298.a_ref, bf16[3,1024,384]{2,1,0:T(8,128)(2,1)} %copy-done, bf16[2048,256]{1,0:T(8,128)(2,1)} %get-tuple-element.201.refs_0_.o_ref, ...), custom_call_target="tpu_custom_call" | custom-call | flops 858993472 | bytes 1048576 | tf_op jit(solution)/shard_map/pallas_call | solution.py:41
  359.5 16.2 %shard_map.272 = (bf16[3,1024,128]{2,1,0:T(8,128)(2,1)}, bf16[3,1024,128]{2,1,0:T(8,128)(2,1)}) custom-call(s32[1]{0:T(128)} %bitcast.s_ref, bf16[3,1024,384]{2,1,0:T(8,128)(2,1)} %get-tuple-element.298.a_ref, bf16[3,1024,384]{2,1,0:T(8,128)(2,1)} %copy-done, bf16[2048,256]{1,0:T(8,128)(2,1)} %get-tuple-element.201.refs_0_.o_ref, ...), custom_call_target="tpu_custom_call" | custom-call | flops 858993472 | bytes 1048576 | tf_op jit(solution)/shard_map/pallas_call | solution.py:41
  378.8 3.9 shard_map.273
  386.1 16.0 %shard_map.275 = (bf16[3,1024,128]{2,1,0:T(8,128)(2,1)}, bf16[3,1024,128]{2,1,0:T(8,128)(2,1)}) custom-call(s32[1]{0:T(128)} %bitcast.s_ref, bf16[3,1024,384]{2,1,0:T(8,128)(2,1)} %get-tuple-element.298.a_ref, bf16[3,1024,384]{2,1,0:T(8,128)(2,1)} %copy-done, bf16[2048,128]{1,0:T(8,128)(2,1)} %get-tuple-element.206.refs_1_.o_ref, ...), custom_call_target="tpu_custom_call" | custom-call | flops 858993472 | bytes 1048576 | tf_op jit(solution)/shard_map/pallas_call | solution.py:41
  402.1 4.3 collective-permute-done.27.g_ref
  407.3 7.0 %shard_map.276 = bf16[3,384,384]{2,1,0:T(8,128)(2,1)} custom-call(s32[9]{0:T(128)} %stack.72.s_ref, bf16[1024,768]{1,0:T(8,128)(2,1)} %get-tuple-element.246.ao, bf16[1024,768]{1,0:T(8,128)(2,1)} %collective-permute-done.18.ai, bf16[3,1024,128]{2,1,0:T(8,128)(2,1)} %get-tuple-element.296.refs_0_, bf16[3,1024,128]{2,1,0:T(8,128)(2,1)} %get-tuple-element.297.refs_1_, ...), custom_call_target="tpu_custom_call" | custom-call | flops 181193936 | bytes 1048576 | tf_op jit(solution)/shard_map/pallas_call | solution.py:41
  415.6 3.0 shard_map.277
  422.1 7.0 %shard_map.278.refs_0_ = bf16[3,384,384]{2,1,0:T(8,128)(2,1)} custom-call(s32[9]{0:T(128)} %stack.72.s_ref, bf16[1024,768]{1,0:T(8,128)(2,1)} %get-tuple-element.246.ao, bf16[1024,768]{1,0:T(8,128)(2,1)} %collective-permute-done.18.ai, bf16[3,1024,128]{2,1,0:T(8,128)(2,1)} %get-tuple-element.296.refs_0_, bf16[3,1024,128]{2,1,0:T(8,128)(2,1)} %get-tuple-element.297.refs_1_, ...), custom_call_target="tpu_custom_call" | custom-call | flops 181193936 | bytes 1048576 | tf_op jit(solution)/shard_map/pallas_call | solution.py:41
  429.2 12.3 %shard_map.279 = (bf16[1024,768]{1,0:T(8,128)(2,1)}, f32[8,768]{1,0:T(8,128)}) custom-call(s32[9]{0:T(128)} %stack.72.s_ref, bf16[3,1024,128]{2,1,0:T(8,128)(2,1)} %get-tuple-element.296.refs_0_, bf16[3,1024,128]{2,1,0:T(8,128)(2,1)} %get-tuple-element.297.refs_1_, bf16[3,1024,128]{2,1,0:T(8,128)(2,1)} %get-tuple-element.314.refs_2_, ...), custom_call_target="tpu_custom_call" | custom-call | flops 362387872 | bytes 1048576 | tf_op jit(solution)/shard_map/pallas_call | solution.py:41
  441.5 5.1 collective-permute-done.32.p3
  449.8 3.1 shard_map.281
  454.2 3.8 collective-permute-start.45
  462.3 5.1 collective-permute-start.39
  470.8 9.9 %collective-permute-done.39.p2 = bf16[5,48,384]{2,1,0:T(8,128)(2,1)S(1)} collective-permute-done((bf16[5,48,384]{2,1,0:T(8,128)(2,1)}, bf16[5,48,384]{2,1,0:T(8,128)(2,1)S(1)}, u32[]{:S(2)}, u32[]{:S(2)}) %collective-permute-start.39) | collective-permute-done | bytes 184352 | tf_op jit(solution)/shard_map/ppermute | solution.py:989
  482.1 2.8 shard_map.284.refs_0_
  486.3 4.4 collective-permute-done.35.p1
  490.7 2.8 broadcast_select_fusion.1
  493.4 7.2 %shard_map.274 = (f32[384,3072]{1,0:T(8,128)}, f32[1536,768]{1,0:T(8,128)}) custom-call(s32[9]{0:T(128)} %stack.72.s_ref, bf16[16,2,96,768]{3,2,1,0:T(8,128)(2,1)} %bitcast.52), custom_call_target="tpu_custom_call" | custom-call | tf_op jit(solution)/shard_map/pallas_call | solution.py:41
  505.9 2.8 broadcast_select_fusion.2
  512.2 2.8 broadcast_select_fusion
  515.8 5.3 shard_map.286
  527.2 12.9 %collective-permute-done.49.refs_1_ = bf16[4,192,384]{2,1,0:T(8,128)(2,1)S(1)} collective-permute-done((bf16[4,192,384]{2,1,0:T(8,128)(2,1)}, bf16[4,192,384]{2,1,0:T(8,128)(2,1)S(1)}, u32[]{:S(2)}, u32[]{:S(2)}) %collective-permute-start.49) | collective-permute-done | bytes 589856 | tf_op jit(solution)/shard_map/ppermute | solution.py:993
  543.8 4.3 shard_map.288
  (257 shorter events, 98.4 us)
Async XLA Ops:
  7.2 157.2 %all-gather.5.cloned.1.call-start = ((), (), s32[]{:S(2)}) async-start(), calls=%async_computation.2 | async-start | bytes 5013504 | tf_op jit(solution)/shard_map/all_gather | solution.py:1045
  7.3 30.2 %collective-permute-start.1 = (s32[1,2048]{1,0:T(1,128)}, s32[1,2048]{1,0:T(1,128)S(1)}, u32[]{:S(2)}, u32[]{:S(2)}) collective-permute-start(s32[1,2048]{1,0:T(1,128)} %param.17), channel_id=1, source_target_pairs={{1,2},{2,1},{5,6},{6,5},{9,10},{10,9},{13,14},{14,13},{17,18},{18,... | collective-permute-start | bytes 24584 | tf_op jit(solution)/shard_map/ppermute | solution.py:1010
  14.9 26.2 %collective-permute-start.4 = (bf16[20,384]{1,0:T(8,128)(2,1)S(1)}, bf16[20,384]{1,0:T(8,128)(2,1)S(1)}, u32[]{:S(2)}, u32[]{:S(2)}) collective-permute-start(bf16[20,384]{1,0:T(8,128)(2,1)S(1)} %concatenate.35), channel_id=1, source_target_pairs={{0,1},{1,0},{2,3},{3,2},{4,5},{5,4},{6,7},{7,6},{8,9},{9,8},{10,11... | collective-permute-start | bytes 46088 | tf_op jit(solution)/shard_map/ppermute | solution.py:993
  17.4 21.2 %collective-permute-start.2 = (bf16[192,2304]{1,0:T(8,128)(2,1)}, bf16[192,2304]{1,0:T(8,128)(2,1)}, u32[]{:S(2)}, u32[]{:S(2)}) collective-permute-start(bf16[192,2304]{1,0:T(8,128)(2,1)} %dynamic-slice_convert_fusion), channel_id=1, source_target_pairs={{0,1},{1,0},{2,3},{3,2},{4,5},{5,4},{6,7},{7,6},{8,9},{9,8},{10,11... | collective-permute-start | bytes 2654216 | tf_op jit(solution)/shard_map/ppermute | solution.py:993
  18.9 37.0 %collective-permute-start = (bf16[1024,768]{1,0:T(8,128)(2,1)S(1)}, bf16[1024,768]{1,0:T(8,128)(2,1)S(1)}, u32[]{:S(2)}, u32[]{:S(2)}) collective-permute-start(bf16[1024,768]{1,0:T(8,128)(2,1)S(1)} %bitcast.45), channel_id=1, source_target_pairs={{1,2},{2,1},{5,6},{6,5},{9,10},{10,9},{13,14},{14,13},{17,18},{18,... | collective-permute-start | bytes 4718600 | tf_op jit(solution)/shard_map/ppermute | solution.py:1010
  38.6 18.0 %collective-permute-start.3 = (bf16[192,2304]{1,0:T(8,128)(2,1)}, bf16[192,2304]{1,0:T(8,128)(2,1)}, u32[]{:S(2)}, u32[]{:S(2)}) collective-permute-start(bf16[192,2304]{1,0:T(8,128)(2,1)} %collective-permute-done.2.mine), channel_id=1, source_target_pairs={{0,2},{2,0},{1,3},{3,1},{4,6},{6,4},{5,7},{7,5},{8,10},{10,8},{9,1... | collective-permute-start | bytes 2654216 | tf_op jit(solution)/shard_map/ppermute | solution.py:993
  55.9 11.4 %collective-permute-start.5 = (bf16[2,96,768]{2,1,0:T(8,128)(2,1)}, bf16[2,96,768]{2,1,0:T(8,128)(2,1)S(1)}, u32[]{:S(2)}, u32[]{:S(2)}) collective-permute-start(bf16[2,96,768]{2,1,0:T(8,128)(2,1)} %pad_maximum_fusion.2), channel_id=1, source_target_pairs={{0,1},{1,0},{2,3},{3,2},{4,5},{5,4},{6,7},{7,6},{8,9},{9,8},{10,11... | collective-permute-start | bytes 884744 | tf_op jit(solution)/shard_map/ppermute | solution.py:993
  68.0 314.7 %reduce-scatter.2.cloned.1.call-start = ((), (), s32[]{:S(2)}) async-start(), calls=%async_computation.1 | async-start | bytes 9732096 | tf_op jit(solution)/shard_map/reduce_scatter | solution.py:1074
  69.2 21.5 %collective-permute-start.7 = (bf16[3,192,768]{2,1,0:T(8,128)(2,1)}, bf16[3,192,768]{2,1,0:T(8,128)(2,1)S(1)}, u32[]{:S(2)}, u32[]{:S(2)}) collective-permute-start(bf16[3,192,768]{2,1,0:T(8,128)(2,1)} %pad_maximum_fusion.1), channel_id=1, source_target_pairs={{0,1},{1,0},{2,3},{3,2},{4,5},{5,4},{6,7},{7,6},{8,9},{9,8},{10,11... | collective-permute-start | bytes 2654216 | tf_op jit(solution)/shard_map/ppermute | solution.py:993
  69.4 48.1 %collective-permute-start.11 = (bf16[1500,384]{1,0:T(8,128)(2,1)}, bf16[1500,384]{1,0:T(8,128)(2,1)}, u32[]{:S(2)}, u32[]{:S(2)}) collective-permute-start(bf16[1500,384]{1,0:T(8,128)(2,1)} %bitcast.56), channel_id=1, source_target_pairs={{1,2},{2,1},{5,6},{6,5},{9,10},{10,9},{13,14},{14,13},{17,18},{18,... | collective-permute-start | bytes 3456008 | tf_op jit(solution)/shard_map/ppermute | solution.py:1010
  90.7 15.2 %collective-permute-start.10 = (bf16[3,192,768]{2,1,0:T(8,128)(2,1)S(1)}, bf16[3,192,768]{2,1,0:T(8,128)(2,1)S(1)}, u32[]{:S(2)}, u32[]{:S(2)}) collective-permute-start(bf16[3,192,768]{2,1,0:T(8,128)(2,1)S(1)} %collective-permute-done.7.refs_7_.refs_10_.o2), channel_id=1, source_target_pairs={{0,2},{2,0},{1,3},{3,1},{4,6},{6,4},{5,7},{7,5},{8,10},{10,8},{9,1... | collective-permute-start | bytes 2654216 | tf_op jit(solution)/shard_map/ppermute | solution.py:993
  91.4 26.0 %collective-permute-start.12 = (bf16[384,768]{1,0:T(8,128)(2,1)}, bf16[384,768]{1,0:T(8,128)(2,1)}, u32[]{:S(2)}, u32[]{:S(2)}) collective-permute-start(bf16[384,768]{1,0:T(8,128)(2,1)} %dynamic-slice_convert_fusion.1), channel_id=1, source_target_pairs={{0,1},{1,0},{2,3},{3,2},{4,5},{5,4},{6,7},{7,6},{8,9},{9,8},{10,11... | collective-permute-start | bytes 1769480 | tf_op jit(solution)/shard_map/ppermute | solution.py:993
  92.3 13.6 %collective-permute-start.8 = (bf16[1024,256]{1,0:T(8,128)(2,1)}, bf16[1024,256]{1,0:T(8,128)(2,1)S(1)}, u32[]{:S(2)}, u32[]{:S(2)}) collective-permute-start(bf16[1024,256]{1,0:T(8,128)(2,1)} %get-tuple-element.207), channel_id=1, source_target_pairs={{0,2},{2,0},{1,3},{3,1},{4,6},{6,4},{5,7},{7,5},{8,10},{10,8},{9,1... | collective-permute-start | bytes 1572872 | tf_op jit(solution)/shard_map/ppermute | solution.py:993
  103.2 61.2 %collective-permute-start.15 = (bf16[1024,768]{1,0:T(8,128)(2,1)}, bf16[1024,768]{1,0:T(8,128)(2,1)}, u32[]{:S(2)}, u32[]{:S(2)}) collective-permute-start(bf16[1024,768]{1,0:T(8,128)(2,1)} %bitcast.24.co), channel_id=1, source_target_pairs={{1,2},{2,1},{5,6},{6,5},{9,10},{10,9},{13,14},{14,13},{17,18},{18,... | collective-permute-start | bytes 4718600 | tf_op jit(solution)/shard_map/ppermute | solution.py:1010
  233.5 259.9 %all-gather.7.cloned.1.call-start = ((), (), s32[]{:S(2)}) async-start(), calls=%async_computation.3 | async-start | bytes 5013504 | tf_op jit(solution)/shard_map/all_gather | solution.py:1119
  259.7 35.9 %collective-permute-start.17 = (bf16[2,1536,384]{2,1,0:T(8,128)(2,1)}, bf16[2,1536,384]{2,1,0:T(8,128)(2,1)S(1)}, u32[]{:S(2)}, u32[]{:S(2)}) collective-permute-start(bf16[2,1536,384]{2,1,0:T(8,128)(2,1)} %get-tuple-element.245), channel_id=1, source_target_pairs={{0,2},{2,0},{1,3},{3,1},{4,6},{6,4},{5,7},{7,5},{8,10},{10,8},{9,1... | collective-permute-start | bytes 7077896 | tf_op jit(solution)/shard_map/ppermute | solution.py:993
  260.0 35.6 %collective-permute-start.18 = (bf16[1024,768]{1,0:T(8,128)(2,1)S(1)}, bf16[1024,768]{1,0:T(8,128)(2,1)}, u32[]{:S(2)}, u32[]{:S(2)}) collective-permute-start(bf16[1024,768]{1,0:T(8,128)(2,1)S(1)} %copy-done.8), channel_id=1, source_target_pairs={{0,2},{2,0},{1,3},{3,1},{4,6},{6,4},{5,7},{7,5},{8,10},{10,8},{9,1... | collective-permute-start | bytes 4718600 | tf_op jit(solution)/shard_map/ppermute | solution.py:993
  260.2 35.4 %collective-permute-start.16 = (bf16[1024,768]{1,0:T(8,128)(2,1)}, bf16[1024,768]{1,0:T(8,128)(2,1)}, u32[]{:S(2)}, u32[]{:S(2)}) collective-permute-start(bf16[1024,768]{1,0:T(8,128)(2,1)} %get-tuple-element.244), channel_id=1, source_target_pairs={{1,2},{2,1},{5,6},{6,5},{9,10},{10,9},{13,14},{14,13},{17,18},{18,... | collective-permute-start | bytes 4718600 | tf_op jit(solution)/shard_map/ppermute | solution.py:1010
  269.4 26.2 %collective-permute-start.19 = (bf16[2,768,384]{2,1,0:T(8,128)(2,1)}, bf16[2,768,384]{2,1,0:T(8,128)(2,1)}, u32[]{:S(2)}, u32[]{:S(2)}) collective-permute-start(bf16[2,768,384]{2,1,0:T(8,128)(2,1)} %shard_map.264), channel_id=1, source_target_pairs={{0,2},{2,0},{1,3},{3,1},{4,6},{6,4},{5,7},{7,5},{8,10},{10,8},{9,1... | collective-permute-start | bytes 3538952 | tf_op jit(solution)/shard_map/ppermute | solution.py:993
  307.6 23.4 %collective-permute-start.20 = (bf16[1500,384]{1,0:T(8,128)(2,1)}, bf16[1500,384]{1,0:T(8,128)(2,1)S(1)}, u32[]{:S(2)}, u32[]{:S(2)}) collective-permute-start(bf16[1500,384]{1,0:T(8,128)(2,1)} %get-tuple-element.265), channel_id=1, source_target_pairs={{0,2},{2,0},{1,3},{3,1},{4,6},{6,4},{5,7},{7,5},{8,10},{10,8},{9,1... | collective-permute-start | bytes 3456008 | tf_op jit(solution)/shard_map/ppermute | solution.py:993
  326.2 15.7 %collective-permute-start.22 = (bf16[1024,384]{1,0:T(8,128)(2,1)}, bf16[1024,384]{1,0:T(8,128)(2,1)S(1)}, u32[]{:S(2)}, u32[]{:S(2)}) collective-permute-start(bf16[1024,384]{1,0:T(8,128)(2,1)} %get-tuple-element.275), channel_id=1, source_target_pairs={{0,2},{2,0},{1,3},{3,1},{4,6},{6,4},{5,7},{7,5},{8,10},{10,8},{9,1... | collective-permute-start | bytes 2359304 | tf_op jit(solution)/shard_map/ppermute | solution.py:993
  326.3 49.4 %collective-permute-start.23 = (bf16[4,384,384]{2,1,0:T(8,128)(2,1)}, bf16[4,384,384]{2,1,0:T(8,128)(2,1)S(1)}, u32[]{:S(2)}, u32[]{:S(2)}) collective-permute-start(bf16[4,384,384]{2,1,0:T(8,128)(2,1)} %get-tuple-element.282), channel_id=1, source_target_pairs={{0,1},{1,0},{2,3},{3,2},{4,5},{5,4},{6,7},{7,6},{8,9},{9,8},{10,11... | collective-permute-start | bytes 3538952 | tf_op jit(solution)/shard_map/ppermute | solution.py:993
  334.2 43.6 %collective-permute-start.26 = (bf16[1500,384]{1,0:T(8,128)(2,1)S(1)}, bf16[1500,384]{1,0:T(8,128)(2,1)}, u32[]{:S(2)}, u32[]{:S(2)}) collective-permute-start(bf16[1500,384]{1,0:T(8,128)(2,1)S(1)} %add_convert_fusion), channel_id=1, source_target_pairs={{1,2},{2,1},{5,6},{6,5},{9,10},{10,9},{13,14},{14,13},{17,18},{18,... | collective-permute-start | bytes 3456008 | tf_op jit(solution)/shard_map/ppermute | solution.py:1010
  358.8 19.0 %collective-permute-start.25 = (bf16[3,1024,128]{2,1,0:T(8,128)(2,1)}, bf16[3,1024,128]{2,1,0:T(8,128)(2,1)S(1)}, u32[]{:S(2)}, u32[]{:S(2)}) collective-permute-start(bf16[3,1024,128]{2,1,0:T(8,128)(2,1)} %get-tuple-element.284.refs_3_), channel_id=1, source_target_pairs={{0,2},{2,0},{1,3},{3,1},{4,6},{6,4},{5,7},{7,5},{8,10},{10,8},{9,1... | collective-permute-start | bytes 2359304 | tf_op jit(solution)/shard_map/ppermute | solution.py:993
  358.8 19.0 %collective-permute-start.24 = (bf16[1,384,384]{2,1,0:T(8,128)(2,1)S(1)}, bf16[1,384,384]{2,1,0:T(8,128)(2,1)S(1)}, u32[]{:S(2)}, u32[]{:S(2)}) collective-permute-start(bf16[1,384,384]{2,1,0:T(8,128)(2,1)S(1)} %copy-done.53), channel_id=1, source_target_pairs={{0,1},{1,0},{2,3},{3,2},{4,5},{5,4},{6,7},{7,6},{8,9},{9,8},{10,11... | collective-permute-start | bytes 884744 | tf_op jit(solution)/shard_map/ppermute | solution.py:993
  382.7 19.4 %collective-permute-start.28 = (bf16[3,1024,128]{2,1,0:T(8,128)(2,1)S(1)}, bf16[3,1024,128]{2,1,0:T(8,128)(2,1)S(1)}, u32[]{:S(2)}, u32[]{:S(2)}) collective-permute-start(bf16[3,1024,128]{2,1,0:T(8,128)(2,1)S(1)} %copy-done.11), channel_id=1, source_target_pairs={{0,2},{2,0},{1,3},{3,1},{4,6},{6,4},{5,7},{7,5},{8,10},{10,8},{9,1... | collective-permute-start | bytes 2359304 | tf_op jit(solution)/shard_map/ppermute | solution.py:993
  384.9 21.5 %collective-permute-start.27 = (bf16[5,192,384]{2,1,0:T(8,128)(2,1)}, bf16[5,192,384]{2,1,0:T(8,128)(2,1)S(1)}, u32[]{:S(2)}, u32[]{:S(2)}) collective-permute-start(bf16[5,192,384]{2,1,0:T(8,128)(2,1)} %get-tuple-element.302), channel_id=1, source_target_pairs={{0,4},{4,0},{1,5},{5,1},{2,6},{6,2},{3,7},{7,3},{8,12},{12,8},{9,1... | collective-permute-start | bytes 2211848 | tf_op jit(solution)/shard_map/ppermute | solution.py:993
  414.3 34.5 %collective-permute-start.33 = (bf16[3,384,384]{2,1,0:T(8,128)(2,1)}, bf16[3,384,384]{2,1,0:T(8,128)(2,1)S(1)}, u32[]{:S(2)}, u32[]{:S(2)}) collective-permute-start(bf16[3,384,384]{2,1,0:T(8,128)(2,1)} %shard_map.276), channel_id=1, source_target_pairs={{0,1},{1,0},{2,3},{3,2},{4,5},{5,4},{6,7},{7,6},{8,9},{9,8},{10,11... | collective-permute-start | bytes 2654216 | tf_op jit(solution)/shard_map/ppermute | solution.py:993
  414.5 14.7 %collective-permute-start.29 = (bf16[3,1024,128]{2,1,0:T(8,128)(2,1)S(1)}, bf16[3,1024,128]{2,1,0:T(8,128)(2,1)}, u32[]{:S(2)}, u32[]{:S(2)}) collective-permute-start(bf16[3,1024,128]{2,1,0:T(8,128)(2,1)S(1)} %copy-done.12), channel_id=1, source_target_pairs={{0,2},{2,0},{1,3},{3,1},{4,6},{6,4},{5,7},{7,5},{8,10},{10,8},{9,1... | collective-permute-start | bytes 2359304 | tf_op jit(solution)/shard_map/ppermute | solution.py:993
  418.6 22.9 %collective-permute-start.30 = (bf16[5,48,384]{2,1,0:T(8,128)(2,1)}, bf16[5,48,384]{2,1,0:T(8,128)(2,1)S(1)}, u32[]{:S(2)}, u32[]{:S(2)}) collective-permute-start(bf16[5,48,384]{2,1,0:T(8,128)(2,1)} %get-tuple-element.321), channel_id=1, source_target_pairs={{0,8},{8,0},{16,24},{24,16},{1,9},{9,1},{17,25},{25,17},{2,10},{10... | collective-permute-start | bytes 552968 | tf_op jit(solution)/shard_map/ppermute | solution.py:989
  419.4 22.1 %collective-permute-start.31 = (bf16[5,48,384]{2,1,0:T(8,128)(2,1)}, bf16[5,48,384]{2,1,0:T(8,128)(2,1)S(1)}, u32[]{:S(2)}, u32[]{:S(2)}) collective-permute-start(bf16[5,48,384]{2,1,0:T(8,128)(2,1)} %get-tuple-element.322), channel_id=1, source_target_pairs={{0,16},{8,24},{16,0},{24,8},{1,17},{9,25},{17,1},{25,9},{2,18},{10... | collective-permute-start | bytes 552968 | tf_op jit(solution)/shard_map/ppermute | solution.py:989
  421.9 24.7 %collective-permute-start.32 = (bf16[5,48,384]{2,1,0:T(8,128)(2,1)}, bf16[5,48,384]{2,1,0:T(8,128)(2,1)S(1)}, u32[]{:S(2)}, u32[]{:S(2)}) collective-permute-start(bf16[5,48,384]{2,1,0:T(8,128)(2,1)} %get-tuple-element.323), channel_id=1, source_target_pairs={{0,24},{8,16},{16,8},{24,0},{1,25},{9,17},{17,9},{25,1},{2,26},{10... | collective-permute-start | bytes 552968 | tf_op jit(solution)/shard_map/ppermute | solution.py:989
  452.9 14.6 %collective-permute-start.34 = (bf16[3,192,384]{2,1,0:T(8,128)(2,1)}, bf16[3,192,384]{2,1,0:T(8,128)(2,1)S(1)}, u32[]{:S(2)}, u32[]{:S(2)}) collective-permute-start(bf16[3,192,384]{2,1,0:T(8,128)(2,1)} %get-tuple-element.334), channel_id=1, source_target_pairs={{0,4},{4,0},{1,5},{5,1},{2,6},{6,2},{3,7},{7,3},{8,12},{12,8},{9,1... | collective-permute-start | bytes 1327112 | tf_op jit(solution)/shard_map/ppermute | solution.py:993
  454.2 56.4 %collective-permute-start.45 = (bf16[1024,768]{1,0:T(8,128)(2,1)}, bf16[1024,768]{1,0:T(8,128)(2,1)}, u32[]{:S(2)}, u32[]{:S(2)}) collective-permute-start(bf16[1024,768]{1,0:T(8,128)(2,1)} %get-tuple-element.358), channel_id=1, source_target_pairs={{1,2},{2,1},{5,6},{6,5},{9,10},{10,9},{13,14},{14,13},{17,18},{18,... | collective-permute-start | bytes 4718600 | tf_op jit(solution)/shard_map/ppermute | solution.py:1010
  460.6 10.2 %collective-permute-start.40 = (bf16[5,48,384]{2,1,0:T(8,128)(2,1)}, bf16[5,48,384]{2,1,0:T(8,128)(2,1)S(1)}, u32[]{:S(2)}, u32[]{:S(2)}) collective-permute-start(bf16[5,48,384]{2,1,0:T(8,128)(2,1)} %shard_map.283.p0), channel_id=1, source_target_pairs={{0,24},{8,16},{16,8},{24,0},{1,25},{9,17},{17,9},{25,1},{2,26},{10... | collective-permute-start | bytes 552968 | tf_op jit(solution)/shard_map/ppermute | solution.py:989
  462.3 18.4 %collective-permute-start.39 = (bf16[5,48,384]{2,1,0:T(8,128)(2,1)}, bf16[5,48,384]{2,1,0:T(8,128)(2,1)S(1)}, u32[]{:S(2)}, u32[]{:S(2)}) collective-permute-start(bf16[5,48,384]{2,1,0:T(8,128)(2,1)} %shard_map.283.p0), channel_id=1, source_target_pairs={{0,16},{8,24},{16,0},{24,8},{1,17},{9,25},{17,1},{25,9},{2,18},{10... | collective-permute-start | bytes 552968 | tf_op jit(solution)/shard_map/ppermute | solution.py:989
  467.5 13.3 %collective-permute-start.38 = (bf16[5,48,384]{2,1,0:T(8,128)(2,1)}, bf16[5,48,384]{2,1,0:T(8,128)(2,1)S(1)}, u32[]{:S(2)}, u32[]{:S(2)}) collective-permute-start(bf16[5,48,384]{2,1,0:T(8,128)(2,1)} %shard_map.283.p0), channel_id=1, source_target_pairs={{0,8},{8,0},{16,24},{24,16},{1,9},{9,1},{17,25},{25,17},{2,10},{10... | collective-permute-start | bytes 552968 | tf_op jit(solution)/shard_map/ppermute | solution.py:989
  484.8 21.0 %collective-permute-start.42 = (bf16[5,192,384]{2,1,0:T(8,128)(2,1)}, bf16[5,192,384]{2,1,0:T(8,128)(2,1)S(1)}, u32[]{:S(2)}, u32[]{:S(2)}) collective-permute-start(bf16[5,192,384]{2,1,0:T(8,128)(2,1)} %shard_map.284.refs_0_), channel_id=1, source_target_pairs={{0,4},{4,0},{1,5},{5,1},{2,6},{6,2},{3,7},{7,3},{8,12},{12,8},{9,1... | collective-permute-start | bytes 2211848 | tf_op jit(solution)/shard_map/ppermute | solution.py:993
  485.2 17.5 %collective-permute-start.41 = (f32[24,384]{1,0:T(8,128)S(1)}, f32[24,384]{1,0:T(8,128)S(1)}, u32[]{:S(2)}, u32[]{:S(2)}) collective-permute-start(f32[24,384]{1,0:T(8,128)S(1)} %copy-done.54), channel_id=1, source_target_pairs={{0,1},{1,0},{2,3},{3,2},{4,5},{5,4},{6,7},{7,6},{8,9},{9,8},{10,11... | collective-permute-start | bytes 110600 | tf_op jit(solution)/shard_map/ppermute | solution.py:993
  485.2 15.4 %collective-permute-start.36 = (bf16[3,48,384]{2,1,0:T(8,128)(2,1)}, bf16[3,48,384]{2,1,0:T(8,128)(2,1)}, u32[]{:S(2)}, u32[]{:S(2)}) collective-permute-start(bf16[3,48,384]{2,1,0:T(8,128)(2,1)} %get-tuple-element.345), channel_id=1, source_target_pairs={{0,16},{8,24},{16,0},{24,8},{1,17},{9,25},{17,1},{25,9},{2,18},{10... | collective-permute-start | bytes 331784 | tf_op jit(solution)/shard_map/ppermute | solution.py:989
  490.6 12.1 %collective-permute-start.37 = (bf16[3,48,384]{2,1,0:T(8,128)(2,1)}, bf16[3,48,384]{2,1,0:T(8,128)(2,1)}, u32[]{:S(2)}, u32[]{:S(2)}) collective-permute-start(bf16[3,48,384]{2,1,0:T(8,128)(2,1)} %get-tuple-element.346), channel_id=1, source_target_pairs={{0,24},{8,16},{16,8},{24,0},{1,25},{9,17},{17,9},{25,1},{2,26},{10... | collective-permute-start | bytes 331784 | tf_op jit(solution)/shard_map/ppermute | solution.py:989
  500.6 14.4 %collective-permute-start.43 = (bf16[5,192,384]{2,1,0:T(8,128)(2,1)S(1)}, bf16[5,192,384]{2,1,0:T(8,128)(2,1)S(1)}, u32[]{:S(2)}, u32[]{:S(2)}) collective-permute-start(bf16[5,192,384]{2,1,0:T(8,128)(2,1)S(1)} %copy-done.13), channel_id=1, source_target_pairs={{0,2},{2,0},{1,3},{3,1},{4,6},{6,4},{5,7},{7,5},{8,10},{10,8},{9,1... | collective-permute-start | bytes 2211848 | tf_op jit(solution)/shard_map/ppermute | solution.py:993
  505.8 9.2 %collective-permute-start.44 = (bf16[5,192,384]{2,1,0:T(8,128)(2,1)S(1)}, bf16[5,192,384]{2,1,0:T(8,128)(2,1)}, u32[]{:S(2)}, u32[]{:S(2)}) collective-permute-start(bf16[5,192,384]{2,1,0:T(8,128)(2,1)S(1)} %collective-permute-done.42.refs_1_), channel_id=1, source_target_pairs={{0,2},{2,0},{1,3},{3,1},{4,6},{6,4},{5,7},{7,5},{8,10},{10,8},{9,1... | collective-permute-start | bytes 2211848 | tf_op jit(solution)/shard_map/ppermute | solution.py:993
  508.7 12.5 %collective-permute-start.48 = (bf16[4,48,384]{2,1,0:T(8,128)(2,1)S(1)}, bf16[4,48,384]{2,1,0:T(8,128)(2,1)S(1)}, u32[]{:S(2)}, u32[]{:S(2)}) collective-permute-start(bf16[4,48,384]{2,1,0:T(8,128)(2,1)S(1)} %copy-done.35), channel_id=1, source_target_pairs={{0,24},{8,16},{16,8},{24,0},{1,25},{9,17},{17,9},{25,1},{2,26},{10... | collective-permute-start | bytes 442376 | tf_op jit(solution)/shard_map/ppermute | solution.py:989
  510.6 11.4 %collective-permute-start.47 = (bf16[4,48,384]{2,1,0:T(8,128)(2,1)S(1)}, bf16[4,48,384]{2,1,0:T(8,128)(2,1)S(1)}, u32[]{:S(2)}, u32[]{:S(2)}) collective-permute-start(bf16[4,48,384]{2,1,0:T(8,128)(2,1)S(1)} %copy-done.35), channel_id=1, source_target_pairs={{0,16},{8,24},{16,0},{24,8},{1,17},{9,25},{17,1},{25,9},{2,18},{10... | collective-permute-start | bytes 442376 | tf_op jit(solution)/shard_map/ppermute | solution.py:989
  510.6 11.4 %collective-permute-start.46 = (bf16[4,48,384]{2,1,0:T(8,128)(2,1)S(1)}, bf16[4,48,384]{2,1,0:T(8,128)(2,1)S(1)}, u32[]{:S(2)}, u32[]{:S(2)}) collective-permute-start(bf16[4,48,384]{2,1,0:T(8,128)(2,1)S(1)} %copy-done.35), channel_id=1, source_target_pairs={{0,8},{8,0},{16,24},{24,16},{1,9},{9,1},{17,25},{25,17},{2,10},{10... | collective-permute-start | bytes 442376 | tf_op jit(solution)/shard_map/ppermute | solution.py:989
  525.4 14.7 %collective-permute-start.49 = (bf16[4,192,384]{2,1,0:T(8,128)(2,1)}, bf16[4,192,384]{2,1,0:T(8,128)(2,1)S(1)}, u32[]{:S(2)}, u32[]{:S(2)}) collective-permute-start(bf16[4,192,384]{2,1,0:T(8,128)(2,1)} %shard_map.287.refs_0_), channel_id=1, source_target_pairs={{0,4},{4,0},{1,5},{5,1},{2,6},{6,2},{3,7},{7,3},{8,12},{12,8},{9,1... | collective-permute-start | bytes 1769480 | tf_op jit(solution)/shard_map/ppermute | solution.py:993
  526.5 14.8 %collective-permute-start.50 = (bf16[4,192,384]{2,1,0:T(8,128)(2,1)}, bf16[4,192,384]{2,1,0:T(8,128)(2,1)S(1)}, u32[]{:S(2)}, u32[]{:S(2)}) collective-permute-start(bf16[4,192,384]{2,1,0:T(8,128)(2,1)} %shard_map.287.refs_0_), channel_id=1, source_target_pairs={{0,2},{2,0},{1,3},{3,1},{4,6},{6,4},{5,7},{7,5},{8,10},{10,8},{9,1... | collective-permute-start | bytes 1769480 | tf_op jit(solution)/shard_map/ppermute | solution.py:993
  (64 other events, 355.6 us)
Sparse Core Ops, SparseCore 0:
  68.1 55.5 all-gather.4
  233.7 141.9 reduce-scatter.1
  382.8 69.9 all-gather.6

commit v4 on v3

--- a/solution.py
+++ b/solution.py
@@ -132,14 +132,20 @@
         delta = delta_of(dd, o_ref[...])
         zero = jnp.zeros((block, 128), bf16)
         dqt, dk, dv = None, dka[...], dva[...]
-        for h in range(2):
+
+        def products(h):
             mine = half_of(lane, h)
             spare = lane == (HD if h == 0 else 0)
             qc = jnp.where(mine, qq, zero)
-            qs = jnp.where(spare, jnp.ones((block, 128), bf16), qc)
             dh = jnp.where(mine, dd, zero)
-            p = jnp.exp(mm_t(ks[h], qs) - l_ref[0, h : h + 1, :])
-            ds = (p * (mm_t(v_ref[...], dh) - delta[h : h + 1])).astype(bf16)
+            return qc, dh, mm_t(ks[h], jnp.where(spare, jnp.ones((block, 128), bf16), qc)), mm_t(v_ref[...], dh)
+
+        now = products(0)
+        for h in range(2):
+            qc, dh, scores, dp = now
+            now = products(1) if h == 0 else None
+            p = jnp.exp(scores - l_ref[0, h : h + 1, :])
+            ds = (p * (dp - delta[h : h + 1])).astype(bf16)
             dv = dv + mm(p.astype(bf16), dh)
             dk = dk + mm(ds, qc)
             part = mm(kts[h], ds)
@@ -271,23 +277,32 @@
             dd = df[spot, :]
             delta = delta_of(dd, o_ref[spot, :])
             dqt = None
+            tasks = []
             for h in range(2):
                 mine = half_of(lane, h)
                 qc = jnp.where(mine, qf[spot, :], none)
                 qs = jnp.where(mine, qf[spot, :], qm_ref[spot, :])
                 dh = jnp.where(mine, dd, none)
+                tasks += [(h, qc, qs, dh, a, b) for a, b in spans(r0, block)]
+
+            def products(task):
+                h, qc, qs, dh, a, b = task
+                s = mm_t(ks[h, pl.ds(a, b - a), :], qs)
+                return jnp.where(hide, NEG, s) if a == r0 else s, mm_t(vf[pl.ds(a, b - a), :], dh)
+
+            now = products(tasks[0])
+            for i, (h, qc, qs, dh, a, b) in enumerate(tasks):
+                later = products(tasks[i + 1]) if i + 1 < len(tasks) else None
                 log_total = l_ref[0, h : h + 1, spot]
-                for a, b in spans(r0, block):
-                    keys = pl.ds(a, b - a)
-                    s = mm_t(ks[h, keys, :], qs)
-                    if a == r0:
-                        s = jnp.where(hide, NEG, s)
-                    p = jnp.exp(s - log_total)
-                    ds = (p * (mm_t(vf[keys, :], dh) - delta[h : h + 1])).astype(bf16)
-                    dva[keys, :] += mm(p.astype(bf16), dh)
-                    dka[keys, :] += mm(ds, qc)
-                    part = mm(kts[h, :, keys], ds)
-                    dqt = part if dqt is None else dqt + part
+                keys = pl.ds(a, b - a)
+                s, dp = now
+                now = later
+                p = jnp.exp(s - log_total)
+                ds = (p * (dp - delta[h : h + 1])).astype(bf16)
+                dva[keys, :] += mm(p.astype(bf16), dh)
+                dka[keys, :] += mm(ds, qc)
+                part = mm(kts[h, :, keys], ds)
+                dqt = part if dqt is None else dqt + part
             dqa[spot, :] = (dqt * 0.125).T.astype(bf16)
         for out, at in ((give_ref, other0), (keep_ref, mine0)):
             spot = pl.ds(at, rows)
@@ -897,10 +912,26 @@
                 for z in range(4):
                     part = rows[48 * z : 48 * z + 48]
                     total = part if total is None else total + part
-            results[-1][...] = total[0:24] + total[24:48]
+            total, at = total[0:24] + total[24:48], 0
+            for ref in results[1:]:
+                ref[...] = total[at : at + ref.shape[0]]
+                at += ref.shape[0]
 
     parts = [part for group, _ in groups for part in group]
     return call(kernel, s, parts, (1,), [const(part.shape) for part in parts], [const(d) for d in outs], [shape(d, f32) for d in outs])
+
+
+def spread_gathered(s, got, spots, outs):
+    _, _, part, hw = got.shape
+
+    def kernel(s_ref, g_ref, *results):
+        for r in range(got.shape[0]):
+            z, y, core = r // 4, r // 2 % 2, r % 2
+            for block, (which, row, col) in enumerate(spots):
+                at_row, at_col = row + (y * 4 + z) * part, col + core * hw
+                results[which][at_row : at_row + part, at_col : at_col + hw] = g_ref[r, block].astype(f32)
+
+    return call(kernel, s, (got,), (1,), [const(got.shape)], [const(d) for d in outs], [shape(d, f32) for d in outs])
 
 
 def spread_ff(s, got):
@@ -1118,7 +1149,7 @@
     m_y = across(m_ygive, "y")
     ff_got = lax.all_gather(ff_mine, REP2, axis=0, tiled=False)
     bg3, bk3 = self_bwd(2, 1, 0, c, keep, recv, ctx_b, dctx_keep, dctx_in, lse_b, kmark, qmark)
-    bg3, bk3, m_y, bi2 = tie(bg3, bk3, m_y, bi2)
+    bg3, bk3, bi2 = tie(bg3, bk3, bi2)
     bi3 = sibling(bg3)
     q_xgive = qkv_grad(s, a1, a1_sib, (bk1, bk2, bk3), (bg1, bg2, bg3), False)
     q_xgive, m_y = tie(q_xgive, m_y)
@@ -1128,43 +1159,37 @@
     m_z = send_z(m_z)
     q_xkeep = qkv_grad(s, a1, a1_sib, (bk1, bk2, bk3), (bg1, bg2, bg3), True)
     grad_hidden, vec_last = last_rows(s, (bk1, bk2, bk3), (bi1, bi2, bi3), x_own, x_in, dh1, w_qkv, table)
-    vec_last, *m_z = tie(vec_last, *m_z)
-    m_all = gather_z(sum_four(s, m_z))
     v_give, v_mine = pack_vectors(s, vec_last, vec_cross, vec_mid, vec_kv)
     v_got = across(v_give, "x")
     v_mine, q_x = tie(v_mine, q_x)
     q_ygive, q_ykeep = split_y(s, (q_xkeep,), (q_x,))
-    q_ygive, grad_hidden = tie(q_ygive, grad_hidden)
+    q_ygive, grad_hidden, *m_z = tie(q_ygive, grad_hidden, *m_z)
+    m_piece = sum_four(s, m_z)
+    m_got = lax.all_gather(m_piece, REP2, axis=0, tiled=False)
     q_y = across(q_ygive, "y")
     hid_in = swap(grad_hidden)
     q_four = split_z(s, q_ykeep, q_y)
-    *q_four, m_first = tie(*q_four, m_all[0])
     q_z = send_z(q_four)
-    m_own = join_z(s, (m_first, *m_all[1:]))
-    m_far = across(m_own, "y")
     fc1_grad, fc2_grad = spread_ff(s, ff_got.reshape(reps, 2, per, width))
-    m_own_sib = sibling(m_own)
     output = jnp.where(stay, out, out_in)
     fc1_grad, fc2_grad, output, *q_z = tie(fc1_grad, fc2_grad, output, *q_z)
     q_piece = sum_four(s, q_z, (v_mine, v_got))
-    q_piece, m_far = tie(q_piece, m_far)
     q_all = gather_z(q_piece)
     spots = ((0, 0, 0), (1, 0, 0), (3, 0, 0), (3, hw, 0), (2, 0, 0))
-    crossout_grad, crossq_grad, selfout_grad, kv_grad = spread_out(
-        s, (((m_own, m_far, m_own_sib, sibling(m_far)), spots),), ((hw, width),) * 3 + ((width, width),)
-    )
+    crossout_grad, crossq_grad, selfout_grad, kv_grad = spread_gathered(s, m_got, spots, ((hw, width),) * 3 + ((width, width),))
     grad_frames = jnp.where(stay, fr_own, fr_swapped)
-    grad_hidden = jnp.where(stay, grad_hidden, hid_in)
-    crossout_grad, grad_frames, grad_hidden, *q_all = tie(crossout_grad, grad_frames, grad_hidden, *q_all)
+    grad_frames, *q_all = tie(grad_frames, *q_all)
     q_own = join_z(s, q_all)
     q_far = across(q_own, "y")
     q_own_sib = sibling(q_own)
+    grad_hidden = jnp.where(stay, grad_hidden, hid_in)
+    q_far, crossout_grad, grad_hidden = tie(q_far, crossout_grad, grad_hidden)
     first = tuple((0, 0, j * width) for j in range(3))
-    qkv_grad_out, mine = spread_out(s, (((q_own, q_far, q_own_sib, sibling(q_far)), first),), ((hw, 3 * width), (24, hw)), True)
+    qkv_grad_out, gain_grad, shift_grad, bias_grad, fc1b_grad = spread_out(s, (((q_own, q_far, q_own_sib, sibling(q_far)), first),), ((hw, 3 * width), (4, hw), (4, hw), (7, hw), (units, hw)), True)
 
     return (
-        output[None], grad_hidden[None], grad_frames[None], mine[:4], mine[4:8],
-        qkv_grad_out, selfout_grad, crossq_grad, kv_grad, crossout_grad, fc1_grad, fc2_grad, mine[8:15], mine[15:19].reshape(-1),
+        output[None], grad_hidden[None], grad_frames[None], gain_grad, shift_grad,
+        qkv_grad_out, selfout_grad, crossq_grad, kv_grad, crossout_grad, fc1_grad, fc2_grad, bias_grad, fc1b_grad.reshape(-1),
     )
 
 

time: 565 us -> 555 us (0.982)
  Pallas kernels: 366 us -> 359 us
    pallas_call x35 -> x34, Pallas kernels: 366 us -> 359 us  [call(): pl.pallas_call(kernel, grid_spec=spec, out_shape=out_shape, cost_estimate...]
    ppermute x33 -> x30, starting transfers between devices: 21 us -> 15.5 us  [across(): return lax.ppermute(x, axis, FLIP)]
    ppermute x12 -> x9, waiting for transfers between devices: 20.2 us -> 24.6 us  [across_z(): return lax.ppermute(x, 'z', [(j, j ^ d) for j in range(4)])]
    ppermute x12 -> x9, starting transfers between devices: 15 us -> 17.5 us  [across_z(): return lax.ppermute(x, 'z', [(j, j ^ d) for j in range(4)])]
    ppermute x33 -> x30, waiting for transfers between devices: 27 us -> 25.7 us  [across(): return lax.ppermute(x, axis, FLIP)]
    unnamed x114 -> x106, local copies, waits for them, and re-layouts: 18.2 us -> 17.1 us
  transfers between devices with their start and end apart: 55 -> 50, of which waited for: 14 -> 13; matrix products, arithmetic and copies ran while one was open for 6% -> 6% of each run, Pallas kernels for 52% -> 52%
where the time goes in v4:
time: 555 us; the launch traced here: 549 us
  Pallas kernels  359 us (65%)
  waiting for transfers between devices  65.2 us (12%)
  starting transfers between devices  58.2 us (10%)
  local copies, waits for them, and re-layouts  29.7 us (5%)
  other arithmetic  22.4 us (4%)
  between operations  14.6 us (3%)
    pallas_call x34, Pallas kernels, call(): pl.pallas_call(kernel, grid_spec=spec, out_shape=out_shape, cost_estimate...  359 us
    ppermute x30, waiting for transfers between devices, across(): return lax.ppermute(x, axis, FLIP)  25.7 us
    ppermute x7, starting transfers between devices, swap(): return lax.ppermute(x, ('core', 'x'), SWAP)  24.6 us
    ppermute x9, waiting for transfers between devices, across_z(): return lax.ppermute(x, 'z', [(j, j ^ d) for j in range(4)])  24.6 us
    ppermute x9, starting transfers between devices, across_z(): return lax.ppermute(x, 'z', [(j, j ^ d) for j in range(4)])  17.5 us
    unnamed x106, local copies, waits for them, and re-layouts  17.1 us
    ppermute x30, starting transfers between devices, across(): return lax.ppermute(x, axis, FLIP)  15.5 us
    ppermute x7, waiting for transfers between devices, swap(): return lax.ppermute(x, ('core', 'x'), SWAP)  14.8 us
  transfers between devices with their start and end apart: 50, of which 13 were waited for; matrix products, arithmetic and copies ran while one was open for 6% of the time, Pallas kernels for 52%

profile of v4, /device:TPU:1, one launch (start us, length us, event | category | flops | bytes accessed | tf_op | source)
XLA Modules:
  0.0 548.8 jit_solution(13627927963128260980)
XLA Ops:
  7.3 4.6 collective-permute-start.1
  22.7 2.8 convert.51
  41.1 14.8 %collective-permute-done.xi.refs_5_.refs_7_ = bf16[1024,768]{1,0:T(8,128)(2,1)S(1)} collective-permute-done((bf16[1024,768]{1,0:T(8,128)(2,1)S(1)}, bf16[1024,768]{1,0:T(8,128)(2,1)S(1)}, u32[]{:S(2)}, u32[]{:S(2)}) %collective-permute-start) | collective-permute-done | bytes 1572896 | tf_op jit(solution)/shard_map/ppermute | solution.py:1041
  57.0 10.2 %shard_map.254 = (bf16[768,2304]{1,0:T(8,128)(2,1)}, bf16[1024,768]{1,0:T(8,128)(2,1)}, bf16[3,1024,384]{2,1,0:T(8,128)(2,1)}, bf16[3,1024,384]{2,1,0:T(8,128)(2,1)}) custom-call(s32[9]{0:T(128)} %stack.72.s_ref, bf16[1024,768]{1,0:T(8,128)(2,1)} %bitcast.43, bf16[1024,768]{1,0:T(8,128)(2,1)} %copy-done.2, f32[384,2304]{1,0:T(8,128)} %own.2, ...), custom_call_target="tpu_custom_call" | custom-call | flops 362387872 | bytes 1048576 | tf_op jit(solution)/shard_map/pallas_call | solution.py:41
  69.4 3.6 collective-permute-start.11
  75.0 15.6 %shard_map.255 = (bf16[2048,256]{1,0:T(8,128)(2,1)}, bf16[1024,256]{1,0:T(8,128)(2,1)}, f32[2,8,2048]{2,1,0:T(8,128)}) custom-call(s32[1]{0:T(128)} %bitcast.s_ref, bf16[3,1024,384]{2,1,0:T(8,128)(2,1)} %get-tuple-element.293.a_ref, bf16[3,1024,384]{2,1,0:T(8,128)(2,1)} %copy-done, bf16[2048,128]{1,0:T(8,128)(2,1)} %get-tuple-element.194.km_ref, ...), custom_call_target="tpu_custom_call" | custom-call | flops 858993472 | bytes 1048576 | tf_op jit(solution)/shard_map/pallas_call | solution.py:41
  92.5 8.9 %shard_map.256 = (bf16[2048,128]{1,0:T(8,128)(2,1)}, bf16[1024,128]{1,0:T(8,128)(2,1)}, f32[1,8,2048]{2,1,0:T(8,128)}) custom-call(s32[1]{0:T(128)} %bitcast.s_ref, bf16[3,1024,384]{2,1,0:T(8,128)(2,1)} %get-tuple-element.293.a_ref, bf16[3,1024,384]{2,1,0:T(8,128)(2,1)} %copy-done, bf16[2048,128]{1,0:T(8,128)(2,1)} %get-tuple-element.194.km_ref, ...), custom_call_target="tpu_custom_call" | custom-call | flops 429496736 | bytes 1048576 | tf_op jit(solution)/shard_map/pallas_call | solution.py:41
  103.2 2.7 collective-permute-start.15
  106.9 10.5 %shard_map.257 = (bf16[768,768]{1,0:T(8,128)(2,1)}, bf16[768,768]{1,0:T(8,128)(2,1)}, f32[1024,768]{1,0:T(8,128)}, bf16[1024,768]{1,0:T(8,128)(2,1)}, bf16[1024,768]{1,0:T(8,128)(2,1)}) custom-call(s32[9]{0:T(128)} %stack.72.s_ref, bf16[2048,256]{1,0:T(8,128)(2,1)} %get-tuple-element.196.refs_0_.o_ref, bf16[2048,128]{1,0:T(8,128)(2,1)} %get-tuple-element.201.refs_1_.o_ref, ...), custom_call_target="tpu_custom_call" | custom-call | flops 241591904 | bytes 1048576 | tf_op jit(solution)/shard_map/pallas_call | solution.py:41
  120.1 2.7 collective-permute-done.14.sib
  124.6 10.2 %shard_map.258 = (bf16[1536,768]{1,0:T(8,128)(2,1)}, bf16[1536,768]{1,0:T(8,128)(2,1)}, bf16[1536,768]{1,0:T(8,128)(2,1)}) custom-call(s32[9]{0:T(128)} %stack.72.s_ref, bf16[1500,384]{1,0:T(8,128)(2,1)} %copy-done.3, bf16[1500,384]{1,0:T(8,128)(2,1)} %copy-done.10, f32[768,768]{1,0:T(8,128)} %own.3, bf16[384,768]{1,0:T(8,128)(2,1)} %collective-permute-done.12.mine, ...), custom_call_target="tpu_custom_call" | custom-call | flops 353894400 | bytes 1048576 | tf_op jit(solution)/shard_map/pallas_call | solution.py:41
  134.8 14.8 %shard_map.260 = (bf16[1024,384]{1,0:T(8,128)(2,1)}, f32[3,8,1024]{2,1,0:T(8,128)}) custom-call(s32[1]{0:T(128)} %bitcast.23.s_ref, bf16[1024,768]{1,0:T(8,128)(2,1)} %get-tuple-element.208.q_ref, bf16[1536,768]{1,0:T(8,128)(2,1)} %get-tuple-element.211.k_ref, bf16[1536,768]{1,0:T(8,128)(2,1)} %get-tuple-element.212.v_ref), custom_call_target="tpu_custom_call" | custom-call | flops 483183808 | bytes 1048576 | tf_op jit(solution)/shard_map/pallas_call | solution.py:41
  149.6 14.8 %shard_map.259 = (bf16[1024,384]{1,0:T(8,128)(2,1)}, f32[3,8,1024]{2,1,0:T(8,128)}) custom-call(s32[1]{0:T(128)} %bitcast.8.s_ref, bf16[1024,768]{1,0:T(8,128)(2,1)} %get-tuple-element.208.q_ref, bf16[1536,768]{1,0:T(8,128)(2,1)} %get-tuple-element.211.k_ref, bf16[1536,768]{1,0:T(8,128)(2,1)} %get-tuple-element.212.v_ref), custom_call_target="tpu_custom_call" | custom-call | flops 483183808 | bytes 1048576 | tf_op jit(solution)/shard_map/pallas_call | solution.py:41
  164.5 51.7 %shard_map.261 = (bf16[768,768]{1,0:T(8,128)(2,1)}, bf16[1024,768]{1,0:T(8,128)(2,1)}, bf16[1024,768]{1,0:T(8,128)(2,1)}, bf16[1024,3072]{1,0:T(8,128)(2,1)}, bf...) custom-call(s32[9]{0:T(128)} %stack.72.s_ref, ...), custom_call_target="tpu_custom_call" | custom-call | flops 2174327296 | bytes 1048576 | tf_op jit(solution)/shard_map/pallas_call | solution.py:41
  216.2 17.4 %shard_map.262 = bf16[2,16,2,96,768]{4,3,2,1,0:T(8,128)(2,1)} custom-call(s32[9]{0:T(128)} %stack.72.s_ref, bf16[1024,768]{1,0:T(8,128)(2,1)} %get-tuple-element.223.a_ref, bf16[1024,3072]{1,0:T(8,128)(2,1)} %get-tuple-element.224.du_ref, bf16[1024,3072]{1,0:T(8,128)(2,1)} %get-tuple-element.225.g0.g1, bf16[1024,3072]{1,0:T(8,128)(2,1)} %get-tuple-element.225.g0.g1, ...), custom_call_target="tpu_custom_call" | custom-call | flops 966367616 | bytes 1048576 | tf_op jit(solution)/shard_map/pallas_call | solution.py:41
  233.7 26.0 %shard_map.263 = (bf16[1024,384]{1,0:T(8,128)(2,1)}, bf16[2,1536,384]{2,1,0:T(8,128)(2,1)}) custom-call(s32[1]{0:T(128)} %bitcast.23.s_ref, bf16[1024,768]{1,0:T(8,128)(2,1)} %get-tuple-element.208.q_ref, bf16[1536,768]{1,0:T(8,128)(2,1)} %get-tuple-element.211.k_ref, bf16[1536,768]{1,0:T(8,128)(2,1)} %get-tuple-element.212.v_ref, ...), custom_call_target="tpu_custom_call" | custom-call | flops 2415919104 | bytes 1048576 | tf_op jit(solution)/shard_map/pallas_call | solution.py:41
  260.2 3.4 collective-permute-start.16
  263.6 5.9 %shard_map.264 = bf16[2,768,384]{2,1,0:T(8,128)(2,1)} custom-call(s32[9]{0:T(128)} %stack.72.s_ref, bf16[1024,384]{1,0:T(8,128)(2,1)} %get-tuple-element.213.ck_ref.k_ref.o_ref.ck, bf16[1024,384]{1,0:T(8,128)(2,1)} %get-tuple-element.214.cg_ref.o_ref.g_ref.cg, bf16[1024,768]{1,0:T(8,128)(2,1)} %get-tuple-element.220.d_ref.d2_ref, ...), custom_call_target="tpu_custom_call" | custom-call | flops 120795952 | bytes 1048576 | tf_op jit(solution)/shard_map/pallas_call | solution.py:41
  269.5 26.2 %shard_map.265 = (bf16[1024,384]{1,0:T(8,128)(2,1)}, bf16[2,1536,384]{2,1,0:T(8,128)(2,1)}) custom-call(s32[1]{0:T(128)} %bitcast.8.s_ref, bf16[1024,768]{1,0:T(8,128)(2,1)} %get-tuple-element.208.q_ref, bf16[1536,768]{1,0:T(8,128)(2,1)} %get-tuple-element.211.k_ref, bf16[1536,768]{1,0:T(8,128)(2,1)} %get-tuple-element.212.v_ref, ...), custom_call_target="tpu_custom_call" | custom-call | flops 2415919104 | bytes 1048576 | tf_op jit(solution)/shard_map/pallas_call | solution.py:41
  297.1 10.5 %shard_map.266 = (bf16[1500,384]{1,0:T(8,128)(2,1)}, bf16[1500,384]{1,0:T(8,128)(2,1)}, bf16[768,384]{1,0:T(8,128)(2,1)}, bf16[768,384]{1,0:T(8,128)(2,1)}, f32[8,384]{1,0:T(8,128)}) custom-call(s32[9]{0:T(128)} %stack.72.s_ref, bf16[2,1536,384]{2,1,0:T(8,128)(2,1)} %get-tuple-element.237.ka, bf16[2,1536,384]{2,1,0:T(8,128)(2,1)} %copy-done.17, ...), custom_call_target="tpu_custom_call" | custom-call | flops 707788800 | bytes 1048576 | tf_op jit(solution)/shard_map/pallas_call | solution.py:41
  308.2 7.1 %shard_map.267 = (bf16[4,384,384]{2,1,0:T(8,128)(2,1)}, bf16[4,384,384]{2,1,0:T(8,128)(2,1)}) custom-call(s32[9]{0:T(128)} %stack.72.s_ref, bf16[1024,384]{1,0:T(8,128)(2,1)} %get-tuple-element.213.ck_ref.k_ref.o_ref.ck, bf16[1024,384]{1,0:T(8,128)(2,1)} %get-tuple-element.214.cg_ref.o_ref.g_ref.cg, bf16[1024,768]{1,0:T(8,128)(2,1)} %get-tuple-element.220.d_ref.d2_ref, ...), custom_call_target="tpu_custom_call" | custom-call | flops 120795952 | bytes 1048576 | tf_op jit(solution)/shard_map/pallas_call | solution.py:41
  315.3 11.0 %shard_map.268 = (f32[1024,768]{1,0:T(8,128)}, bf16[1024,768]{1,0:T(8,128)(2,1)}, bf16[1024,384]{1,0:T(8,128)(2,1)}, bf16[1024,384]{1,0:T(8,128)(2,1)}, f32[8,768]{1,0:T(8,128)}) custom-call(s32[9]{0:T(128)} %stack.72.s_ref, bf16[1024,384]{1,0:T(8,128)(2,1)} %get-tuple-element.253.q_ref.dk_ref, bf16[1024,384]{1,0:T(8,128)(2,1)} %get-tuple-element.233.q_ref.dg_ref, ...), custom_call_target="tpu_custom_call" | custom-call | flops 241591904 | bytes 1048576 | tf_op jit(solution)/shard_map/pallas_call | solution.py:41
  326.7 4.2 shard_map.269
  334.2 3.5 collective-permute-start.26
  337.7 4.3 shard_map.270
  342.9 14.6 %shard_map.271 = (bf16[3,1024,128]{2,1,0:T(8,128)(2,1)}, bf16[3,1024,128]{2,1,0:T(8,128)(2,1)}) custom-call(s32[1]{0:T(128)} %bitcast.s_ref, bf16[3,1024,384]{2,1,0:T(8,128)(2,1)} %get-tuple-element.293.a_ref, bf16[3,1024,384]{2,1,0:T(8,128)(2,1)} %copy-done, bf16[2048,256]{1,0:T(8,128)(2,1)} %get-tuple-element.196.refs_0_.o_ref, ...), custom_call_target="tpu_custom_call" | custom-call | flops 858993472 | bytes 1048576 | tf_op jit(solution)/shard_map/pallas_call | solution.py:41
  357.9 14.5 %shard_map.272 = (bf16[3,1024,128]{2,1,0:T(8,128)(2,1)}, bf16[3,1024,128]{2,1,0:T(8,128)(2,1)}) custom-call(s32[1]{0:T(128)} %bitcast.s_ref, bf16[3,1024,384]{2,1,0:T(8,128)(2,1)} %get-tuple-element.293.a_ref, bf16[3,1024,384]{2,1,0:T(8,128)(2,1)} %copy-done, bf16[2048,256]{1,0:T(8,128)(2,1)} %get-tuple-element.196.refs_0_.o_ref, ...), custom_call_target="tpu_custom_call" | custom-call | flops 858993472 | bytes 1048576 | tf_op jit(solution)/shard_map/pallas_call | solution.py:41
  372.4 5.3 collective-permute-done.24.refs_3_
  378.7 3.9 shard_map.273
  385.7 14.5 %shard_map.275 = (bf16[3,1024,128]{2,1,0:T(8,128)(2,1)}, bf16[3,1024,128]{2,1,0:T(8,128)(2,1)}) custom-call(s32[1]{0:T(128)} %bitcast.s_ref, bf16[3,1024,384]{2,1,0:T(8,128)(2,1)} %get-tuple-element.293.a_ref, bf16[3,1024,384]{2,1,0:T(8,128)(2,1)} %copy-done, bf16[2048,128]{1,0:T(8,128)(2,1)} %get-tuple-element.201.refs_1_.o_ref, ...), custom_call_target="tpu_custom_call" | custom-call | flops 858993472 | bytes 1048576 | tf_op jit(solution)/shard_map/pallas_call | solution.py:41
  400.2 7.3 %shard_map.276 = bf16[3,384,384]{2,1,0:T(8,128)(2,1)} custom-call(s32[9]{0:T(128)} %stack.72.s_ref, bf16[1024,768]{1,0:T(8,128)(2,1)} %get-tuple-element.241.ao, bf16[1024,768]{1,0:T(8,128)(2,1)} %collective-permute-done.18.ai, bf16[3,1024,128]{2,1,0:T(8,128)(2,1)} %get-tuple-element.291.refs_0_, bf16[3,1024,128]{2,1,0:T(8,128)(2,1)} %get-tuple-element.292.refs_1_, ...), custom_call_target="tpu_custom_call" | custom-call | flops 181193936 | bytes 1048576 | tf_op jit(solution)/shard_map/pallas_call | solution.py:41
  409.3 3.0 shard_map.277
  415.9 6.9 %shard_map.278.refs_0_ = bf16[3,384,384]{2,1,0:T(8,128)(2,1)} custom-call(s32[9]{0:T(128)} %stack.72.s_ref, bf16[1024,768]{1,0:T(8,128)(2,1)} %get-tuple-element.241.ao, bf16[1024,768]{1,0:T(8,128)(2,1)} %collective-permute-done.18.ai, bf16[3,1024,128]{2,1,0:T(8,128)(2,1)} %get-tuple-element.291.refs_0_, bf16[3,1024,128]{2,1,0:T(8,128)(2,1)} %get-tuple-element.292.refs_1_, ...), custom_call_target="tpu_custom_call" | custom-call | flops 181193936 | bytes 1048576 | tf_op jit(solution)/shard_map/pallas_call | solution.py:41
  422.8 12.4 %shard_map.279 = (bf16[1024,768]{1,0:T(8,128)(2,1)}, f32[8,768]{1,0:T(8,128)}) custom-call(s32[9]{0:T(128)} %stack.72.s_ref, bf16[3,1024,128]{2,1,0:T(8,128)(2,1)} %get-tuple-element.291.refs_0_, bf16[3,1024,128]{2,1,0:T(8,128)(2,1)} %get-tuple-element.292.refs_1_, bf16[3,1024,128]{2,1,0:T(8,128)(2,1)} %get-tuple-element.308.refs_2_, ...), custom_call_target="tpu_custom_call" | custom-call | flops 362387872 | bytes 1048576 | tf_op jit(solution)/shard_map/pallas_call | solution.py:41
  438.3 3.2 shard_map.281
  442.4 2.6 shard_map.285
  445.2 4.4 collective-permute-start.43
  449.6 6.5 %collective-permute-done.34.g_ref = bf16[3,192,384]{2,1,0:T(8,128)(2,1)S(1)} collective-permute-done((bf16[3,192,384]{2,1,0:T(8,128)(2,1)}, bf16[3,192,384]{2,1,0:T(8,128)(2,1)S(1)}, u32[]{:S(2)}, u32[]{:S(2)}) %collective-permute-start.34) | collective-permute-done | bytes 442400 | tf_op jit(solution)/shard_map/ppermute | solution.py:1024
  456.9 2.6 shard_map.282
  459.5 7.4 %collective-permute-start.35 = (bf16[3,48,384]{2,1,0:T(8,128)(2,1)}, bf16[3,48,384]{2,1,0:T(8,128)(2,1)S(1)}, u32[]{:S(2)}, u32[]{:S(2)}) collective-permute-start(bf16[3,48,384]{2,1,0:T(8,128)(2,1)} %get-tuple-element.329), channel_id=1, source_target_pairs={{0,8},{8,0},{16,24},{24,16},{1,9},{9,1},{17,25},{25,17},{2,10},{10... | collective-permute-start | bytes 331784 | tf_op jit(solution)/shard_map/ppermute | solution.py:1020
  469.6 2.8 broadcast_select_fusion.1
  472.3 7.0 %shard_map.274 = (f32[384,3072]{1,0:T(8,128)}, f32[1536,768]{1,0:T(8,128)}) custom-call(s32[9]{0:T(128)} %stack.72.s_ref, bf16[16,2,96,768]{3,2,1,0:T(8,128)(2,1)} %bitcast.53), custom_call_target="tpu_custom_call" | custom-call | tf_op jit(solution)/shard_map/pallas_call | solution.py:41
  493.6 20.4 %collective-permute-done.40.p2 = bf16[4,48,384]{2,1,0:T(8,128)(2,1)S(1)} collective-permute-done((bf16[4,48,384]{2,1,0:T(8,128)(2,1)}, bf16[4,48,384]{2,1,0:T(8,128)(2,1)S(1)}, u32[]{:S(2)}, u32[]{:S(2)}) %collective-permute-start.40) | collective-permute-done | bytes 147488 | tf_op jit(solution)/shard_map/ppermute | solution.py:1020
  515.3 2.7 shard_map.284.refs_0_
  518.6 2.8 broadcast_select_fusion
  521.3 5.3 shard_map.286
  526.6 6.1 %collective-permute-done.42.refs_1_ = bf16[4,192,384]{2,1,0:T(8,128)(2,1)S(1)} collective-permute-done((bf16[4,192,384]{2,1,0:T(8,128)(2,1)}, bf16[4,192,384]{2,1,0:T(8,128)(2,1)S(1)}, u32[]{:S(2)}, u32[]{:S(2)}) %collective-permute-start.42) | collective-permute-done | bytes 589856 | tf_op jit(solution)/shard_map/ppermute | solution.py:1024
  536.4 4.3 shard_map.287
  (237 shorter events, 86.4 us)
Async XLA Ops:
  7.2 157.2 %all-gather.7.cloned.1.call-start = ((), (), s32[]{:S(2)}) async-start(), calls=%async_computation.2 | async-start | bytes 5013504 | tf_op jit(solution)/shard_map/all_gather | solution.py:1076
  7.3 30.2 %collective-permute-start.1 = (s32[1,2048]{1,0:T(1,128)}, s32[1,2048]{1,0:T(1,128)S(1)}, u32[]{:S(2)}, u32[]{:S(2)}) collective-permute-start(s32[1,2048]{1,0:T(1,128)} %param.17), channel_id=1, source_target_pairs={{1,2},{2,1},{5,6},{6,5},{9,10},{10,9},{13,14},{14,13},{17,18},{18,... | collective-permute-start | bytes 24584 | tf_op jit(solution)/shard_map/ppermute | solution.py:1041
  14.9 26.2 %collective-permute-start.4 = (bf16[20,384]{1,0:T(8,128)(2,1)S(1)}, bf16[20,384]{1,0:T(8,128)(2,1)S(1)}, u32[]{:S(2)}, u32[]{:S(2)}) collective-permute-start(bf16[20,384]{1,0:T(8,128)(2,1)S(1)} %concatenate.35), channel_id=1, source_target_pairs={{0,1},{1,0},{2,3},{3,2},{4,5},{5,4},{6,7},{7,6},{8,9},{9,8},{10,11... | collective-permute-start | bytes 46088 | tf_op jit(solution)/shard_map/ppermute | solution.py:1024
  17.4 21.2 %collective-permute-start.2 = (bf16[192,2304]{1,0:T(8,128)(2,1)}, bf16[192,2304]{1,0:T(8,128)(2,1)}, u32[]{:S(2)}, u32[]{:S(2)}) collective-permute-start(bf16[192,2304]{1,0:T(8,128)(2,1)} %dynamic-slice_convert_fusion), channel_id=1, source_target_pairs={{0,1},{1,0},{2,3},{3,2},{4,5},{5,4},{6,7},{7,6},{8,9},{9,8},{10,11... | collective-permute-start | bytes 2654216 | tf_op jit(solution)/shard_map/ppermute | solution.py:1024
  18.9 37.0 %collective-permute-start = (bf16[1024,768]{1,0:T(8,128)(2,1)S(1)}, bf16[1024,768]{1,0:T(8,128)(2,1)S(1)}, u32[]{:S(2)}, u32[]{:S(2)}) collective-permute-start(bf16[1024,768]{1,0:T(8,128)(2,1)S(1)} %bitcast.46), channel_id=1, source_target_pairs={{1,2},{2,1},{5,6},{6,5},{9,10},{10,9},{13,14},{14,13},{17,18},{18,... | collective-permute-start | bytes 4718600 | tf_op jit(solution)/shard_map/ppermute | solution.py:1041
  38.6 18.0 %collective-permute-start.3 = (bf16[192,2304]{1,0:T(8,128)(2,1)}, bf16[192,2304]{1,0:T(8,128)(2,1)}, u32[]{:S(2)}, u32[]{:S(2)}) collective-permute-start(bf16[192,2304]{1,0:T(8,128)(2,1)} %collective-permute-done.2.mine), channel_id=1, source_target_pairs={{0,2},{2,0},{1,3},{3,1},{4,6},{6,4},{5,7},{7,5},{8,10},{10,8},{9,1... | collective-permute-start | bytes 2654216 | tf_op jit(solution)/shard_map/ppermute | solution.py:1024
  55.9 11.4 %collective-permute-start.5 = (bf16[2,96,768]{2,1,0:T(8,128)(2,1)}, bf16[2,96,768]{2,1,0:T(8,128)(2,1)S(1)}, u32[]{:S(2)}, u32[]{:S(2)}) collective-permute-start(bf16[2,96,768]{2,1,0:T(8,128)(2,1)} %pad_maximum_fusion.2), channel_id=1, source_target_pairs={{0,1},{1,0},{2,3},{3,2},{4,5},{5,4},{6,7},{7,6},{8,9},{9,8},{10,11... | collective-permute-start | bytes 884744 | tf_op jit(solution)/shard_map/ppermute | solution.py:1024
  68.0 314.6 %reduce-scatter.2.cloned.1.call-start = ((), (), s32[]{:S(2)}) async-start(), calls=%async_computation.1 | async-start | bytes 9732096 | tf_op jit(solution)/shard_map/reduce_scatter | solution.py:1105
  68.1 5.5 collective-permute-start.6
  69.2 21.5 %collective-permute-start.7 = (bf16[3,192,768]{2,1,0:T(8,128)(2,1)}, bf16[3,192,768]{2,1,0:T(8,128)(2,1)S(1)}, u32[]{:S(2)}, u32[]{:S(2)}) collective-permute-start(bf16[3,192,768]{2,1,0:T(8,128)(2,1)} %pad_maximum_fusion.1), channel_id=1, source_target_pairs={{0,1},{1,0},{2,3},{3,2},{4,5},{5,4},{6,7},{7,6},{8,9},{9,8},{10,11... | collective-permute-start | bytes 2654216 | tf_op jit(solution)/shard_map/ppermute | solution.py:1024
  69.4 48.0 %collective-permute-start.11 = (bf16[1500,384]{1,0:T(8,128)(2,1)}, bf16[1500,384]{1,0:T(8,128)(2,1)}, u32[]{:S(2)}, u32[]{:S(2)}) collective-permute-start(bf16[1500,384]{1,0:T(8,128)(2,1)} %bitcast.58), channel_id=1, source_target_pairs={{1,2},{2,1},{5,6},{6,5},{9,10},{10,9},{13,14},{14,13},{17,18},{18,... | collective-permute-start | bytes 3456008 | tf_op jit(solution)/shard_map/ppermute | solution.py:1041
  90.7 15.2 %collective-permute-start.10 = (bf16[3,192,768]{2,1,0:T(8,128)(2,1)S(1)}, bf16[3,192,768]{2,1,0:T(8,128)(2,1)S(1)}, u32[]{:S(2)}, u32[]{:S(2)}) collective-permute-start(bf16[3,192,768]{2,1,0:T(8,128)(2,1)S(1)} %collective-permute-done.7.refs_7_.refs_10_.o2), channel_id=1, source_target_pairs={{0,2},{2,0},{1,3},{3,1},{4,6},{6,4},{5,7},{7,5},{8,10},{10,8},{9,1... | collective-permute-start | bytes 2654216 | tf_op jit(solution)/shard_map/ppermute | solution.py:1024
  91.5 26.0 %collective-permute-start.12 = (bf16[384,768]{1,0:T(8,128)(2,1)}, bf16[384,768]{1,0:T(8,128)(2,1)}, u32[]{:S(2)}, u32[]{:S(2)}) collective-permute-start(bf16[384,768]{1,0:T(8,128)(2,1)} %dynamic-slice_convert_fusion.1), channel_id=1, source_target_pairs={{0,1},{1,0},{2,3},{3,2},{4,5},{5,4},{6,7},{7,6},{8,9},{9,8},{10,11... | collective-permute-start | bytes 1769480 | tf_op jit(solution)/shard_map/ppermute | solution.py:1024
  92.3 13.6 %collective-permute-start.8 = (bf16[1024,256]{1,0:T(8,128)(2,1)}, bf16[1024,256]{1,0:T(8,128)(2,1)S(1)}, u32[]{:S(2)}, u32[]{:S(2)}) collective-permute-start(bf16[1024,256]{1,0:T(8,128)(2,1)} %get-tuple-element.202), channel_id=1, source_target_pairs={{0,2},{2,0},{1,3},{3,1},{4,6},{6,4},{5,7},{7,5},{8,10},{10,8},{9,1... | collective-permute-start | bytes 1572872 | tf_op jit(solution)/shard_map/ppermute | solution.py:1024
  103.2 61.3 %collective-permute-start.15 = (bf16[1024,768]{1,0:T(8,128)(2,1)}, bf16[1024,768]{1,0:T(8,128)(2,1)}, u32[]{:S(2)}, u32[]{:S(2)}) collective-permute-start(bf16[1024,768]{1,0:T(8,128)(2,1)} %bitcast.24.co), channel_id=1, source_target_pairs={{1,2},{2,1},{5,6},{6,5},{9,10},{10,9},{13,14},{14,13},{17,18},{18,... | collective-permute-start | bytes 4718600 | tf_op jit(solution)/shard_map/ppermute | solution.py:1041
  118.9 3.9 collective-permute-start.13
  118.9 3.8 collective-permute-start.14
  233.6 238.8 %all-gather.9.cloned.1.call-start = ((), (), s32[]{:S(2)}) async-start(), calls=%async_computation.3 | async-start | bytes 5013504 | tf_op jit(solution)/shard_map/all_gather | solution.py:1150
  259.7 36.0 %collective-permute-start.17 = (bf16[2,1536,384]{2,1,0:T(8,128)(2,1)}, bf16[2,1536,384]{2,1,0:T(8,128)(2,1)S(1)}, u32[]{:S(2)}, u32[]{:S(2)}) collective-permute-start(bf16[2,1536,384]{2,1,0:T(8,128)(2,1)} %get-tuple-element.240), channel_id=1, source_target_pairs={{0,2},{2,0},{1,3},{3,1},{4,6},{6,4},{5,7},{7,5},{8,10},{10,8},{9,1... | collective-permute-start | bytes 7077896 | tf_op jit(solution)/shard_map/ppermute | solution.py:1024
  260.0 35.7 %collective-permute-start.18 = (bf16[1024,768]{1,0:T(8,128)(2,1)S(1)}, bf16[1024,768]{1,0:T(8,128)(2,1)}, u32[]{:S(2)}, u32[]{:S(2)}) collective-permute-start(bf16[1024,768]{1,0:T(8,128)(2,1)S(1)} %copy-done.8), channel_id=1, source_target_pairs={{0,2},{2,0},{1,3},{3,1},{4,6},{6,4},{5,7},{7,5},{8,10},{10,8},{9,1... | collective-permute-start | bytes 4718600 | tf_op jit(solution)/shard_map/ppermute | solution.py:1024
  260.2 35.5 %collective-permute-start.16 = (bf16[1024,768]{1,0:T(8,128)(2,1)}, bf16[1024,768]{1,0:T(8,128)(2,1)}, u32[]{:S(2)}, u32[]{:S(2)}) collective-permute-start(bf16[1024,768]{1,0:T(8,128)(2,1)} %get-tuple-element.239), channel_id=1, source_target_pairs={{1,2},{2,1},{5,6},{6,5},{9,10},{10,9},{13,14},{14,13},{17,18},{18,... | collective-permute-start | bytes 4718600 | tf_op jit(solution)/shard_map/ppermute | solution.py:1041
  269.5 26.2 %collective-permute-start.19 = (bf16[2,768,384]{2,1,0:T(8,128)(2,1)}, bf16[2,768,384]{2,1,0:T(8,128)(2,1)}, u32[]{:S(2)}, u32[]{:S(2)}) collective-permute-start(bf16[2,768,384]{2,1,0:T(8,128)(2,1)} %shard_map.264), channel_id=1, source_target_pairs={{0,2},{2,0},{1,3},{3,1},{4,6},{6,4},{5,7},{7,5},{8,10},{10,8},{9,1... | collective-permute-start | bytes 3538952 | tf_op jit(solution)/shard_map/ppermute | solution.py:1024
  307.7 23.2 %collective-permute-start.20 = (bf16[1500,384]{1,0:T(8,128)(2,1)}, bf16[1500,384]{1,0:T(8,128)(2,1)S(1)}, u32[]{:S(2)}, u32[]{:S(2)}) collective-permute-start(bf16[1500,384]{1,0:T(8,128)(2,1)} %get-tuple-element.260), channel_id=1, source_target_pairs={{0,2},{2,0},{1,3},{3,1},{4,6},{6,4},{5,7},{7,5},{8,10},{10,8},{9,1... | collective-permute-start | bytes 3456008 | tf_op jit(solution)/shard_map/ppermute | solution.py:1024
  326.3 15.7 %collective-permute-start.22 = (bf16[1024,384]{1,0:T(8,128)(2,1)}, bf16[1024,384]{1,0:T(8,128)(2,1)S(1)}, u32[]{:S(2)}, u32[]{:S(2)}) collective-permute-start(bf16[1024,384]{1,0:T(8,128)(2,1)} %get-tuple-element.270), channel_id=1, source_target_pairs={{0,2},{2,0},{1,3},{3,1},{4,6},{6,4},{5,7},{7,5},{8,10},{10,8},{9,1... | collective-permute-start | bytes 2359304 | tf_op jit(solution)/shard_map/ppermute | solution.py:1024
  326.4 46.0 %collective-permute-start.23 = (bf16[4,384,384]{2,1,0:T(8,128)(2,1)}, bf16[4,384,384]{2,1,0:T(8,128)(2,1)S(1)}, u32[]{:S(2)}, u32[]{:S(2)}) collective-permute-start(bf16[4,384,384]{2,1,0:T(8,128)(2,1)} %get-tuple-element.277), channel_id=1, source_target_pairs={{0,1},{1,0},{2,3},{3,2},{4,5},{5,4},{6,7},{7,6},{8,9},{9,8},{10,11... | collective-permute-start | bytes 3538952 | tf_op jit(solution)/shard_map/ppermute | solution.py:1024
  331.9 5.8 %collective-permute-start.21 = (bf16[768,384]{1,0:T(8,128)(2,1)}, bf16[768,384]{1,0:T(8,128)(2,1)}, u32[]{:S(2)}, u32[]{:S(2)}) collective-permute-start(bf16[768,384]{1,0:T(8,128)(2,1)} %shard_map.269), channel_id=1, source_target_pairs={{0,2},{2,0},{1,3},{3,1},{4,6},{6,4},{5,7},{7,5},{8,10},{10,8},{9,1... | collective-permute-start | bytes 1769480 | tf_op jit(solution)/shard_map/ppermute | solution.py:1024
  334.2 43.6 %collective-permute-start.26 = (bf16[1500,384]{1,0:T(8,128)(2,1)S(1)}, bf16[1500,384]{1,0:T(8,128)(2,1)}, u32[]{:S(2)}, u32[]{:S(2)}) collective-permute-start(bf16[1500,384]{1,0:T(8,128)(2,1)S(1)} %add_convert_fusion), channel_id=1, source_target_pairs={{1,2},{2,1},{5,6},{6,5},{9,10},{10,9},{13,14},{14,13},{17,18},{18,... | collective-permute-start | bytes 3456008 | tf_op jit(solution)/shard_map/ppermute | solution.py:1041
  357.4 20.3 %collective-permute-start.25 = (bf16[3,1024,128]{2,1,0:T(8,128)(2,1)}, bf16[3,1024,128]{2,1,0:T(8,128)(2,1)S(1)}, u32[]{:S(2)}, u32[]{:S(2)}) collective-permute-start(bf16[3,1024,128]{2,1,0:T(8,128)(2,1)} %get-tuple-element.279.refs_3_), channel_id=1, source_target_pairs={{0,2},{2,0},{1,3},{3,1},{4,6},{6,4},{5,7},{7,5},{8,10},{10,8},{9,1... | collective-permute-start | bytes 2359304 | tf_op jit(solution)/shard_map/ppermute | solution.py:1024
  357.4 20.3 %collective-permute-start.24 = (bf16[1,384,384]{2,1,0:T(8,128)(2,1)S(1)}, bf16[1,384,384]{2,1,0:T(8,128)(2,1)S(1)}, u32[]{:S(2)}, u32[]{:S(2)}) collective-permute-start(bf16[1,384,384]{2,1,0:T(8,128)(2,1)S(1)} %copy-done.49), channel_id=1, source_target_pairs={{0,1},{1,0},{2,3},{3,2},{4,5},{5,4},{6,7},{7,6},{8,9},{9,8},{10,11... | collective-permute-start | bytes 884744 | tf_op jit(solution)/shard_map/ppermute | solution.py:1024
  382.6 138.7 %all-gather.11.cloned.1.call-start = ((), (), s32[]{:S(2)}) async-start(), calls=%async_computation.4 | async-start | bytes 3133440 | tf_op jit(solution)/shard_map/all_gather | solution.py:1168
  383.1 17.1 %collective-permute-start.27 = (bf16[3,1024,128]{2,1,0:T(8,128)(2,1)S(1)}, bf16[3,1024,128]{2,1,0:T(8,128)(2,1)S(1)}, u32[]{:S(2)}, u32[]{:S(2)}) collective-permute-start(bf16[3,1024,128]{2,1,0:T(8,128)(2,1)S(1)} %copy-done.11), channel_id=1, source_target_pairs={{0,2},{2,0},{1,3},{3,1},{4,6},{6,4},{5,7},{7,5},{8,10},{10,8},{9,1... | collective-permute-start | bytes 2359304 | tf_op jit(solution)/shard_map/ppermute | solution.py:1024
  385.4 22.1 %collective-permute-start.28 = (bf16[5,192,384]{2,1,0:T(8,128)(2,1)}, bf16[5,192,384]{2,1,0:T(8,128)(2,1)}, u32[]{:S(2)}, u32[]{:S(2)}) collective-permute-start(bf16[5,192,384]{2,1,0:T(8,128)(2,1)} %get-tuple-element.302), channel_id=1, source_target_pairs={{0,4},{4,0},{1,5},{5,1},{2,6},{6,2},{3,7},{7,3},{8,12},{12,8},{9,1... | collective-permute-start | bytes 2211848 | tf_op jit(solution)/shard_map/ppermute | solution.py:1024
  407.5 29.9 %collective-permute-start.30 = (bf16[3,384,384]{2,1,0:T(8,128)(2,1)}, bf16[3,384,384]{2,1,0:T(8,128)(2,1)S(1)}, u32[]{:S(2)}, u32[]{:S(2)}) collective-permute-start(bf16[3,384,384]{2,1,0:T(8,128)(2,1)} %shard_map.276), channel_id=1, source_target_pairs={{0,1},{1,0},{2,3},{3,2},{4,5},{5,4},{6,7},{7,6},{8,9},{9,8},{10,11... | collective-permute-start | bytes 2654216 | tf_op jit(solution)/shard_map/ppermute | solution.py:1024
  408.3 14.4 %collective-permute-start.29 = (bf16[3,1024,128]{2,1,0:T(8,128)(2,1)S(1)}, bf16[3,1024,128]{2,1,0:T(8,128)(2,1)}, u32[]{:S(2)}, u32[]{:S(2)}) collective-permute-start(bf16[3,1024,128]{2,1,0:T(8,128)(2,1)S(1)} %copy-done.12), channel_id=1, source_target_pairs={{0,2},{2,0},{1,3},{3,1},{4,6},{6,4},{5,7},{7,5},{8,10},{10,8},{9,1... | collective-permute-start | bytes 2359304 | tf_op jit(solution)/shard_map/ppermute | solution.py:1024
  412.3 29.3 %collective-permute-start.31 = (bf16[5,48,384]{2,1,0:T(8,128)(2,1)}, bf16[5,48,384]{2,1,0:T(8,128)(2,1)S(1)}, u32[]{:S(2)}, u32[]{:S(2)}) collective-permute-start(bf16[5,48,384]{2,1,0:T(8,128)(2,1)} %get-tuple-element.324), channel_id=1, source_target_pairs={{0,8},{8,0},{16,24},{24,16},{1,9},{9,1},{17,25},{25,17},{2,10},{10... | collective-permute-start | bytes 552968 | tf_op jit(solution)/shard_map/ppermute | solution.py:1020
  413.1 28.4 %collective-permute-start.32 = (bf16[5,48,384]{2,1,0:T(8,128)(2,1)}, bf16[5,48,384]{2,1,0:T(8,128)(2,1)S(1)}, u32[]{:S(2)}, u32[]{:S(2)}) collective-permute-start(bf16[5,48,384]{2,1,0:T(8,128)(2,1)} %get-tuple-element.325), channel_id=1, source_target_pairs={{0,16},{8,24},{16,0},{24,8},{1,17},{9,25},{17,1},{25,9},{2,18},{10... | collective-permute-start | bytes 552968 | tf_op jit(solution)/shard_map/ppermute | solution.py:1020
  415.6 26.0 %collective-permute-start.33 = (bf16[5,48,384]{2,1,0:T(8,128)(2,1)}, bf16[5,48,384]{2,1,0:T(8,128)(2,1)S(1)}, u32[]{:S(2)}, u32[]{:S(2)}) collective-permute-start(bf16[5,48,384]{2,1,0:T(8,128)(2,1)} %get-tuple-element.326), channel_id=1, source_target_pairs={{0,24},{8,16},{16,8},{24,0},{1,25},{9,17},{17,9},{25,1},{2,26},{10... | collective-permute-start | bytes 552968 | tf_op jit(solution)/shard_map/ppermute | solution.py:1020
  445.0 11.2 %collective-permute-start.34 = (bf16[3,192,384]{2,1,0:T(8,128)(2,1)}, bf16[3,192,384]{2,1,0:T(8,128)(2,1)S(1)}, u32[]{:S(2)}, u32[]{:S(2)}) collective-permute-start(bf16[3,192,384]{2,1,0:T(8,128)(2,1)} %get-tuple-element.327), channel_id=1, source_target_pairs={{0,4},{4,0},{1,5},{5,1},{2,6},{6,2},{3,7},{7,3},{8,12},{12,8},{9,1... | collective-permute-start | bytes 1327112 | tf_op jit(solution)/shard_map/ppermute | solution.py:1024
  445.2 73.4 %collective-permute-start.43 = (bf16[1024,768]{1,0:T(8,128)(2,1)}, bf16[1024,768]{1,0:T(8,128)(2,1)}, u32[]{:S(2)}, u32[]{:S(2)}) collective-permute-start(bf16[1024,768]{1,0:T(8,128)(2,1)} %get-tuple-element.349), channel_id=1, source_target_pairs={{1,2},{2,1},{5,6},{6,5},{9,10},{10,9},{13,14},{14,13},{17,18},{18,... | collective-permute-start | bytes 4718600 | tf_op jit(solution)/shard_map/ppermute | solution.py:1041
  449.5 31.7 %collective-permute-start.38 = (f32[24,384]{1,0:T(8,128)S(1)}, f32[24,384]{1,0:T(8,128)S(1)}, u32[]{:S(2)}, u32[]{:S(2)}) collective-permute-start(f32[24,384]{1,0:T(8,128)S(1)} %copy-done.50), channel_id=1, source_target_pairs={{0,1},{1,0},{2,3},{3,2},{4,5},{5,4},{6,7},{7,6},{8,9},{9,8},{10,11... | collective-permute-start | bytes 110600 | tf_op jit(solution)/shard_map/ppermute | solution.py:1024
  459.5 19.9 %collective-permute-start.35 = (bf16[3,48,384]{2,1,0:T(8,128)(2,1)}, bf16[3,48,384]{2,1,0:T(8,128)(2,1)S(1)}, u32[]{:S(2)}, u32[]{:S(2)}) collective-permute-start(bf16[3,48,384]{2,1,0:T(8,128)(2,1)} %get-tuple-element.329), channel_id=1, source_target_pairs={{0,8},{8,0},{16,24},{24,16},{1,9},{9,1},{17,25},{25,17},{2,10},{10... | collective-permute-start | bytes 331784 | tf_op jit(solution)/shard_map/ppermute | solution.py:1020
  466.9 12.5 %collective-permute-start.36 = (bf16[3,48,384]{2,1,0:T(8,128)(2,1)}, bf16[3,48,384]{2,1,0:T(8,128)(2,1)S(1)}, u32[]{:S(2)}, u32[]{:S(2)}) collective-permute-start(bf16[3,48,384]{2,1,0:T(8,128)(2,1)} %get-tuple-element.330), channel_id=1, source_target_pairs={{0,16},{8,24},{16,0},{24,8},{1,17},{9,25},{17,1},{25,9},{2,18},{10... | collective-permute-start | bytes 331784 | tf_op jit(solution)/shard_map/ppermute | solution.py:1020
  468.4 12.8 %collective-permute-start.37 = (bf16[3,48,384]{2,1,0:T(8,128)(2,1)}, bf16[3,48,384]{2,1,0:T(8,128)(2,1)S(1)}, u32[]{:S(2)}, u32[]{:S(2)}) collective-permute-start(bf16[3,48,384]{2,1,0:T(8,128)(2,1)} %get-tuple-element.331), channel_id=1, source_target_pairs={{0,24},{8,16},{16,8},{24,0},{1,25},{9,17},{17,9},{25,1},{2,26},{10... | collective-permute-start | bytes 331784 | tf_op jit(solution)/shard_map/ppermute | solution.py:1020
  485.0 8.6 %collective-permute-start.41 = (bf16[4,48,384]{2,1,0:T(8,128)(2,1)}, bf16[4,48,384]{2,1,0:T(8,128)(2,1)S(1)}, u32[]{:S(2)}, u32[]{:S(2)}) collective-permute-start(bf16[4,48,384]{2,1,0:T(8,128)(2,1)} %shard_map.283.p0), channel_id=1, source_target_pairs={{0,24},{8,16},{16,8},{24,0},{1,25},{9,17},{17,9},{25,1},{2,26},{10... | collective-permute-start | bytes 442376 | tf_op jit(solution)/shard_map/ppermute | solution.py:1020
  487.1 26.9 %collective-permute-start.40 = (bf16[4,48,384]{2,1,0:T(8,128)(2,1)}, bf16[4,48,384]{2,1,0:T(8,128)(2,1)S(1)}, u32[]{:S(2)}, u32[]{:S(2)}) collective-permute-start(bf16[4,48,384]{2,1,0:T(8,128)(2,1)} %shard_map.283.p0), channel_id=1, source_target_pairs={{0,16},{8,24},{16,0},{24,8},{1,17},{9,25},{17,1},{25,9},{2,18},{10... | collective-permute-start | bytes 442376 | tf_op jit(solution)/shard_map/ppermute | solution.py:1020
  488.6 25.5 %collective-permute-start.39 = (bf16[4,48,384]{2,1,0:T(8,128)(2,1)}, bf16[4,48,384]{2,1,0:T(8,128)(2,1)S(1)}, u32[]{:S(2)}, u32[]{:S(2)}) collective-permute-start(bf16[4,48,384]{2,1,0:T(8,128)(2,1)} %shard_map.283.p0), channel_id=1, source_target_pairs={{0,8},{8,0},{16,24},{24,16},{1,9},{9,1},{17,25},{25,17},{2,10},{10... | collective-permute-start | bytes 442376 | tf_op jit(solution)/shard_map/ppermute | solution.py:1020
  518.0 14.7 %collective-permute-start.42 = (bf16[4,192,384]{2,1,0:T(8,128)(2,1)}, bf16[4,192,384]{2,1,0:T(8,128)(2,1)S(1)}, u32[]{:S(2)}, u32[]{:S(2)}) collective-permute-start(bf16[4,192,384]{2,1,0:T(8,128)(2,1)} %shard_map.284.refs_0_), channel_id=1, source_target_pairs={{0,4},{4,0},{1,5},{5,1},{2,6},{6,2},{3,7},{7,3},{8,12},{12,8},{9,1... | collective-permute-start | bytes 1769480 | tf_op jit(solution)/shard_map/ppermute | solution.py:1024
  526.6 7.4 %collective-permute-start.44 = (bf16[4,192,384]{2,1,0:T(8,128)(2,1)S(1)}, bf16[4,192,384]{2,1,0:T(8,128)(2,1)S(1)}, u32[]{:S(2)}, u32[]{:S(2)}) collective-permute-start(bf16[4,192,384]{2,1,0:T(8,128)(2,1)S(1)} %copy-done.19), channel_id=1, source_target_pairs={{0,2},{2,0},{1,3},{3,1},{4,6},{6,4},{5,7},{7,5},{8,10},{10,8},{9,1... | collective-permute-start | bytes 1769480 | tf_op jit(solution)/shard_map/ppermute | solution.py:1024
  (55 other events, 298.8 us)
Sparse Core Ops, SparseCore 0:
  68.1 55.4 all-gather.6
  233.7 141.8 reduce-scatter.1
  382.7 71.0 all-gather.8
  456.6 58.7 all-gather.10

commit v5 on v4

--- a/solution.py
+++ b/solution.py
@@ -1126,8 +1126,6 @@
     so_give, fr_in, fkeep = tie(so_give, fr_in, fkeep)
     so_in = sibling(so_give)
     fr_own = (fkeep.astype(f32) + fr_in.astype(f32)).astype(bf16)
-    fr_own, dctx_keep = tie(fr_own, dctx_keep)
-    fr_swapped = swap(fr_own)
     so_xgive, so_xkeep = keep_grad_out(s, ctx, ctx_in, d1, so_in)
     so_xgive, dctx_keep = tie(so_xgive, dctx_keep)
     so_x = across(so_xgive, "x")
@@ -1142,7 +1140,8 @@
     bg1, bk1, keep = tie(bg1, bk1, keep)
     bi1 = sibling(bg1)
     bg2, bk2 = self_bwd(1, 1, 1, c, keep, recv, ctx_a, dctx_keep, dctx_in, lse_a, kmark, qmark)
-    bg2, bk2, got_x, so_x, keep, bi1, fr_swapped = tie(bg2, bk2, got_x, so_x, keep, bi1, fr_swapped)
+    bg2, bk2, got_x, so_x, keep, bi1, fr_own = tie(bg2, bk2, got_x, so_x, keep, bi1, fr_own)
+    fr_swapped = swap(fr_own)
     bi2 = sibling(bg2)
     m_ygive, m_ykeep = split_y(s, (xkeep, so_xkeep), (got_x, so_x))
     m_ygive, keep, ff_mine = tie(m_ygive, keep, ff_mine)
@@ -1152,7 +1151,7 @@
     bg3, bk3, bi2 = tie(bg3, bk3, bi2)
     bi3 = sibling(bg3)
     q_xgive = qkv_grad(s, a1, a1_sib, (bk1, bk2, bk3), (bg1, bg2, bg3), False)
-    q_xgive, m_y = tie(q_xgive, m_y)
+    q_xgive, m_y, fr_swapped = tie(q_xgive, m_y, fr_swapped)
     q_x = across(q_xgive, "x")
     m_z = split_z(s, m_ykeep, m_y)
     bk3, dh1, *m_z = tie(bk3, dh1, *m_z)
@@ -1163,12 +1162,14 @@
     v_got = across(v_give, "x")
     v_mine, q_x = tie(v_mine, q_x)
     q_ygive, q_ykeep = split_y(s, (q_xkeep,), (q_x,))
-    q_ygive, grad_hidden, *m_z = tie(q_ygive, grad_hidden, *m_z)
-    m_piece = sum_four(s, m_z)
-    m_got = lax.all_gather(m_piece, REP2, axis=0, tiled=False)
+    q_ygive, grad_hidden = tie(q_ygive, grad_hidden)
     q_y = across(q_ygive, "y")
     hid_in = swap(grad_hidden)
     q_four = split_z(s, q_ykeep, q_y)
+    q_first, *m_z = tie(q_four[0], *m_z)
+    q_four = (q_first, *q_four[1:])
+    m_piece = sum_four(s, m_z)
+    m_got = lax.all_gather(m_piece, REP2, axis=0, tiled=False)
     q_z = send_z(q_four)
     fc1_grad, fc2_grad = spread_ff(s, ff_got.reshape(reps, 2, per, width))
     output = jnp.where(stay, out, out_in)

time: 555 us -> 547 us (0.986)
  transfers between devices with their start and end apart: 50 -> 50, of which waited for: 13 -> 14; matrix products, arithmetic and copies ran while one was open for 6% -> 6% of each run, Pallas kernels for 52% -> 53%
where the time goes in v5:
time: 547 us; the launch traced here: 539 us
  Pallas kernels  360 us (66%)
  waiting for transfers between devices  60.4 us (11%)
  starting transfers between devices  54.8 us (10%)
  local copies, waits for them, and re-layouts  27.1 us (5%)
  other arithmetic  22.4 us (4%)
  between operations  14.7 us (3%)
    pallas_call x34, Pallas kernels, call(): pl.pallas_call(kernel, grid_spec=spec, out_shape=out_shape, cost_estimate...  360 us
    ppermute x30, waiting for transfers between devices, across(): return lax.ppermute(x, axis, FLIP)  24.6 us
    ppermute x7, starting transfers between devices, swap(): return lax.ppermute(x, ('core', 'x'), SWAP)  24.4 us
    ppermute x9, waiting for transfers between devices, across_z(): return lax.ppermute(x, 'z', [(j, j ^ d) for j in range(4)])  20.9 us
    ppermute x30, starting transfers between devices, across(): return lax.ppermute(x, axis, FLIP)  16.3 us
    ppermute x7, waiting for transfers between devices, swap(): return lax.ppermute(x, ('core', 'x'), SWAP)  14.8 us
    unnamed x106, local copies, waits for them, and re-layouts  14.5 us
    ppermute x9, starting transfers between devices, across_z(): return lax.ppermute(x, 'z', [(j, j ^ d) for j in range(4)])  13.9 us
  transfers between devices with their start and end apart: 50, of which 14 were waited for; matrix products, arithmetic and copies ran while one was open for 6% of the time, Pallas kernels for 53%

profile of v5, /device:TPU:1, one launch (start us, length us, event | category | flops | bytes accessed | tf_op | source)
XLA Modules:
  0.0 539.5 jit_solution(11384126814975892694)
XLA Ops:
  7.3 4.6 collective-permute-start.1
  22.7 2.8 convert.51
  41.1 14.8 %collective-permute-done.xi.refs_5_.refs_7_ = bf16[1024,768]{1,0:T(8,128)(2,1)S(1)} collective-permute-done((bf16[1024,768]{1,0:T(8,128)(2,1)S(1)}, bf16[1024,768]{1,0:T(8,128)(2,1)S(1)}, u32[]{:S(2)}, u32[]{:S(2)}) %collective-permute-start) | collective-permute-done | bytes 1572896 | tf_op jit(solution)/shard_map/ppermute | solution.py:1041
  57.0 10.2 %shard_map.254 = (bf16[768,2304]{1,0:T(8,128)(2,1)}, bf16[1024,768]{1,0:T(8,128)(2,1)}, bf16[3,1024,384]{2,1,0:T(8,128)(2,1)}, bf16[3,1024,384]{2,1,0:T(8,128)(2,1)}) custom-call(s32[9]{0:T(128)} %stack.72.s_ref, bf16[1024,768]{1,0:T(8,128)(2,1)} %bitcast.43, bf16[1024,768]{1,0:T(8,128)(2,1)} %copy-done.2, f32[384,2304]{1,0:T(8,128)} %own.2, ...), custom_call_target="tpu_custom_call" | custom-call | flops 362387872 | bytes 1048576 | tf_op jit(solution)/shard_map/pallas_call | solution.py:41
  69.4 3.6 collective-permute-start.11
  75.0 15.6 %shard_map.255 = (bf16[2048,256]{1,0:T(8,128)(2,1)}, bf16[1024,256]{1,0:T(8,128)(2,1)}, f32[2,8,2048]{2,1,0:T(8,128)}) custom-call(s32[1]{0:T(128)} %bitcast.s_ref, bf16[3,1024,384]{2,1,0:T(8,128)(2,1)} %get-tuple-element.291.a_ref, bf16[3,1024,384]{2,1,0:T(8,128)(2,1)} %copy-done, bf16[2048,128]{1,0:T(8,128)(2,1)} %get-tuple-element.194.km_ref, ...), custom_call_target="tpu_custom_call" | custom-call | flops 858993472 | bytes 1048576 | tf_op jit(solution)/shard_map/pallas_call | solution.py:41
  92.5 8.9 %shard_map.256 = (bf16[2048,128]{1,0:T(8,128)(2,1)}, bf16[1024,128]{1,0:T(8,128)(2,1)}, f32[1,8,2048]{2,1,0:T(8,128)}) custom-call(s32[1]{0:T(128)} %bitcast.s_ref, bf16[3,1024,384]{2,1,0:T(8,128)(2,1)} %get-tuple-element.291.a_ref, bf16[3,1024,384]{2,1,0:T(8,128)(2,1)} %copy-done, bf16[2048,128]{1,0:T(8,128)(2,1)} %get-tuple-element.194.km_ref, ...), custom_call_target="tpu_custom_call" | custom-call | flops 429496736 | bytes 1048576 | tf_op jit(solution)/shard_map/pallas_call | solution.py:41
  103.2 2.7 collective-permute-start.15
  106.9 10.5 %shard_map.257 = (bf16[768,768]{1,0:T(8,128)(2,1)}, bf16[768,768]{1,0:T(8,128)(2,1)}, f32[1024,768]{1,0:T(8,128)}, bf16[1024,768]{1,0:T(8,128)(2,1)}, bf16[1024,768]{1,0:T(8,128)(2,1)}) custom-call(s32[9]{0:T(128)} %stack.72.s_ref, bf16[2048,256]{1,0:T(8,128)(2,1)} %get-tuple-element.196.refs_0_.o_ref, bf16[2048,128]{1,0:T(8,128)(2,1)} %get-tuple-element.201.refs_1_.o_ref, ...), custom_call_target="tpu_custom_call" | custom-call | flops 241591904 | bytes 1048576 | tf_op jit(solution)/shard_map/pallas_call | solution.py:41
  120.1 2.7 collective-permute-done.14.sib
  124.6 10.2 %shard_map.258 = (bf16[1536,768]{1,0:T(8,128)(2,1)}, bf16[1536,768]{1,0:T(8,128)(2,1)}, bf16[1536,768]{1,0:T(8,128)(2,1)}) custom-call(s32[9]{0:T(128)} %stack.72.s_ref, bf16[1500,384]{1,0:T(8,128)(2,1)} %copy-done.3, bf16[1500,384]{1,0:T(8,128)(2,1)} %copy-done.10, f32[768,768]{1,0:T(8,128)} %own.3, bf16[384,768]{1,0:T(8,128)(2,1)} %collective-permute-done.12.mine, ...), custom_call_target="tpu_custom_call" | custom-call | flops 353894400 | bytes 1048576 | tf_op jit(solution)/shard_map/pallas_call | solution.py:41
  134.8 14.8 %shard_map.260 = (bf16[1024,384]{1,0:T(8,128)(2,1)}, f32[3,8,1024]{2,1,0:T(8,128)}) custom-call(s32[1]{0:T(128)} %bitcast.23.s_ref, bf16[1024,768]{1,0:T(8,128)(2,1)} %get-tuple-element.208.q_ref, bf16[1536,768]{1,0:T(8,128)(2,1)} %get-tuple-element.211.k_ref, bf16[1536,768]{1,0:T(8,128)(2,1)} %get-tuple-element.212.v_ref), custom_call_target="tpu_custom_call" | custom-call | flops 483183808 | bytes 1048576 | tf_op jit(solution)/shard_map/pallas_call | solution.py:41
  149.6 14.8 %shard_map.259 = (bf16[1024,384]{1,0:T(8,128)(2,1)}, f32[3,8,1024]{2,1,0:T(8,128)}) custom-call(s32[1]{0:T(128)} %bitcast.8.s_ref, bf16[1024,768]{1,0:T(8,128)(2,1)} %get-tuple-element.208.q_ref, bf16[1536,768]{1,0:T(8,128)(2,1)} %get-tuple-element.211.k_ref, bf16[1536,768]{1,0:T(8,128)(2,1)} %get-tuple-element.212.v_ref), custom_call_target="tpu_custom_call" | custom-call | flops 483183808 | bytes 1048576 | tf_op jit(solution)/shard_map/pallas_call | solution.py:41
  164.5 51.7 %shard_map.261 = (bf16[768,768]{1,0:T(8,128)(2,1)}, bf16[1024,768]{1,0:T(8,128)(2,1)}, bf16[1024,768]{1,0:T(8,128)(2,1)}, bf16[1024,3072]{1,0:T(8,128)(2,1)}, bf...) custom-call(s32[9]{0:T(128)} %stack.72.s_ref, ...), custom_call_target="tpu_custom_call" | custom-call | flops 2174327296 | bytes 1048576 | tf_op jit(solution)/shard_map/pallas_call | solution.py:41
  216.2 17.4 %shard_map.262 = bf16[2,16,2,96,768]{4,3,2,1,0:T(8,128)(2,1)} custom-call(s32[9]{0:T(128)} %stack.72.s_ref, bf16[1024,768]{1,0:T(8,128)(2,1)} %get-tuple-element.223.a_ref, bf16[1024,3072]{1,0:T(8,128)(2,1)} %get-tuple-element.224.du_ref, bf16[1024,3072]{1,0:T(8,128)(2,1)} %get-tuple-element.225.g0.g1, bf16[1024,3072]{1,0:T(8,128)(2,1)} %get-tuple-element.225.g0.g1, ...), custom_call_target="tpu_custom_call" | custom-call | flops 966367616 | bytes 1048576 | tf_op jit(solution)/shard_map/pallas_call | solution.py:41
  233.7 26.0 %shard_map.263 = (bf16[1024,384]{1,0:T(8,128)(2,1)}, bf16[2,1536,384]{2,1,0:T(8,128)(2,1)}) custom-call(s32[1]{0:T(128)} %bitcast.23.s_ref, bf16[1024,768]{1,0:T(8,128)(2,1)} %get-tuple-element.208.q_ref, bf16[1536,768]{1,0:T(8,128)(2,1)} %get-tuple-element.211.k_ref, bf16[1536,768]{1,0:T(8,128)(2,1)} %get-tuple-element.212.v_ref, ...), custom_call_target="tpu_custom_call" | custom-call | flops 2415919104 | bytes 1048576 | tf_op jit(solution)/shard_map/pallas_call | solution.py:41
  260.2 3.4 collective-permute-start.16
  263.6 5.9 %shard_map.264 = bf16[2,768,384]{2,1,0:T(8,128)(2,1)} custom-call(s32[9]{0:T(128)} %stack.72.s_ref, bf16[1024,384]{1,0:T(8,128)(2,1)} %get-tuple-element.213.ck_ref.k_ref.o_ref.ck, bf16[1024,384]{1,0:T(8,128)(2,1)} %get-tuple-element.214.cg_ref.o_ref.g_ref.cg, bf16[1024,768]{1,0:T(8,128)(2,1)} %get-tuple-element.220.d_ref.d2_ref, ...), custom_call_target="tpu_custom_call" | custom-call | flops 120795952 | bytes 1048576 | tf_op jit(solution)/shard_map/pallas_call | solution.py:41
  269.5 26.2 %shard_map.265 = (bf16[1024,384]{1,0:T(8,128)(2,1)}, bf16[2,1536,384]{2,1,0:T(8,128)(2,1)}) custom-call(s32[1]{0:T(128)} %bitcast.8.s_ref, bf16[1024,768]{1,0:T(8,128)(2,1)} %get-tuple-element.208.q_ref, bf16[1536,768]{1,0:T(8,128)(2,1)} %get-tuple-element.211.k_ref, bf16[1536,768]{1,0:T(8,128)(2,1)} %get-tuple-element.212.v_ref, ...), custom_call_target="tpu_custom_call" | custom-call | flops 2415919104 | bytes 1048576 | tf_op jit(solution)/shard_map/pallas_call | solution.py:41
  297.1 10.5 %shard_map.266 = (bf16[1500,384]{1,0:T(8,128)(2,1)}, bf16[1500,384]{1,0:T(8,128)(2,1)}, bf16[768,384]{1,0:T(8,128)(2,1)}, bf16[768,384]{1,0:T(8,128)(2,1)}, f32[8,384]{1,0:T(8,128)}) custom-call(s32[9]{0:T(128)} %stack.72.s_ref, bf16[2,1536,384]{2,1,0:T(8,128)(2,1)} %get-tuple-element.237.ka, bf16[2,1536,384]{2,1,0:T(8,128)(2,1)} %copy-done.17, ...), custom_call_target="tpu_custom_call" | custom-call | flops 707788800 | bytes 1048576 | tf_op jit(solution)/shard_map/pallas_call | solution.py:41
  308.2 7.1 %shard_map.267 = (bf16[4,384,384]{2,1,0:T(8,128)(2,1)}, bf16[4,384,384]{2,1,0:T(8,128)(2,1)}) custom-call(s32[9]{0:T(128)} %stack.72.s_ref, bf16[1024,384]{1,0:T(8,128)(2,1)} %get-tuple-element.213.ck_ref.k_ref.o_ref.ck, bf16[1024,384]{1,0:T(8,128)(2,1)} %get-tuple-element.214.cg_ref.o_ref.g_ref.cg, bf16[1024,768]{1,0:T(8,128)(2,1)} %get-tuple-element.220.d_ref.d2_ref, ...), custom_call_target="tpu_custom_call" | custom-call | flops 120795952 | bytes 1048576 | tf_op jit(solution)/shard_map/pallas_call | solution.py:41
  315.3 11.1 %shard_map.268 = (f32[1024,768]{1,0:T(8,128)}, bf16[1024,768]{1,0:T(8,128)(2,1)}, bf16[1024,384]{1,0:T(8,128)(2,1)}, bf16[1024,384]{1,0:T(8,128)(2,1)}, f32[8,768]{1,0:T(8,128)}) custom-call(s32[9]{0:T(128)} %stack.72.s_ref, bf16[1024,384]{1,0:T(8,128)(2,1)} %get-tuple-element.253.q_ref.dk_ref, bf16[1024,384]{1,0:T(8,128)(2,1)} %get-tuple-element.233.q_ref.dg_ref, ...), custom_call_target="tpu_custom_call" | custom-call | flops 241591904 | bytes 1048576 | tf_op jit(solution)/shard_map/pallas_call | solution.py:41
  326.6 4.2 shard_map.269
  333.2 4.3 shard_map.270
  338.4 15.0 %shard_map.271 = (bf16[3,1024,128]{2,1,0:T(8,128)(2,1)}, bf16[3,1024,128]{2,1,0:T(8,128)(2,1)}) custom-call(s32[1]{0:T(128)} %bitcast.s_ref, bf16[3,1024,384]{2,1,0:T(8,128)(2,1)} %get-tuple-element.291.a_ref, bf16[3,1024,384]{2,1,0:T(8,128)(2,1)} %copy-done, bf16[2048,256]{1,0:T(8,128)(2,1)} %get-tuple-element.196.refs_0_.o_ref, ...), custom_call_target="tpu_custom_call" | custom-call | flops 858993472 | bytes 1048576 | tf_op jit(solution)/shard_map/pallas_call | solution.py:41
  355.7 14.7 %shard_map.272 = (bf16[3,1024,128]{2,1,0:T(8,128)(2,1)}, bf16[3,1024,128]{2,1,0:T(8,128)(2,1)}) custom-call(s32[1]{0:T(128)} %bitcast.s_ref, bf16[3,1024,384]{2,1,0:T(8,128)(2,1)} %get-tuple-element.291.a_ref, bf16[3,1024,384]{2,1,0:T(8,128)(2,1)} %copy-done, bf16[2048,256]{1,0:T(8,128)(2,1)} %get-tuple-element.196.refs_0_.o_ref, ...), custom_call_target="tpu_custom_call" | custom-call | flops 858993472 | bytes 1048576 | tf_op jit(solution)/shard_map/pallas_call | solution.py:41
  372.6 3.9 shard_map.273
  376.5 3.1 collective-permute-start.28
  381.0 14.5 %shard_map.275 = (bf16[3,1024,128]{2,1,0:T(8,128)(2,1)}, bf16[3,1024,128]{2,1,0:T(8,128)(2,1)}) custom-call(s32[1]{0:T(128)} %bitcast.s_ref, bf16[3,1024,384]{2,1,0:T(8,128)(2,1)} %get-tuple-element.291.a_ref, bf16[3,1024,384]{2,1,0:T(8,128)(2,1)} %copy-done, bf16[2048,128]{1,0:T(8,128)(2,1)} %get-tuple-element.201.refs_1_.o_ref, ...), custom_call_target="tpu_custom_call" | custom-call | flops 858993472 | bytes 1048576 | tf_op jit(solution)/shard_map/pallas_call | solution.py:41
  395.5 7.3 %shard_map.276 = bf16[3,384,384]{2,1,0:T(8,128)(2,1)} custom-call(s32[9]{0:T(128)} %stack.72.s_ref, bf16[1024,768]{1,0:T(8,128)(2,1)} %get-tuple-element.241.ao, bf16[1024,768]{1,0:T(8,128)(2,1)} %collective-permute-done.18.ai, bf16[3,1024,128]{2,1,0:T(8,128)(2,1)} %get-tuple-element.289.refs_0_, bf16[3,1024,128]{2,1,0:T(8,128)(2,1)} %get-tuple-element.290.refs_1_, ...), custom_call_target="tpu_custom_call" | custom-call | flops 181193936 | bytes 1048576 | tf_op jit(solution)/shard_map/pallas_call | solution.py:41
  403.7 2.9 shard_map.277
  406.6 7.4 %shard_map.278.refs_0_ = bf16[3,384,384]{2,1,0:T(8,128)(2,1)} custom-call(s32[9]{0:T(128)} %stack.72.s_ref, bf16[1024,768]{1,0:T(8,128)(2,1)} %get-tuple-element.241.ao, bf16[1024,768]{1,0:T(8,128)(2,1)} %collective-permute-done.18.ai, bf16[3,1024,128]{2,1,0:T(8,128)(2,1)} %get-tuple-element.289.refs_0_, bf16[3,1024,128]{2,1,0:T(8,128)(2,1)} %get-tuple-element.290.refs_1_, ...), custom_call_target="tpu_custom_call" | custom-call | flops 181193936 | bytes 1048576 | tf_op jit(solution)/shard_map/pallas_call | solution.py:41
  414.0 12.3 %shard_map.279 = (bf16[1024,768]{1,0:T(8,128)(2,1)}, f32[8,768]{1,0:T(8,128)}) custom-call(s32[9]{0:T(128)} %stack.72.s_ref, bf16[3,1024,128]{2,1,0:T(8,128)(2,1)} %get-tuple-element.289.refs_0_, bf16[3,1024,128]{2,1,0:T(8,128)(2,1)} %get-tuple-element.290.refs_1_, bf16[3,1024,128]{2,1,0:T(8,128)(2,1)} %get-tuple-element.307.refs_2_, ...), custom_call_target="tpu_custom_call" | custom-call | flops 362387872 | bytes 1048576 | tf_op jit(solution)/shard_map/pallas_call | solution.py:41
  428.7 3.2 shard_map.281
  435.8 8.3 %collective-permute-done.31.g_ref = bf16[3,192,384]{2,1,0:T(8,128)(2,1)S(1)} collective-permute-done((bf16[3,192,384]{2,1,0:T(8,128)(2,1)}, bf16[3,192,384]{2,1,0:T(8,128)(2,1)S(1)}, u32[]{:S(2)}, u32[]{:S(2)}) %collective-permute-start.31) | collective-permute-done | bytes 442400 | tf_op jit(solution)/shard_map/ppermute | solution.py:1024
  449.3 2.6 shard_map.285
  452.0 4.5 collective-permute-start.43
  456.6 3.4 collective-permute-start.35
  462.2 2.8 broadcast_select_fusion.1
  465.0 7.0 %shard_map.274 = (f32[384,3072]{1,0:T(8,128)}, f32[1536,768]{1,0:T(8,128)}) custom-call(s32[9]{0:T(128)} %stack.72.s_ref, bf16[16,2,96,768]{3,2,1,0:T(8,128)(2,1)} %bitcast.53), custom_call_target="tpu_custom_call" | custom-call | tf_op jit(solution)/shard_map/pallas_call | solution.py:41
  472.1 2.7 collective-permute-done.38.refs_1_
  485.0 19.7 %collective-permute-done.40.p2 = bf16[4,48,384]{2,1,0:T(8,128)(2,1)S(1)} collective-permute-done((bf16[4,48,384]{2,1,0:T(8,128)(2,1)}, bf16[4,48,384]{2,1,0:T(8,128)(2,1)S(1)}, u32[]{:S(2)}, u32[]{:S(2)}) %collective-permute-start.40) | collective-permute-done | bytes 147488 | tf_op jit(solution)/shard_map/ppermute | solution.py:1020
  506.0 2.7 shard_map.284.refs_0_
  509.7 2.8 broadcast_select_fusion
  512.5 5.3 shard_map.286
  518.9 2.8 collective-permute-done.42.refs_1_
  521.7 3.0 collective-permute-start.45
  527.1 4.3 shard_map.287
  (237 shorter events, 84.5 us)
Async XLA Ops:
  7.2 157.2 %all-gather.7.cloned.1.call-start = ((), (), s32[]{:S(2)}) async-start(), calls=%async_computation.2 | async-start | bytes 5013504 | tf_op jit(solution)/shard_map/all_gather | solution.py:1076
  7.3 30.2 %collective-permute-start.1 = (s32[1,2048]{1,0:T(1,128)}, s32[1,2048]{1,0:T(1,128)S(1)}, u32[]{:S(2)}, u32[]{:S(2)}) collective-permute-start(s32[1,2048]{1,0:T(1,128)} %param.17), channel_id=1, source_target_pairs={{1,2},{2,1},{5,6},{6,5},{9,10},{10,9},{13,14},{14,13},{17,18},{18,... | collective-permute-start | bytes 24584 | tf_op jit(solution)/shard_map/ppermute | solution.py:1041
  14.9 26.2 %collective-permute-start.4 = (bf16[20,384]{1,0:T(8,128)(2,1)S(1)}, bf16[20,384]{1,0:T(8,128)(2,1)S(1)}, u32[]{:S(2)}, u32[]{:S(2)}) collective-permute-start(bf16[20,384]{1,0:T(8,128)(2,1)S(1)} %concatenate.35), channel_id=1, source_target_pairs={{0,1},{1,0},{2,3},{3,2},{4,5},{5,4},{6,7},{7,6},{8,9},{9,8},{10,11... | collective-permute-start | bytes 46088 | tf_op jit(solution)/shard_map/ppermute | solution.py:1024
  17.4 21.2 %collective-permute-start.2 = (bf16[192,2304]{1,0:T(8,128)(2,1)}, bf16[192,2304]{1,0:T(8,128)(2,1)}, u32[]{:S(2)}, u32[]{:S(2)}) collective-permute-start(bf16[192,2304]{1,0:T(8,128)(2,1)} %dynamic-slice_convert_fusion), channel_id=1, source_target_pairs={{0,1},{1,0},{2,3},{3,2},{4,5},{5,4},{6,7},{7,6},{8,9},{9,8},{10,11... | collective-permute-start | bytes 2654216 | tf_op jit(solution)/shard_map/ppermute | solution.py:1024
  18.9 37.0 %collective-permute-start = (bf16[1024,768]{1,0:T(8,128)(2,1)S(1)}, bf16[1024,768]{1,0:T(8,128)(2,1)S(1)}, u32[]{:S(2)}, u32[]{:S(2)}) collective-permute-start(bf16[1024,768]{1,0:T(8,128)(2,1)S(1)} %bitcast.46), channel_id=1, source_target_pairs={{1,2},{2,1},{5,6},{6,5},{9,10},{10,9},{13,14},{14,13},{17,18},{18,... | collective-permute-start | bytes 4718600 | tf_op jit(solution)/shard_map/ppermute | solution.py:1041
  38.6 18.0 %collective-permute-start.3 = (bf16[192,2304]{1,0:T(8,128)(2,1)}, bf16[192,2304]{1,0:T(8,128)(2,1)}, u32[]{:S(2)}, u32[]{:S(2)}) collective-permute-start(bf16[192,2304]{1,0:T(8,128)(2,1)} %collective-permute-done.2.mine), channel_id=1, source_target_pairs={{0,2},{2,0},{1,3},{3,1},{4,6},{6,4},{5,7},{7,5},{8,10},{10,8},{9,1... | collective-permute-start | bytes 2654216 | tf_op jit(solution)/shard_map/ppermute | solution.py:1024
  55.9 11.4 %collective-permute-start.5 = (bf16[2,96,768]{2,1,0:T(8,128)(2,1)}, bf16[2,96,768]{2,1,0:T(8,128)(2,1)S(1)}, u32[]{:S(2)}, u32[]{:S(2)}) collective-permute-start(bf16[2,96,768]{2,1,0:T(8,128)(2,1)} %pad_maximum_fusion.2), channel_id=1, source_target_pairs={{0,1},{1,0},{2,3},{3,2},{4,5},{5,4},{6,7},{7,6},{8,9},{9,8},{10,11... | collective-permute-start | bytes 884744 | tf_op jit(solution)/shard_map/ppermute | solution.py:1024
  68.0 308.4 %reduce-scatter.2.cloned.1.call-start = ((), (), s32[]{:S(2)}) async-start(), calls=%async_computation.1 | async-start | bytes 9732096 | tf_op jit(solution)/shard_map/reduce_scatter | solution.py:1105
  68.1 5.5 %collective-permute-start.6 = (bf16[3,1024,384]{2,1,0:T(8,128)(2,1)}, bf16[3,1024,384]{2,1,0:T(8,128)(2,1)S(1)}, u32[]{:S(2)}, u32[]{:S(2)}) collective-permute-start(bf16[3,1024,384]{2,1,0:T(8,128)(2,1)} %get-tuple-element.193), channel_id=1, source_target_pairs={{0,2},{2,0},{1,3},{3,1},{4,6},{6,4},{5,7},{7,5},{8,10},{10,8},{9,1... | collective-permute-start | bytes 7077896 | tf_op jit(solution)/shard_map/ppermute | solution.py:1024
  69.2 21.5 %collective-permute-start.7 = (bf16[3,192,768]{2,1,0:T(8,128)(2,1)}, bf16[3,192,768]{2,1,0:T(8,128)(2,1)S(1)}, u32[]{:S(2)}, u32[]{:S(2)}) collective-permute-start(bf16[3,192,768]{2,1,0:T(8,128)(2,1)} %pad_maximum_fusion.1), channel_id=1, source_target_pairs={{0,1},{1,0},{2,3},{3,2},{4,5},{5,4},{6,7},{7,6},{8,9},{9,8},{10,11... | collective-permute-start | bytes 2654216 | tf_op jit(solution)/shard_map/ppermute | solution.py:1024
  69.4 48.0 %collective-permute-start.11 = (bf16[1500,384]{1,0:T(8,128)(2,1)}, bf16[1500,384]{1,0:T(8,128)(2,1)}, u32[]{:S(2)}, u32[]{:S(2)}) collective-permute-start(bf16[1500,384]{1,0:T(8,128)(2,1)} %bitcast.58), channel_id=1, source_target_pairs={{1,2},{2,1},{5,6},{6,5},{9,10},{10,9},{13,14},{14,13},{17,18},{18,... | collective-permute-start | bytes 3456008 | tf_op jit(solution)/shard_map/ppermute | solution.py:1041
  90.7 15.2 %collective-permute-start.10 = (bf16[3,192,768]{2,1,0:T(8,128)(2,1)S(1)}, bf16[3,192,768]{2,1,0:T(8,128)(2,1)S(1)}, u32[]{:S(2)}, u32[]{:S(2)}) collective-permute-start(bf16[3,192,768]{2,1,0:T(8,128)(2,1)S(1)} %collective-permute-done.7.refs_7_.refs_10_.o2), channel_id=1, source_target_pairs={{0,2},{2,0},{1,3},{3,1},{4,6},{6,4},{5,7},{7,5},{8,10},{10,8},{9,1... | collective-permute-start | bytes 2654216 | tf_op jit(solution)/shard_map/ppermute | solution.py:1024
  91.5 26.0 %collective-permute-start.12 = (bf16[384,768]{1,0:T(8,128)(2,1)}, bf16[384,768]{1,0:T(8,128)(2,1)}, u32[]{:S(2)}, u32[]{:S(2)}) collective-permute-start(bf16[384,768]{1,0:T(8,128)(2,1)} %dynamic-slice_convert_fusion.1), channel_id=1, source_target_pairs={{0,1},{1,0},{2,3},{3,2},{4,5},{5,4},{6,7},{7,6},{8,9},{9,8},{10,11... | collective-permute-start | bytes 1769480 | tf_op jit(solution)/shard_map/ppermute | solution.py:1024
  92.3 13.6 %collective-permute-start.8 = (bf16[1024,256]{1,0:T(8,128)(2,1)}, bf16[1024,256]{1,0:T(8,128)(2,1)S(1)}, u32[]{:S(2)}, u32[]{:S(2)}) collective-permute-start(bf16[1024,256]{1,0:T(8,128)(2,1)} %get-tuple-element.202), channel_id=1, source_target_pairs={{0,2},{2,0},{1,3},{3,1},{4,6},{6,4},{5,7},{7,5},{8,10},{10,8},{9,1... | collective-permute-start | bytes 1572872 | tf_op jit(solution)/shard_map/ppermute | solution.py:1024
  103.2 61.3 %collective-permute-start.15 = (bf16[1024,768]{1,0:T(8,128)(2,1)}, bf16[1024,768]{1,0:T(8,128)(2,1)}, u32[]{:S(2)}, u32[]{:S(2)}) collective-permute-start(bf16[1024,768]{1,0:T(8,128)(2,1)} %bitcast.24.co), channel_id=1, source_target_pairs={{1,2},{2,1},{5,6},{6,5},{9,10},{10,9},{13,14},{14,13},{17,18},{18,... | collective-permute-start | bytes 4718600 | tf_op jit(solution)/shard_map/ppermute | solution.py:1041
  118.9 3.9 collective-permute-start.13
  118.9 3.8 collective-permute-start.14
  233.6 231.4 %all-gather.9.cloned.1.call-start = ((), (), s32[]{:S(2)}) async-start(), calls=%async_computation.3 | async-start | bytes 5013504 | tf_op jit(solution)/shard_map/all_gather | solution.py:1149
  259.7 36.0 %collective-permute-start.17 = (bf16[2,1536,384]{2,1,0:T(8,128)(2,1)}, bf16[2,1536,384]{2,1,0:T(8,128)(2,1)S(1)}, u32[]{:S(2)}, u32[]{:S(2)}) collective-permute-start(bf16[2,1536,384]{2,1,0:T(8,128)(2,1)} %get-tuple-element.240), channel_id=1, source_target_pairs={{0,2},{2,0},{1,3},{3,1},{4,6},{6,4},{5,7},{7,5},{8,10},{10,8},{9,1... | collective-permute-start | bytes 7077896 | tf_op jit(solution)/shard_map/ppermute | solution.py:1024
  260.0 35.7 %collective-permute-start.18 = (bf16[1024,768]{1,0:T(8,128)(2,1)S(1)}, bf16[1024,768]{1,0:T(8,128)(2,1)}, u32[]{:S(2)}, u32[]{:S(2)}) collective-permute-start(bf16[1024,768]{1,0:T(8,128)(2,1)S(1)} %copy-done.8), channel_id=1, source_target_pairs={{0,2},{2,0},{1,3},{3,1},{4,6},{6,4},{5,7},{7,5},{8,10},{10,8},{9,1... | collective-permute-start | bytes 4718600 | tf_op jit(solution)/shard_map/ppermute | solution.py:1024
  260.2 35.5 %collective-permute-start.16 = (bf16[1024,768]{1,0:T(8,128)(2,1)}, bf16[1024,768]{1,0:T(8,128)(2,1)}, u32[]{:S(2)}, u32[]{:S(2)}) collective-permute-start(bf16[1024,768]{1,0:T(8,128)(2,1)} %get-tuple-element.239), channel_id=1, source_target_pairs={{1,2},{2,1},{5,6},{6,5},{9,10},{10,9},{13,14},{14,13},{17,18},{18,... | collective-permute-start | bytes 4718600 | tf_op jit(solution)/shard_map/ppermute | solution.py:1041
  269.5 26.2 %collective-permute-start.19 = (bf16[2,768,384]{2,1,0:T(8,128)(2,1)}, bf16[2,768,384]{2,1,0:T(8,128)(2,1)}, u32[]{:S(2)}, u32[]{:S(2)}) collective-permute-start(bf16[2,768,384]{2,1,0:T(8,128)(2,1)} %shard_map.264), channel_id=1, source_target_pairs={{0,2},{2,0},{1,3},{3,1},{4,6},{6,4},{5,7},{7,5},{8,10},{10,8},{9,1... | collective-permute-start | bytes 3538952 | tf_op jit(solution)/shard_map/ppermute | solution.py:1024
  307.7 23.1 %collective-permute-start.20 = (bf16[1500,384]{1,0:T(8,128)(2,1)}, bf16[1500,384]{1,0:T(8,128)(2,1)S(1)}, u32[]{:S(2)}, u32[]{:S(2)}) collective-permute-start(bf16[1500,384]{1,0:T(8,128)(2,1)} %get-tuple-element.260), channel_id=1, source_target_pairs={{0,2},{2,0},{1,3},{3,1},{4,6},{6,4},{5,7},{7,5},{8,10},{10,8},{9,1... | collective-permute-start | bytes 3456008 | tf_op jit(solution)/shard_map/ppermute | solution.py:1024
  326.5 11.0 %collective-permute-start.22 = (bf16[1024,384]{1,0:T(8,128)(2,1)}, bf16[1024,384]{1,0:T(8,128)(2,1)S(1)}, u32[]{:S(2)}, u32[]{:S(2)}) collective-permute-start(bf16[1024,384]{1,0:T(8,128)(2,1)} %get-tuple-element.267), channel_id=1, source_target_pairs={{0,2},{2,0},{1,3},{3,1},{4,6},{6,4},{5,7},{7,5},{8,10},{10,8},{9,1... | collective-permute-start | bytes 2359304 | tf_op jit(solution)/shard_map/ppermute | solution.py:1024
  331.2 39.2 %collective-permute-start.23 = (bf16[4,384,384]{2,1,0:T(8,128)(2,1)}, bf16[4,384,384]{2,1,0:T(8,128)(2,1)S(1)}, u32[]{:S(2)}, u32[]{:S(2)}) collective-permute-start(bf16[4,384,384]{2,1,0:T(8,128)(2,1)} %get-tuple-element.274), channel_id=1, source_target_pairs={{0,1},{1,0},{2,3},{3,2},{4,5},{5,4},{6,7},{7,6},{8,9},{9,8},{10,11... | collective-permute-start | bytes 3538952 | tf_op jit(solution)/shard_map/ppermute | solution.py:1024
  353.4 18.2 %collective-permute-start.25 = (bf16[3,1024,128]{2,1,0:T(8,128)(2,1)}, bf16[3,1024,128]{2,1,0:T(8,128)(2,1)S(1)}, u32[]{:S(2)}, u32[]{:S(2)}) collective-permute-start(bf16[3,1024,128]{2,1,0:T(8,128)(2,1)} %get-tuple-element.276.refs_3_), channel_id=1, source_target_pairs={{0,2},{2,0},{1,3},{3,1},{4,6},{6,4},{5,7},{7,5},{8,10},{10,8},{9,1... | collective-permute-start | bytes 2359304 | tf_op jit(solution)/shard_map/ppermute | solution.py:1024
  353.7 17.9 %collective-permute-start.24 = (bf16[1,384,384]{2,1,0:T(8,128)(2,1)S(1)}, bf16[1,384,384]{2,1,0:T(8,128)(2,1)S(1)}, u32[]{:S(2)}, u32[]{:S(2)}) collective-permute-start(bf16[1,384,384]{2,1,0:T(8,128)(2,1)S(1)} %copy-done.48), channel_id=1, source_target_pairs={{0,1},{1,0},{2,3},{3,2},{4,5},{5,4},{6,7},{7,6},{8,9},{9,8},{10,11... | collective-permute-start | bytes 884744 | tf_op jit(solution)/shard_map/ppermute | solution.py:1024
  376.5 136.0 %all-gather.11.cloned.1.call-start = ((), (), s32[]{:S(2)}) async-start(), calls=%async_computation.4 | async-start | bytes 3133440 | tf_op jit(solution)/shard_map/all_gather | solution.py:1172
  376.5 26.3 %collective-permute-start.28 = (bf16[1500,384]{1,0:T(8,128)(2,1)S(1)}, bf16[1500,384]{1,0:T(8,128)(2,1)S(1)}, u32[]{:S(2)}, u32[]{:S(2)}) collective-permute-start(bf16[1500,384]{1,0:T(8,128)(2,1)S(1)} %add_convert_fusion), channel_id=1, source_target_pairs={{1,2},{2,1},{5,6},{6,5},{9,10},{10,9},{13,14},{14,13},{17,18},{18,... | collective-permute-start | bytes 3456008 | tf_op jit(solution)/shard_map/ppermute | solution.py:1041
  379.7 15.8 %collective-permute-start.26 = (bf16[3,1024,128]{2,1,0:T(8,128)(2,1)S(1)}, bf16[3,1024,128]{2,1,0:T(8,128)(2,1)}, u32[]{:S(2)}, u32[]{:S(2)}) collective-permute-start(bf16[3,1024,128]{2,1,0:T(8,128)(2,1)S(1)} %copy-done.11), channel_id=1, source_target_pairs={{0,2},{2,0},{1,3},{3,1},{4,6},{6,4},{5,7},{7,5},{8,10},{10,8},{9,1... | collective-permute-start | bytes 2359304 | tf_op jit(solution)/shard_map/ppermute | solution.py:1024
  379.8 23.0 %collective-permute-start.27 = (bf16[5,192,384]{2,1,0:T(8,128)(2,1)}, bf16[5,192,384]{2,1,0:T(8,128)(2,1)}, u32[]{:S(2)}, u32[]{:S(2)}) collective-permute-start(bf16[5,192,384]{2,1,0:T(8,128)(2,1)} %get-tuple-element.300), channel_id=1, source_target_pairs={{0,4},{4,0},{1,5},{5,1},{2,6},{6,2},{3,7},{7,3},{8,12},{12,8},{9,1... | collective-permute-start | bytes 2211848 | tf_op jit(solution)/shard_map/ppermute | solution.py:1024
  402.8 25.9 %collective-permute-start.30 = (bf16[3,384,384]{2,1,0:T(8,128)(2,1)}, bf16[3,384,384]{2,1,0:T(8,128)(2,1)}, u32[]{:S(2)}, u32[]{:S(2)}) collective-permute-start(bf16[3,384,384]{2,1,0:T(8,128)(2,1)} %shard_map.276), channel_id=1, source_target_pairs={{0,1},{1,0},{2,3},{3,2},{4,5},{5,4},{6,7},{7,6},{8,9},{9,8},{10,11... | collective-permute-start | bytes 2654216 | tf_op jit(solution)/shard_map/ppermute | solution.py:1024
  403.0 11.0 %collective-permute-start.29 = (bf16[3,1024,128]{2,1,0:T(8,128)(2,1)S(1)}, bf16[3,1024,128]{2,1,0:T(8,128)(2,1)}, u32[]{:S(2)}, u32[]{:S(2)}) collective-permute-start(bf16[3,1024,128]{2,1,0:T(8,128)(2,1)S(1)} %copy-done.12), channel_id=1, source_target_pairs={{0,2},{2,0},{1,3},{3,1},{4,6},{6,4},{5,7},{7,5},{8,10},{10,8},{9,1... | collective-permute-start | bytes 2359304 | tf_op jit(solution)/shard_map/ppermute | solution.py:1024
  432.0 12.1 %collective-permute-start.31 = (bf16[3,192,384]{2,1,0:T(8,128)(2,1)}, bf16[3,192,384]{2,1,0:T(8,128)(2,1)S(1)}, u32[]{:S(2)}, u32[]{:S(2)}) collective-permute-start(bf16[3,192,384]{2,1,0:T(8,128)(2,1)} %get-tuple-element.322), channel_id=1, source_target_pairs={{0,4},{4,0},{1,5},{5,1},{2,6},{6,2},{3,7},{7,3},{8,12},{12,8},{9,1... | collective-permute-start | bytes 1327112 | tf_op jit(solution)/shard_map/ppermute | solution.py:1024
  432.3 15.2 %collective-permute-start.32 = (bf16[5,48,384]{2,1,0:T(8,128)(2,1)}, bf16[5,48,384]{2,1,0:T(8,128)(2,1)S(1)}, u32[]{:S(2)}, u32[]{:S(2)}) collective-permute-start(bf16[5,48,384]{2,1,0:T(8,128)(2,1)} %get-tuple-element.325), channel_id=1, source_target_pairs={{0,8},{8,0},{16,24},{24,16},{1,9},{9,1},{17,25},{25,17},{2,10},{10... | collective-permute-start | bytes 552968 | tf_op jit(solution)/shard_map/ppermute | solution.py:1020
  433.7 13.8 %collective-permute-start.33 = (bf16[5,48,384]{2,1,0:T(8,128)(2,1)}, bf16[5,48,384]{2,1,0:T(8,128)(2,1)S(1)}, u32[]{:S(2)}, u32[]{:S(2)}) collective-permute-start(bf16[5,48,384]{2,1,0:T(8,128)(2,1)} %get-tuple-element.326), channel_id=1, source_target_pairs={{0,16},{8,24},{16,0},{24,8},{1,17},{9,25},{17,1},{25,9},{2,18},{10... | collective-permute-start | bytes 552968 | tf_op jit(solution)/shard_map/ppermute | solution.py:1020
  435.8 12.9 %collective-permute-start.34 = (bf16[5,48,384]{2,1,0:T(8,128)(2,1)S(1)}, bf16[5,48,384]{2,1,0:T(8,128)(2,1)S(1)}, u32[]{:S(2)}, u32[]{:S(2)}) collective-permute-start(bf16[5,48,384]{2,1,0:T(8,128)(2,1)S(1)} %copy-done.49), channel_id=1, source_target_pairs={{0,24},{8,16},{16,8},{24,0},{1,25},{9,17},{17,9},{25,1},{2,26},{10... | collective-permute-start | bytes 552968 | tf_op jit(solution)/shard_map/ppermute | solution.py:1020
  452.0 57.7 %collective-permute-start.43 = (bf16[1024,768]{1,0:T(8,128)(2,1)}, bf16[1024,768]{1,0:T(8,128)(2,1)}, u32[]{:S(2)}, u32[]{:S(2)}) collective-permute-start(bf16[1024,768]{1,0:T(8,128)(2,1)} %get-tuple-element.349), channel_id=1, source_target_pairs={{1,2},{2,1},{5,6},{6,5},{9,10},{10,9},{13,14},{14,13},{17,18},{18,... | collective-permute-start | bytes 4718600 | tf_op jit(solution)/shard_map/ppermute | solution.py:1041
  456.5 18.3 %collective-permute-start.38 = (f32[24,384]{1,0:T(8,128)S(1)}, f32[24,384]{1,0:T(8,128)S(1)}, u32[]{:S(2)}, u32[]{:S(2)}) collective-permute-start(f32[24,384]{1,0:T(8,128)S(1)} %copy-done.50), channel_id=1, source_target_pairs={{0,1},{1,0},{2,3},{3,2},{4,5},{5,4},{6,7},{7,6},{8,9},{9,8},{10,11... | collective-permute-start | bytes 110600 | tf_op jit(solution)/shard_map/ppermute | solution.py:1024
  456.6 15.5 %collective-permute-start.35 = (bf16[3,48,384]{2,1,0:T(8,128)(2,1)}, bf16[3,48,384]{2,1,0:T(8,128)(2,1)S(1)}, u32[]{:S(2)}, u32[]{:S(2)}) collective-permute-start(bf16[3,48,384]{2,1,0:T(8,128)(2,1)} %get-tuple-element.329), channel_id=1, source_target_pairs={{0,8},{8,0},{16,24},{24,16},{1,9},{9,1},{17,25},{25,17},{2,10},{10... | collective-permute-start | bytes 331784 | tf_op jit(solution)/shard_map/ppermute | solution.py:1020
  460.0 12.1 %collective-permute-start.36 = (bf16[3,48,384]{2,1,0:T(8,128)(2,1)}, bf16[3,48,384]{2,1,0:T(8,128)(2,1)S(1)}, u32[]{:S(2)}, u32[]{:S(2)}) collective-permute-start(bf16[3,48,384]{2,1,0:T(8,128)(2,1)} %get-tuple-element.330), channel_id=1, source_target_pairs={{0,16},{8,24},{16,0},{24,8},{1,17},{9,25},{17,1},{25,9},{2,18},{10... | collective-permute-start | bytes 331784 | tf_op jit(solution)/shard_map/ppermute | solution.py:1020
  461.1 11.0 %collective-permute-start.37 = (bf16[3,48,384]{2,1,0:T(8,128)(2,1)}, bf16[3,48,384]{2,1,0:T(8,128)(2,1)S(1)}, u32[]{:S(2)}, u32[]{:S(2)}) collective-permute-start(bf16[3,48,384]{2,1,0:T(8,128)(2,1)} %get-tuple-element.331), channel_id=1, source_target_pairs={{0,24},{8,16},{16,8},{24,0},{1,25},{9,17},{17,9},{25,1},{2,26},{10... | collective-permute-start | bytes 331784 | tf_op jit(solution)/shard_map/ppermute | solution.py:1020
  477.9 7.1 %collective-permute-start.41 = (bf16[4,48,384]{2,1,0:T(8,128)(2,1)}, bf16[4,48,384]{2,1,0:T(8,128)(2,1)S(1)}, u32[]{:S(2)}, u32[]{:S(2)}) collective-permute-start(bf16[4,48,384]{2,1,0:T(8,128)(2,1)} %shard_map.283.p0), channel_id=1, source_target_pairs={{0,24},{8,16},{16,8},{24,0},{1,25},{9,17},{17,9},{25,1},{2,26},{10... | collective-permute-start | bytes 442376 | tf_op jit(solution)/shard_map/ppermute | solution.py:1020
  480.2 24.5 %collective-permute-start.40 = (bf16[4,48,384]{2,1,0:T(8,128)(2,1)}, bf16[4,48,384]{2,1,0:T(8,128)(2,1)S(1)}, u32[]{:S(2)}, u32[]{:S(2)}) collective-permute-start(bf16[4,48,384]{2,1,0:T(8,128)(2,1)} %shard_map.283.p0), channel_id=1, source_target_pairs={{0,16},{8,24},{16,0},{24,8},{1,17},{9,25},{17,1},{25,9},{2,18},{10... | collective-permute-start | bytes 442376 | tf_op jit(solution)/shard_map/ppermute | solution.py:1020
  482.4 22.3 %collective-permute-start.39 = (bf16[4,48,384]{2,1,0:T(8,128)(2,1)}, bf16[4,48,384]{2,1,0:T(8,128)(2,1)S(1)}, u32[]{:S(2)}, u32[]{:S(2)}) collective-permute-start(bf16[4,48,384]{2,1,0:T(8,128)(2,1)} %shard_map.283.p0), channel_id=1, source_target_pairs={{0,8},{8,0},{16,24},{24,16},{1,9},{9,1},{17,25},{25,17},{2,10},{10... | collective-permute-start | bytes 442376 | tf_op jit(solution)/shard_map/ppermute | solution.py:1020
  508.7 13.0 %collective-permute-start.42 = (bf16[4,192,384]{2,1,0:T(8,128)(2,1)}, bf16[4,192,384]{2,1,0:T(8,128)(2,1)S(1)}, u32[]{:S(2)}, u32[]{:S(2)}) collective-permute-start(bf16[4,192,384]{2,1,0:T(8,128)(2,1)} %shard_map.284.refs_0_), channel_id=1, source_target_pairs={{0,4},{4,0},{1,5},{5,1},{2,6},{6,2},{3,7},{7,3},{8,12},{12,8},{9,1... | collective-permute-start | bytes 1769480 | tf_op jit(solution)/shard_map/ppermute | solution.py:1024
  517.7 6.9 %collective-permute-start.44 = (bf16[4,192,384]{2,1,0:T(8,128)(2,1)S(1)}, bf16[4,192,384]{2,1,0:T(8,128)(2,1)S(1)}, u32[]{:S(2)}, u32[]{:S(2)}) collective-permute-start(bf16[4,192,384]{2,1,0:T(8,128)(2,1)S(1)} %copy-done.19), channel_id=1, source_target_pairs={{0,2},{2,0},{1,3},{3,1},{4,6},{6,4},{5,7},{7,5},{8,10},{10,8},{9,1... | collective-permute-start | bytes 1769480 | tf_op jit(solution)/shard_map/ppermute | solution.py:1024
  521.7 4.6 collective-permute-start.45
  (55 other events, 337.0 us)
Sparse Core Ops, SparseCore 0:
  68.1 55.4 all-gather.6
  233.7 142.0 reduce-scatter.1
  378.4 56.2 all-gather.8
  452.1 56.8 all-gather.10

commit v6 on v5

--- a/solution.py
+++ b/solution.py
@@ -1158,13 +1158,13 @@
     m_z = send_z(m_z)
     q_xkeep = qkv_grad(s, a1, a1_sib, (bk1, bk2, bk3), (bg1, bg2, bg3), True)
     grad_hidden, vec_last = last_rows(s, (bk1, bk2, bk3), (bi1, bi2, bi3), x_own, x_in, dh1, w_qkv, table)
+    vec_last, q_x = tie(vec_last, q_x)
+    q_ygive, q_ykeep = split_y(s, (q_xkeep,), (q_x,))
+    q_ygive, grad_hidden, vec_last = tie(q_ygive, grad_hidden, vec_last)
+    q_y = across(q_ygive, "y")
+    hid_in = swap(grad_hidden)
     v_give, v_mine = pack_vectors(s, vec_last, vec_cross, vec_mid, vec_kv)
     v_got = across(v_give, "x")
-    v_mine, q_x = tie(v_mine, q_x)
-    q_ygive, q_ykeep = split_y(s, (q_xkeep,), (q_x,))
-    q_ygive, grad_hidden = tie(q_ygive, grad_hidden)
-    q_y = across(q_ygive, "y")
-    hid_in = swap(grad_hidden)
     q_four = split_z(s, q_ykeep, q_y)
     q_first, *m_z = tie(q_four[0], *m_z)
     q_four = (q_first, *q_four[1:])

time: 547 us -> 548 us (level)
    unnamed x106 -> x104, local copies, waits for them, and re-layouts: 14.5 us -> 14.5 us
where the time goes in v6:
time: 548 us; the launch traced here: 541 us
  Pallas kernels  360 us (66%)
  waiting for transfers between devices  59.5 us (11%)
  starting transfers between devices  57 us (10%)
  local copies, waits for them, and re-layouts  27.2 us (5%)
  other arithmetic  22.5 us (4%)
  between operations  14.7 us (3%)
    pallas_call x34, Pallas kernels, call(): pl.pallas_call(kernel, grid_spec=spec, out_shape=out_shape, cost_estimate...  360 us
    ppermute x7, starting transfers between devices, swap(): return lax.ppermute(x, ('core', 'x'), SWAP)  24.6 us
    ppermute x30, waiting for transfers between devices, across(): return lax.ppermute(x, axis, FLIP)  22.4 us
    ppermute x9, waiting for transfers between devices, across_z(): return lax.ppermute(x, 'z', [(j, j ^ d) for j in range(4)])  22.2 us
    ppermute x30, starting transfers between devices, across(): return lax.ppermute(x, axis, FLIP)  16.1 us
    ppermute x9, starting transfers between devices, across_z(): return lax.ppermute(x, 'z', [(j, j ^ d) for j in range(4)])  16.1 us
    ppermute x7, waiting for transfers between devices, swap(): return lax.ppermute(x, ('core', 'x'), SWAP)  14.8 us
    unnamed x104, local copies, waits for them, and re-layouts  14.5 us
  transfers between devices with their start and end apart: 50, of which 14 were waited for; matrix products, arithmetic and copies ran while one was open for 6% of the time, Pallas kernels for 53%

profile of v6, /device:TPU:1, one launch (start us, length us, event | category | flops | bytes accessed | tf_op | source)
XLA Modules:
  0.0 541.0 jit_solution(3036370097055197687)
XLA Ops:
  7.3 4.6 collective-permute-start.1
  22.7 2.8 convert.51
  41.1 14.8 %collective-permute-done.xi.refs_5_.refs_7_ = bf16[1024,768]{1,0:T(8,128)(2,1)S(1)} collective-permute-done((bf16[1024,768]{1,0:T(8,128)(2,1)S(1)}, bf16[1024,768]{1,0:T(8,128)(2,1)S(1)}, u32[]{:S(2)}, u32[]{:S(2)}) %collective-permute-start) | collective-permute-done | bytes 1572896 | tf_op jit(solution)/shard_map/ppermute | solution.py:1041
  57.0 10.2 %shard_map.254 = (bf16[768,2304]{1,0:T(8,128)(2,1)}, bf16[1024,768]{1,0:T(8,128)(2,1)}, bf16[3,1024,384]{2,1,0:T(8,128)(2,1)}, bf16[3,1024,384]{2,1,0:T(8,128)(2,1)}) custom-call(s32[9]{0:T(128)} %stack.72.s_ref, bf16[1024,768]{1,0:T(8,128)(2,1)} %bitcast.43, bf16[1024,768]{1,0:T(8,128)(2,1)} %copy-done.2, f32[384,2304]{1,0:T(8,128)} %own.2, ...), custom_call_target="tpu_custom_call" | custom-call | flops 362387872 | bytes 1048576 | tf_op jit(solution)/shard_map/pallas_call | solution.py:41
  69.4 3.6 collective-permute-start.11
  75.0 15.6 %shard_map.255 = (bf16[2048,256]{1,0:T(8,128)(2,1)}, bf16[1024,256]{1,0:T(8,128)(2,1)}, f32[2,8,2048]{2,1,0:T(8,128)}) custom-call(s32[1]{0:T(128)} %bitcast.s_ref, bf16[3,1024,384]{2,1,0:T(8,128)(2,1)} %get-tuple-element.292.a_ref, bf16[3,1024,384]{2,1,0:T(8,128)(2,1)} %copy-done, bf16[2048,128]{1,0:T(8,128)(2,1)} %get-tuple-element.195.km_ref, ...), custom_call_target="tpu_custom_call" | custom-call | flops 858993472 | bytes 1048576 | tf_op jit(solution)/shard_map/pallas_call | solution.py:41
  92.5 9.0 %shard_map.256 = (bf16[2048,128]{1,0:T(8,128)(2,1)}, bf16[1024,128]{1,0:T(8,128)(2,1)}, f32[1,8,2048]{2,1,0:T(8,128)}) custom-call(s32[1]{0:T(128)} %bitcast.s_ref, bf16[3,1024,384]{2,1,0:T(8,128)(2,1)} %get-tuple-element.292.a_ref, bf16[3,1024,384]{2,1,0:T(8,128)(2,1)} %copy-done, bf16[2048,128]{1,0:T(8,128)(2,1)} %get-tuple-element.195.km_ref, ...), custom_call_target="tpu_custom_call" | custom-call | flops 429496736 | bytes 1048576 | tf_op jit(solution)/shard_map/pallas_call | solution.py:41
  103.3 2.7 collective-permute-start.15
  107.0 10.4 %shard_map.257 = (bf16[768,768]{1,0:T(8,128)(2,1)}, bf16[768,768]{1,0:T(8,128)(2,1)}, f32[1024,768]{1,0:T(8,128)}, bf16[1024,768]{1,0:T(8,128)(2,1)}, bf16[1024,768]{1,0:T(8,128)(2,1)}) custom-call(s32[9]{0:T(128)} %stack.72.s_ref, bf16[2048,256]{1,0:T(8,128)(2,1)} %get-tuple-element.197.refs_0_.o_ref, bf16[2048,128]{1,0:T(8,128)(2,1)} %get-tuple-element.202.refs_1_.o_ref, ...), custom_call_target="tpu_custom_call" | custom-call | flops 241591904 | bytes 1048576 | tf_op jit(solution)/shard_map/pallas_call | solution.py:41
  120.1 2.7 collective-permute-done.14.sib
  124.7 10.1 %shard_map.258 = (bf16[1536,768]{1,0:T(8,128)(2,1)}, bf16[1536,768]{1,0:T(8,128)(2,1)}, bf16[1536,768]{1,0:T(8,128)(2,1)}) custom-call(s32[9]{0:T(128)} %stack.72.s_ref, bf16[1500,384]{1,0:T(8,128)(2,1)} %copy-done.3, bf16[1500,384]{1,0:T(8,128)(2,1)} %copy-done.10, f32[768,768]{1,0:T(8,128)} %own.3, bf16[384,768]{1,0:T(8,128)(2,1)} %collective-permute-done.12.mine, ...), custom_call_target="tpu_custom_call" | custom-call | flops 353894400 | bytes 1048576 | tf_op jit(solution)/shard_map/pallas_call | solution.py:41
  134.8 14.8 %shard_map.260 = (bf16[1024,384]{1,0:T(8,128)(2,1)}, f32[3,8,1024]{2,1,0:T(8,128)}) custom-call(s32[1]{0:T(128)} %bitcast.23.s_ref, bf16[1024,768]{1,0:T(8,128)(2,1)} %get-tuple-element.209.q_ref, bf16[1536,768]{1,0:T(8,128)(2,1)} %get-tuple-element.212.k_ref, bf16[1536,768]{1,0:T(8,128)(2,1)} %get-tuple-element.213.v_ref), custom_call_target="tpu_custom_call" | custom-call | flops 483183808 | bytes 1048576 | tf_op jit(solution)/shard_map/pallas_call | solution.py:41
  149.6 14.9 %shard_map.259 = (bf16[1024,384]{1,0:T(8,128)(2,1)}, f32[3,8,1024]{2,1,0:T(8,128)}) custom-call(s32[1]{0:T(128)} %bitcast.8.s_ref, bf16[1024,768]{1,0:T(8,128)(2,1)} %get-tuple-element.209.q_ref, bf16[1536,768]{1,0:T(8,128)(2,1)} %get-tuple-element.212.k_ref, bf16[1536,768]{1,0:T(8,128)(2,1)} %get-tuple-element.213.v_ref), custom_call_target="tpu_custom_call" | custom-call | flops 483183808 | bytes 1048576 | tf_op jit(solution)/shard_map/pallas_call | solution.py:41
  164.5 51.7 %shard_map.261 = (bf16[768,768]{1,0:T(8,128)(2,1)}, bf16[1024,768]{1,0:T(8,128)(2,1)}, bf16[1024,768]{1,0:T(8,128)(2,1)}, bf16[1024,3072]{1,0:T(8,128)(2,1)}, bf...) custom-call(s32[9]{0:T(128)} %stack.72.s_ref, ...), custom_call_target="tpu_custom_call" | custom-call | flops 2174327296 | bytes 1048576 | tf_op jit(solution)/shard_map/pallas_call | solution.py:41
  216.3 17.4 %shard_map.262 = bf16[2,16,2,96,768]{4,3,2,1,0:T(8,128)(2,1)} custom-call(s32[9]{0:T(128)} %stack.72.s_ref, bf16[1024,768]{1,0:T(8,128)(2,1)} %get-tuple-element.224.a_ref, bf16[1024,3072]{1,0:T(8,128)(2,1)} %get-tuple-element.225.du_ref, bf16[1024,3072]{1,0:T(8,128)(2,1)} %get-tuple-element.226.g0.g1, bf16[1024,3072]{1,0:T(8,128)(2,1)} %get-tuple-element.226.g0.g1, ...), custom_call_target="tpu_custom_call" | custom-call | flops 966367616 | bytes 1048576 | tf_op jit(solution)/shard_map/pallas_call | solution.py:41
  233.7 26.1 %shard_map.263 = (bf16[1024,384]{1,0:T(8,128)(2,1)}, bf16[2,1536,384]{2,1,0:T(8,128)(2,1)}) custom-call(s32[1]{0:T(128)} %bitcast.23.s_ref, bf16[1024,768]{1,0:T(8,128)(2,1)} %get-tuple-element.209.q_ref, bf16[1536,768]{1,0:T(8,128)(2,1)} %get-tuple-element.212.k_ref, bf16[1536,768]{1,0:T(8,128)(2,1)} %get-tuple-element.213.v_ref, ...), custom_call_target="tpu_custom_call" | custom-call | flops 2415919104 | bytes 1048576 | tf_op jit(solution)/shard_map/pallas_call | solution.py:41
  260.3 3.4 collective-permute-start.16
  263.7 5.9 %shard_map.264 = bf16[2,768,384]{2,1,0:T(8,128)(2,1)} custom-call(s32[9]{0:T(128)} %stack.72.s_ref, bf16[1024,384]{1,0:T(8,128)(2,1)} %get-tuple-element.214.ck_ref.k_ref.o_ref.ck, bf16[1024,384]{1,0:T(8,128)(2,1)} %get-tuple-element.215.cg_ref.o_ref.g_ref.cg, bf16[1024,768]{1,0:T(8,128)(2,1)} %get-tuple-element.221.d_ref.d2_ref, ...), custom_call_target="tpu_custom_call" | custom-call | flops 120795952 | bytes 1048576 | tf_op jit(solution)/shard_map/pallas_call | solution.py:41
  269.6 26.2 %shard_map.265 = (bf16[1024,384]{1,0:T(8,128)(2,1)}, bf16[2,1536,384]{2,1,0:T(8,128)(2,1)}) custom-call(s32[1]{0:T(128)} %bitcast.8.s_ref, bf16[1024,768]{1,0:T(8,128)(2,1)} %get-tuple-element.209.q_ref, bf16[1536,768]{1,0:T(8,128)(2,1)} %get-tuple-element.212.k_ref, bf16[1536,768]{1,0:T(8,128)(2,1)} %get-tuple-element.213.v_ref, ...), custom_call_target="tpu_custom_call" | custom-call | flops 2415919104 | bytes 1048576 | tf_op jit(solution)/shard_map/pallas_call | solution.py:41
  297.2 10.5 %shard_map.266 = (bf16[1500,384]{1,0:T(8,128)(2,1)}, bf16[1500,384]{1,0:T(8,128)(2,1)}, bf16[768,384]{1,0:T(8,128)(2,1)}, bf16[768,384]{1,0:T(8,128)(2,1)}, f32[8,384]{1,0:T(8,128)}) custom-call(s32[9]{0:T(128)} %stack.72.s_ref, bf16[2,1536,384]{2,1,0:T(8,128)(2,1)} %get-tuple-element.238.ka, bf16[2,1536,384]{2,1,0:T(8,128)(2,1)} %copy-done.17, ...), custom_call_target="tpu_custom_call" | custom-call | flops 707788800 | bytes 1048576 | tf_op jit(solution)/shard_map/pallas_call | solution.py:41
  308.3 7.1 %shard_map.267 = (bf16[4,384,384]{2,1,0:T(8,128)(2,1)}, bf16[4,384,384]{2,1,0:T(8,128)(2,1)}) custom-call(s32[9]{0:T(128)} %stack.72.s_ref, bf16[1024,384]{1,0:T(8,128)(2,1)} %get-tuple-element.214.ck_ref.k_ref.o_ref.ck, bf16[1024,384]{1,0:T(8,128)(2,1)} %get-tuple-element.215.cg_ref.o_ref.g_ref.cg, bf16[1024,768]{1,0:T(8,128)(2,1)} %get-tuple-element.221.d_ref.d2_ref, ...), custom_call_target="tpu_custom_call" | custom-call | flops 120795952 | bytes 1048576 | tf_op jit(solution)/shard_map/pallas_call | solution.py:41
  315.4 11.1 %shard_map.268 = (f32[1024,768]{1,0:T(8,128)}, bf16[1024,768]{1,0:T(8,128)(2,1)}, bf16[1024,384]{1,0:T(8,128)(2,1)}, bf16[1024,384]{1,0:T(8,128)(2,1)}, f32[8,768]{1,0:T(8,128)}) custom-call(s32[9]{0:T(128)} %stack.72.s_ref, bf16[1024,384]{1,0:T(8,128)(2,1)} %get-tuple-element.254.q_ref.dk_ref, bf16[1024,384]{1,0:T(8,128)(2,1)} %get-tuple-element.234.q_ref.dg_ref, ...), custom_call_target="tpu_custom_call" | custom-call | flops 241591904 | bytes 1048576 | tf_op jit(solution)/shard_map/pallas_call | solution.py:41
  326.7 4.2 shard_map.269
  333.3 4.3 shard_map.270
  338.5 15.0 %shard_map.271 = (bf16[3,1024,128]{2,1,0:T(8,128)(2,1)}, bf16[3,1024,128]{2,1,0:T(8,128)(2,1)}) custom-call(s32[1]{0:T(128)} %bitcast.s_ref, bf16[3,1024,384]{2,1,0:T(8,128)(2,1)} %get-tuple-element.292.a_ref, bf16[3,1024,384]{2,1,0:T(8,128)(2,1)} %copy-done, bf16[2048,256]{1,0:T(8,128)(2,1)} %get-tuple-element.197.refs_0_.o_ref, ...), custom_call_target="tpu_custom_call" | custom-call | flops 858993472 | bytes 1048576 | tf_op jit(solution)/shard_map/pallas_call | solution.py:41
  355.8 14.7 %shard_map.272 = (bf16[3,1024,128]{2,1,0:T(8,128)(2,1)}, bf16[3,1024,128]{2,1,0:T(8,128)(2,1)}) custom-call(s32[1]{0:T(128)} %bitcast.s_ref, bf16[3,1024,384]{2,1,0:T(8,128)(2,1)} %get-tuple-element.292.a_ref, bf16[3,1024,384]{2,1,0:T(8,128)(2,1)} %copy-done, bf16[2048,256]{1,0:T(8,128)(2,1)} %get-tuple-element.197.refs_0_.o_ref, ...), custom_call_target="tpu_custom_call" | custom-call | flops 858993472 | bytes 1048576 | tf_op jit(solution)/shard_map/pallas_call | solution.py:41
  372.7 3.9 shard_map.273
  376.6 3.2 collective-permute-start.28
  381.2 14.5 %shard_map.275 = (bf16[3,1024,128]{2,1,0:T(8,128)(2,1)}, bf16[3,1024,128]{2,1,0:T(8,128)(2,1)}) custom-call(s32[1]{0:T(128)} %bitcast.s_ref, bf16[3,1024,384]{2,1,0:T(8,128)(2,1)} %get-tuple-element.292.a_ref, bf16[3,1024,384]{2,1,0:T(8,128)(2,1)} %copy-done, bf16[2048,128]{1,0:T(8,128)(2,1)} %get-tuple-element.202.refs_1_.o_ref, ...), custom_call_target="tpu_custom_call" | custom-call | flops 858993472 | bytes 1048576 | tf_op jit(solution)/shard_map/pallas_call | solution.py:41
  395.7 7.3 %shard_map.276 = bf16[3,384,384]{2,1,0:T(8,128)(2,1)} custom-call(s32[9]{0:T(128)} %stack.72.s_ref, bf16[1024,768]{1,0:T(8,128)(2,1)} %get-tuple-element.242.ao, bf16[1024,768]{1,0:T(8,128)(2,1)} %collective-permute-done.18.ai, bf16[3,1024,128]{2,1,0:T(8,128)(2,1)} %get-tuple-element.290.refs_0_, bf16[3,1024,128]{2,1,0:T(8,128)(2,1)} %get-tuple-element.291.refs_1_, ...), custom_call_target="tpu_custom_call" | custom-call | flops 181193936 | bytes 1048576 | tf_op jit(solution)/shard_map/pallas_call | solution.py:41
  404.2 2.9 shard_map.277
  407.1 7.5 %shard_map.278.refs_0_ = bf16[3,384,384]{2,1,0:T(8,128)(2,1)} custom-call(s32[9]{0:T(128)} %stack.72.s_ref, bf16[1024,768]{1,0:T(8,128)(2,1)} %get-tuple-element.242.ao, bf16[1024,768]{1,0:T(8,128)(2,1)} %collective-permute-done.18.ai, bf16[3,1024,128]{2,1,0:T(8,128)(2,1)} %get-tuple-element.290.refs_0_, bf16[3,1024,128]{2,1,0:T(8,128)(2,1)} %get-tuple-element.291.refs_1_, ...), custom_call_target="tpu_custom_call" | custom-call | flops 181193936 | bytes 1048576 | tf_op jit(solution)/shard_map/pallas_call | solution.py:41
  414.6 12.4 %shard_map.279 = (bf16[1024,768]{1,0:T(8,128)(2,1)}, f32[8,768]{1,0:T(8,128)}) custom-call(s32[9]{0:T(128)} %stack.72.s_ref, bf16[3,1024,128]{2,1,0:T(8,128)(2,1)} %get-tuple-element.290.refs_0_, bf16[3,1024,128]{2,1,0:T(8,128)(2,1)} %get-tuple-element.291.refs_1_, bf16[3,1024,128]{2,1,0:T(8,128)(2,1)} %get-tuple-element.308.refs_2_, ...), custom_call_target="tpu_custom_call" | custom-call | flops 362387872 | bytes 1048576 | tf_op jit(solution)/shard_map/pallas_call | solution.py:41
  427.0 3.3 shard_map.280
  433.8 8.6 %collective-permute-done.31.g_ref = bf16[3,192,384]{2,1,0:T(8,128)(2,1)S(1)} collective-permute-done((bf16[3,192,384]{2,1,0:T(8,128)(2,1)}, bf16[3,192,384]{2,1,0:T(8,128)(2,1)S(1)}, u32[]{:S(2)}, u32[]{:S(2)}) %collective-permute-start.31) | collective-permute-done | bytes 442400 | tf_op jit(solution)/shard_map/ppermute | solution.py:1024
  449.5 4.6 collective-permute-start.43
  456.4 3.4 collective-permute-start.35
  462.1 2.8 broadcast_select_fusion.1
  464.9 7.0 %shard_map.274 = (f32[384,3072]{1,0:T(8,128)}, f32[1536,768]{1,0:T(8,128)}) custom-call(s32[9]{0:T(128)} %stack.72.s_ref, bf16[16,2,96,768]{3,2,1,0:T(8,128)(2,1)} %bitcast.53), custom_call_target="tpu_custom_call" | custom-call | tf_op jit(solution)/shard_map/pallas_call | solution.py:41
  476.7 3.6 collective-permute-start.41
  480.3 3.0 collective-permute-start.40
  486.1 20.1 %collective-permute-done.40.p2 = bf16[4,48,384]{2,1,0:T(8,128)(2,1)S(1)} collective-permute-done((bf16[4,48,384]{2,1,0:T(8,128)(2,1)}, bf16[4,48,384]{2,1,0:T(8,128)(2,1)S(1)}, u32[]{:S(2)}, u32[]{:S(2)}) %collective-permute-start.40) | collective-permute-done | bytes 147488 | tf_op jit(solution)/shard_map/ppermute | solution.py:1020
  507.5 2.7 shard_map.284.refs_0_
  510.2 2.8 broadcast_select_fusion
  513.0 5.3 shard_map.286
  520.2 3.1 collective-permute-done.42.refs_1_
  523.3 2.8 collective-permute-start.45
  528.6 4.3 shard_map.287
  (235 shorter events, 83.4 us)
Async XLA Ops:
  7.2 157.3 %all-gather.7.cloned.1.call-start = ((), (), s32[]{:S(2)}) async-start(), calls=%async_computation.2 | async-start | bytes 5013504 | tf_op jit(solution)/shard_map/all_gather | solution.py:1076
  7.3 30.2 %collective-permute-start.1 = (s32[1,2048]{1,0:T(1,128)}, s32[1,2048]{1,0:T(1,128)S(1)}, u32[]{:S(2)}, u32[]{:S(2)}) collective-permute-start(s32[1,2048]{1,0:T(1,128)} %param.17), channel_id=1, source_target_pairs={{1,2},{2,1},{5,6},{6,5},{9,10},{10,9},{13,14},{14,13},{17,18},{18,... | collective-permute-start | bytes 24584 | tf_op jit(solution)/shard_map/ppermute | solution.py:1041
  14.9 26.2 %collective-permute-start.4 = (bf16[20,384]{1,0:T(8,128)(2,1)S(1)}, bf16[20,384]{1,0:T(8,128)(2,1)S(1)}, u32[]{:S(2)}, u32[]{:S(2)}) collective-permute-start(bf16[20,384]{1,0:T(8,128)(2,1)S(1)} %concatenate.35), channel_id=1, source_target_pairs={{0,1},{1,0},{2,3},{3,2},{4,5},{5,4},{6,7},{7,6},{8,9},{9,8},{10,11... | collective-permute-start | bytes 46088 | tf_op jit(solution)/shard_map/ppermute | solution.py:1024
  17.4 21.2 %collective-permute-start.2 = (bf16[192,2304]{1,0:T(8,128)(2,1)}, bf16[192,2304]{1,0:T(8,128)(2,1)}, u32[]{:S(2)}, u32[]{:S(2)}) collective-permute-start(bf16[192,2304]{1,0:T(8,128)(2,1)} %dynamic-slice_convert_fusion), channel_id=1, source_target_pairs={{0,1},{1,0},{2,3},{3,2},{4,5},{5,4},{6,7},{7,6},{8,9},{9,8},{10,11... | collective-permute-start | bytes 2654216 | tf_op jit(solution)/shard_map/ppermute | solution.py:1024
  18.9 37.0 %collective-permute-start = (bf16[1024,768]{1,0:T(8,128)(2,1)S(1)}, bf16[1024,768]{1,0:T(8,128)(2,1)S(1)}, u32[]{:S(2)}, u32[]{:S(2)}) collective-permute-start(bf16[1024,768]{1,0:T(8,128)(2,1)S(1)} %bitcast.46), channel_id=1, source_target_pairs={{1,2},{2,1},{5,6},{6,5},{9,10},{10,9},{13,14},{14,13},{17,18},{18,... | collective-permute-start | bytes 4718600 | tf_op jit(solution)/shard_map/ppermute | solution.py:1041
  38.6 18.0 %collective-permute-start.3 = (bf16[192,2304]{1,0:T(8,128)(2,1)}, bf16[192,2304]{1,0:T(8,128)(2,1)}, u32[]{:S(2)}, u32[]{:S(2)}) collective-permute-start(bf16[192,2304]{1,0:T(8,128)(2,1)} %collective-permute-done.2.mine), channel_id=1, source_target_pairs={{0,2},{2,0},{1,3},{3,1},{4,6},{6,4},{5,7},{7,5},{8,10},{10,8},{9,1... | collective-permute-start | bytes 2654216 | tf_op jit(solution)/shard_map/ppermute | solution.py:1024
  55.9 11.4 %collective-permute-start.5 = (bf16[2,96,768]{2,1,0:T(8,128)(2,1)}, bf16[2,96,768]{2,1,0:T(8,128)(2,1)S(1)}, u32[]{:S(2)}, u32[]{:S(2)}) collective-permute-start(bf16[2,96,768]{2,1,0:T(8,128)(2,1)} %pad_maximum_fusion.2), channel_id=1, source_target_pairs={{0,1},{1,0},{2,3},{3,2},{4,5},{5,4},{6,7},{7,6},{8,9},{9,8},{10,11... | collective-permute-start | bytes 884744 | tf_op jit(solution)/shard_map/ppermute | solution.py:1024
  68.0 308.5 %reduce-scatter.2.cloned.1.call-start = ((), (), s32[]{:S(2)}) async-start(), calls=%async_computation.1 | async-start | bytes 9732096 | tf_op jit(solution)/shard_map/reduce_scatter | solution.py:1105
  68.1 5.5 %collective-permute-start.6 = (bf16[3,1024,384]{2,1,0:T(8,128)(2,1)}, bf16[3,1024,384]{2,1,0:T(8,128)(2,1)S(1)}, u32[]{:S(2)}, u32[]{:S(2)}) collective-permute-start(bf16[3,1024,384]{2,1,0:T(8,128)(2,1)} %get-tuple-element.194), channel_id=1, source_target_pairs={{0,2},{2,0},{1,3},{3,1},{4,6},{6,4},{5,7},{7,5},{8,10},{10,8},{9,1... | collective-permute-start | bytes 7077896 | tf_op jit(solution)/shard_map/ppermute | solution.py:1024
  69.2 21.5 %collective-permute-start.7 = (bf16[3,192,768]{2,1,0:T(8,128)(2,1)}, bf16[3,192,768]{2,1,0:T(8,128)(2,1)S(1)}, u32[]{:S(2)}, u32[]{:S(2)}) collective-permute-start(bf16[3,192,768]{2,1,0:T(8,128)(2,1)} %pad_maximum_fusion.1), channel_id=1, source_target_pairs={{0,1},{1,0},{2,3},{3,2},{4,5},{5,4},{6,7},{7,6},{8,9},{9,8},{10,11... | collective-permute-start | bytes 2654216 | tf_op jit(solution)/shard_map/ppermute | solution.py:1024
  69.4 48.1 %collective-permute-start.11 = (bf16[1500,384]{1,0:T(8,128)(2,1)}, bf16[1500,384]{1,0:T(8,128)(2,1)}, u32[]{:S(2)}, u32[]{:S(2)}) collective-permute-start(bf16[1500,384]{1,0:T(8,128)(2,1)} %bitcast.58), channel_id=1, source_target_pairs={{1,2},{2,1},{5,6},{6,5},{9,10},{10,9},{13,14},{14,13},{17,18},{18,... | collective-permute-start | bytes 3456008 | tf_op jit(solution)/shard_map/ppermute | solution.py:1041
  90.7 15.3 %collective-permute-start.10 = (bf16[3,192,768]{2,1,0:T(8,128)(2,1)S(1)}, bf16[3,192,768]{2,1,0:T(8,128)(2,1)S(1)}, u32[]{:S(2)}, u32[]{:S(2)}) collective-permute-start(bf16[3,192,768]{2,1,0:T(8,128)(2,1)S(1)} %collective-permute-done.7.refs_7_.refs_10_.o2), channel_id=1, source_target_pairs={{0,2},{2,0},{1,3},{3,1},{4,6},{6,4},{5,7},{7,5},{8,10},{10,8},{9,1... | collective-permute-start | bytes 2654216 | tf_op jit(solution)/shard_map/ppermute | solution.py:1024
  91.5 26.0 %collective-permute-start.12 = (bf16[384,768]{1,0:T(8,128)(2,1)}, bf16[384,768]{1,0:T(8,128)(2,1)}, u32[]{:S(2)}, u32[]{:S(2)}) collective-permute-start(bf16[384,768]{1,0:T(8,128)(2,1)} %dynamic-slice_convert_fusion.1), channel_id=1, source_target_pairs={{0,1},{1,0},{2,3},{3,2},{4,5},{5,4},{6,7},{7,6},{8,9},{9,8},{10,11... | collective-permute-start | bytes 1769480 | tf_op jit(solution)/shard_map/ppermute | solution.py:1024
  92.3 13.7 %collective-permute-start.8 = (bf16[1024,256]{1,0:T(8,128)(2,1)}, bf16[1024,256]{1,0:T(8,128)(2,1)S(1)}, u32[]{:S(2)}, u32[]{:S(2)}) collective-permute-start(bf16[1024,256]{1,0:T(8,128)(2,1)} %get-tuple-element.203), channel_id=1, source_target_pairs={{0,2},{2,0},{1,3},{3,1},{4,6},{6,4},{5,7},{7,5},{8,10},{10,8},{9,1... | collective-permute-start | bytes 1572872 | tf_op jit(solution)/shard_map/ppermute | solution.py:1024
  103.3 61.2 %collective-permute-start.15 = (bf16[1024,768]{1,0:T(8,128)(2,1)}, bf16[1024,768]{1,0:T(8,128)(2,1)}, u32[]{:S(2)}, u32[]{:S(2)}) collective-permute-start(bf16[1024,768]{1,0:T(8,128)(2,1)} %bitcast.24.co), channel_id=1, source_target_pairs={{1,2},{2,1},{5,6},{6,5},{9,10},{10,9},{13,14},{14,13},{17,18},{18,... | collective-permute-start | bytes 4718600 | tf_op jit(solution)/shard_map/ppermute | solution.py:1041
  118.9 3.9 collective-permute-start.13
  119.0 3.8 collective-permute-start.14
  233.7 231.2 %all-gather.9.cloned.1.call-start = ((), (), s32[]{:S(2)}) async-start(), calls=%async_computation.3 | async-start | bytes 5013504 | tf_op jit(solution)/shard_map/all_gather | solution.py:1149
  259.8 36.0 %collective-permute-start.17 = (bf16[2,1536,384]{2,1,0:T(8,128)(2,1)}, bf16[2,1536,384]{2,1,0:T(8,128)(2,1)S(1)}, u32[]{:S(2)}, u32[]{:S(2)}) collective-permute-start(bf16[2,1536,384]{2,1,0:T(8,128)(2,1)} %get-tuple-element.241), channel_id=1, source_target_pairs={{0,2},{2,0},{1,3},{3,1},{4,6},{6,4},{5,7},{7,5},{8,10},{10,8},{9,1... | collective-permute-start | bytes 7077896 | tf_op jit(solution)/shard_map/ppermute | solution.py:1024
  260.1 35.7 %collective-permute-start.18 = (bf16[1024,768]{1,0:T(8,128)(2,1)S(1)}, bf16[1024,768]{1,0:T(8,128)(2,1)}, u32[]{:S(2)}, u32[]{:S(2)}) collective-permute-start(bf16[1024,768]{1,0:T(8,128)(2,1)S(1)} %copy-done.8), channel_id=1, source_target_pairs={{0,2},{2,0},{1,3},{3,1},{4,6},{6,4},{5,7},{7,5},{8,10},{10,8},{9,1... | collective-permute-start | bytes 4718600 | tf_op jit(solution)/shard_map/ppermute | solution.py:1024
  260.3 35.5 %collective-permute-start.16 = (bf16[1024,768]{1,0:T(8,128)(2,1)}, bf16[1024,768]{1,0:T(8,128)(2,1)}, u32[]{:S(2)}, u32[]{:S(2)}) collective-permute-start(bf16[1024,768]{1,0:T(8,128)(2,1)} %get-tuple-element.240), channel_id=1, source_target_pairs={{1,2},{2,1},{5,6},{6,5},{9,10},{10,9},{13,14},{14,13},{17,18},{18,... | collective-permute-start | bytes 4718600 | tf_op jit(solution)/shard_map/ppermute | solution.py:1041
  269.6 26.2 %collective-permute-start.19 = (bf16[2,768,384]{2,1,0:T(8,128)(2,1)}, bf16[2,768,384]{2,1,0:T(8,128)(2,1)}, u32[]{:S(2)}, u32[]{:S(2)}) collective-permute-start(bf16[2,768,384]{2,1,0:T(8,128)(2,1)} %shard_map.264), channel_id=1, source_target_pairs={{0,2},{2,0},{1,3},{3,1},{4,6},{6,4},{5,7},{7,5},{8,10},{10,8},{9,1... | collective-permute-start | bytes 3538952 | tf_op jit(solution)/shard_map/ppermute | solution.py:1024
  307.8 23.1 %collective-permute-start.20 = (bf16[1500,384]{1,0:T(8,128)(2,1)}, bf16[1500,384]{1,0:T(8,128)(2,1)S(1)}, u32[]{:S(2)}, u32[]{:S(2)}) collective-permute-start(bf16[1500,384]{1,0:T(8,128)(2,1)} %get-tuple-element.261), channel_id=1, source_target_pairs={{0,2},{2,0},{1,3},{3,1},{4,6},{6,4},{5,7},{7,5},{8,10},{10,8},{9,1... | collective-permute-start | bytes 3456008 | tf_op jit(solution)/shard_map/ppermute | solution.py:1024
  326.5 11.0 %collective-permute-start.22 = (bf16[1024,384]{1,0:T(8,128)(2,1)}, bf16[1024,384]{1,0:T(8,128)(2,1)S(1)}, u32[]{:S(2)}, u32[]{:S(2)}) collective-permute-start(bf16[1024,384]{1,0:T(8,128)(2,1)} %get-tuple-element.268), channel_id=1, source_target_pairs={{0,2},{2,0},{1,3},{3,1},{4,6},{6,4},{5,7},{7,5},{8,10},{10,8},{9,1... | collective-permute-start | bytes 2359304 | tf_op jit(solution)/shard_map/ppermute | solution.py:1024
  331.3 39.2 %collective-permute-start.23 = (bf16[4,384,384]{2,1,0:T(8,128)(2,1)}, bf16[4,384,384]{2,1,0:T(8,128)(2,1)S(1)}, u32[]{:S(2)}, u32[]{:S(2)}) collective-permute-start(bf16[4,384,384]{2,1,0:T(8,128)(2,1)} %get-tuple-element.275), channel_id=1, source_target_pairs={{0,1},{1,0},{2,3},{3,2},{4,5},{5,4},{6,7},{7,6},{8,9},{9,8},{10,11... | collective-permute-start | bytes 3538952 | tf_op jit(solution)/shard_map/ppermute | solution.py:1024
  353.4 18.3 %collective-permute-start.25 = (bf16[3,1024,128]{2,1,0:T(8,128)(2,1)}, bf16[3,1024,128]{2,1,0:T(8,128)(2,1)S(1)}, u32[]{:S(2)}, u32[]{:S(2)}) collective-permute-start(bf16[3,1024,128]{2,1,0:T(8,128)(2,1)} %get-tuple-element.277.refs_3_), channel_id=1, source_target_pairs={{0,2},{2,0},{1,3},{3,1},{4,6},{6,4},{5,7},{7,5},{8,10},{10,8},{9,1... | collective-permute-start | bytes 2359304 | tf_op jit(solution)/shard_map/ppermute | solution.py:1024
  353.8 17.9 %collective-permute-start.24 = (bf16[1,384,384]{2,1,0:T(8,128)(2,1)S(1)}, bf16[1,384,384]{2,1,0:T(8,128)(2,1)S(1)}, u32[]{:S(2)}, u32[]{:S(2)}) collective-permute-start(bf16[1,384,384]{2,1,0:T(8,128)(2,1)S(1)} %copy-done.48), channel_id=1, source_target_pairs={{0,1},{1,0},{2,3},{3,2},{4,5},{5,4},{6,7},{7,6},{8,9},{9,8},{10,11... | collective-permute-start | bytes 884744 | tf_op jit(solution)/shard_map/ppermute | solution.py:1024
  376.6 136.4 %all-gather.11.cloned.1.call-start = ((), (), s32[]{:S(2)}) async-start(), calls=%async_computation.4 | async-start | bytes 3133440 | tf_op jit(solution)/shard_map/all_gather | solution.py:1172
  376.6 26.3 %collective-permute-start.28 = (bf16[1500,384]{1,0:T(8,128)(2,1)S(1)}, bf16[1500,384]{1,0:T(8,128)(2,1)S(1)}, u32[]{:S(2)}, u32[]{:S(2)}) collective-permute-start(bf16[1500,384]{1,0:T(8,128)(2,1)S(1)} %add_convert_fusion), channel_id=1, source_target_pairs={{1,2},{2,1},{5,6},{6,5},{9,10},{10,9},{13,14},{14,13},{17,18},{18,... | collective-permute-start | bytes 3456008 | tf_op jit(solution)/shard_map/ppermute | solution.py:1041
  379.8 15.8 %collective-permute-start.26 = (bf16[3,1024,128]{2,1,0:T(8,128)(2,1)S(1)}, bf16[3,1024,128]{2,1,0:T(8,128)(2,1)}, u32[]{:S(2)}, u32[]{:S(2)}) collective-permute-start(bf16[3,1024,128]{2,1,0:T(8,128)(2,1)S(1)} %copy-done.11), channel_id=1, source_target_pairs={{0,2},{2,0},{1,3},{3,1},{4,6},{6,4},{5,7},{7,5},{8,10},{10,8},{9,1... | collective-permute-start | bytes 2359304 | tf_op jit(solution)/shard_map/ppermute | solution.py:1024
  379.9 23.1 %collective-permute-start.27 = (bf16[5,192,384]{2,1,0:T(8,128)(2,1)}, bf16[5,192,384]{2,1,0:T(8,128)(2,1)}, u32[]{:S(2)}, u32[]{:S(2)}) collective-permute-start(bf16[5,192,384]{2,1,0:T(8,128)(2,1)} %get-tuple-element.301), channel_id=1, source_target_pairs={{0,4},{4,0},{1,5},{5,1},{2,6},{6,2},{3,7},{7,3},{8,12},{12,8},{9,1... | collective-permute-start | bytes 2211848 | tf_op jit(solution)/shard_map/ppermute | solution.py:1024
  403.0 24.0 %collective-permute-start.30 = (bf16[3,384,384]{2,1,0:T(8,128)(2,1)}, bf16[3,384,384]{2,1,0:T(8,128)(2,1)}, u32[]{:S(2)}, u32[]{:S(2)}) collective-permute-start(bf16[3,384,384]{2,1,0:T(8,128)(2,1)} %shard_map.276), channel_id=1, source_target_pairs={{0,1},{1,0},{2,3},{3,2},{4,5},{5,4},{6,7},{7,6},{8,9},{9,8},{10,11... | collective-permute-start | bytes 2654216 | tf_op jit(solution)/shard_map/ppermute | solution.py:1024
  403.6 11.1 %collective-permute-start.29 = (bf16[3,1024,128]{2,1,0:T(8,128)(2,1)S(1)}, bf16[3,1024,128]{2,1,0:T(8,128)(2,1)}, u32[]{:S(2)}, u32[]{:S(2)}) collective-permute-start(bf16[3,1024,128]{2,1,0:T(8,128)(2,1)S(1)} %copy-done.12), channel_id=1, source_target_pairs={{0,2},{2,0},{1,3},{3,1},{4,6},{6,4},{5,7},{7,5},{8,10},{10,8},{9,1... | collective-permute-start | bytes 2359304 | tf_op jit(solution)/shard_map/ppermute | solution.py:1024
  430.3 12.1 %collective-permute-start.31 = (bf16[3,192,384]{2,1,0:T(8,128)(2,1)}, bf16[3,192,384]{2,1,0:T(8,128)(2,1)S(1)}, u32[]{:S(2)}, u32[]{:S(2)}) collective-permute-start(bf16[3,192,384]{2,1,0:T(8,128)(2,1)} %get-tuple-element.320), channel_id=1, source_target_pairs={{0,4},{4,0},{1,5},{5,1},{2,6},{6,2},{3,7},{7,3},{8,12},{12,8},{9,1... | collective-permute-start | bytes 1327112 | tf_op jit(solution)/shard_map/ppermute | solution.py:1024
  430.3 15.5 %collective-permute-start.32 = (bf16[5,48,384]{2,1,0:T(8,128)(2,1)}, bf16[5,48,384]{2,1,0:T(8,128)(2,1)S(1)}, u32[]{:S(2)}, u32[]{:S(2)}) collective-permute-start(bf16[5,48,384]{2,1,0:T(8,128)(2,1)} %get-tuple-element.323), channel_id=1, source_target_pairs={{0,8},{8,0},{16,24},{24,16},{1,9},{9,1},{17,25},{25,17},{2,10},{10... | collective-permute-start | bytes 552968 | tf_op jit(solution)/shard_map/ppermute | solution.py:1020
  431.3 14.4 %collective-permute-start.33 = (bf16[5,48,384]{2,1,0:T(8,128)(2,1)}, bf16[5,48,384]{2,1,0:T(8,128)(2,1)S(1)}, u32[]{:S(2)}, u32[]{:S(2)}) collective-permute-start(bf16[5,48,384]{2,1,0:T(8,128)(2,1)} %get-tuple-element.324), channel_id=1, source_target_pairs={{0,16},{8,24},{16,0},{24,8},{1,17},{9,25},{17,1},{25,9},{2,18},{10... | collective-permute-start | bytes 552968 | tf_op jit(solution)/shard_map/ppermute | solution.py:1020
  433.4 12.8 %collective-permute-start.34 = (bf16[5,48,384]{2,1,0:T(8,128)(2,1)S(1)}, bf16[5,48,384]{2,1,0:T(8,128)(2,1)S(1)}, u32[]{:S(2)}, u32[]{:S(2)}) collective-permute-start(bf16[5,48,384]{2,1,0:T(8,128)(2,1)S(1)} %copy-done.49), channel_id=1, source_target_pairs={{0,24},{8,16},{16,8},{24,0},{1,25},{9,17},{17,9},{25,1},{2,26},{10... | collective-permute-start | bytes 552968 | tf_op jit(solution)/shard_map/ppermute | solution.py:1020
  449.5 60.7 %collective-permute-start.43 = (bf16[1024,768]{1,0:T(8,128)(2,1)}, bf16[1024,768]{1,0:T(8,128)(2,1)}, u32[]{:S(2)}, u32[]{:S(2)}) collective-permute-start(bf16[1024,768]{1,0:T(8,128)(2,1)} %get-tuple-element.351), channel_id=1, source_target_pairs={{1,2},{2,1},{5,6},{6,5},{9,10},{10,9},{13,14},{14,13},{17,18},{18,... | collective-permute-start | bytes 4718600 | tf_op jit(solution)/shard_map/ppermute | solution.py:1041
  456.4 17.2 %collective-permute-start.38 = (f32[24,384]{1,0:T(8,128)}, f32[24,384]{1,0:T(8,128)S(1)}, u32[]{:S(2)}, u32[]{:S(2)}) collective-permute-start(f32[24,384]{1,0:T(8,128)} %get-tuple-element.341), channel_id=1, source_target_pairs={{0,1},{1,0},{2,3},{3,2},{4,5},{5,4},{6,7},{7,6},{8,9},{9,8},{10,11... | collective-permute-start | bytes 110600 | tf_op jit(solution)/shard_map/ppermute | solution.py:1024
  456.4 15.5 %collective-permute-start.35 = (bf16[3,48,384]{2,1,0:T(8,128)(2,1)}, bf16[3,48,384]{2,1,0:T(8,128)(2,1)S(1)}, u32[]{:S(2)}, u32[]{:S(2)}) collective-permute-start(bf16[3,48,384]{2,1,0:T(8,128)(2,1)} %get-tuple-element.327), channel_id=1, source_target_pairs={{0,8},{8,0},{16,24},{24,16},{1,9},{9,1},{17,25},{25,17},{2,10},{10... | collective-permute-start | bytes 331784 | tf_op jit(solution)/shard_map/ppermute | solution.py:1020
  459.9 12.1 %collective-permute-start.36 = (bf16[3,48,384]{2,1,0:T(8,128)(2,1)}, bf16[3,48,384]{2,1,0:T(8,128)(2,1)S(1)}, u32[]{:S(2)}, u32[]{:S(2)}) collective-permute-start(bf16[3,48,384]{2,1,0:T(8,128)(2,1)} %get-tuple-element.328), channel_id=1, source_target_pairs={{0,16},{8,24},{16,0},{24,8},{1,17},{9,25},{17,1},{25,9},{2,18},{10... | collective-permute-start | bytes 331784 | tf_op jit(solution)/shard_map/ppermute | solution.py:1020
  461.0 12.6 %collective-permute-start.37 = (bf16[3,48,384]{2,1,0:T(8,128)(2,1)}, bf16[3,48,384]{2,1,0:T(8,128)(2,1)S(1)}, u32[]{:S(2)}, u32[]{:S(2)}) collective-permute-start(bf16[3,48,384]{2,1,0:T(8,128)(2,1)} %get-tuple-element.329), channel_id=1, source_target_pairs={{0,24},{8,16},{16,8},{24,0},{1,25},{9,17},{17,9},{25,1},{2,26},{10... | collective-permute-start | bytes 331784 | tf_op jit(solution)/shard_map/ppermute | solution.py:1020
  476.7 9.4 %collective-permute-start.41 = (bf16[4,48,384]{2,1,0:T(8,128)(2,1)}, bf16[4,48,384]{2,1,0:T(8,128)(2,1)S(1)}, u32[]{:S(2)}, u32[]{:S(2)}) collective-permute-start(bf16[4,48,384]{2,1,0:T(8,128)(2,1)} %shard_map.283.p0), channel_id=1, source_target_pairs={{0,24},{8,16},{16,8},{24,0},{1,25},{9,17},{17,9},{25,1},{2,26},{10... | collective-permute-start | bytes 442376 | tf_op jit(solution)/shard_map/ppermute | solution.py:1020
  480.3 25.9 %collective-permute-start.40 = (bf16[4,48,384]{2,1,0:T(8,128)(2,1)}, bf16[4,48,384]{2,1,0:T(8,128)(2,1)S(1)}, u32[]{:S(2)}, u32[]{:S(2)}) collective-permute-start(bf16[4,48,384]{2,1,0:T(8,128)(2,1)} %shard_map.283.p0), channel_id=1, source_target_pairs={{0,16},{8,24},{16,0},{24,8},{1,17},{9,25},{17,1},{25,9},{2,18},{10... | collective-permute-start | bytes 442376 | tf_op jit(solution)/shard_map/ppermute | solution.py:1020
  483.3 22.9 %collective-permute-start.39 = (bf16[4,48,384]{2,1,0:T(8,128)(2,1)}, bf16[4,48,384]{2,1,0:T(8,128)(2,1)S(1)}, u32[]{:S(2)}, u32[]{:S(2)}) collective-permute-start(bf16[4,48,384]{2,1,0:T(8,128)(2,1)} %shard_map.283.p0), channel_id=1, source_target_pairs={{0,8},{8,0},{16,24},{24,16},{1,9},{9,1},{17,25},{25,17},{2,10},{10... | collective-permute-start | bytes 442376 | tf_op jit(solution)/shard_map/ppermute | solution.py:1020
  510.2 13.1 %collective-permute-start.42 = (bf16[4,192,384]{2,1,0:T(8,128)(2,1)}, bf16[4,192,384]{2,1,0:T(8,128)(2,1)S(1)}, u32[]{:S(2)}, u32[]{:S(2)}) collective-permute-start(bf16[4,192,384]{2,1,0:T(8,128)(2,1)} %shard_map.284.refs_0_), channel_id=1, source_target_pairs={{0,4},{4,0},{1,5},{5,1},{2,6},{6,2},{3,7},{7,3},{8,12},{12,8},{9,1... | collective-permute-start | bytes 1769480 | tf_op jit(solution)/shard_map/ppermute | solution.py:1024
  518.2 7.9 %collective-permute-start.44 = (bf16[4,192,384]{2,1,0:T(8,128)(2,1)S(1)}, bf16[4,192,384]{2,1,0:T(8,128)(2,1)S(1)}, u32[]{:S(2)}, u32[]{:S(2)}) collective-permute-start(bf16[4,192,384]{2,1,0:T(8,128)(2,1)S(1)} %copy-done.19), channel_id=1, source_target_pairs={{0,2},{2,0},{1,3},{3,1},{4,6},{6,4},{5,7},{7,5},{8,10},{10,8},{9,1... | collective-permute-start | bytes 1769480 | tf_op jit(solution)/shard_map/ppermute | solution.py:1024
  523.3 4.4 collective-permute-start.45
  (54 other events, 305.4 us)
Sparse Core Ops, SparseCore 0:
  68.1 55.5 all-gather.6
  233.8 142.1 reduce-scatter.1
  378.5 56.2 all-gather.8
  449.6 59.6 all-gather.10
